TPU v7x, 32 devices: a whole 2x2x4 slice. The times are simulated.
32 devices in a mesh: dp: 8 (over y, x, core), tensor: 4 (over z).
Axes of the slice: x: 2, y: 2, z: 4, core: 2. Of those that a mesh axis runs over, the one named last changes fastest.
Arguments:
- hidden: bfloat16 [8, 1024, 1024], P('dp', 'tensor'), may hold values from -6 to 6
- seg_ids: int32 [8, 1024], P('dp', 'tensor'), may hold values from 0 to 4, as said below
- cotangent: bfloat16 [8, 1024, 1024], P('dp', 'tensor'), may hold values from -6 to 6
- norm_gain: bfloat16 [1024], P('dp'), may hold values from 0.099609375 to 1.8984375
- w_in_z: bfloat16 [1024, 2048], P('dp', 'tensor'), may hold values from -0.1875 to 0.1875
- w_in_x: bfloat16 [1024, 2048], P('dp', 'tensor'), may hold values from -0.1875 to 0.1875
- w_in_bc: bfloat16 [1024, 256], P('dp'), may hold values from -0.1875 to 0.1875
- w_in_dt: bfloat16 [1024, 32], P('dp', 'tensor'), may hold values from -0.1875 to 0.1875
- conv_x: float32 [4, 2048], P(None, 'tensor'), may hold values from -3 to 3
- conv_x_bias: float32 [2048], P('tensor'), may hold values from -1.75 to 1.75
- conv_bc: float32 [4, 256], replicated, may hold values from -3 to 3
- conv_bc_bias: float32 [256], replicated, may hold values from -1.75 to 1.75
- dt_bias: float32 [32], P('tensor'), may hold values from -5 to -1
- a_log: float32 [32], P('tensor'), may hold values from 0 to 2.77
- d_skip: float32 [32], P('tensor'), may hold values from 0.5 to 1.5
- gate_gain: float32 [2048], P('tensor'), may hold values from 0.1 to 1.9
- w_out: bfloat16 [1024, 2048], P('dp', 'tensor'), may hold values from -0.125 to 0.125
Outputs:
- layer_out: bfloat16 [8, 1024, 1024], P('dp', 'tensor')
- grad_hidden: bfloat16 [8, 1024, 1024], P('dp', 'tensor')
- grad_norm_gain: float32 [1024], P('dp')
- grad_w_in_z: float32 [1024, 2048], P('dp', 'tensor')
- grad_w_in_x: float32 [1024, 2048], P('dp', 'tensor')
- grad_w_in_bc: float32 [1024, 256], P('dp')
- grad_w_in_dt: float32 [1024, 32], P('dp', 'tensor')
- grad_conv_x: float32 [4, 2048], P(None, 'tensor')
- grad_conv_x_bias: float32 [2048], P('tensor')
- grad_conv_bc: float32 [4, 256], replicated
- grad_conv_bc_bias: float32 [256], replicated
- grad_dt_bias: float32 [32], P('tensor')
- grad_a_log: float32 [32], P('tensor')
- grad_d_skip: float32 [32], P('tensor')
- grad_gate_gain: float32 [2048], P('tensor')
- grad_w_out: float32 [1024, 2048], P('dp', 'tensor')
Inputs may be any that keep to these rules, and one draw needn't show every extreme that they name: `seg_ids`: within a row the ids never fall; ids restart in each row and are compared within a row only; id 0 marks padding, which comes after all documents of its row; in every draw some row is a single document of 1024 positions, and other rows are filled to between 128 and 1024 positions.
All inputs are finite; a program needn't handle non-finite values.
Results may differ from a plain program's by a relative error of at most 0.011.
Values may be sent and summed in bfloat16 or wider, within the bound.
No kernel may reach another device: no remote copies, remote signals or barrier semaphores. Data moves between devices by JAX's collectives and lax.ppermute only.
A program may use at most 128 MiB of HBM per device.

v0:
```python
import jax
import jax.numpy as jnp
from jax import lax
from jax.sharding import PartitionSpec as P

N = 128
CONV = 4
GROUP = 256


full_precision = lax.Precision.HIGHEST
norm_epsilon = 1e-05


def causal_conv(values, seg_row, kernel, conv_bias):
    length = values.shape[0]
    padded = jnp.pad(values, ((CONV - 1, 0), (0, 0)))
    seg_padded = jnp.pad(seg_row, (CONV - 1, 0), constant_values=-1)
    summed = conv_bias[None, :] + jnp.zeros_like(values)
    for offset in range(CONV):
        matches = (seg_padded[offset : offset + length] == seg_row).astype(jnp.float32)
        summed = (
            summed + kernel[offset][None, :] * padded[offset : offset + length] * matches[:, None]
        )
    return jax.nn.silu(summed)


def block_step(carry_state, inputs):
    x_block, dt_block, decay_block, b_block, c_block, seg_block, prev_seg = inputs
    block_len = seg_block.shape[0]
    head_count = dt_block.shape[1]
    x_heads = x_block.reshape(block_len, head_count, -1)
    cumulative = jnp.cumsum(decay_block, axis=0)
    places = jnp.arange(block_len)
    keep_mask = (places[:, None] >= places[None, :]) & (seg_block[:, None] == seg_block[None, :])
    spread_mask = keep_mask[:, :, None]
    decays = jnp.where(
        spread_mask,
        jnp.exp(jnp.where(spread_mask, cumulative[:, None, :] - cumulative[None, :, :], -60.0)),
        0.0,
    )
    scores = jnp.dot(c_block, b_block.T, precision=full_precision)
    weighted = x_heads * dt_block[:, :, None]
    y_inner = jnp.einsum(
        "tsh,shp->thp", scores[:, :, None] * decays, weighted, precision=full_precision
    )
    from_prev = (seg_block == prev_seg).astype(jnp.float32)
    carried = jnp.einsum("tn,hpn->thp", c_block, carry_state, precision=full_precision)
    y_outer = carried * (jnp.exp(cumulative) * from_prev[:, None])[:, :, None]
    last_seg = seg_block[block_len - 1]
    to_end = (
        jnp.exp(cumulative[block_len - 1][None, :] - cumulative)
        * (seg_block == last_seg).astype(jnp.float32)[:, None]
    )
    new_state = jnp.einsum(
        "shp,sn->hpn", weighted * to_end[:, :, None], b_block, precision=full_precision
    )
    survive = jnp.exp(cumulative[block_len - 1]) * (last_seg == prev_seg).astype(jnp.float32)
    new_state = new_state + carry_state * survive[:, None, None]
    return (new_state, (y_inner + y_outer).reshape(block_len, -1))


def scan_row(x_row, dt_row, decay_row, b_row, c_row, seg_row):
    length = seg_row.shape[0]
    blocks = length // GROUP
    head_count = dt_row.shape[1]
    head_size = x_row.shape[1] // head_count

    def to_blocks(source):
        return source.reshape((blocks, GROUP) + source.shape[1:])

    seg_blocks = to_blocks(seg_row)
    prev_segs = jnp.concatenate(
        [jnp.full((1,), -1, jnp.int32), seg_blocks[:-1, GROUP - 1].astype(jnp.int32)]
    )
    initial = jnp.zeros((head_count, head_size, N), jnp.float32)
    final_state, outputs = lax.scan(
        jax.checkpoint(block_step),
        initial,
        (
            to_blocks(x_row),
            to_blocks(dt_row),
            to_blocks(decay_row),
            to_blocks(b_row),
            to_blocks(c_row),
            seg_blocks,
            prev_segs,
        ),
    )
    return outputs.reshape(length, -1)


def mixer_core(
    z_proj,
    x_proj,
    bc_proj,
    dt_proj,
    seg_row,
    conv_x,
    conv_x_bias,
    conv_bc,
    conv_bc_bias,
    dt_bias,
    a_log,
    d_skip,
):
    x_conv = causal_conv(x_proj, seg_row, conv_x, conv_x_bias)
    bc_conv = causal_conv(bc_proj, seg_row, conv_bc, conv_bc_bias)
    dt_row = jax.nn.softplus(dt_proj + dt_bias[None, :])
    decay_row = -dt_row * jnp.exp(a_log)[None, :]
    scanned = scan_row(x_conv, dt_row, decay_row, bc_conv[:, :N], bc_conv[:, N:], seg_row)
    head_count = dt_row.shape[1]
    length = x_conv.shape[0]
    skipped = (x_conv.reshape(length, head_count, -1) * d_skip[None, :, None]).reshape(length, -1)
    return (scanned + skipped) * jax.nn.silu(z_proj)


def shards(
    hidden,
    seg_ids,
    cotangent,
    norm_gain,
    w_in_z,
    w_in_x,
    w_in_bc,
    w_in_dt,
    conv_x,
    conv_x_bias,
    conv_bc,
    conv_bc_bias,
    dt_bias,
    a_log,
    d_skip,
    gate_gain,
    w_out,
):
    full_inner = gate_gain.shape[0] * lax.axis_size("tensor")
    gathered = (
        lax.all_gather(norm_gain, "dp", axis=0, tiled=True),
        lax.all_gather(w_in_z, "dp", axis=0, tiled=True),
        lax.all_gather(w_in_x, "dp", axis=0, tiled=True),
        lax.all_gather(w_in_bc, "dp", axis=0, tiled=True),
        lax.all_gather(w_in_dt, "dp", axis=0, tiled=True),
        lax.all_gather(w_out, "dp", axis=0, tiled=True),
    )
    gain_full, z_full, x_full, bc_full, dt_full, out_full = gathered
    hidden_rows = jnp.swapaxes(hidden, 0, 1).astype(jnp.float32)
    inverse = lax.rsqrt(jnp.mean(hidden_rows * hidden_rows, axis=2, keepdims=True) + norm_epsilon)
    scaled_in = hidden_rows * inverse
    normed = (scaled_in * gain_full.astype(jnp.float32)).astype(jnp.bfloat16)
    tokens, seg_full = (
        lax.all_gather(normed, "tensor", axis=0, tiled=True),
        lax.all_gather(jnp.swapaxes(seg_ids, 0, 1), "tensor", axis=0, tiled=True),
    )
    z_proj = jnp.einsum("trd,dc->trc", tokens, z_full, preferred_element_type=jnp.float32)
    x_proj = jnp.einsum("trd,dc->trc", tokens, x_full, preferred_element_type=jnp.float32)
    bc_proj = jnp.einsum("trd,dc->trc", tokens, bc_full, preferred_element_type=jnp.float32)
    dt_proj = jnp.einsum("trd,dc->trc", tokens, dt_full, preferred_element_type=jnp.float32)
    row_core = jax.vmap(
        mixer_core, in_axes=(1, 1, 1, 1, 1, None, None, None, None, None, None, None), out_axes=1
    )

    def local_core(
        z_in,
        x_in,
        bc_in,
        dt_in,
        kernel_x,
        bias_x,
        kernel_bc,
        bias_bc,
        step_bias,
        log_rate,
        skip_weight,
    ):
        return row_core(
            z_in,
            x_in,
            bc_in,
            dt_in,
            seg_full,
            kernel_x,
            bias_x,
            kernel_bc,
            bias_bc,
            step_bias,
            log_rate,
            skip_weight,
        )

    gated, core_pullback = jax.vjp(
        local_core,
        z_proj,
        x_proj,
        bc_proj,
        dt_proj,
        conv_x,
        conv_x_bias,
        conv_bc,
        conv_bc_bias,
        dt_bias,
        a_log,
        d_skip,
    )
    live = (seg_full > 0).astype(jnp.float32)[:, :, None]
    square_sum = lax.psum(jnp.sum(gated * gated, axis=2), "tensor")
    gate_inverse = lax.rsqrt(square_sum / full_inner + norm_epsilon)[:, :, None]
    gain_inner = gate_gain[None, None, :]
    normed_out = (gated * gate_inverse * gain_inner * live).astype(jnp.bfloat16)
    total_rows = normed_out.shape[0]
    local_rows = total_rows // lax.axis_size("tensor")
    mixed = lax.psum_scatter(
        jnp.einsum("trc,dc->trd", normed_out, out_full, preferred_element_type=jnp.float32).astype(
            jnp.bfloat16
        ),
        "tensor",
        scatter_dimension=0,
        tiled=True,
    ).astype(jnp.float32)
    layer_out = jnp.swapaxes(hidden_rows + mixed, 0, 1).astype(jnp.bfloat16)
    cot_local = jnp.swapaxes(cotangent, 0, 1)
    cot_rows = lax.all_gather(cot_local, "tensor", axis=0, tiled=True)
    regathered = (
        lax.all_gather(norm_gain, "dp", axis=0, tiled=True),
        lax.all_gather(w_in_z, "dp", axis=0, tiled=True),
        lax.all_gather(w_in_x, "dp", axis=0, tiled=True),
        lax.all_gather(w_in_bc, "dp", axis=0, tiled=True),
        lax.all_gather(w_in_dt, "dp", axis=0, tiled=True),
        lax.all_gather(w_out, "dp", axis=0, tiled=True),
    )
    gain_full, z_full, x_full, bc_full, dt_full, out_full = regathered
    grad_normed_out = (
        jnp.einsum("trd,dc->trc", cot_rows, out_full, preferred_element_type=jnp.float32) * live
    )
    grad_out_weight = jnp.einsum(
        "trd,trc->dc", cot_rows, normed_out, preferred_element_type=jnp.float32
    )
    grad_gate_gain = jnp.sum(grad_normed_out * gated * gate_inverse, axis=(0, 1))
    along = lax.psum(jnp.sum(gated * gain_inner * grad_normed_out, axis=2), "tensor")
    grad_gated = (
        gate_inverse * gain_inner * grad_normed_out
        - gated * gate_inverse**3 * (along / full_inner)[:, :, None]
    )
    core_grads = core_pullback(grad_gated)
    grad_z = core_grads[0].astype(jnp.bfloat16)
    grad_x = core_grads[1].astype(jnp.bfloat16)
    grad_bc = core_grads[2].astype(jnp.bfloat16)
    grad_dt = core_grads[3].astype(jnp.bfloat16)
    grad_z_weight = jnp.einsum("trd,trc->dc", tokens, grad_z, preferred_element_type=jnp.float32)
    grad_x_weight = jnp.einsum("trd,trc->dc", tokens, grad_x, preferred_element_type=jnp.float32)
    grad_bc_weight = jnp.einsum("trd,trc->dc", tokens, grad_bc, preferred_element_type=jnp.float32)
    grad_dt_weight = jnp.einsum("trd,trc->dc", tokens, grad_dt, preferred_element_type=jnp.float32)
    term_sum = jnp.einsum("trc,dc->trd", grad_z, z_full, preferred_element_type=jnp.float32)
    term_sum = term_sum + jnp.einsum(
        "trc,dc->trd", grad_x, x_full, preferred_element_type=jnp.float32
    )
    term_sum = term_sum + jnp.einsum(
        "trc,dc->trd", grad_bc, bc_full, preferred_element_type=jnp.float32
    )
    whole_sum = lax.psum(
        (
            term_sum
            + jnp.einsum("trc,dc->trd", grad_dt, dt_full, preferred_element_type=jnp.float32)
        ).astype(jnp.bfloat16),
        "tensor",
    ).astype(jnp.float32)
    grad_normed = lax.dynamic_slice_in_dim(
        whole_sum, lax.axis_index("tensor") * local_rows, local_rows, 0
    )
    grad_gain_part = jnp.sum(grad_normed * scaled_in, axis=(0, 1))
    grad_scaled = grad_normed * gain_full.astype(jnp.float32)
    grad_pre = inverse * (
        grad_scaled - scaled_in * jnp.mean(grad_scaled * scaled_in, axis=2, keepdims=True)
    )
    grad_hidden = jnp.swapaxes(cot_local.astype(jnp.float32) + grad_pre, 0, 1).astype(jnp.bfloat16)
    summed = (
        lax.psum_scatter(grad_gain_part, "dp", scatter_dimension=0, tiled=True),
        lax.psum_scatter(grad_z_weight, "dp", scatter_dimension=0, tiled=True),
        lax.psum_scatter(grad_x_weight, "dp", scatter_dimension=0, tiled=True),
        lax.psum_scatter(grad_bc_weight, "dp", scatter_dimension=0, tiled=True),
        lax.psum_scatter(grad_dt_weight, "dp", scatter_dimension=0, tiled=True),
        lax.psum_scatter(grad_out_weight, "dp", scatter_dimension=0, tiled=True),
    )
    head_sums = lax.psum(
        (
            core_grads[4],
            core_grads[5],
            core_grads[6],
            core_grads[7],
            core_grads[8],
            core_grads[9],
            core_grads[10],
            grad_gate_gain,
        ),
        "dp",
    )
    shared = lax.psum((summed[0], summed[3], head_sums[2], head_sums[3]), "tensor")
    return (
        layer_out,
        grad_hidden,
        shared[0],
        summed[1],
        summed[2],
        shared[1],
        summed[4],
        head_sums[0],
        head_sums[1],
        shared[2],
        shared[3],
        head_sums[4],
        head_sums[5],
        head_sums[6],
        head_sums[7],
        summed[5],
    )


def solution(mesh):
    in_specs = (
        P("dp", "tensor", None),
        P("dp", "tensor"),
        P("dp", "tensor", None),
        P("dp"),
        P("dp", "tensor"),
        P("dp", "tensor"),
        P("dp", None),
        P("dp", "tensor"),
        P(None, "tensor"),
        P("tensor"),
        P(),
        P(),
        P("tensor"),
        P("tensor"),
        P("tensor"),
        P("tensor"),
        P("dp", "tensor"),
    )
    out_specs = (
        P("dp", "tensor", None),
        P("dp", "tensor", None),
        P("dp"),
        P("dp", "tensor"),
        P("dp", "tensor"),
        P("dp", None),
        P("dp", "tensor"),
        P(None, "tensor"),
        P("tensor"),
        P(),
        P(),
        P("tensor"),
        P("tensor"),
        P("tensor"),
        P("tensor"),
        P("dp", "tensor"),
    )
    return jax.shard_map(shards, mesh=mesh, in_specs=in_specs, out_specs=out_specs, check_vma=False)
```

profile of v0, /device:TPU:0, one launch (start us, length us, event | category | flops | bytes accessed | tf_op | source)
XLA Modules:
  0.0 722.0 jit_solution(3537949391519004188)
XLA Ops:
  7.3 10.3 %all-gather.2 = bf16[8,1,128]{2,1,0:T(2,128)(2,1)S(1)} all-gather(bf16[1,1,128]{2,1,0:T(2,128)(2,1)} %bitcast.859), channel_id=1, replica_groups=mesh['dp'=8,'tensor'=4] {'dp'}, dimensions={0}, use_global_device_ids=true | all-gather | bytes 2304 | tf_op jit(solution)/shard_map/all_gather | solution.py:139
  18.9 2.0 fusion.159
  23.6 9.7 %all_gather.38 = bf16[1024,256]{1,0:T(8,128)(2,1)S(1)} all-gather(bf16[128,256]{1,0:T(8,128)(2,1)S(1)} %copy-done.18), channel_id=1, replica_groups=mesh['dp'=8,'tensor'=4] {'dp'}, dimensions={0}, use_global_device_ids=true | all-gather | bytes 589824 | tf_op jit(solution)/shard_map/all_gather | solution.py:142
  33.4 11.3 %all-gather = s32[1,1024]{1,0:T(1,128)S(1)} all-gather(s32[1,256]{1,0:T(1,128)S(1)} %copy-done.43), channel_id=2, replica_groups=mesh['dp'=8,'tensor'=4] {'tensor'}, dimensions={1}, use_global_device_ids=true | all-gather | bytes 5120 | tf_op jit(solution)/shard_map/all_gather | solution.py:153
  45.5 8.1 %all_gather.37 = bf16[1024,8]{0,1:T(8,128)(2,1)S(1)} all-gather(bf16[128,8]{0,1:T(8,128)(2,1)S(1)} %copy-done.38), channel_id=1, replica_groups=mesh['dp'=8,'tensor'=4] {'dp'}, dimensions={0}, use_global_device_ids=true | all-gather | bytes 18432 | tf_op jit(solution)/shard_map/all_gather | solution.py:143
  56.3 10.9 %all-gather.9.cloned.1.call-done = bf16[1024,1,1024]{2,0,1:T(8,128)(2,1)} async-done(((bf16[256,1,1024]{2,0,1:T(8,128)(2,1)}), bf16[1024,1,1024]{2,0,1:T(8,128)(2,1)}) %all-gather.9.cloned.1.call-update) | async-done | bytes 2097168 | tf_op jit(solution)/shard_map/all_gather | solution.py:152
  67.3 2.3 fusion.133
  69.6 1.9 multiply_bitcast_fusion.13
  72.7 18.8 %all-gather.11.cloned.1.call-done = bf16[1024,512]{1,0:T(8,128)(2,1)} async-done(((bf16[128,512]{1,0:T(8,128)(2,1)}), bf16[1024,512]{1,0:T(8,128)(2,1)}) %all-gather.11.cloned.1.call-update) | async-done | bytes 1048592 | tf_op jit(solution)/shard_map/all_gather | solution.py:141
  91.4 2.5 fusion.137
  93.9 2.8 fusion.140
  96.8 3.6 copy.130
  100.4 2.9 negate_multiply_fusion
  104.9 71.2 %while.41 = (s32[]{:T(128)}, f32[1,8,64,128]{3,2,1,0:T(8,128)S(1)}, f32[4,1,256,512]{3,2,0,1:T(8,128)}, f32[4,1,8,64,128]{4,3,2,1,0:T(8,128)}, f32[4,1,256,512]{...) while((s32[]{:T(128)}, f32[1,8,64,128]{3,2,1,0:T(8,128)S(1)}, ...), condition=%wide.region_4.5_spmd.clone, body=%wide.region_1.4_spmd.clone.sunk | while | flops 909517824 | bytes 11040699 | solution.py:77
  113.6 3.3 fusion.288
  121.1 1.6 fusion.283
  131.4 3.3 fusion.288
  138.9 1.6 fusion.283
  149.2 3.3 fusion.288
  156.7 1.6 fusion.283
  167.0 3.3 fusion.288
  174.5 1.6 fusion.283
  176.2 6.7 multiply_reduce_fusion.7
  182.9 11.7 %psum.105 = f32[1024,1]{0,1:T(1,128)S(1)} all-reduce(f32[1024,1]{0,1:T(1,128)S(1)} %bitcast.853), channel_id=1, replica_groups=mesh['dp'=8,'tensor'=4] {'tensor'}, use_global_device_ids=true, to_apply=%region_6.7 | all-reduce | flops 1024 | bytes 8192 | tf_op jit(solution)/shard_map/psum | solution.py:206
  194.7 5.4 multiply_reduce_fusion.3
  200.0 8.7 %psum.106 = f32[1024,1]{0,1:T(1,128)S(1)} all-reduce(f32[1024,1]{0,1:T(1,128)S(1)} %bitcast.854), channel_id=1, replica_groups=mesh['dp'=8,'tensor'=4] {'tensor'}, use_global_device_ids=true, to_apply=%region_9.10 | all-reduce | flops 1024 | bytes 8192 | tf_op jit(solution)/shard_map/psum | solution.py:239
  208.8 5.7 multiply_reduce_fusion.4
  214.4 1.6 broadcast.837.clone
  217.7 102.5 %while.42 = (s32[]{:T(128)}, f32[1,8,64,128]{3,2,1,0:T(8,128)S(1)}, f32[4,1,256,512]{3,2,0,1:T(8,128)}, f32[4,1,256,8]{2,3,1,0:T(8,128)S(1)}, f32[4,1,256,8]{2,3...) while((s32[]{:T(128)}, f32[1,8,64,128]{3,2,1,0:T(8,128)S(1)}, ...), condition=%wide.region_23.24_spmd.clone, body=%wide.region_10.23_spmd.clone.sunk | while | flops 2124708864 | bytes 21116792 | solution.py:77
  224.7 3.0 fusion.312
  236.0 2.0 multiply_reduce_fusion.12
  239.0 2.5 reduce-window.74
  250.4 3.0 fusion.312
  261.6 2.0 multiply_reduce_fusion.12
  264.6 2.5 reduce-window.74
  276.0 3.0 fusion.312
  287.3 2.0 multiply_reduce_fusion.12
  290.2 2.5 reduce-window.74
  301.6 3.0 fusion.312
  312.9 2.0 multiply_reduce_fusion.12
  315.9 2.5 reduce-window.74
  320.3 7.2 fusion.116
  327.5 3.7 multiply_bitcast_fusion.8
  334.1 2.7 fusion.202
  336.8 1.7 fusion.125
  338.7 4.6 fusion.164
  347.5 2.1 fusion.141
  349.7 4.9 fusion.142
  354.7 4.5 convert_bitcast_fusion
  360.3 13.1 %reduce-scatter.13.cloned.1.call-done = f32[128,256]{1,0:T(8,128)} async-done(((f32[1024,256]{1,0:T(8,128)}), f32[128,256]{1,0:T(8,128)}) %reduce-scatter.13.cloned.1.call-update) | async-done | bytes 131088 | tf_op jit(solution)/shard_map/reduce_scatter | solution.py:280
  373.7 2.7 fusion.127
  377.6 2.6 fusion.129
  382.3 80.0 %all-reduce.29.cloned.1.call-done = bf16[1024,1,1024]{2,0,1:T(8,128)(2,1)} async-done(((bf16[1024,1,1024]{2,0,1:T(8,128)(2,1)}), bf16[1024,1,1024]{2,0,1:T(8,128)(2,1)}) %all-reduce.29.cloned.1.call-update) | async-done | bytes 2097168 | tf_op jit(solution)/shard_map/psum | solution.py:260
  463.8 24.6 %all-reduce.24 = (f32[1024]{0:T(1024)S(1)}, f32[4,512]{1,0:T(4,128)}, f32[512]{0:T(512)}, f32[4,256]{1,0:T(4,128)S(1)}, f32[256]{0:T(256)S(1)}, /*index=5*/f32[8]{0:T(128)}, f32[8]{0:T(128)}, f32[8]{0:T(128)}, f32[512]{0:T(512)}) all-reduce(f32[1024]{0:T(1024)S(1)} %get-tuple-element.781, ...), channel_id=5, replica_groups=mesh['dp'=8,'tensor'=4] {'dp'}, use_global_device_ids=true, to_apply=%region_27.28.clone | all-reduce | flops 5400 | bytes 43200
  488.5 10.6 %all-reduce.25 = (f32[128]{0:T(128)}, f32[4,256]{1,0:T(4,128)}, f32[256]{0:T(256)}) all-reduce(f32[128]{0:T(128)S(1)} %dynamic-slice.1, f32[4,256]{1,0:T(4,128)S(1)} %get-tuple-element.847, f32[256]{0:T(256)S(1)} %get-tuple-element.848), channel_id=1, replica_groups=mesh['dp'=8,'tensor'=4] {'tensor'}, use_global_device_ids=true, to_apply=%region_28.29 | all-reduce | flops 1408 | bytes 11264 | tf_op jit(solution)/shard_map/psum | solution.py:297
  499.1 7.0 reduce-scatter.17.cloned.1.call-done
  506.2 1.8 copy.146
  508.0 44.4 %reduce-scatter.7.cloned.1.call-done = bf16[256,1,1024]{2,0,1:T(8,128)(2,1)} async-done(((bf16[1024,1,1024]{2,0,1:T(8,128)(2,1)}), bf16[256,1,1024]{2,0,1:T(8,128)(2,1)}) %reduce-scatter.7.cloned.1.call-update) | async-done | bytes 524304 | tf_op jit(solution)/shard_map/reduce_scatter | solution.py:212
  552.4 2.6 fusion.181
  555.0 31.7 %reduce-scatter.15.cloned.1.call-done = f32[128,8]{0,1:T(8,128)} async-done(((f32[1024,8]{0,1:T(8,128)}), f32[128,8]{0,1:T(8,128)}) %reduce-scatter.15.cloned.1.call-update) | async-done | bytes 4112 | tf_op jit(solution)/shard_map/reduce_scatter | solution.py:281
  586.7 36.8 %all-reduce.31.cloned.1.call-done = f32[128,256]{1,0:T(8,128)} async-done(((f32[128,256]{1,0:T(8,128)}), f32[128,256]{1,0:T(8,128)}) %all-reduce.31.cloned.1.call-update) | async-done | bytes 131088 | tf_op jit(solution)/shard_map/psum | solution.py:297
  623.5 45.0 %reduce-scatter.11.cloned.1.call-done = f32[128,512]{1,0:T(8,128)} async-done(((f32[1024,512]{1,0:T(8,128)}), f32[128,512]{1,0:T(8,128)}) %reduce-scatter.11.cloned.1.call-update) | async-done | bytes 262160 | tf_op jit(solution)/shard_map/reduce_scatter | solution.py:279
  668.5 45.1 %reduce-scatter.9.cloned.1.call-done = f32[128,512]{1,0:T(8,128)} async-done(((f32[1024,512]{1,0:T(8,128)}), f32[128,512]{1,0:T(8,128)}) %reduce-scatter.9.cloned.1.call-update) | async-done | bytes 262160 | tf_op jit(solution)/shard_map/reduce_scatter | solution.py:278
  713.6 1.6 copy.254
  (459 shorter events, 137.1 us)
Async XLA Ops:
  7.2 16.5 %copy-start.18 = (bf16[128,256]{1,0:T(8,128)(2,1)S(1)}, bf16[128,256]{1,0:T(8,128)(2,1)}, u32[]{:S(2)}) copy-start(bf16[128,256]{1,0:T(8,128)(2,1)} %param.27) | copy-start | bytes 196612
  7.2 26.2 %copy-start.43 = (s32[1,256]{1,0:T(1,128)S(1)}, s32[1,256]{1,0:T(1,128)}, u32[]{:S(2)}) copy-start(s32[1,256]{1,0:T(1,128)} %param.22) | copy-start | bytes 3076
  7.2 38.2 %copy-start.36 = (f32[4,256]{1,0:T(4,128)S(1)}, f32[4,256]{1,0:T(4,128)}, u32[]{:S(2)}) copy-start(f32[4,256]{1,0:T(4,128)} %param.31) | copy-start | bytes 12292
  7.2 38.2 %copy-start.35 = (f32[4,512]{1,0:T(4,128)S(1)}, f32[4,512]{1,0:T(4,128)}, u32[]{:S(2)}) copy-start(f32[4,512]{1,0:T(4,128)} %param.29) | copy-start | bytes 24580
  7.2 38.3 %copy-start.38 = (bf16[128,8]{0,1:T(8,128)(2,1)S(1)}, bf16[128,8]{0,1:T(8,128)(2,1)}, u32[]{:S(2)}) copy-start(bf16[128,8]{0,1:T(8,128)(2,1)} %param.28) | copy-start | bytes 6148
  7.2 46.4 %copy-start.48 = (f32[8]{0:T(128)S(1)}, f32[8]{0:T(128)}, u32[]{:S(2)}) copy-start(f32[8]{0:T(128)} %param.34) | copy-start | bytes 100
  7.2 47.8 %copy-start.44 = (f32[8]{0:T(128)S(1)}, f32[8]{0:T(128)}, u32[]{:S(2)}) copy-start(f32[8]{0:T(128)} %param.35) | copy-start | bytes 100
  7.3 60.0 %all-gather.9.cloned.1.call-start = ((), (), s32[]{:S(2)}) async-start(), calls=%async_computation.6 | async-start | bytes 2621440 | tf_op jit(solution)/shard_map/all_gather | solution.py:152
  18.9 50.7 %copy-start.25 = (f32[256]{0:T(256)}, f32[256]{0:T(256)S(1)}, u32[]{:S(2)}) copy-start(f32[256]{0:T(256)S(1)} %add_rsqrt_fusion.1) | copy-start | bytes 3076
  20.9 70.5 %all-gather.11.cloned.1.call-start = ((), (), s32[]{:S(2)}) async-start(), calls=%async_computation.7 | async-start | bytes 1179648 | tf_op jit(solution)/shard_map/all_gather | solution.py:141
  21.7 154.5 %all-gather.13.cloned.1.call-start = ((), (), s32[]{:S(2)}) async-start(), calls=%async_computation.8 | async-start | bytes 1179648 | tf_op jit(solution)/shard_map/all_gather | solution.py:140
  22.4 172.2 %all-gather.15.cloned.1.call-start = ((), (), s32[]{:S(2)}) async-start(), calls=%async_computation.9 | async-start | bytes 1179648 | tf_op jit(solution)/shard_map/all_gather | solution.py:144
  23.0 171.7 %all-gather.17.cloned.1.call-start = ((), (), s32[]{:S(2)}) async-start(), calls=%async_computation.18 | async-start | bytes 2621440 | tf_op jit(solution)/shard_map/all_gather | solution.py:222
  23.6 349.9 %reduce-scatter.13.cloned.1.call-start = ((), (), s32[]{:S(2)}) async-start(), calls=%async_computation.14 | async-start | bytes 1179648 | tf_op jit(solution)/shard_map/reduce_scatter | solution.py:280
  33.4 36.2 %copy-start.10 = (bf16[1024,256]{1,0:T(8,128)(2,1)}, bf16[1024,256]{1,0:T(8,128)(2,1)S(1)}, u32[]{:S(2)}) copy-start(bf16[1024,256]{1,0:T(8,128)(2,1)S(1)} %all_gather.38) | copy-start | bytes 1572868
  45.4 24.2 %copy-start.27 = (f32[1,256]{1,0:T(1,128)}, f32[1,256]{1,0:T(1,128)S(1)}, u32[]{:S(2)}) copy-start(f32[1,256]{1,0:T(1,128)S(1)} %get-tuple-element.905) | copy-start | bytes 3076
  45.4 24.2 %copy-start.29 = (f32[1,256]{1,0:T(1,128)}, f32[1,256]{1,0:T(1,128)S(1)}, u32[]{:S(2)}) copy-start(f32[1,256]{1,0:T(1,128)S(1)} %get-tuple-element.906) | copy-start | bytes 3076
  45.5 24.2 %copy-start.31 = (f32[1,256]{1,0:T(1,128)}, f32[1,256]{1,0:T(1,128)S(1)}, u32[]{:S(2)}) copy-start(f32[1,256]{1,0:T(1,128)S(1)} %get-tuple-element.907) | copy-start | bytes 3076
  45.5 24.2 %copy-start.33 = (f32[1,256]{1,0:T(1,128)}, f32[1,256]{1,0:T(1,128)S(1)}, u32[]{:S(2)}) copy-start(f32[1,256]{1,0:T(1,128)S(1)} %get-tuple-element.908) | copy-start | bytes 3076
  45.5 48.4 %copy-start.19 = (f32[1,512]{1,0:T(1,128)}, f32[1,512]{1,0:T(1,128)S(1)}, u32[]{:S(2)}) copy-start(f32[1,512]{1,0:T(1,128)S(1)} %get-tuple-element.903) | copy-start | bytes 6148
  45.5 48.4 %copy-start.21 = (f32[1,512]{1,0:T(1,128)}, f32[1,512]{1,0:T(1,128)S(1)}, u32[]{:S(2)}) copy-start(f32[1,512]{1,0:T(1,128)S(1)} %get-tuple-element.904) | copy-start | bytes 6148
  53.6 46.8 %copy-start.39 = (f32[8]{0:T(128)}, f32[8]{0:T(128)S(1)}, u32[]{:S(2)}) copy-start(f32[8]{0:T(128)S(1)} %exp.139) | copy-start | bytes 100
  56.3 13.3 %copy-start.42 = (f32[256]{0:T(256)S(1)}, f32[256]{0:T(256)}, u32[]{:S(2)}) copy-start(f32[256]{0:T(256)} %param.32) | copy-start | bytes 3076
  69.6 2.0 copy-start.3
  71.6 19.8 %copy-start.5 = (bf16[1024,1,1024]{2,0,1:T(8,128)(2,1)S(1)}, bf16[1024,1,1024]{2,0,1:T(8,128)(2,1)}, u32[]{:S(2)}) copy-start(bf16[1024,1,1024]{2,0,1:T(8,128)(2,1)} %all-gather.9.cloned.1.call-done) | copy-start | bytes 6291460
  72.7 21.3 %copy-start.37 = (f32[512]{0:T(512)S(1)}, f32[512]{0:T(512)}, u32[]{:S(2)}) copy-start(f32[512]{0:T(512)} %param.30) | copy-start | bytes 6148
  93.9 2.9 copy-start
  96.8 112.0 %copy-start.1 = (f32[1024,512]{1,0:T(8,128)}, f32[1024,512]{1,0:T(8,128)S(1)}, u32[]{:S(2)}) copy-start(f32[1024,512]{1,0:T(8,128)S(1)} %get-tuple-element.873) | copy-start | bytes 6291460
  96.8 3.7 copy-start.45
  176.1 18.5 %copy-start.24 = (f32[1024,1]{0,1:T(1,128)S(1)}, f32[1024,1]{0,1:T(1,128)}, u32[]{:S(2)}) copy-start(f32[1024,1]{0,1:T(1,128)} %compare_convert_fusion.4) | copy-start | bytes 12292
  176.2 18.5 %copy-start.41 = (f32[512]{0:T(512)S(1)}, f32[512]{0:T(512)}, u32[]{:S(2)}) copy-start(f32[512]{0:T(512)} %param.36) | copy-start | bytes 6148
  194.7 14.1 %copy-start.23 = (f32[512]{0:T(512)S(1)}, f32[512]{0:T(512)}, u32[]{:S(2)}) copy-start(f32[512]{0:T(512)} %mul.1279) | copy-start | bytes 6148
  214.4 3.3 copy-start.8
  320.2 7.2 copy-start.20
  320.3 7.2 copy-start.22
  327.5 3.8 copy-start.4
  327.5 3.8 copy-start.9
  327.5 3.8 copy-start.12
  327.5 3.8 copy-start.13
  331.3 1.3 copy-start.28
  331.3 1.3 copy-start.30
  331.3 1.3 copy-start.32
  331.3 1.3 copy-start.34
  333.1 1.0 copy-start.11
  334.1 2.7 copy-start.6
  338.6 123.7 %all-reduce.29.cloned.1.call-start = ((), (), s32[]{:S(2)}) async-start(), calls=%async_computation.11 | async-start | bytes 4194304 | tf_op jit(solution)/shard_map/psum | solution.py:260
  338.6 4.7 copy-start.17
  338.6 4.7 copy-start.40
  338.7 4.9 copy-start.46
  343.5 1.3 copy-start.15
  343.5 1.6 copy-start.47
  345.1 2.3 copy-start.2
  349.6 156.6 %reduce-scatter.17.cloned.1.call-start = ((), (), s32[]{:S(2)}) async-start(), calls=%async_computation.17 | async-start | bytes 2359296 | tf_op jit(solution)/shard_map/reduce_scatter | solution.py:282
  354.6 197.8 %reduce-scatter.7.cloned.1.call-start = ((), (), s32[]{:S(2)}) async-start(), calls=%async_computation.10 | async-start | bytes 2621440 | tf_op jit(solution)/shard_map/reduce_scatter | solution.py:212
  359.2 227.5 %reduce-scatter.15.cloned.1.call-start = ((), (), s32[]{:S(2)}) async-start(), calls=%async_computation.16 | async-start | bytes 36864 | tf_op jit(solution)/shard_map/reduce_scatter | solution.py:281
  360.3 263.2 %all-reduce.31.cloned.1.call-start = ((), (), s32[]{:S(2)}) async-start(), calls=%async_computation.15 | async-start | bytes 262144 | tf_op jit(solution)/shard_map/psum | solution.py:297
  373.4 295.1 %reduce-scatter.11.cloned.1.call-start = ((), (), s32[]{:S(2)}) async-start(), calls=%async_computation.13 | async-start | bytes 2359296 | tf_op jit(solution)/shard_map/reduce_scatter | solution.py:279
  376.4 1.2 copy-start.16
  376.4 337.2 %reduce-scatter.9.cloned.1.call-start = ((), (), s32[]{:S(2)}) async-start(), calls=%async_computation.12 | async-start | bytes 2359296 | tf_op jit(solution)/shard_map/reduce_scatter | solution.py:278
  380.2 0.7 copy-start.50
  380.2 2.1 copy-start.49
  380.2 82.1 %copy-start.7 = (bf16[1,256,1024]{2,1,0:T(8,128)(2,1)S(1)}, bf16[1,256,1024]{2,1,0:T(8,128)(2,1)}, u32[]{:S(2)}) copy-start(bf16[1,256,1024]{2,1,0:T(8,128)(2,1)} %param.21) | copy-start | bytes 1572868
  380.2 82.1 %copy-start.26 = (f32[256]{0:T(256)S(1)}, f32[256]{0:T(256)}, u32[]{:S(2)}) copy-start(f32[256]{0:T(256)} %copy-done.25) | copy-start | bytes 3076
  380.2 172.2 %copy-start.14 = (bf16[1,256,1024]{2,1,0:T(8,128)(2,1)S(1)}, bf16[1,256,1024]{2,1,0:T(8,128)(2,1)}, u32[]{:S(2)}) copy-start(bf16[1,256,1024]{2,1,0:T(8,128)(2,1)} %param.23) | copy-start | bytes 1572868
Sparse Core Ops, SparseCore 0:
  21.0 46.1 all-gather.8
  69.1 22.2 all-gather.10
  93.3 23.5 all-gather.12
  118.6 23.5 all-gather.14
  143.6 46.0 all-gather.16
  338.7 34.6 reduce-scatter.12
  375.8 86.4 all-reduce.28
  466.0 40.1 reduce-scatter.16
  508.5 43.8 reduce-scatter.6
  556.1 30.5 reduce-scatter.14
  589.0 34.4 all-reduce.30
  627.5 40.9 reduce-scatter.10
  672.4 41.2 reduce-scatter.8
where the time goes:
time: 734 us; the launch traced here: 722 us
  waiting for transfers between devices  336 us (46%)
  matrix products  116 us (16%)
  blocking collectives  95.1 us (13%)
  other arithmetic  76.9 us (10%)
  local copies, waits for them, and re-layouts  70.4 us (10%)
  between operations  15.6 us (2%)
  loops' own time  11.8 us (2%)
    psum x1, waiting for transfers between devices, shards(): lax.psum((term_sum + jnp.einsum('trc,dc->trd', grad_dt, dt_full, preferre...  80 us
    reduce_scatter x1, waiting for transfers between devices, shards(): lax.psum_scatter(grad_z_weight, 'dp', scatter_dimension=0, tiled=True)  45.1 us
    reduce_scatter x1, waiting for transfers between devices, shards(): lax.psum_scatter(grad_x_weight, 'dp', scatter_dimension=0, tiled=True)  45 us
    reduce_scatter x1, waiting for transfers between devices, shards(): lax.psum_scatter(jnp.einsum('trc,dc->trd', normed_out, out_full, preferre...  44.4 us
    psum x1, waiting for transfers between devices, shards(): lax.psum((summed[0], summed[3], head_sums[2], head_sums[3]), 'tensor')  36.8 us
    dot_general x12, matrix products, block_step(): jnp.einsum('tsh,shp->thp', scores[:, :, None] * decays, weighted, precisi...  33.1 us
    reduce_scatter x1, waiting for transfers between devices, shards(): lax.psum_scatter(grad_dt_weight, 'dp', scatter_dimension=0, tiled=True)  31.7 us
    unnamed x1, blocking collectives  24.6 us
  transfers between devices with their start and end apart: 13, of which 10 were waited for; matrix products, arithmetic and copies ran while one was open for 17% of the time, Pallas kernels for 0%

commit v1 on v0

v1 whole, which is shorter than its diff:
```python
import functools

import jax
import jax.numpy as jnp
from jax import lax
from jax.experimental import pallas as pl
from jax.experimental.pallas import tpu as pltpu
from jax.sharding import PartitionSpec as P

N = 128
CONV = 4
Q = 256
LANES = 128
HALO = 8
EPS = 1e-05
NEG = -1e30
F32 = jnp.float32
BF16 = jnp.bfloat16
VMEM_LIMIT = 52 * 1024 * 1024


def dot(a, b):
    return jnp.dot(a, b, preferred_element_type=F32)


def dot_nt(a, b):
    return lax.dot_general(a, b, (((1,), (1,)), ((), ())), preferred_element_type=F32)


def dot_tn(a, b):
    return lax.dot_general(a, b, (((0,), (0,)), ((), ())), preferred_element_type=F32)


def dot_exact(a, b):
    return jnp.dot(a, b, preferred_element_type=F32, precision=lax.Precision.HIGHEST)


def spread(cols, heads, size):
    rows = cols.shape[0]
    per = LANES // size
    lane = lax.broadcasted_iota(jnp.int32, (rows, LANES), 1)
    parts = []
    for first in range(0, heads, per):
        part = jnp.broadcast_to(cols[:, first : first + 1], (rows, LANES))
        for extra in range(1, per):
            part = jnp.where(lane < extra * size, part, cols[:, first + extra : first + extra + 1])
        parts.append(part)
    return jnp.concatenate(parts, axis=1)


def head_sums(values, heads, size):
    width = heads * size
    channel = lax.broadcasted_iota(jnp.int32, (width, LANES), 0)
    column = lax.broadcasted_iota(jnp.int32, (width, LANES), 1)
    first = column * size
    picks = jnp.where((channel >= first) & (channel < first + size), 1.0, 0.0).astype(BF16)
    high = values.astype(BF16)
    low = (values - high.astype(F32)).astype(BF16)
    return dot(high, picks) + dot(low, picks)


def widen(tile, width):
    return jnp.concatenate([tile] * (width // tile.shape[1]), axis=1)


def softplus(v):
    return jnp.maximum(v, 0.0) + jnp.log1p(jnp.exp(-jnp.abs(v)))


def sigmoid(v):
    return 1.0 / (1.0 + jnp.exp(-v))


def as_row(column):
    rows = column.shape[0]
    return jnp.broadcast_to(column, (rows, LANES)).T[:8]


def triangle(lower):
    row = lax.broadcasted_iota(jnp.int32, (Q, Q), 0)
    col = lax.broadcasted_iota(jnp.int32, (Q, Q), 1)
    return row >= col if lower else row <= col


def block_masks(window, seg_row):
    seg = window[HALO : HALO + Q]
    before = window[HALO - 1 : HALO]
    last = window[HALO + Q - 1 : HALO + Q]
    from_prev = (seg == before).astype(F32)
    same_last = (seg == last).astype(F32)
    passes = (last == before).astype(F32)
    keep = (widen(seg, Q) == seg_row) & triangle(True)
    bias = jnp.where(keep, 0.0, NEG)
    return seg, from_prev, same_last, passes, bias


def conv_forward(buffer, window, seg, kernel, conv_bias, width):
    total = conv_bias + kernel[CONV - 1 : CONV] * buffer[HALO : HALO + Q, :]
    for back in range(1, CONV):
        match = (window[HALO - back : HALO - back + Q] == seg).astype(F32)
        tap = kernel[CONV - 1 - back : CONV - back]
        total = total + tap * (buffer[HALO - back : HALO - back + Q, :] * widen(match, width))
    return total


def conv_backward(buffer, window, seg, kernel, values, width):
    here = buffer[0:Q, :]
    total = kernel[CONV - 1 : CONV] * here
    taps = [jnp.sum(values * here, axis=0, keepdims=True)]
    for ahead in range(1, CONV):
        match = (window[HALO + ahead : HALO + ahead + Q] == seg).astype(F32)
        moved = buffer[ahead : ahead + Q, :] * widen(match, width)
        total = total + kernel[CONV - 1 - ahead : CONV - ahead] * moved
        taps.append(jnp.sum(values * moved, axis=0, keepdims=True))
    return total, taps


def forward_kernel(
    heads,
    size,
    hidden_ref,
    gain_ref,
    window_ref,
    seg_row_ref,
    weights_ref,
    kernel_x_ref,
    kernel_bc_ref,
    head_ref,
    channel_ref,
    tokens_ref,
    z_ref,
    mixed_ref,
    x_ref,
    pre_ref,
    bcdt_ref,
    pre_bc_ref,
    state_ref,
    scaled_ref,
    part_ref,
    square_ref,
    x_buffer,
    bc_buffer,
    carry,
):
    step = pl.program_id(0)
    width = heads * size
    rest = 2 * N + LANES

    @pl.when(step == 0)
    def _():
        x_buffer[0:HALO, :] = jnp.zeros((HALO, width), F32)
        bc_buffer[0:HALO, :] = jnp.zeros((HALO, 2 * N), F32)
        carry[...] = jnp.zeros((N, width), F32)

    window = window_ref[pl.ds(pl.multiple_of(step * Q, Q), Q + 2 * HALO), :]
    seg, from_prev, same_last, passes, bias = block_masks(window, seg_row_ref[0:1, :])

    hidden = hidden_ref[...].astype(F32)
    inverse = lax.rsqrt(jnp.mean(hidden * hidden, axis=1, keepdims=True) + EPS)
    tokens = (hidden * inverse * gain_ref[0:1, :]).astype(BF16)
    tokens_ref[...] = tokens
    x_proj = dot(tokens, weights_ref[:, width : 2 * width])
    z_proj = dot(tokens, weights_ref[:, 2 * width : 3 * width])
    bcdt = dot(tokens, weights_ref[:, 3 * width : 3 * width + rest])
    z_ref[...] = z_proj
    x_ref[...] = x_proj
    bcdt_ref[...] = bcdt

    x_buffer[HALO : HALO + Q, :] = x_proj
    bc_buffer[HALO : HALO + Q, :] = bcdt[:, : 2 * N]
    pre = conv_forward(
        x_buffer, window, seg, kernel_x_ref[...], kernel_x_ref[CONV : CONV + 1, :], width
    )
    pre_bc = conv_forward(
        bc_buffer, window, seg, kernel_bc_ref[...], kernel_bc_ref[CONV : CONV + 1, :], 2 * N
    )
    x_buffer[0:HALO, :] = x_buffer[Q : Q + HALO, :]
    bc_buffer[0:HALO, :] = bc_buffer[Q : Q + HALO, :]
    pre_ref[...] = pre
    pre_bc_ref[...] = pre_bc
    x_conv = pre * sigmoid(pre)
    bc_conv = (pre_bc * sigmoid(pre_bc)).astype(BF16)
    b_in = bc_conv[:, :N]
    c_in = bc_conv[:, N:]

    dt = softplus(bcdt[:, 2 * N :] + head_ref[0:1, :])
    decay = -dt * jnp.exp(head_ref[1:2, :])
    total = dot_exact(triangle(True).astype(F32), decay)
    total_t = total.T
    weighted = x_conv * spread(dt, heads, size)
    scores = dot_nt(c_in, b_in)
    before = carry[...]
    state_ref[0] = before

    per = LANES // size
    lane = lax.broadcasted_iota(jnp.int32, (Q, LANES), 1)
    inner = []
    for first in range(0, heads, per):
        group = weighted[:, first * size : first * size + LANES]
        summed = jnp.zeros((Q, LANES), F32)
        for extra in range(per):
            h = first + extra
            shape = jnp.exp(total[:, h : h + 1] - total_t[h : h + 1, :] + bias)
            mine = (lane >= extra * size) & (lane < (extra + 1) * size)
            summed = summed + dot(
                (scores * shape).astype(BF16), jnp.where(mine, group, 0.0).astype(BF16)
            )
        inner.append(summed)
    scanned = jnp.concatenate(inner, axis=1)
    scanned = scanned + dot(c_in, before.astype(BF16)) * spread(
        jnp.exp(total) * from_prev, heads, size
    )
    last = total[Q - 1 : Q, :]
    to_end = jnp.exp(last - total) * same_last
    carry[...] = dot_tn(
        b_in, (weighted * spread(to_end, heads, size)).astype(BF16)
    ) + before * spread(jnp.exp(last) * passes, heads, size)

    mixed = scanned + channel_ref[1:2, :] * x_conv
    mixed_ref[...] = mixed
    gated = mixed * (z_proj * sigmoid(z_proj))
    scaled = (gated * channel_ref[0:1, :]).astype(BF16)
    scaled_ref[...] = scaled
    part_ref[...] = dot_nt(scaled, weights_ref[:, :width]).astype(BF16)
    square_ref[...] = as_row(jnp.sum(gated * gated, axis=1, keepdims=True))


def gradient_kernel(width, cot_ref, weights_ref, scaled_ref, window_ref, grad_ref, along_ref):
    step = pl.program_id(0)
    window = window_ref[pl.ds(pl.multiple_of(step * Q, Q), Q + 2 * HALO), :]
    live = (window[HALO : HALO + Q] > 0).astype(F32)
    grad = dot(cot_ref[...], weights_ref[...]) * widen(live, width)
    grad_ref[...] = grad
    along_ref[...] = as_row(jnp.sum(scaled_ref[...].astype(F32) * grad, axis=1, keepdims=True))


def backward_kernel(
    heads,
    size,
    full_inner,
    stat_ref,
    hidden_ref,
    window_ref,
    seg_row_ref,
    weights_ref,
    kernel_x_ref,
    kernel_bc_ref,
    head_ref,
    channel_ref,
    z_ref,
    mixed_ref,
    x_ref,
    pre_ref,
    bcdt_ref,
    pre_bc_ref,
    state_ref,
    grad_ref,
    proj_ref,
    part_ref,
    out_ref,
    sum_x_ref,
    sum_bc_ref,
    sum_head_ref,
    sum_gain_ref,
    x_buffer,
    bc_buffer,
    carry,
    tail,
):
    turn = pl.program_id(0)
    step = pl.num_programs(0) - 1 - turn
    width = heads * size

    @pl.when(turn == 0)
    def _():
        x_buffer[...] = jnp.zeros((Q + HALO, width), F32)
        bc_buffer[...] = jnp.zeros((Q + HALO, 2 * N), F32)
        carry[...] = jnp.zeros((N, width), F32)
        tail[...] = jnp.zeros((8, LANES), F32)
        sum_x_ref[...] = jnp.zeros((8, width), F32)
        sum_bc_ref[...] = jnp.zeros((8, 2 * N), F32)
        sum_head_ref[...] = jnp.zeros((8, LANES), F32)
        sum_gain_ref[...] = jnp.zeros(sum_gain_ref.shape, F32)

    window = window_ref[pl.ds(pl.multiple_of(step * Q, Q), Q + 2 * HALO), :]
    seg, from_prev, same_last, passes, bias = block_masks(window, seg_row_ref[0:1, :])
    live = (seg[:, 0:1] > 0).astype(F32)

    stat = stat_ref[...].T
    gate_inverse = lax.rsqrt(stat[:, 0:1] / full_inner + EPS)
    along = stat[:, 1:2] * (gate_inverse * gate_inverse * gate_inverse / full_inner)

    gain = channel_ref[0:1, :]
    skip = channel_ref[1:2, :]
    z_proj = z_ref[...]
    mixed = mixed_ref[...]
    grad_out = grad_ref[...]
    gate = sigmoid(z_proj)
    opened = z_proj * gate
    gated = mixed * opened
    normal = gated * gate_inverse
    sum_gate = jnp.sum(grad_out * normal, axis=0, keepdims=True)
    out_ref[...] = (normal * gain * live).astype(BF16)
    grad_gated = grad_out * gain * gate_inverse - gated * along
    grad_z = grad_gated * mixed * (gate * (1.0 + z_proj * (1.0 - gate)))
    dy = grad_gated * opened

    pre = pre_ref[...]
    gate_x = sigmoid(pre)
    x_conv = pre * gate_x
    pre_bc = pre_bc_ref[...]
    gate_bc = sigmoid(pre_bc)
    bc_conv = (pre_bc * gate_bc).astype(BF16)
    b_in = bc_conv[:, :N]
    c_in = bc_conv[:, N:]
    bcdt = bcdt_ref[...]
    raw = bcdt[:, 2 * N :] + head_ref[0:1, :]
    dt = softplus(raw)
    rate = jnp.exp(head_ref[1:2, :])
    decay = -dt * rate
    total = dot_exact(triangle(True).astype(F32), decay)
    total_t = total.T
    dt_wide = spread(dt, heads, size)
    weighted = x_conv * dt_wide
    scores = dot_nt(c_in, b_in)
    before = state_ref[0]
    before_low = before.astype(BF16)
    last = total[Q - 1 : Q, :]
    to_end = spread(jnp.exp(last - total) * same_last, heads, size)
    from_start = spread(jnp.exp(total) * from_prev, heads, size)
    after = carry[...]
    after_low = after.astype(BF16)

    dy_low = dy.astype(BF16)
    weighted_low = weighted.astype(BF16)
    dy_start = (dy * from_start).astype(BF16)
    grad_c = dot_nt(dy_start, before_low)
    carried = dot(c_in, before_low)
    returned = dot(b_in, after_low)
    grad_weighted = to_end * returned
    weighted_end = (weighted * to_end).astype(BF16)
    grad_b = dot_nt(weighted_end, after_low)
    new_after = dot_tn(c_in, dy_start) + after * spread(jnp.exp(last) * passes, heads, size)
    carry[...] = new_after

    per = LANES // size
    lane = lax.broadcasted_iota(jnp.int32, (Q, LANES), 1)
    grad_scores = jnp.zeros((Q, Q), F32)
    inner = []
    none = jnp.zeros((Q, LANES), BF16)
    for first in range(0, heads, per):
        at = first * size
        dy_group = dy_low[:, at : at + LANES]
        weighted_group = weighted_low[:, at : at + LANES]
        summed = jnp.zeros((Q, LANES), F32)
        for extra in range(per):
            h = first + extra
            shape = jnp.exp(total[:, h : h + 1] - total_t[h : h + 1, :] + bias)
            mine = (lane >= extra * size) & (lane < (extra + 1) * size)
            dy_mine = jnp.where(mine, dy_group, none)
            grad_scores = grad_scores + dot_nt(dy_mine, weighted_group) * shape
            summed = summed + dot_tn((scores * shape).astype(BF16), dy_mine)
        inner.append(summed)
    grad_inner = jnp.concatenate(inner, axis=1)
    grad_weighted = grad_weighted + grad_inner
    grad_scores = grad_scores.astype(BF16)
    grad_c = grad_c + dot(grad_scores, b_in)
    grad_b = grad_b + dot_tn(grad_scores, c_in)

    scanned = mixed - skip * x_conv - carried * from_start
    pairs = head_sums(
        dy_low.astype(F32) * scanned
        + dy_start.astype(F32) * carried
        - weighted_low.astype(F32) * grad_inner
        - weighted_end.astype(F32) * returned,
        heads,
        size,
    )
    grad_decay = dot_exact(triangle(False).astype(F32), pairs) + tail[0:1, :]
    kept = jnp.sum(new_after.astype(BF16).astype(F32) * before, axis=0, keepdims=True)
    kept = jnp.broadcast_to(kept, (8, width))
    tail[...] = head_sums(kept, heads, size)
    grad_dt = head_sums(grad_weighted * x_conv, heads, size) - grad_decay * rate
    grad_raw = grad_dt * sigmoid(raw)
    sum_head_ref[0:1, :] += jnp.sum(grad_raw, axis=0, keepdims=True)
    sum_head_ref[1:2, :] += jnp.sum(grad_decay * decay, axis=0, keepdims=True)

    grad_x = grad_weighted * dt_wide + skip * dy
    sum_skip = jnp.sum(dy * x_conv, axis=0, keepdims=True)
    grad_pre = grad_x * (gate_x * (1.0 + pre * (1.0 - gate_x)))
    x_buffer[Q : Q + HALO, :] = x_buffer[0:HALO, :]
    x_buffer[0:Q, :] = grad_pre
    grad_proj, taps = conv_backward(
        x_buffer, window, seg, kernel_x_ref[...], x_ref[...], width
    )
    sum_bias = jnp.sum(grad_pre, axis=0, keepdims=True)
    blank = jnp.zeros((1, width), F32)
    sum_x_ref[...] += jnp.concatenate(
        [taps[3], taps[2], taps[1], taps[0], sum_bias, sum_gate, sum_skip, blank], axis=0
    )

    grad_pre_bc = jnp.concatenate([grad_b, grad_c], axis=1) * (
        gate_bc * (1.0 + pre_bc * (1.0 - gate_bc))
    )
    bc_buffer[Q : Q + HALO, :] = bc_buffer[0:HALO, :]
    bc_buffer[0:Q, :] = grad_pre_bc
    grad_bc, taps_bc = conv_backward(
        bc_buffer, window, seg, kernel_bc_ref[...], bcdt[:, : 2 * N], 2 * N
    )
    sum_bias_bc = jnp.sum(grad_pre_bc, axis=0, keepdims=True)
    blank_bc = jnp.zeros((3, 2 * N), F32)
    sum_bc_ref[...] += jnp.concatenate(
        [taps_bc[3], taps_bc[2], taps_bc[1], taps_bc[0], sum_bias_bc, blank_bc], axis=0
    )

    grads = jnp.concatenate(
        [
            grad_proj.astype(BF16),
            grad_z.astype(BF16),
            grad_bc.astype(BF16),
            grad_raw.astype(BF16),
        ],
        axis=1,
    )
    proj_ref[...] = grads
    part = dot_nt(grads, weights_ref[:, width:])
    part_ref[...] = part.astype(BF16)
    hidden = hidden_ref[...].astype(F32)
    inverse = lax.rsqrt(jnp.mean(hidden * hidden, axis=1, keepdims=True) + EPS)
    sum_gain_ref[0:1, :] += jnp.sum(part * (hidden * inverse), axis=0, keepdims=True)


def whole(shape):
    return pl.BlockSpec(shape, lambda i: (0,) * len(shape))


def run_forward(heads, size, hidden, gain, window, seg_row, weights, kernel_x, kernel_bc, head, channel):
    length, features = hidden.shape
    width = heads * size
    blocks = length // Q
    rest = 2 * N + LANES

    def rows(columns):
        return pl.BlockSpec((Q, columns), lambda i: (i, 0))

    def made(columns, dtype):
        return jax.ShapeDtypeStruct((length, columns), dtype)

    return pl.pallas_call(
        functools.partial(forward_kernel, heads, size),
        grid=(blocks,),
        in_specs=[
            rows(features),
            whole(gain.shape),
            whole(window.shape),
            pl.BlockSpec((8, Q), lambda i: (0, i)),
            whole(weights.shape),
            whole(kernel_x.shape),
            whole(kernel_bc.shape),
            whole(head.shape),
            whole(channel.shape),
        ],
        out_specs=[
            rows(features),
            rows(width),
            rows(width),
            rows(width),
            rows(width),
            rows(rest),
            rows(2 * N),
            pl.BlockSpec((1, N, width), lambda i: (i, 0, 0)),
            rows(width),
            rows(features),
            pl.BlockSpec((8, Q), lambda i: (0, i)),
        ],
        out_shape=[
            made(features, BF16),
            made(width, F32),
            made(width, F32),
            made(width, F32),
            made(width, F32),
            made(rest, F32),
            made(2 * N, F32),
            jax.ShapeDtypeStruct((blocks, N, width), F32),
            made(width, BF16),
            made(features, BF16),
            jax.ShapeDtypeStruct((8, length), F32),
        ],
        scratch_shapes=[
            pltpu.VMEM((Q + HALO, width), F32),
            pltpu.VMEM((Q + HALO, 2 * N), F32),
            pltpu.VMEM((N, width), F32),
        ],
        compiler_params=pltpu.CompilerParams(vmem_limit_bytes=VMEM_LIMIT),
        name="forward",
    )(hidden, gain, window, seg_row, weights, kernel_x, kernel_bc, head, channel)


def run_gradient(cot, weights, scaled, window):
    length, features = cot.shape
    width = scaled.shape[1]
    return pl.pallas_call(
        functools.partial(gradient_kernel, width),
        grid=(length // Q,),
        in_specs=[
            pl.BlockSpec((Q, features), lambda i: (i, 0)),
            pl.BlockSpec((features, width), lambda i: (0, 0)),
            pl.BlockSpec((Q, width), lambda i: (i, 0)),
            whole(window.shape),
        ],
        out_specs=[
            pl.BlockSpec((Q, width), lambda i: (i, 0)),
            pl.BlockSpec((8, Q), lambda i: (0, i)),
        ],
        out_shape=[
            jax.ShapeDtypeStruct((length, width), F32),
            jax.ShapeDtypeStruct((8, length), F32),
        ],
        compiler_params=pltpu.CompilerParams(vmem_limit_bytes=VMEM_LIMIT),
        name="out_gradient",
    )(cot, weights, scaled, window)


def run_backward(
    heads, size, full_inner, stat, hidden, window, seg_row, weights, kernel_x, kernel_bc, head, channel,
    z_proj, mixed, x_proj, pre, bcdt, pre_bc, states, grad_out,
):
    length, features = hidden.shape
    width = heads * size
    blocks = length // Q
    rest = 2 * N + LANES
    total = 2 * width + rest

    def rows(columns):
        return pl.BlockSpec((Q, columns), lambda i: (blocks - 1 - i, 0))

    def made(columns, dtype):
        return jax.ShapeDtypeStruct((length, columns), dtype)

    across = pl.BlockSpec((8, Q), lambda i: (0, blocks - 1 - i))
    sums = [(8, width), (8, 2 * N), (8, LANES), (8, features)]
    return pl.pallas_call(
        functools.partial(backward_kernel, heads, size, full_inner),
        grid=(blocks,),
        in_specs=[
            across,
            rows(features),
            whole(window.shape),
            across,
            whole(weights.shape),
            whole(kernel_x.shape),
            whole(kernel_bc.shape),
            whole(head.shape),
            whole(channel.shape),
            rows(width),
            rows(width),
            rows(width),
            rows(width),
            rows(rest),
            rows(2 * N),
            pl.BlockSpec((1, N, width), lambda i: (blocks - 1 - i, 0, 0)),
            rows(width),
        ],
        out_specs=[rows(total), rows(features), rows(width)] + [whole(shape) for shape in sums],
        out_shape=[made(total, BF16), made(features, BF16), made(width, BF16)]
        + [jax.ShapeDtypeStruct(shape, F32) for shape in sums],
        scratch_shapes=[
            pltpu.VMEM((Q + HALO, width), F32),
            pltpu.VMEM((Q + HALO, 2 * N), F32),
            pltpu.VMEM((N, width), F32),
            pltpu.VMEM((8, LANES), F32),
        ],
        compiler_params=pltpu.CompilerParams(vmem_limit_bytes=VMEM_LIMIT),
        name="backward",
    )(
        stat, hidden, window, seg_row, weights, kernel_x, kernel_bc, head, channel,
        z_proj, mixed, x_proj, pre, bcdt, pre_bc, states, grad_out,
    )


def pad_lanes(values):
    return jnp.pad(values, ((0, 0), (0, LANES - values.shape[1])))


def shards(
    hidden,
    seg_ids,
    cotangent,
    norm_gain,
    w_in_z,
    w_in_x,
    w_in_bc,
    w_in_dt,
    conv_x,
    conv_x_bias,
    conv_bc,
    conv_bc_bias,
    dt_bias,
    a_log,
    d_skip,
    gate_gain,
    w_out,
):
    heads = dt_bias.shape[0]
    width = gate_gain.shape[0]
    size = width // heads
    full_inner = width * lax.axis_size("tensor")
    features = hidden.shape[2]
    hidden_local = hidden[0]

    packed = jnp.concatenate([w_out, w_in_x, w_in_z, w_in_bc, pad_lanes(w_in_dt)], axis=1)
    hidden_full = lax.all_gather(hidden_local, "tensor", axis=0, tiled=True)
    weights = lax.all_gather(packed, "dp", axis=0, tiled=True)
    gain_full = lax.all_gather(norm_gain, "dp", axis=0, tiled=True)
    seg_full = lax.all_gather(seg_ids[0], "tensor", axis=0, tiled=True)
    cot_full = lax.all_gather(cotangent[0], "tensor", axis=0, tiled=True)

    gain = gain_full.astype(F32)[None, :]
    window = jnp.broadcast_to(
        jnp.pad(seg_full, (HALO, HALO), constant_values=-1)[:, None],
        (seg_full.shape[0] + 2 * HALO, LANES),
    )
    seg_row = jnp.broadcast_to(seg_full[None, :], (8, seg_full.shape[0]))
    kernel_x = jnp.concatenate([conv_x, conv_x_bias[None, :]], axis=0)
    kernel_bc = jnp.concatenate([conv_bc, conv_bc_bias[None, :]], axis=0)
    head = pad_lanes(jnp.stack([dt_bias, a_log]))
    channel = jnp.stack([gate_gain, jnp.repeat(d_skip, size)])

    (
        tokens, z_proj, mixed, x_proj, pre, bcdt, pre_bc, states, scaled, out_part, square,
    ) = run_forward(
        heads, size, hidden_full, gain, window, seg_row, weights, kernel_x, kernel_bc, head, channel
    )
    out_sum = lax.psum_scatter(out_part, "tensor", scatter_dimension=0, tiled=True)
    grad_out, along = run_gradient(cot_full, weights, scaled, window)
    stat = lax.psum(jnp.stack([square[0], along[0]]), "tensor")
    stat_full = jnp.pad(stat, ((0, 6), (0, 0)))

    grads, in_part, normed_out, sum_x, sum_bc, sum_head, sum_gain = run_backward(
        heads, size, full_inner, stat_full, hidden_full, window, seg_row, weights, kernel_x,
        kernel_bc, head, channel, z_proj, mixed, x_proj, pre, bcdt, pre_bc, states, grad_out,
    )
    in_sum = lax.psum_scatter(in_part, "tensor", scatter_dimension=0, tiled=True)

    grad_weights = dot_tn(tokens, grads).astype(BF16)
    grad_w_out = dot_tn(cot_full, normed_out).astype(BF16)
    sum_weights = lax.psum_scatter(
        jnp.concatenate([grad_w_out, grad_weights], axis=1), "dp", scatter_dimension=0, tiled=True
    )
    shared = lax.psum(
        (sum_gain[0], sum_bc, sum_weights[:, 3 * width : 3 * width + 2 * N].astype(F32)),
        "tensor",
    )
    gain_bc, sum_bc, grad_bc = shared
    small = lax.psum((sum_x, sum_head, gain_bc, sum_bc), "dp")
    sum_x, sum_head, sum_gain, sum_bc = small
    local_features = norm_gain.shape[0]
    grad_norm_gain = lax.dynamic_slice_in_dim(
        sum_gain, lax.axis_index("dp") * local_features, local_features, 0
    )

    local = hidden_local.shape[0]
    place = lax.axis_index("tensor") * local
    hidden_rows = hidden_local.astype(F32)
    live = (seg_ids[0] > 0).astype(F32)[:, None]
    square_here = lax.dynamic_slice_in_dim(stat[0], place, local, 0)[:, None]
    out_scale = lax.rsqrt(square_here / full_inner + EPS) * live
    layer_out = (hidden_rows + out_sum.astype(F32) * out_scale).astype(BF16)

    inverse = lax.rsqrt(jnp.mean(hidden_rows * hidden_rows, axis=1, keepdims=True) + EPS)
    unit = hidden_rows * inverse
    grad_scaled = in_sum.astype(F32) * gain
    grad_hidden = (
        cotangent[0].astype(F32)
        + inverse * (grad_scaled - unit * jnp.mean(grad_scaled * unit, axis=1, keepdims=True))
    ).astype(BF16)

    sum_weights = sum_weights.astype(F32)
    return (
        layer_out[None],
        grad_hidden[None],
        grad_norm_gain,
        sum_weights[:, 2 * width : 3 * width],
        sum_weights[:, width : 2 * width],
        grad_bc,
        sum_weights[:, 3 * width + 2 * N : 3 * width + 2 * N + heads],
        sum_x[0:CONV],
        sum_x[CONV],
        sum_bc[0:CONV],
        sum_bc[CONV],
        sum_head[0, :heads],
        sum_head[1, :heads],
        jnp.sum(sum_x[CONV + 2].reshape(heads, size), axis=1),
        sum_x[CONV + 1],
        sum_weights[:, :width],
    )


def solution(mesh):
    in_specs = (
        P("dp", "tensor", None),
        P("dp", "tensor"),
        P("dp", "tensor", None),
        P("dp"),
        P("dp", "tensor"),
        P("dp", "tensor"),
        P("dp", None),
        P("dp", "tensor"),
        P(None, "tensor"),
        P("tensor"),
        P(),
        P(),
        P("tensor"),
        P("tensor"),
        P("tensor"),
        P("tensor"),
        P("dp", "tensor"),
    )
    out_specs = (
        P("dp", "tensor", None),
        P("dp", "tensor", None),
        P("dp"),
        P("dp", "tensor"),
        P("dp", "tensor"),
        P("dp", None),
        P("dp", "tensor"),
        P(None, "tensor"),
        P("tensor"),
        P(),
        P(),
        P("tensor"),
        P("tensor"),
        P("tensor"),
        P("tensor"),
        P("dp", "tensor"),
    )
    return jax.shard_map(shards, mesh=mesh, in_specs=in_specs, out_specs=out_specs, check_vma=False)
```

time: 734 us -> 374 us (0.51); the launches traced: 722 us -> 374 us
  waiting for transfers between devices: 336 us -> 198 us
  matrix products: 116 us -> 7.79 us
  other arithmetic: 76.9 us -> 8.58 us
  Pallas kernels: 0 us -> 52.3 us
  local copies, waits for them, and re-layouts: 70.4 us -> 20.3 us
  blocking collectives: 95.1 us -> 71.4 us
  loops' own time: 11.8 us -> 0 us
    reduce_scatter x6 -> x3, waiting for transfers between devices: 186 us -> 77.9 us  [the longest x1 50.2 us: shards(): lax.psum_scatter(jnp.concatenate([grad_w_out, grad_weights], axis=1), 'dp...]
    dot_general x71 -> x2, matrix products: 116 us -> 7.79 us  [dot_tn(): lax.dot_general(a, b, (((0,), (0,)), ((), ())), preferred_element_type=F32)]
    psum x2 -> x1, waiting for transfers between devices: 117 us -> 32.7 us  [shards(): lax.psum((sum_gain[0], sum_bc, sum_weights[:, 3 * width:3 * width + 2 * N...]
    all_gather x5 -> x3, waiting for transfers between devices: 29.8 us -> 86 us  [the longest x1 36.9 us: shards(): weights = lax.all_gather(packed, 'dp', axis=0, tiled=True)]
    pallas_call x0 -> x3, Pallas kernels: none -> 52.3 us  [the longest x1 27.4 us: run_backward(): pl.pallas_call(functools.partial(backward_kernel, heads, size, full_inner...]
    unnamed x1 -> x0, blocking collectives: 24.6 us -> none
    another operation x34 -> x3, other arithmetic: 20.5 us -> 0.03 us  [the longest x1 0.01 us: shards(): stat = lax.psum(jnp.stack([square[0], along[0]]), 'tensor')]
    psum x3, blocking collectives: 31 us -> 50 us  [the longest x1 23.2 us: shards(): small = lax.psum((sum_x, sum_head, gain_bc, sum_bc), 'dp')]
  transfers between devices with their start and end apart: 13 -> 7, of which waited for: 10 -> 6; matrix products, arithmetic and copies ran while one was open for 17% -> 7% of each run, Pallas kernels for 0% -> 5%
where the time goes in v1:
time: 374 us
  waiting for transfers between devices  198 us (53%)
  blocking collectives  71.4 us (19%)
  Pallas kernels  52.3 us (14%)
  local copies, waits for them, and re-layouts  20.3 us (5%)
  between operations  14.4 us (4%)
  other arithmetic  8.58 us (2%)
  matrix products  7.79 us (2%)
    reduce_scatter x1, waiting for transfers between devices, shards(): lax.psum_scatter(jnp.concatenate([grad_w_out, grad_weights], axis=1), 'dp...  50.2 us
    all_gather x1, waiting for transfers between devices, shards(): weights = lax.all_gather(packed, 'dp', axis=0, tiled=True)  36.9 us
    psum x1, waiting for transfers between devices, shards(): lax.psum((sum_gain[0], sum_bc, sum_weights[:, 3 * width:3 * width + 2 * N...  32.7 us
    reduce_scatter x1, waiting for transfers between devices, shards(): lax.psum_scatter(out_part, 'tensor', scatter_dimension=0, tiled=True)  27.8 us
    pallas_call x1, Pallas kernels, run_backward(): pl.pallas_call(functools.partial(backward_kernel, heads, size, full_inner...  27.4 us
    all_gather x1, waiting for transfers between devices, shards(): cot_full = lax.all_gather(cotangent[0], 'tensor', axis=0, tiled=True)  26.4 us
    psum x1, blocking collectives, shards(): small = lax.psum((sum_x, sum_head, gain_bc, sum_bc), 'dp')  23.2 us
    all_gather x1, waiting for transfers between devices, shards(): hidden_full = lax.all_gather(hidden_local, 'tensor', axis=0, tiled=True)  22.6 us
  transfers between devices with their start and end apart: 7, of which 6 were waited for; matrix products, arithmetic and copies ran while one was open for 7% of the time, Pallas kernels for 5%

profile of v1, /device:TPU:0, one launch (start us, length us, event | category | flops | bytes accessed | tf_op | source)
XLA Modules:
  0.0 373.7 jit_solution(14698944445331287224)
XLA Ops:
  7.3 0.0 all-gather.10.cloned.1.call-start
  7.3 0.7 all-gather.10.cloned.1.call-update
  8.0 0.0 all-gather.8.cloned.1.call-start
  8.1 0.8 copy.36
  8.9 0.9 constant_dynamic-update-slice_fusion.3
  9.8 0.9 constant_dynamic-update-slice_fusion.2
  10.7 0.9 constant_dynamic-update-slice_fusion.1
  11.6 0.8 constant_dynamic-update-slice_fusion
  12.5 0.0 copy-start.5
  12.5 0.8 copy-done.5
  13.3 0.0 all-gather.8.cloned.1.call-update
  13.3 0.0 all-gather.12.cloned.1.call-start
  13.3 0.7 all-gather.12.cloned.1.call-update
  14.0 0.0 reduce-scatter.6.cloned.1.call-start
  14.1 0.1 broadcast_in_dim.39
  14.2 0.1 stack_reshape.3
  14.2 12.7 %all-gather.1 = s32[1,1024]{1,0:T(1,128)S(1)} all-gather(s32[1,256]{1,0:T(1,128)S(1)} %copy-done.7), channel_id=3, replica_groups=mesh['dp'=8,'tensor'=4] {'tensor'}, dimensions={1}, use_global_device_ids=true | all-gather | bytes 5120 | tf_op jit(solution)/shard_map/all_gather | solution.py:615
  26.9 0.1 pad.16
  27.0 8.7 %all-gather.3 = bf16[8,1,128]{2,1,0:T(2,128)(2,1)S(1)} all-gather(bf16[1,1,128]{2,1,0:T(2,128)(2,1)S(1)} %bitcast.56), channel_id=1, replica_groups=mesh['dp'=8,'tensor'=4] {'dp'}, dimensions={0}, use_global_device_ids=true | all-gather | bytes 2304 | tf_op jit(solution)/shard_map/all_gather | solution.py:614
  35.9 22.6 %all-gather.10.cloned.1.call-done = bf16[1,1024,1024]{2,1,0:T(8,128)(2,1)} async-done(((bf16[1,256,1024]{2,1,0:T(8,128)(2,1)}), bf16[1,1024,1024]{2,1,0:T(8,128)(2,1)}) %all-gather.10.cloned.1.call-update) | async-done | bytes 2097168 | tf_op jit(solution)/shard_map/all_gather | solution.py:612
  58.5 36.9 %all-gather.8.cloned.1.call-done.weights_ref = bf16[1024,1920]{1,0:T(8,128)(2,1)} async-done(((bf16[128,1920]{1,0:T(8,128)(2,1)}), bf16[1024,1920]{1,0:T(8,128)(2,1)}) %all-gather.8.cloned.1.call-update) | async-done | bytes 3932176 | tf_op jit(solution)/shard_map/all_gather | solution.py:613
  95.4 0.2 broadcast_in_dim.17.window_ref
  95.6 20.0 %forward.1 = (bf16[1024,1024]{1,0:T(8,128)(2,1)}, f32[1024,512]{1,0:T(8,128)}, f32[1024,512]{1,0:T(8,128)}, f32[1024,512]{1,0:T(8,128)}, f32[1024,512]{1,0:T(8,1...) custom-call(bf16[1024,1024]{1,0:T(8,128)(2,1)} %bitcast.42, ...), custom_call_target="tpu_custom_call" | custom-call | tf_op jit(solution)/shard_map/forward/pallas_call | solution.py:449
  115.6 1.0 copy-done
  116.6 26.4 %all-gather.12.cloned.1.call-done = bf16[1,1024,1024]{2,1,0:T(8,128)(2,1)} async-done(((bf16[1,256,1024]{2,1,0:T(8,128)(2,1)}), bf16[1,1024,1024]{2,1,0:T(8,128)(2,1)}) %all-gather.12.cloned.1.call-update) | async-done | bytes 2097168 | tf_op jit(solution)/shard_map/all_gather | solution.py:616
  143.0 1.2 copy-done.1
  144.2 5.0 %out_gradient.1 = (f32[1024,512]{1,0:T(8,128)}, f32[8,1024]{1,0:T(8,128)S(1)}) custom-call(bf16[1024,1024]{1,0:T(8,128)(2,1)} %bitcast.41, bf16[1024,1920]{1,0:T(8,128)(2,1)} %all-gather.8.cloned.1.call-done.weights_ref, bf16[1024,512]{1,0:T(8,128)(2,1)S(1)} %copy-done.1, s32[1040,128]{1,0:T(8,128)S(1)} %broadcast_in_dim.17.window_ref), custom_call_target="tpu_custom_call" | custom-call | tf_op jit(solution)/shard_map/out_gradient/pallas_call | solution.py:502
  149.2 9.7 %psum.56 = f32[2,1024]{1,0:T(2,128)S(1)} all-reduce(f32[2,1024]{1,0:T(2,128)S(1)} %pad_maximum_fusion.3), channel_id=1, replica_groups=mesh['dp'=8,'tensor'=4] {'tensor'}, use_global_device_ids=true, to_apply=%region_1.2 | all-reduce | flops 2048 | bytes 16384 | tf_op jit(solution)/shard_map/psum | solution.py:636
  158.9 27.4 %backward.1 = (bf16[1024,1408]{1,0:T(8,128)(2,1)}, bf16[1024,1024]{1,0:T(8,128)(2,1)}, bf16[1024,512]{1,0:T(8,128)(2,1)S(1)}, f32[8,512]{1,0:T(8,128)S(1)}, f32[...) custom-call(f32[8,1024]{1,0:T(8,128)S(1)} %pad.19.stat_ref, bf16[1024,1024]{1,0:T(8,128)(2,1)} %bitcast.43, ...), custom_call_target="tpu_custom_call" | custom-call | tf_op jit(solution)/shard_map/backward/pallas_call | solution.py:542
  186.2 0.0 reduce-scatter.6.cloned.1.call-update
  186.3 0.0 reduce-scatter.4.cloned.1.call-start
  186.3 0.5 reduce-scatter.4.cloned.1.call-update
  186.8 0.2 reduce-scatter.8.cloned.1.call-start
  187.1 0.7 copy-done.2
  187.8 2.2 fusion
  190.0 1.8 copy.37
  191.9 0.5 copy-done.16
  192.3 5.6 %convolution_convert_fusion = bf16[1024,1408]{1,0:T(8,128)(2,1)S(1)} fusion(bf16[1024,1024]{1,0:T(8,128)(2,1)S(1)} %copy-done.16, bf16[1024,1408]{1,0:T(8,128)(2,1)} %get-tuple-element.52), kind=kOutput, calls=%fused_computation.1 | convolution fusion | flops 2954231808 | bytes 7864320 | tf_op jit(solution)/shard_map/dot_general | solution.py:31
  197.9 2.1 pad_maximum_fusion
  200.0 0.0 reduce-scatter.8.cloned.1.call-update
  200.0 0.0 all-reduce.8.cloned.1.call-start
  200.1 1.0 copy-done.3
  201.1 0.2 fusion.9
  201.3 17.1 %all-reduce.5 = (f32[1024]{0:T(1024)S(1)}, f32[8,256]{1,0:T(8,128)S(1)}) all-reduce(f32[1024]{0:T(1024)S(1)} %bitcast.48, f32[8,256]{1,0:T(8,128)S(1)} %get-tuple-element.54), channel_id=1, replica_groups=mesh['dp'=8,'tensor'=4] {'tensor'}, use_global_device_ids=true, to_apply=%region_5.6 | all-reduce | flops 3072 | bytes 24576 | tf_op jit(solution)/shard_map/psum | solution.py:650
  218.4 23.2 %all-reduce.4 = (f32[1024]{0:T(1024)S(1)}, f32[8,512]{1,0:T(8,128)S(1)}, f32[8,256]{1,0:T(8,128)S(1)}, f32[8,128]{1,0:T(8,128)S(1)}) all-reduce(f32[1024]{0:T(1024)S(1)} %get-tuple-element.92, f32[8,512]{1,0:T(8,128)S(1)} %get-tuple-element.53, f32[8,256]{1,0:T(8,128)S(1)} %get-tuple-element.93, ...), channel_id=1, replica_groups=mesh['dp'=8,'tensor'=4] {'dp'}, use_global_device_ids=true, to_apply=%region_6.7 | all-reduce | flops 8192 | bytes 65536 | tf_op jit(solution)/shard_map/psum | solution.py:655
  241.6 0.6 slice.76
  242.2 0.6 slice.75
  242.8 0.6 slice.73
  243.4 0.6 fusion.14
  244.0 0.1 reshape_squeeze.3
  244.0 0.6 reduce_sum.29
  244.7 0.6 dynamic_slice.7
  245.3 0.5 slice_bitcast_fusion
  245.8 1.4 fusion.3
  247.2 27.8 %reduce-scatter.4.cloned.1.call-done = bf16[256,1024]{1,0:T(8,128)(2,1)} async-done(((bf16[1024,1024]{1,0:T(8,128)(2,1)}), bf16[256,1024]{1,0:T(8,128)(2,1)}) %reduce-scatter.4.cloned.1.call-update) | async-done | bytes 524304 | tf_op jit(solution)/shard_map/reduce_scatter | solution.py:634
  275.0 2.7 fusion.11
  277.6 50.2 %reduce-scatter.8.cloned.1.call-done = bf16[128,1920]{1,0:T(8,128)(2,1)} async-done(((bf16[1024,1920]{1,0:T(8,128)(2,1)}), bf16[128,1920]{1,0:T(8,128)(2,1)}) %reduce-scatter.8.cloned.1.call-update) | async-done | bytes 491536 | tf_op jit(solution)/shard_map/reduce_scatter | solution.py:647
  327.8 0.8 slice.72
  328.5 0.7 copy.38
  329.2 1.5 slice_convert_fusion
  330.7 0.0 all-reduce.8.cloned.1.call-update
  330.7 1.9 fusion.13
  332.7 32.7 %all-reduce.8.cloned.1.call-done = f32[128,256]{1,0:T(8,128)} async-done(((f32[128,256]{1,0:T(8,128)}), f32[128,256]{1,0:T(8,128)}) %all-reduce.8.cloned.1.call-update) | async-done | bytes 131088 | tf_op jit(solution)/shard_map/psum | solution.py:650
  365.3 1.6 copy.44
  (44 shorter events, 0.2 us)
Async XLA Ops:
  7.2 6.9 %copy-start.12 = (f32[8]{0:T(128)S(1)}, f32[8]{0:T(128)}, u32[]{:S(2)}) copy-start(f32[8]{0:T(128)} %param.31) | copy-start | bytes 100
  7.2 7.0 %copy-start.7 = (s32[1,256]{1,0:T(1,128)S(1)}, s32[1,256]{1,0:T(1,128)}, u32[]{:S(2)}) copy-start(s32[1,256]{1,0:T(1,128)} %param.18) | copy-start | bytes 3076
  7.2 19.8 %copy-start.13 = (bf16[128]{0:T(256)(128)(2,1)S(1)}, bf16[128]{0:T(256)(128)(2,1)}, u32[]{:S(2)}) copy-start(bf16[128]{0:T(256)(128)(2,1)} %param.20) | copy-start | bytes 772
  7.2 28.6 %copy-start.14 = (f32[8]{0:T(128)S(1)}, f32[8]{0:T(128)}, u32[]{:S(2)}) copy-start(f32[8]{0:T(128)} %param.30) | copy-start | bytes 100
  7.2 28.5 %copy-start.15 = (f32[8]{0:T(128)S(1)}, f32[8]{0:T(128)}, u32[]{:S(2)}) copy-start(f32[8]{0:T(128)} %param.29) | copy-start | bytes 100
  7.2 28.5 %copy-start.9 = (f32[512]{0:T(512)S(1)}, f32[512]{0:T(512)}, u32[]{:S(2)}) copy-start(f32[512]{0:T(512)} %param.32) | copy-start | bytes 6148
  7.2 28.6 %copy-start.11 = (f32[256]{0:T(256)S(1)}, f32[256]{0:T(256)}, u32[]{:S(2)}) copy-start(f32[256]{0:T(256)} %param.28) | copy-start | bytes 3076
  7.3 28.6 %copy-start.8 = (f32[4,256]{1,0:T(4,128)S(1)}, f32[4,256]{1,0:T(4,128)}, u32[]{:S(2)}) copy-start(f32[4,256]{1,0:T(4,128)} %param.27) | copy-start | bytes 12292
  7.3 28.6 %copy-start.10 = (f32[512]{0:T(512)S(1)}, f32[512]{0:T(512)}, u32[]{:S(2)}) copy-start(f32[512]{0:T(512)} %param.26) | copy-start | bytes 6148
  7.3 28.6 %copy-start.6 = (f32[4,512]{1,0:T(4,128)S(1)}, f32[4,512]{1,0:T(4,128)}, u32[]{:S(2)}) copy-start(f32[4,512]{1,0:T(4,128)} %param.25) | copy-start | bytes 24580
  7.3 51.2 %all-gather.10.cloned.1.call-start = ((), (), s32[]{:S(2)}) async-start(), calls=%async_computation.8 | async-start | bytes 2621440 | tf_op jit(solution)/shard_map/all_gather | solution.py:612
  8.0 87.4 %all-gather.8.cloned.1.call-start = ((), (), s32[]{:S(2)}) async-start(), calls=%async_computation.3 | async-start | bytes 4423680 | tf_op jit(solution)/shard_map/all_gather | solution.py:613
  12.5 0.8 copy-start.5
  13.3 129.7 %all-gather.12.cloned.1.call-start = ((), (), s32[]{:S(2)}) async-start(), calls=%async_computation.9 | async-start | bytes 2621440 | tf_op jit(solution)/shard_map/all_gather | solution.py:616
  14.0 231.8 %reduce-scatter.6.cloned.1.call-start = ((), (), s32[]{:S(2)}) async-start(), calls=%async_computation.5 | async-start | bytes 2621440 | tf_op jit(solution)/shard_map/reduce_scatter | solution.py:643
  115.6 1.0 copy-start
  143.0 1.2 copy-start.1
  186.2 1.6 copy-start.2
  186.3 88.7 %reduce-scatter.4.cloned.1.call-start = ((), (), s32[]{:S(2)}) async-start(), calls=%async_computation.4 | async-start | bytes 2621440 | tf_op jit(solution)/shard_map/reduce_scatter | solution.py:634
  186.8 140.9 %reduce-scatter.8.cloned.1.call-start = ((), (), s32[]{:S(2)}) async-start(), calls=%async_computation.6 | async-start | bytes 4423680 | tf_op jit(solution)/shard_map/reduce_scatter | solution.py:647
  190.0 2.3 copy-start.16
  200.0 1.1 copy-start.3
  200.0 74.9 %copy-start.4 = (bf16[1,256,1024]{2,1,0:T(8,128)(2,1)S(1)}, bf16[1,256,1024]{2,1,0:T(8,128)(2,1)}, u32[]{:S(2)}) copy-start(bf16[1,256,1024]{2,1,0:T(8,128)(2,1)} %param.19) | copy-start | bytes 1572868
  200.0 165.3 %all-reduce.8.cloned.1.call-start = ((), (), s32[]{:S(2)}) async-start(), calls=%async_computation.7 | async-start | bytes 262144 | tf_op jit(solution)/shard_map/psum | solution.py:650
Sparse Core Ops, SparseCore 0:
  9.7 48.7 all-gather.9
  61.0 34.4 all-gather.7
  97.0 45.9 all-gather.11
  186.4 43.0 reduce-scatter.5
  231.7 43.1 reduce-scatter.3
  278.3 49.3 reduce-scatter.7
  330.8 34.4 all-reduce.7

commit v2 on v1

--- a/solution.py
+++ b/solution.py
@@ -115,11 +115,32 @@
     return total, taps
 
 
+def pick_block(place, near_refs, block):
+    reach = len(near_refs) // 2
+    away = pl.program_id(0) - place
+    for index, ref in enumerate(near_refs):
+
+        @pl.when(away == index - reach)
+        def _():
+            block[...] = ref[...]
+
+
 def forward_kernel(
     heads,
     size,
-    hidden_ref,
-    gain_ref,
+    near,
+    place_ref,
+    *refs,
+):
+    near_refs, refs = refs[:near], refs[near:]
+    forward_body(heads, size, place_ref[0], near_refs, *refs)
+
+
+def forward_body(
+    heads,
+    size,
+    place,
+    near_refs,
     window_ref,
     seg_row_ref,
     weights_ref,
@@ -127,6 +148,7 @@
     kernel_bc_ref,
     head_ref,
     channel_ref,
+    hidden_ref,
     tokens_ref,
     z_ref,
     mixed_ref,
@@ -138,6 +160,7 @@
     scaled_ref,
     part_ref,
     square_ref,
+    gain_ref,
     x_buffer,
     bc_buffer,
     carry,
@@ -151,7 +174,10 @@
         x_buffer[0:HALO, :] = jnp.zeros((HALO, width), F32)
         bc_buffer[0:HALO, :] = jnp.zeros((HALO, 2 * N), F32)
         carry[...] = jnp.zeros((N, width), F32)
-
+        tail_columns = weights_ref[:, 3 * width + 2 * N :].astype(F32).T
+        gain_ref[...] = jnp.broadcast_to(tail_columns[heads : heads + 1], gain_ref.shape)
+
+    pick_block(place, near_refs, hidden_ref)
     window = window_ref[pl.ds(pl.multiple_of(step * Q, Q), Q + 2 * HALO), :]
     seg, from_prev, same_last, passes, bias = block_masks(window, seg_row_ref[0:1, :])
 
@@ -225,8 +251,11 @@
     square_ref[...] = as_row(jnp.sum(gated * gated, axis=1, keepdims=True))
 
 
-def gradient_kernel(width, cot_ref, weights_ref, scaled_ref, window_ref, grad_ref, along_ref):
+def gradient_kernel(width, near, place_ref, *refs):
+    near_refs, refs = refs[:near], refs[near:]
+    weights_ref, scaled_ref, window_ref, cot_ref, grad_ref, along_ref = refs
     step = pl.program_id(0)
+    pick_block(place_ref[0], near_refs, cot_ref)
     window = window_ref[pl.ds(pl.multiple_of(step * Q, Q), Q + 2 * HALO), :]
     live = (window[HALO : HALO + Q] > 0).astype(F32)
     grad = dot(cot_ref[...], weights_ref[...]) * widen(live, width)
@@ -257,7 +286,6 @@
     grad_ref,
     proj_ref,
     part_ref,
-    out_ref,
     sum_x_ref,
     sum_bc_ref,
     sum_head_ref,
@@ -284,8 +312,6 @@
 
     window = window_ref[pl.ds(pl.multiple_of(step * Q, Q), Q + 2 * HALO), :]
     seg, from_prev, same_last, passes, bias = block_masks(window, seg_row_ref[0:1, :])
-    live = (seg[:, 0:1] > 0).astype(F32)
-
     stat = stat_ref[...].T
     gate_inverse = lax.rsqrt(stat[:, 0:1] / full_inner + EPS)
     along = stat[:, 1:2] * (gate_inverse * gate_inverse * gate_inverse / full_inner)
@@ -300,7 +326,6 @@
     gated = mixed * opened
     normal = gated * gate_inverse
     sum_gate = jnp.sum(grad_out * normal, axis=0, keepdims=True)
-    out_ref[...] = (normal * gain * live).astype(BF16)
     grad_gated = grad_out * gain * gate_inverse - gated * along
     grad_z = grad_gated * mixed * (gate * (1.0 + z_proj * (1.0 - gate)))
     dy = grad_gated * opened
@@ -434,8 +459,12 @@
     return pl.BlockSpec(shape, lambda i: (0,) * len(shape))
 
 
-def run_forward(heads, size, hidden, gain, window, seg_row, weights, kernel_x, kernel_bc, head, channel):
-    length, features = hidden.shape
+def scalar():
+    return pl.BlockSpec(memory_space=pltpu.SMEM)
+
+
+def run_forward(heads, size, place, near, window, seg_row, weights, kernel_x, kernel_bc, head, channel):
+    length, features = seg_row.shape[1], near[0].shape[1]
     width = heads * size
     blocks = length // Q
     rest = 2 * N + LANES
@@ -447,11 +476,11 @@
         return jax.ShapeDtypeStruct((length, columns), dtype)
 
     return pl.pallas_call(
-        functools.partial(forward_kernel, heads, size),
+        functools.partial(forward_kernel, heads, size, len(near)),
         grid=(blocks,),
         in_specs=[
-            rows(features),
-            whole(gain.shape),
+            scalar(),
+            *[whole(block.shape) for block in near],
             whole(window.shape),
             pl.BlockSpec((8, Q), lambda i: (0, i)),
             whole(weights.shape),
@@ -462,6 +491,7 @@
         ],
         out_specs=[
             rows(features),
+            rows(features),
             rows(width),
             rows(width),
             rows(width),
@@ -472,8 +502,10 @@
             rows(width),
             rows(features),
             pl.BlockSpec((8, Q), lambda i: (0, i)),
+            whole((8, features)),
         ],
         out_shape=[
+            made(features, BF16),
             made(features, BF16),
             made(width, F32),
             made(width, F32),
@@ -485,6 +517,7 @@
             made(width, BF16),
             made(features, BF16),
             jax.ShapeDtypeStruct((8, length), F32),
+            jax.ShapeDtypeStruct((8, features), F32),
         ],
         scratch_shapes=[
             pltpu.VMEM((Q + HALO, width), F32),
@@ -493,32 +526,35 @@
         ],
         compiler_params=pltpu.CompilerParams(vmem_limit_bytes=VMEM_LIMIT),
         name="forward",
-    )(hidden, gain, window, seg_row, weights, kernel_x, kernel_bc, head, channel)
-
-
-def run_gradient(cot, weights, scaled, window):
-    length, features = cot.shape
-    width = scaled.shape[1]
+    )(place, *near, window, seg_row, weights, kernel_x, kernel_bc, head, channel)
+
+
+def run_gradient(place, near, weights, scaled, window):
+    features = near[0].shape[1]
+    length, width = scaled.shape
     return pl.pallas_call(
-        functools.partial(gradient_kernel, width),
+        functools.partial(gradient_kernel, width, len(near)),
         grid=(length // Q,),
         in_specs=[
-            pl.BlockSpec((Q, features), lambda i: (i, 0)),
+            scalar(),
+            *[whole(block.shape) for block in near],
             pl.BlockSpec((features, width), lambda i: (0, 0)),
             pl.BlockSpec((Q, width), lambda i: (i, 0)),
             whole(window.shape),
         ],
         out_specs=[
+            pl.BlockSpec((Q, features), lambda i: (i, 0)),
             pl.BlockSpec((Q, width), lambda i: (i, 0)),
             pl.BlockSpec((8, Q), lambda i: (0, i)),
         ],
         out_shape=[
+            jax.ShapeDtypeStruct((length, features), BF16),
             jax.ShapeDtypeStruct((length, width), F32),
             jax.ShapeDtypeStruct((8, length), F32),
         ],
         compiler_params=pltpu.CompilerParams(vmem_limit_bytes=VMEM_LIMIT),
         name="out_gradient",
-    )(cot, weights, scaled, window)
+    )(place, *near, weights, scaled, window)
 
 
 def run_backward(
@@ -561,8 +597,8 @@
             pl.BlockSpec((1, N, width), lambda i: (blocks - 1 - i, 0, 0)),
             rows(width),
         ],
-        out_specs=[rows(total), rows(features), rows(width)] + [whole(shape) for shape in sums],
-        out_shape=[made(total, BF16), made(features, BF16), made(width, BF16)]
+        out_specs=[rows(total), rows(features)] + [whole(shape) for shape in sums],
+        out_shape=[made(total, BF16), made(features, BF16)]
         + [jax.ShapeDtypeStruct(shape, F32) for shape in sums],
         scratch_shapes=[
             pltpu.VMEM((Q + HALO, width), F32),
@@ -580,6 +616,61 @@
 
 def pad_lanes(values):
     return jnp.pad(values, ((0, 0), (0, LANES - values.shape[1])))
+
+
+def line_gather(block, axis):
+    n = lax.axis_size(axis)
+    from_left, from_right = [], []
+    right = left = block
+    for step in range(1, n):
+        right = lax.ppermute(right, axis, [(i, i + 1) for i in range(step - 1, n - 1)])
+        left = lax.ppermute(left, axis, [(i, i - 1) for i in range(1, n - step + 1)])
+        from_left.append(right)
+        from_right.append(left)
+    return from_left[::-1] + [block] + from_right
+
+
+def line_scatter(part, axis):
+    n = lax.axis_size(axis)
+    place = lax.axis_index(axis)
+    count = part.shape[0] // n
+
+    def block(index):
+        start = jnp.clip(index, 0, n - 1) * count
+        return lax.dynamic_slice_in_dim(part, start, count, 0)
+
+    right = left = None
+    for step in range(1, n):
+        send_right = block(n - step + place)
+        send_left = block(step + place - n)
+        if step > 1:
+            send_right = (send_right.astype(F32) + right.astype(F32)).astype(part.dtype)
+            send_left = (send_left.astype(F32) + left.astype(F32)).astype(part.dtype)
+        right = lax.ppermute(send_right, axis, [(i, i + 1) for i in range(step)])
+        left = lax.ppermute(send_left, axis, [(n - 1 - i, n - 2 - i) for i in range(step)])
+    return block(place).astype(F32) + right.astype(F32) + left.astype(F32)
+
+
+def around(values, axis):
+    n = lax.axis_size(axis)
+    return [values] + [
+        lax.ppermute(values, axis, [(i, (i - k) % n) for i in range(n)]) for k in range(1, n)
+    ]
+
+
+def sum_around(values, axis):
+    return functools.reduce(jnp.add, around(values, axis))
+
+
+def sum_pairwise(values, axis):
+    n = lax.axis_size(axis)
+    if n & (n - 1):
+        return lax.psum(values, axis)
+    bit = 1
+    while bit < n:
+        values = values + lax.ppermute(values, axis, [(i, i ^ bit) for i in range(n)])
+        bit *= 2
+    return values
 
 
 def shards(
@@ -608,14 +699,23 @@
     features = hidden.shape[2]
     hidden_local = hidden[0]
 
-    packed = jnp.concatenate([w_out, w_in_x, w_in_z, w_in_bc, pad_lanes(w_in_dt)], axis=1)
-    hidden_full = lax.all_gather(hidden_local, "tensor", axis=0, tiled=True)
+    steps = jnp.pad(
+        jnp.concatenate([w_in_dt, norm_gain[:, None]], axis=1), ((0, 0), (0, LANES - heads - 1))
+    )
+    packed = jnp.concatenate([w_out, w_in_x, w_in_z, w_in_bc, steps], axis=1)
+    n = lax.axis_size("tensor")
+    axis_place = lax.axis_index("tensor")
+    place = axis_place[None]
+    near_hidden = line_gather(hidden_local, "tensor")
     weights = lax.all_gather(packed, "dp", axis=0, tiled=True)
-    gain_full = lax.all_gather(norm_gain, "dp", axis=0, tiled=True)
-    seg_full = lax.all_gather(seg_ids[0], "tensor", axis=0, tiled=True)
-    cot_full = lax.all_gather(cotangent[0], "tensor", axis=0, tiled=True)
-
-    gain = gain_full.astype(F32)[None, :]
+    seg_stack = around(seg_ids[0], "tensor")
+    count = seg_ids.shape[1]
+    seg_full = lax.dynamic_slice_in_dim(
+        jnp.concatenate(seg_stack + seg_stack), (n - axis_place) * count, n * count, 0
+    )
+    cot_local, _, _ = lax.optimization_barrier((cotangent[0], near_hidden[0], near_hidden[-1]))
+    near_cot = line_gather(cot_local, "tensor")
+
     window = jnp.broadcast_to(
         jnp.pad(seg_full, (HALO, HALO), constant_values=-1)[:, None],
         (seg_full.shape[0] + 2 * HALO, LANES),
@@ -627,49 +727,54 @@
     channel = jnp.stack([gate_gain, jnp.repeat(d_skip, size)])
 
     (
-        tokens, z_proj, mixed, x_proj, pre, bcdt, pre_bc, states, scaled, out_part, square,
+        hidden_full, tokens, z_proj, mixed, x_proj, pre, bcdt, pre_bc, states, scaled, out_part,
+        square, gain,
     ) = run_forward(
-        heads, size, hidden_full, gain, window, seg_row, weights, kernel_x, kernel_bc, head, channel
-    )
-    out_sum = lax.psum_scatter(out_part, "tensor", scatter_dimension=0, tiled=True)
-    grad_out, along = run_gradient(cot_full, weights, scaled, window)
-    stat = lax.psum(jnp.stack([square[0], along[0]]), "tensor")
+        heads, size, place, near_hidden, window, seg_row, weights, kernel_x, kernel_bc, head, channel
+    )
+    out_sum = line_scatter(out_part, "tensor")
+    cot_full, grad_out, along = run_gradient(place, near_cot, weights, scaled, window)
+    stat = sum_around(jnp.stack([square[0], along[0]]), "tensor")
     stat_full = jnp.pad(stat, ((0, 6), (0, 0)))
-
-    grads, in_part, normed_out, sum_x, sum_bc, sum_head, sum_gain = run_backward(
+    out_scale = lax.rsqrt(stat[0] / full_inner + EPS) * (seg_full > 0).astype(F32)
+    normed_out = (scaled.astype(F32) * out_scale[:, None]).astype(BF16)
+    grad_w_out = lax.psum_scatter(
+        dot_tn(cot_full, normed_out).astype(BF16), "dp", scatter_dimension=0, tiled=True
+    )
+
+    grads, in_part, sum_x, sum_bc, sum_head, sum_gain = run_backward(
         heads, size, full_inner, stat_full, hidden_full, window, seg_row, weights, kernel_x,
         kernel_bc, head, channel, z_proj, mixed, x_proj, pre, bcdt, pre_bc, states, grad_out,
     )
-    in_sum = lax.psum_scatter(in_part, "tensor", scatter_dimension=0, tiled=True)
-
-    grad_weights = dot_tn(tokens, grads).astype(BF16)
-    grad_w_out = dot_tn(cot_full, normed_out).astype(BF16)
+    in_sum = line_scatter(in_part, "tensor")
+
     sum_weights = lax.psum_scatter(
-        jnp.concatenate([grad_w_out, grad_weights], axis=1), "dp", scatter_dimension=0, tiled=True
-    )
-    shared = lax.psum(
-        (sum_gain[0], sum_bc, sum_weights[:, 3 * width : 3 * width + 2 * N].astype(F32)),
-        "tensor",
-    )
-    gain_bc, sum_bc, grad_bc = shared
-    small = lax.psum((sum_x, sum_head, gain_bc, sum_bc), "dp")
-    sum_x, sum_head, sum_gain, sum_bc = small
+        dot_tn(tokens, grads).astype(BF16), "dp", scatter_dimension=0, tiled=True
+    )
+    sum_bc_weights = sum_weights[:, 2 * width : 2 * width + 2 * N]
+    grad_bc = sum(part.astype(F32) for part in around(sum_bc_weights, "tensor"))
+    own = jnp.concatenate([sum_x.reshape(-1, LANES), sum_head])
+    both = jnp.concatenate([sum_gain[0].reshape(-1, LANES), sum_bc.reshape(-1, LANES)])
+    both = sum_around(both, "tensor")
+    small = sum_pairwise(jnp.concatenate([own, both]), "dp")
+    cuts = [sum_x.size // LANES, 8, features // LANES]
+    sum_x = small[: cuts[0]].reshape(8, width)
+    sum_head = small[cuts[0] : cuts[0] + 8]
+    sum_gain = small[cuts[0] + 8 : cuts[0] + 8 + cuts[2]].reshape(features)
+    sum_bc = small[cuts[0] + 8 + cuts[2] :].reshape(8, 2 * N)
     local_features = norm_gain.shape[0]
     grad_norm_gain = lax.dynamic_slice_in_dim(
         sum_gain, lax.axis_index("dp") * local_features, local_features, 0
     )
 
     local = hidden_local.shape[0]
-    place = lax.axis_index("tensor") * local
     hidden_rows = hidden_local.astype(F32)
-    live = (seg_ids[0] > 0).astype(F32)[:, None]
-    square_here = lax.dynamic_slice_in_dim(stat[0], place, local, 0)[:, None]
-    out_scale = lax.rsqrt(square_here / full_inner + EPS) * live
-    layer_out = (hidden_rows + out_sum.astype(F32) * out_scale).astype(BF16)
+    scale_here = lax.dynamic_slice_in_dim(out_scale, axis_place * local, local, 0)[:, None]
+    layer_out = (hidden_rows + out_sum * scale_here).astype(BF16)
 
     inverse = lax.rsqrt(jnp.mean(hidden_rows * hidden_rows, axis=1, keepdims=True) + EPS)
     unit = hidden_rows * inverse
-    grad_scaled = in_sum.astype(F32) * gain
+    grad_scaled = in_sum * gain[0:1]
     grad_hidden = (
         cotangent[0].astype(F32)
         + inverse * (grad_scaled - unit * jnp.mean(grad_scaled * unit, axis=1, keepdims=True))
@@ -680,10 +785,10 @@
         layer_out[None],
         grad_hidden[None],
         grad_norm_gain,
-        sum_weights[:, 2 * width : 3 * width],
         sum_weights[:, width : 2 * width],
+        sum_weights[:, :width],
         grad_bc,
-        sum_weights[:, 3 * width + 2 * N : 3 * width + 2 * N + heads],
+        sum_weights[:, 2 * width + 2 * N : 2 * width + 2 * N + heads],
         sum_x[0:CONV],
         sum_x[CONV],
         sum_bc[0:CONV],
@@ -692,7 +797,7 @@
         sum_head[1, :heads],
         jnp.sum(sum_x[CONV + 2].reshape(heads, size), axis=1),
         sum_x[CONV + 1],
-        sum_weights[:, :width],
+        grad_w_out.astype(F32),
     )
 
 

time: 374 us -> 279 us (0.75)
  waiting for transfers between devices: 198 us -> 81.5 us
  starting transfers between devices: 0.46 us -> 72.8 us
  blocking collectives: 71.4 us -> 0 us
  other arithmetic: 8.58 us -> 23.1 us
    ppermute x0 -> x39, waiting for transfers between devices: none -> 81.5 us  [the longest x6 39.9 us: line_gather(): lax.ppermute(left, axis, [(i, i - 1) for i in range(1, n - step + 1)])]
    reduce_scatter x3 -> x2, waiting for transfers between devices: 77.9 us -> 0.01 us  [the longest x1 0.01 us: shards(): lax.psum_scatter(dot_tn(cot_full, normed_out).astype(BF16), 'dp', scatter...]
    ppermute x0 -> x39, starting transfers between devices: none -> 72.5 us  [the longest x6 25.9 us: line_scatter(): right = lax.ppermute(send_right, axis, [(i, i + 1) for i in range(step)])]
    psum x3 -> x0, blocking collectives: 50 us -> none  [the longest x1 23.2 us: shards(): small = lax.psum((sum_x, sum_head, gain_bc, sum_bc), 'dp')]
    all_gather x2 -> x0, waiting for transfers between devices: 49 us -> none  [the longest x1 26.4 us: shards(): cot_full = lax.all_gather(cotangent[0], 'tensor', axis=0, tiled=True)]
    all_gather x1, waiting for transfers between devices: 36.9 us -> 0.01 us  [shards(): weights = lax.all_gather(packed, 'dp', axis=0, tiled=True)]
    psum x1 -> x0, waiting for transfers between devices: 32.7 us -> none  [shards(): lax.psum((sum_gain[0], sum_bc, sum_weights[:, 3 * width:3 * width + 2 * N...]
    all_gather x2 -> x0, blocking collectives: 21.4 us -> none  [the longest x1 12.7 us: shards(): seg_full = lax.all_gather(seg_ids[0], 'tensor', axis=0, tiled=True)]
  transfers between devices with their start and end apart: 7 -> 42, of which waited for: 6 -> 19; matrix products, arithmetic and copies ran while one was open for 7% -> 15% of each run, Pallas kernels for 5% -> 17%
where the time goes in v2:
time: 279 us; the launch traced here: 277 us
  waiting for transfers between devices  81.5 us (29%)
  starting transfers between devices  72.8 us (26%)
  Pallas kernels  54.3 us (19%)
  other arithmetic  23.1 us (8%)
  local copies, waits for them, and re-layouts  19.9 us (7%)
  between operations  14.3 us (5%)
  matrix products  11.5 us (4%)
    ppermute x6, waiting for transfers between devices, line_gather(): lax.ppermute(left, axis, [(i, i - 1) for i in range(1, n - step + 1)])  39.9 us
    pallas_call x1, Pallas kernels, run_backward(): pl.pallas_call(functools.partial(backward_kernel, heads, size, full_inner...  27 us
    ppermute x6, starting transfers between devices, line_scatter(): right = lax.ppermute(send_right, axis, [(i, i + 1) for i in range(step)])  25.9 us
    pallas_call x1, Pallas kernels, run_forward(): pl.pallas_call(functools.partial(forward_kernel, heads, size, len(near)),...  21.3 us
    ppermute x12, starting transfers between devices, around(): lax.ppermute(values, axis, [(i, (i - k) % n) for i in range(n)])  19.3 us
    ppermute x6, waiting for transfers between devices, line_scatter(): right = lax.ppermute(send_right, axis, [(i, i + 1) for i in range(step)])  15.9 us
    dot_general x2, matrix products, dot_tn(): lax.dot_general(a, b, (((0,), (0,)), ((), ())), preferred_element_type=F32)  11.5 us
    ppermute x6, waiting for transfers between devices, line_gather(): lax.ppermute(right, axis, [(i, i + 1) for i in range(step - 1, n - 1)])  10.5 us
  transfers between devices with their start and end apart: 42, of which 19 were waited for; matrix products, arithmetic and copies ran while one was open for 15% of the time, Pallas kernels for 17%

profile of v2, /device:TPU:0, one launch (start us, length us, event | category | flops | bytes accessed | tf_op | source)
XLA Modules:
  0.0 277.3 jit_solution(6970717645552352335)
XLA Ops:
  7.2 0.9 constant_dynamic-update-slice_fusion.4
  9.0 0.9 constant_dynamic-update-slice_fusion.3
  9.9 0.9 constant_dynamic-update-slice_fusion.2
  10.8 0.8 constant_dynamic-update-slice_fusion.1
  12.6 5.0 %collective-permute-start = (bf16[256,1024]{1,0:T(8,128)(2,1)}, bf16[256,1024]{1,0:T(8,128)(2,1)S(1)}, u32[]{:S(2)}, u32[]{:S(2)}) collective-permute-start(bf16[256,1024]{1,0:T(8,128)(2,1)} %bitcast.37), channel_id=1, source_target_pairs={{0,1},{1,2},{2,3},{4,5},{5,6},{6,7},{8,9},{9,10},{10,11},{12,13},{... | collective-permute-start | bytes 1572872 | tf_op jit(solution)/shard_map/ppermute | solution.py:626
  17.5 1.3 collective-permute-start.3
  18.8 10.2 %collective-permute-done.refs_2_ = bf16[256,1024]{1,0:T(8,128)(2,1)S(1)} collective-permute-done((bf16[256,1024]{1,0:T(8,128)(2,1)}, bf16[256,1024]{1,0:T(8,128)(2,1)S(1)}, u32[]{:S(2)}, u32[]{:S(2)}) %collective-permute-start) | collective-permute-done | bytes 524320 | tf_op jit(solution)/shard_map/ppermute | solution.py:626
  29.7 3.4 %collective-permute-done.3.refs_4_ = bf16[256,1024]{1,0:T(8,128)(2,1)S(1)} collective-permute-done((bf16[256,1024]{1,0:T(8,128)(2,1)}, bf16[256,1024]{1,0:T(8,128)(2,1)S(1)}, u32[]{:S(2)}, u32[]{:S(2)}) %collective-permute-start.3) | collective-permute-done | bytes 524320 | tf_op jit(solution)/shard_map/ppermute | solution.py:627
  33.1 1.3 collective-permute-start.4
  35.1 12.6 %collective-permute-done.4.refs_5_ = bf16[256,1024]{1,0:T(8,128)(2,1)S(1)} collective-permute-done((bf16[256,1024]{1,0:T(8,128)(2,1)S(1)}, bf16[256,1024]{1,0:T(8,128)(2,1)S(1)}, u32[]{:S(2)}, u32[]{:S(2)}) %collective-permute-start.4) | collective-permute-done | bytes 524320 | tf_op jit(solution)/shard_map/ppermute | solution.py:627
  47.7 1.3 collective-permute-start.5
  49.0 12.5 %collective-permute-done.5.refs_6_ = bf16[256,1024]{1,0:T(8,128)(2,1)S(1)} collective-permute-done((bf16[256,1024]{1,0:T(8,128)(2,1)S(1)}, bf16[256,1024]{1,0:T(8,128)(2,1)S(1)}, u32[]{:S(2)}, u32[]{:S(2)}) %collective-permute-start.5) | collective-permute-done | bytes 524320 | tf_op jit(solution)/shard_map/ppermute | solution.py:627
  61.5 1.5 collective-permute-start.15
  63.0 1.3 collective-permute-start.18
  64.3 4.6 %collective-permute-start.6 = (s32[256]{0:T(256)}, s32[256]{0:T(256)S(1)}, u32[]{:S(2)}, u32[]{:S(2)}) collective-permute-start(s32[256]{0:T(256)} %bitcast.48), channel_id=1, source_target_pairs={{0,3},{1,0},{2,1},{3,2},{4,7},{5,4},{6,5},{7,6},{8,11},{9,8},{10,9... | collective-permute-start | bytes 3080 | tf_op jit(solution)/shard_map/ppermute | solution.py:657
  72.6 3.5 %collective-permute-done.18.refs_4_ = bf16[256,1024]{1,0:T(8,128)(2,1)} collective-permute-done((bf16[256,1024]{1,0:T(8,128)(2,1)}, bf16[256,1024]{1,0:T(8,128)(2,1)}, u32[]{:S(2)}, u32[]{:S(2)}) %collective-permute-start.18) | collective-permute-done | bytes 524320 | tf_op jit(solution)/shard_map/ppermute | solution.py:627
  76.0 1.3 collective-permute-start.19
  80.2 8.0 %collective-permute-done.19.refs_5_ = bf16[256,1024]{1,0:T(8,128)(2,1)} collective-permute-done((bf16[256,1024]{1,0:T(8,128)(2,1)}, bf16[256,1024]{1,0:T(8,128)(2,1)}, u32[]{:S(2)}, u32[]{:S(2)}) %collective-permute-start.19) | collective-permute-done | bytes 524320 | tf_op jit(solution)/shard_map/ppermute | solution.py:627
  88.1 1.3 collective-permute-start.20
  90.3 1.0 broadcast_in_dim.38.refs_7_.refs_9_.window_ref
  91.3 21.3 %forward.1 = (bf16[1024,1024]{1,0:T(8,128)(2,1)}, bf16[1024,1024]{1,0:T(8,128)(2,1)}, f32[1024,512]{1,0:T(8,128)}, f32[1024,512]{1,0:T(8,128)}, f32[1024,512]{1,...) custom-call(s32[1]{0:T(128)} %bitcast.1.place_ref, ...), custom_call_target="tpu_custom_call" | custom-call | tf_op jit(solution)/shard_map/forward/pallas_call | solution.py:478
  112.6 6.1 %out_gradient.1 = (bf16[1024,1024]{1,0:T(8,128)(2,1)}, f32[1024,512]{1,0:T(8,128)}, f32[8,1024]{1,0:T(8,128)S(1)}) custom-call(s32[1]{0:T(128)} %bitcast.1.place_ref, bf16[256,1024]{1,0:T(8,128)(2,1)S(1)} %collective-permute-done.17.refs_0_, bf16[256,1024]{1,0:T(8,128)(2,1)S(1)} %collective-permute-done.16.refs_1_, ...), custom_call_target="tpu_custom_call" | custom-call | tf_op jit(solution)/shard_map/out_gradient/pallas_call | solution.py:535
  118.7 1.0 collective-permute-start.21
  119.7 3.9 %collective-permute-start.22 = (f32[2,1024]{1,0:T(2,128)S(1)}, f32[2,1024]{1,0:T(2,128)S(1)}, u32[]{:S(2)}, u32[]{:S(2)}) collective-permute-start(f32[2,1024]{1,0:T(2,128)S(1)} %pad_maximum_fusion.4), channel_id=1, source_target_pairs={{0,2},{1,3},{2,0},{3,1},{4,6},{5,7},{6,4},{7,5},{8,10},{9,11},{10,... | collective-permute-start | bytes 24584 | tf_op jit(solution)/shard_map/ppermute | solution.py:657
  123.8 1.5 collective-permute-done.22
  125.3 3.7 %collective-permute-done.23 = f32[2,1024]{1,0:T(2,128)S(1)} collective-permute-done((f32[2,1024]{1,0:T(2,128)S(1)}, f32[2,1024]{1,0:T(2,128)S(1)}, u32[]{:S(2)}, u32[]{:S(2)}) %collective-permute-start.23) | collective-permute-done | bytes 8224 | tf_op jit(solution)/shard_map/ppermute | solution.py:657
  129.2 4.0 %convolution_convert_fusion.1 = bf16[1024,512]{1,0:T(8,128)(2,1)} fusion(bf16[1024,1024]{1,0:T(8,128)(2,1)} %get-tuple-element.61, bf16[1024,512]{1,0:T(8,128)(2,1)S(1)} %copy-done.5, f32[1024]{0:T(1024)S(1)} %compare_select_fusion), kind=kOutput, calls=%fused_computation.5 | convolution fusion | flops 1075838976 | bytes 4198400 | tf_op jit(solution)/shard_map/dot_general | solution.py:31
  133.5 27.0 %backward.1 = (bf16[1024,1408]{1,0:T(8,128)(2,1)}, bf16[1024,1024]{1,0:T(8,128)(2,1)}, f32[8,512]{1,0:T(8,128)S(1)}, f32[8,256]{1,0:T(8,128)S(1)}, f32[8,128]{1,0:T(8,128)S(1)}, /*index=5*/f32[8,1024]{1,0:T(8,128)S(1)}) custom-call(f32[8,1024]{1,0:T(8,128)S(1)} %pad.19.stat_ref, bf16[1024,1024]{1,0:T(8,128)(2,1)} %get-tuple-element.44.hidden_ref, ...), custom_call_target="tpu_custom_call" | custom-call | tf_op jit(solution)/shard_map/backward/pallas_call | solution.py:578
  160.7 1.9 collective-permute-start.32
  162.6 7.5 %convolution_convert_fusion = bf16[1024,1408]{1,0:T(8,128)(2,1)} fusion(bf16[1024,1024]{1,0:T(8,128)(2,1)} %get-tuple-element.59, bf16[1024,1408]{1,0:T(8,128)(2,1)} %get-tuple-element.60), kind=kOutput, calls=%fused_computation | convolution fusion | flops 2954231808 | bytes 7864320 | tf_op jit(solution)/shard_map/dot_general | solution.py:31
  170.1 2.1 constant_dynamic-slice_fusion.1
  172.2 3.7 %collective-permute-start.24 = (bf16[256,1024]{1,0:T(8,128)(2,1)S(1)}, bf16[256,1024]{1,0:T(8,128)(2,1)S(1)}, u32[]{:S(2)}, u32[]{:S(2)}) collective-permute-start(bf16[256,1024]{1,0:T(8,128)(2,1)S(1)} %get-tuple-element.96), channel_id=1, source_target_pairs={{0,1},{4,5},{8,9},{12,13},{16,17},{20,21},{24,25},{28,29}} | collective-permute-start | bytes 1572872 | tf_op jit(solution)/shard_map/ppermute | solution.py:649
  176.0 2.1 constant_dynamic-slice_fusion.3
  178.1 1.3 collective-permute-start.9
  179.5 1.5 collective-permute-start.27
  180.9 1.7 collective-permute-start.34
  182.6 2.1 collective-permute-done.24
  184.7 1.2 add_convert_fusion.3
  186.0 4.4 %collective-permute-start.25 = (bf16[256,1024]{1,0:T(8,128)(2,1)S(1)}, bf16[256,1024]{1,0:T(8,128)(2,1)S(1)}, u32[]{:S(2)}, u32[]{:S(2)}) collective-permute-start(bf16[256,1024]{1,0:T(8,128)(2,1)S(1)} %add_convert_fusion.3), channel_id=1, source_target_pairs={{0,1},{1,2},{4,5},{5,6},{8,9},{9,10},{12,13},{13,14},{16,17},{17,1... | collective-permute-start | bytes 1572872 | tf_op jit(solution)/shard_map/ppermute | solution.py:649
  190.6 1.5 collective-permute-start.12
  192.1 1.6 collective-permute-start.35
  193.7 2.2 collective-permute-done.9
  195.9 1.2 add_convert_fusion.7
  197.2 5.2 %collective-permute-start.10 = (bf16[256,1024]{1,0:T(8,128)(2,1)S(1)}, bf16[256,1024]{1,0:T(8,128)(2,1)}, u32[]{:S(2)}, u32[]{:S(2)}) collective-permute-start(bf16[256,1024]{1,0:T(8,128)(2,1)S(1)} %add_convert_fusion.7), channel_id=1, source_target_pairs={{0,1},{1,2},{4,5},{5,6},{8,9},{9,10},{12,13},{13,14},{16,17},{17,1... | collective-permute-start | bytes 1572872 | tf_op jit(solution)/shard_map/ppermute | solution.py:649
  202.5 4.6 %collective-permute-done.25 = bf16[256,1024]{1,0:T(8,128)(2,1)S(1)} collective-permute-done((bf16[256,1024]{1,0:T(8,128)(2,1)S(1)}, bf16[256,1024]{1,0:T(8,128)(2,1)S(1)}, u32[]{:S(2)}, u32[]{:S(2)}) %collective-permute-start.25) | collective-permute-done | bytes 524320 | tf_op jit(solution)/shard_map/ppermute | solution.py:649
  207.2 2.5 add_convert_fusion.2
  210.5 5.7 %collective-permute-done.10 = bf16[256,1024]{1,0:T(8,128)(2,1)} collective-permute-done((bf16[256,1024]{1,0:T(8,128)(2,1)S(1)}, bf16[256,1024]{1,0:T(8,128)(2,1)}, u32[]{:S(2)}, u32[]{:S(2)}) %collective-permute-start.10) | collective-permute-done | bytes 524320 | tf_op jit(solution)/shard_map/ppermute | solution.py:649
  216.2 2.7 add_convert_fusion.6
  220.2 5.3 %collective-permute-start.26 = (bf16[256,1024]{1,0:T(8,128)(2,1)}, bf16[256,1024]{1,0:T(8,128)(2,1)S(1)}, u32[]{:S(2)}, u32[]{:S(2)}) collective-permute-start(bf16[256,1024]{1,0:T(8,128)(2,1)} %get-tuple-element.94), channel_id=1, source_target_pairs={{0,1},{1,2},{2,3},{4,5},{5,6},{6,7},{8,9},{9,10},{10,11},{12,13},{... | collective-permute-start | bytes 1572872 | tf_op jit(solution)/shard_map/ppermute | solution.py:649
  225.5 1.0 add_convert_fusion
  226.5 1.3 collective-permute-start.29
  228.3 6.0 %collective-permute-start.11 = (bf16[256,1024]{1,0:T(8,128)(2,1)}, bf16[256,1024]{1,0:T(8,128)(2,1)}, u32[]{:S(2)}, u32[]{:S(2)}) collective-permute-start(bf16[256,1024]{1,0:T(8,128)(2,1)} %get-tuple-element.98), channel_id=1, source_target_pairs={{0,1},{1,2},{2,3},{4,5},{5,6},{6,7},{8,9},{9,10},{10,11},{12,13},{... | collective-permute-start | bytes 1572872 | tf_op jit(solution)/shard_map/ppermute | solution.py:649
  234.3 2.0 add_convert_fusion.4
  236.4 1.3 collective-permute-start.14
  240.7 1.7 convert_element_type.182
  242.4 0.9 collective-permute-done.29
  243.3 1.5 fusion.2
  244.8 1.3 collective-permute-done.11
  246.1 6.0 %collective-permute-done.14 = bf16[256,1024]{1,0:T(8,128)(2,1)} collective-permute-done((bf16[256,1024]{1,0:T(8,128)(2,1)}, bf16[256,1024]{1,0:T(8,128)(2,1)}, u32[]{:S(2)}, u32[]{:S(2)}) %collective-permute-start.14) | collective-permute-done | bytes 524320 | tf_op jit(solution)/shard_map/ppermute | solution.py:650
  252.1 3.1 %fusion.11 = (bf16[1,256,1024]{2,1,0:T(8,128)(2,1)}, bf16[1,256,1024]{2,1,0:T(8,128)(2,1)}) fusion(bf16[256,1024]{1,0:T(8,128)(2,1)} %collective-permute-done.29, bf16[256,1024]{1,0:T(8,128)(2,1)S(1)} %collective-permute-done.26, f32[256]{0:T(256)S(1)} %broadcast_multiply_fusion, f32[1024]{0:T(1024)S(1)} %bitcast.44, f32[256]{0:T(256)S(1)} %add_rsqrt_fusion, ...), kind=kLoop, calls=%fused_computation.26 | loop fusion | flops 5767168 | bytes 5250052 | tf_op jit(solution)/shard_map/broadcast_in_dim | solution.py:786
  256.5 6.7 %collective-permute-start.37 = (bf16[128,256]{1,0:T(8,128)(2,1)S(1)}, bf16[128,256]{1,0:T(8,128)(2,1)S(1)}, u32[]{:S(2)}, u32[]{:S(2)}) collective-permute-start(bf16[128,256]{1,0:T(8,128)(2,1)S(1)} %slice.99), channel_id=1, source_target_pairs={{0,2},{1,3},{2,0},{3,1},{4,6},{5,7},{6,4},{7,5},{8,10},{9,11},{10,... | collective-permute-start | bytes 196616 | tf_op jit(solution)/shard_map/ppermute | solution.py:657
  263.2 1.8 fusion.15
  267.2 2.1 collective-permute-done.38
  269.2 1.5 convert_add_fusion.1
  (121 shorter events, 20.8 us)
Async XLA Ops:
  7.2 83.1 %all-gather.2.cloned.1.call-start = ((), (), s32[]{:S(2)}) async-start(), calls=%async_computation.2 | async-start | bytes 4423680 | tf_op jit(solution)/shard_map/all_gather | solution.py:710
  11.7 0.8 copy-start.6
  12.5 228.2 %reduce-scatter.5.cloned.1.call-start = ((), (), s32[]{:S(2)}) async-start(), calls=%async_computation.4 | async-start | bytes 1179648 | tf_op jit(solution)/shard_map/reduce_scatter | solution.py:741
  12.6 16.4 %collective-permute-start = (bf16[256,1024]{1,0:T(8,128)(2,1)}, bf16[256,1024]{1,0:T(8,128)(2,1)S(1)}, u32[]{:S(2)}, u32[]{:S(2)}) collective-permute-start(bf16[256,1024]{1,0:T(8,128)(2,1)} %bitcast.37), channel_id=1, source_target_pairs={{0,1},{1,2},{2,3},{4,5},{5,6},{6,7},{8,9},{9,10},{10,11},{12,13},{... | collective-permute-start | bytes 1572872 | tf_op jit(solution)/shard_map/ppermute | solution.py:626
  17.5 15.5 %collective-permute-start.3 = (bf16[256,1024]{1,0:T(8,128)(2,1)}, bf16[256,1024]{1,0:T(8,128)(2,1)S(1)}, u32[]{:S(2)}, u32[]{:S(2)}) collective-permute-start(bf16[256,1024]{1,0:T(8,128)(2,1)} %bitcast.38), channel_id=1, source_target_pairs={{1,0},{2,1},{3,2},{5,4},{6,5},{7,6},{9,8},{10,9},{11,10},{13,12},{... | collective-permute-start | bytes 1572872 | tf_op jit(solution)/shard_map/ppermute | solution.py:627
  29.0 5.3 %collective-permute-start.1 = (bf16[256,1024]{1,0:T(8,128)(2,1)S(1)}, bf16[256,1024]{1,0:T(8,128)(2,1)S(1)}, u32[]{:S(2)}, u32[]{:S(2)}) collective-permute-start(bf16[256,1024]{1,0:T(8,128)(2,1)S(1)} %collective-permute-done.refs_2_), channel_id=1, source_target_pairs={{1,2},{2,3},{5,6},{6,7},{9,10},{10,11},{13,14},{14,15},{17,18},{18... | collective-permute-start | bytes 1572872 | tf_op jit(solution)/shard_map/ppermute | solution.py:626
  33.1 28.4 %copy-start.7 = (bf16[256,1024]{1,0:T(8,128)(2,1)}, bf16[256,1024]{1,0:T(8,128)(2,1)S(1)}, u32[]{:S(2)}) copy-start(bf16[256,1024]{1,0:T(8,128)(2,1)S(1)} %collective-permute-done.3.refs_4_) | copy-start | bytes 1572868
  33.1 14.6 %collective-permute-start.4 = (bf16[256,1024]{1,0:T(8,128)(2,1)S(1)}, bf16[256,1024]{1,0:T(8,128)(2,1)S(1)}, u32[]{:S(2)}, u32[]{:S(2)}) collective-permute-start(bf16[256,1024]{1,0:T(8,128)(2,1)S(1)} %collective-permute-done.3.refs_4_), channel_id=1, source_target_pairs={{1,0},{2,1},{5,4},{6,5},{9,8},{10,9},{13,12},{14,13},{17,16},{18,1... | collective-permute-start | bytes 1572872 | tf_op jit(solution)/shard_map/ppermute | solution.py:627
  34.4 14.6 %collective-permute-start.2 = (bf16[256,1024]{1,0:T(8,128)(2,1)S(1)}, bf16[256,1024]{1,0:T(8,128)(2,1)S(1)}, u32[]{:S(2)}, u32[]{:S(2)}) collective-permute-start(bf16[256,1024]{1,0:T(8,128)(2,1)S(1)} %collective-permute-done.1.refs_1_), channel_id=1, source_target_pairs={{2,3},{6,7},{10,11},{14,15},{18,19},{22,23},{26,27},{30,31}} | collective-permute-start | bytes 1572872 | tf_op jit(solution)/shard_map/ppermute | solution.py:626
  47.7 13.8 %copy-start.8 = (bf16[256,1024]{1,0:T(8,128)(2,1)}, bf16[256,1024]{1,0:T(8,128)(2,1)S(1)}, u32[]{:S(2)}) copy-start(bf16[256,1024]{1,0:T(8,128)(2,1)S(1)} %collective-permute-done.4.refs_5_) | copy-start | bytes 1572868
  47.7 13.8 %collective-permute-start.5 = (bf16[256,1024]{1,0:T(8,128)(2,1)S(1)}, bf16[256,1024]{1,0:T(8,128)(2,1)S(1)}, u32[]{:S(2)}, u32[]{:S(2)}) collective-permute-start(bf16[256,1024]{1,0:T(8,128)(2,1)S(1)} %collective-permute-done.4.refs_5_), channel_id=1, source_target_pairs={{1,0},{5,4},{9,8},{13,12},{17,16},{21,20},{25,24},{29,28}} | collective-permute-start | bytes 1572872 | tf_op jit(solution)/shard_map/ppermute | solution.py:627
  61.5 1.5 copy-start.9
  61.5 10.4 %collective-permute-start.15 = (bf16[256,1024]{1,0:T(8,128)(2,1)}, bf16[256,1024]{1,0:T(8,128)(2,1)S(1)}, u32[]{:S(2)}, u32[]{:S(2)}) collective-permute-start(bf16[256,1024]{1,0:T(8,128)(2,1)} %bitcast.40), channel_id=1, source_target_pairs={{0,1},{1,2},{2,3},{4,5},{5,6},{6,7},{8,9},{9,10},{10,11},{12,13},{... | collective-permute-start | bytes 1572872 | tf_op jit(solution)/shard_map/ppermute | solution.py:626
  63.0 13.1 %collective-permute-start.18 = (bf16[256,1024]{1,0:T(8,128)(2,1)}, bf16[256,1024]{1,0:T(8,128)(2,1)}, u32[]{:S(2)}, u32[]{:S(2)}) collective-permute-start(bf16[256,1024]{1,0:T(8,128)(2,1)} %bitcast.41), channel_id=1, source_target_pairs={{1,0},{2,1},{3,2},{5,4},{6,5},{7,6},{9,8},{10,9},{11,10},{13,12},{... | collective-permute-start | bytes 1572872 | tf_op jit(solution)/shard_map/ppermute | solution.py:627
  64.3 15.2 %collective-permute-start.6 = (s32[256]{0:T(256)}, s32[256]{0:T(256)S(1)}, u32[]{:S(2)}, u32[]{:S(2)}) collective-permute-start(s32[256]{0:T(256)} %bitcast.48), channel_id=1, source_target_pairs={{0,3},{1,0},{2,1},{3,2},{4,7},{5,4},{6,5},{7,6},{8,11},{9,8},{10,9... | collective-permute-start | bytes 3080 | tf_op jit(solution)/shard_map/ppermute | solution.py:657
  68.8 10.6 %collective-permute-start.7 = (s32[256]{0:T(256)}, s32[256]{0:T(256)S(1)}, u32[]{:S(2)}, u32[]{:S(2)}) collective-permute-start(s32[256]{0:T(256)} %bitcast.49), channel_id=1, source_target_pairs={{0,2},{1,3},{2,0},{3,1},{4,6},{5,7},{6,4},{7,5},{8,10},{9,11},{10,... | collective-permute-start | bytes 3080 | tf_op jit(solution)/shard_map/ppermute | solution.py:657
  68.8 20.6 %collective-permute-start.8 = (s32[256]{0:T(256)}, s32[256]{0:T(256)S(1)}, u32[]{:S(2)}, u32[]{:S(2)}) collective-permute-start(s32[256]{0:T(256)} %bitcast.50), channel_id=1, source_target_pairs={{0,1},{1,2},{2,3},{3,0},{4,5},{5,6},{6,7},{7,4},{8,9},{9,10},{10,1... | collective-permute-start | bytes 3080 | tf_op jit(solution)/shard_map/ppermute | solution.py:657
  71.9 7.6 %collective-permute-start.16 = (bf16[256,1024]{1,0:T(8,128)(2,1)S(1)}, bf16[256,1024]{1,0:T(8,128)(2,1)S(1)}, u32[]{:S(2)}, u32[]{:S(2)}) collective-permute-start(bf16[256,1024]{1,0:T(8,128)(2,1)S(1)} %collective-permute-done.15.refs_2_), channel_id=1, source_target_pairs={{1,2},{2,3},{5,6},{6,7},{9,10},{10,11},{13,14},{14,15},{17,18},{18... | collective-permute-start | bytes 1572872 | tf_op jit(solution)/shard_map/ppermute | solution.py:626
  76.0 12.1 %collective-permute-start.19 = (bf16[256,1024]{1,0:T(8,128)(2,1)}, bf16[256,1024]{1,0:T(8,128)(2,1)}, u32[]{:S(2)}, u32[]{:S(2)}) collective-permute-start(bf16[256,1024]{1,0:T(8,128)(2,1)} %collective-permute-done.18.refs_4_), channel_id=1, source_target_pairs={{1,0},{2,1},{5,4},{6,5},{9,8},{10,9},{13,12},{14,13},{17,16},{18,1... | collective-permute-start | bytes 1572872 | tf_op jit(solution)/shard_map/ppermute | solution.py:627
  79.5 33.1 %collective-permute-start.17 = (bf16[256,1024]{1,0:T(8,128)(2,1)S(1)}, bf16[256,1024]{1,0:T(8,128)(2,1)S(1)}, u32[]{:S(2)}, u32[]{:S(2)}) collective-permute-start(bf16[256,1024]{1,0:T(8,128)(2,1)S(1)} %collective-permute-done.16.refs_1_), channel_id=1, source_target_pairs={{2,3},{6,7},{10,11},{14,15},{18,19},{22,23},{26,27},{30,31}} | collective-permute-start | bytes 1572872 | tf_op jit(solution)/shard_map/ppermute | solution.py:626
  88.1 24.5 %collective-permute-start.20 = (bf16[256,1024]{1,0:T(8,128)(2,1)}, bf16[256,1024]{1,0:T(8,128)(2,1)}, u32[]{:S(2)}, u32[]{:S(2)}) collective-permute-start(bf16[256,1024]{1,0:T(8,128)(2,1)} %collective-permute-done.19.refs_5_), channel_id=1, source_target_pairs={{1,0},{5,4},{9,8},{13,12},{17,16},{21,20},{25,24},{29,28}} | collective-permute-start | bytes 1572872 | tf_op jit(solution)/shard_map/ppermute | solution.py:627
  112.6 16.6 %copy-start.5 = (bf16[1024,512]{1,0:T(8,128)(2,1)S(1)}, bf16[1024,512]{1,0:T(8,128)(2,1)}, u32[]{:S(2)}) copy-start(bf16[1024,512]{1,0:T(8,128)(2,1)} %get-tuple-element.42.refs_8_) | copy-start | bytes 3145732
  118.7 5.1 %collective-permute-start.21 = (f32[2,1024]{1,0:T(2,128)S(1)}, f32[2,1024]{1,0:T(2,128)S(1)}, u32[]{:S(2)}, u32[]{:S(2)}) collective-permute-start(f32[2,1024]{1,0:T(2,128)S(1)} %pad_maximum_fusion.4), channel_id=1, source_target_pairs={{0,3},{1,0},{2,1},{3,2},{4,7},{5,4},{6,5},{7,6},{8,11},{9,8},{10,9... | collective-permute-start | bytes 24584 | tf_op jit(solution)/shard_map/ppermute | solution.py:657
  119.7 5.7 %collective-permute-start.22 = (f32[2,1024]{1,0:T(2,128)S(1)}, f32[2,1024]{1,0:T(2,128)S(1)}, u32[]{:S(2)}, u32[]{:S(2)}) collective-permute-start(f32[2,1024]{1,0:T(2,128)S(1)} %pad_maximum_fusion.4), channel_id=1, source_target_pairs={{0,2},{1,3},{2,0},{3,1},{4,6},{5,7},{6,4},{7,5},{8,10},{9,11},{10,... | collective-permute-start | bytes 24584 | tf_op jit(solution)/shard_map/ppermute | solution.py:657
  123.6 5.4 %collective-permute-start.23 = (f32[2,1024]{1,0:T(2,128)S(1)}, f32[2,1024]{1,0:T(2,128)S(1)}, u32[]{:S(2)}, u32[]{:S(2)}) collective-permute-start(f32[2,1024]{1,0:T(2,128)S(1)} %pad_maximum_fusion.4), channel_id=1, source_target_pairs={{0,1},{1,2},{2,3},{3,0},{4,5},{5,6},{6,7},{7,4},{8,9},{9,10},{10,1... | collective-permute-start | bytes 24584 | tf_op jit(solution)/shard_map/ppermute | solution.py:657
  129.2 4.3 %copy-start = (s32[1040,128]{1,0:T(8,128)S(1)}, s32[1040,128]{1,0:T(8,128)}, u32[]{:S(2)}) copy-start(s32[1040,128]{1,0:T(8,128)} %broadcast_in_dim.38.refs_7_.refs_9_.window_ref) | copy-start | bytes 1597444
  129.2 4.3 %copy-start.1 = (f32[1024,256]{1,0:T(8,128)S(1)}, f32[1024,256]{1,0:T(8,128)}, u32[]{:S(2)}) copy-start(f32[1024,256]{1,0:T(8,128)} %get-tuple-element.50.pre_bc_ref) | copy-start | bytes 3145732
  133.3 122.0 %reduce-scatter.3.cloned.1.call-start = ((), (), s32[]{:S(2)}) async-start(), calls=%async_computation.3 | async-start | bytes 3244032 | tf_op jit(solution)/shard_map/reduce_scatter | solution.py:751
  160.5 15.3 %collective-permute-start.30 = (f32[24,128]{1,0:T(8,128)S(1)}, f32[24,128]{1,0:T(8,128)S(1)}, u32[]{:S(2)}, u32[]{:S(2)}) collective-permute-start(f32[24,128]{1,0:T(8,128)S(1)} %pad_maximum_fusion.2), channel_id=1, source_target_pairs={{0,3},{1,0},{2,1},{3,2},{4,7},{5,4},{6,5},{7,6},{8,11},{9,8},{10,9... | collective-permute-start | bytes 36872 | tf_op jit(solution)/shard_map/ppermute | solution.py:657
  160.6 15.3 %collective-permute-start.31 = (f32[24,128]{1,0:T(8,128)S(1)}, f32[24,128]{1,0:T(8,128)S(1)}, u32[]{:S(2)}, u32[]{:S(2)}) collective-permute-start(f32[24,128]{1,0:T(8,128)S(1)} %pad_maximum_fusion.2), channel_id=1, source_target_pairs={{0,2},{1,3},{2,0},{3,1},{4,6},{5,7},{6,4},{7,5},{8,10},{9,11},{10,... | collective-permute-start | bytes 36872 | tf_op jit(solution)/shard_map/ppermute | solution.py:657
  160.7 15.2 %collective-permute-start.32 = (f32[24,128]{1,0:T(8,128)S(1)}, f32[24,128]{1,0:T(8,128)S(1)}, u32[]{:S(2)}, u32[]{:S(2)}) collective-permute-start(f32[24,128]{1,0:T(8,128)S(1)} %pad_maximum_fusion.2), channel_id=1, source_target_pairs={{0,1},{1,2},{2,3},{3,0},{4,5},{5,6},{6,7},{7,4},{8,9},{9,10},{10,1... | collective-permute-start | bytes 36872 | tf_op jit(solution)/shard_map/ppermute | solution.py:657
  172.2 18.2 %copy-start.2 = (bf16[1,256,1024]{2,1,0:T(8,128)(2,1)S(1)}, bf16[1,256,1024]{2,1,0:T(8,128)(2,1)}, u32[]{:S(2)}) copy-start(bf16[1,256,1024]{2,1,0:T(8,128)(2,1)} %param.17) | copy-start | bytes 1572868
  172.2 12.5 %collective-permute-start.24 = (bf16[256,1024]{1,0:T(8,128)(2,1)S(1)}, bf16[256,1024]{1,0:T(8,128)(2,1)S(1)}, u32[]{:S(2)}, u32[]{:S(2)}) collective-permute-start(bf16[256,1024]{1,0:T(8,128)(2,1)S(1)} %get-tuple-element.96), channel_id=1, source_target_pairs={{0,1},{4,5},{8,9},{12,13},{16,17},{20,21},{24,25},{28,29}} | collective-permute-start | bytes 1572872 | tf_op jit(solution)/shard_map/ppermute | solution.py:649
  175.9 5.0 %collective-permute-start.33 = (f32[64,128]{1,0:T(8,128)S(1)}, f32[64,128]{1,0:T(8,128)S(1)}, u32[]{:S(2)}, u32[]{:S(2)}) collective-permute-start(f32[64,128]{1,0:T(8,128)S(1)} %pad_maximum_fusion), channel_id=1, source_target_pairs={{0,4},{4,0},{8,12},{12,8},{16,20},{20,16},{24,28},{28,24},{1,5},{5... | collective-permute-start | bytes 98312 | tf_op jit(solution)/shard_map/ppermute | solution.py:671
  178.1 17.8 %collective-permute-start.9 = (bf16[256,1024]{1,0:T(8,128)(2,1)S(1)}, bf16[256,1024]{1,0:T(8,128)(2,1)S(1)}, u32[]{:S(2)}, u32[]{:S(2)}) collective-permute-start(bf16[256,1024]{1,0:T(8,128)(2,1)S(1)} %get-tuple-element.100), channel_id=1, source_target_pairs={{0,1},{4,5},{8,9},{12,13},{16,17},{20,21},{24,25},{28,29}} | collective-permute-start | bytes 1572872 | tf_op jit(solution)/shard_map/ppermute | solution.py:649
  179.5 23.1 %collective-permute-start.27 = (bf16[256,1024]{1,0:T(8,128)(2,1)}, bf16[256,1024]{1,0:T(8,128)(2,1)}, u32[]{:S(2)}, u32[]{:S(2)}) collective-permute-start(bf16[256,1024]{1,0:T(8,128)(2,1)} %get-tuple-element.97), channel_id=1, source_target_pairs={{3,2},{7,6},{11,10},{15,14},{19,18},{23,22},{27,26},{31,30}} | collective-permute-start | bytes 1572872 | tf_op jit(solution)/shard_map/ppermute | solution.py:650
  180.9 11.2 %collective-permute-start.34 = (f32[64,128]{1,0:T(8,128)S(1)}, f32[64,128]{1,0:T(8,128)S(1)}, u32[]{:S(2)}, u32[]{:S(2)}) collective-permute-start(f32[64,128]{1,0:T(8,128)S(1)} %fusion.14), channel_id=1, source_target_pairs={{0,8},{4,12},{8,0},{12,4},{16,24},{20,28},{24,16},{28,20},{1,9},{5... | collective-permute-start | bytes 98312 | tf_op jit(solution)/shard_map/ppermute | solution.py:671
  186.0 21.2 %collective-permute-start.25 = (bf16[256,1024]{1,0:T(8,128)(2,1)S(1)}, bf16[256,1024]{1,0:T(8,128)(2,1)S(1)}, u32[]{:S(2)}, u32[]{:S(2)}) collective-permute-start(bf16[256,1024]{1,0:T(8,128)(2,1)S(1)} %add_convert_fusion.3), channel_id=1, source_target_pairs={{0,1},{1,2},{4,5},{5,6},{8,9},{9,10},{12,13},{13,14},{16,17},{17,1... | collective-permute-start | bytes 1572872 | tf_op jit(solution)/shard_map/ppermute | solution.py:649
  190.6 20.0 %collective-permute-start.12 = (bf16[256,1024]{1,0:T(8,128)(2,1)}, bf16[256,1024]{1,0:T(8,128)(2,1)}, u32[]{:S(2)}, u32[]{:S(2)}) collective-permute-start(bf16[256,1024]{1,0:T(8,128)(2,1)} %get-tuple-element.101), channel_id=1, source_target_pairs={{3,2},{7,6},{11,10},{15,14},{19,18},{23,22},{27,26},{31,30}} | collective-permute-start | bytes 1572872 | tf_op jit(solution)/shard_map/ppermute | solution.py:650
  192.1 10.4 %collective-permute-start.35 = (f32[64,128]{1,0:T(8,128)S(1)}, f32[64,128]{1,0:T(8,128)S(1)}, u32[]{:S(2)}, u32[]{:S(2)}) collective-permute-start(f32[64,128]{1,0:T(8,128)S(1)} %add.209), channel_id=1, source_target_pairs={{0,16},{4,20},{8,24},{12,28},{16,0},{20,4},{24,8},{28,12},{1,17},{... | collective-permute-start | bytes 98312 | tf_op jit(solution)/shard_map/ppermute | solution.py:671
  197.2 19.0 %collective-permute-start.10 = (bf16[256,1024]{1,0:T(8,128)(2,1)S(1)}, bf16[256,1024]{1,0:T(8,128)(2,1)}, u32[]{:S(2)}, u32[]{:S(2)}) collective-permute-start(bf16[256,1024]{1,0:T(8,128)(2,1)S(1)} %add_convert_fusion.7), channel_id=1, source_target_pairs={{0,1},{1,2},{4,5},{5,6},{8,9},{9,10},{12,13},{13,14},{16,17},{17,1... | collective-permute-start | bytes 1572872 | tf_op jit(solution)/shard_map/ppermute | solution.py:649
  209.7 15.8 %copy-start.3 = (bf16[1024,1024]{1,0:T(8,128)(2,1)S(1)}, bf16[1024,1024]{1,0:T(8,128)(2,1)}, u32[]{:S(2)}) copy-start(bf16[1024,1024]{1,0:T(8,128)(2,1)} %get-tuple-element.53) | copy-start | bytes 6291460
  209.7 15.8 %collective-permute-start.28 = (bf16[256,1024]{1,0:T(8,128)(2,1)S(1)}, bf16[256,1024]{1,0:T(8,128)(2,1)S(1)}, u32[]{:S(2)}, u32[]{:S(2)}) collective-permute-start(bf16[256,1024]{1,0:T(8,128)(2,1)S(1)} %get-tuple-element.95), channel_id=1, source_target_pairs={{3,2},{2,1},{7,6},{6,5},{11,10},{10,9},{15,14},{14,13},{19,18},{18... | collective-permute-start | bytes 1572872 | tf_op jit(solution)/shard_map/ppermute | solution.py:650
  218.9 15.4 %collective-permute-start.13 = (bf16[256,1024]{1,0:T(8,128)(2,1)S(1)}, bf16[256,1024]{1,0:T(8,128)(2,1)S(1)}, u32[]{:S(2)}, u32[]{:S(2)}) collective-permute-start(bf16[256,1024]{1,0:T(8,128)(2,1)S(1)} %get-tuple-element.99), channel_id=1, source_target_pairs={{3,2},{2,1},{7,6},{6,5},{11,10},{10,9},{15,14},{14,13},{19,18},{18... | collective-permute-start | bytes 1572872 | tf_op jit(solution)/shard_map/ppermute | solution.py:650
  220.2 22.2 %collective-permute-start.26 = (bf16[256,1024]{1,0:T(8,128)(2,1)}, bf16[256,1024]{1,0:T(8,128)(2,1)S(1)}, u32[]{:S(2)}, u32[]{:S(2)}) collective-permute-start(bf16[256,1024]{1,0:T(8,128)(2,1)} %get-tuple-element.94), channel_id=1, source_target_pairs={{0,1},{1,2},{2,3},{4,5},{5,6},{6,7},{8,9},{9,10},{10,11},{12,13},{... | collective-permute-start | bytes 1572872 | tf_op jit(solution)/shard_map/ppermute | solution.py:649
  226.5 16.8 %collective-permute-start.29 = (bf16[256,1024]{1,0:T(8,128)(2,1)}, bf16[256,1024]{1,0:T(8,128)(2,1)}, u32[]{:S(2)}, u32[]{:S(2)}) collective-permute-start(bf16[256,1024]{1,0:T(8,128)(2,1)} %add_convert_fusion), channel_id=1, source_target_pairs={{3,2},{2,1},{1,0},{7,6},{6,5},{5,4},{11,10},{10,9},{9,8},{15,14},{... | collective-permute-start | bytes 1572872 | tf_op jit(solution)/shard_map/ppermute | solution.py:650
  228.3 17.8 %collective-permute-start.11 = (bf16[256,1024]{1,0:T(8,128)(2,1)}, bf16[256,1024]{1,0:T(8,128)(2,1)}, u32[]{:S(2)}, u32[]{:S(2)}) collective-permute-start(bf16[256,1024]{1,0:T(8,128)(2,1)} %get-tuple-element.98), channel_id=1, source_target_pairs={{0,1},{1,2},{2,3},{4,5},{5,6},{6,7},{8,9},{9,10},{10,11},{12,13},{... | collective-permute-start | bytes 1572872 | tf_op jit(solution)/shard_map/ppermute | solution.py:649
  236.4 15.7 %collective-permute-start.14 = (bf16[256,1024]{1,0:T(8,128)(2,1)}, bf16[256,1024]{1,0:T(8,128)(2,1)}, u32[]{:S(2)}, u32[]{:S(2)}) collective-permute-start(bf16[256,1024]{1,0:T(8,128)(2,1)} %add_convert_fusion.4), channel_id=1, source_target_pairs={{3,2},{2,1},{1,0},{7,6},{6,5},{5,4},{11,10},{10,9},{9,8},{15,14},{... | collective-permute-start | bytes 1572872 | tf_op jit(solution)/shard_map/ppermute | solution.py:650
  240.7 11.3 %copy-start.4 = (bf16[1,256,1024]{2,1,0:T(8,128)(2,1)S(1)}, bf16[1,256,1024]{2,1,0:T(8,128)(2,1)}, u32[]{:S(2)}) copy-start(bf16[1,256,1024]{2,1,0:T(8,128)(2,1)} %param.19) | copy-start | bytes 1572868
  256.1 10.4 %collective-permute-start.36 = (bf16[128,256]{1,0:T(8,128)(2,1)S(1)}, bf16[128,256]{1,0:T(8,128)(2,1)S(1)}, u32[]{:S(2)}, u32[]{:S(2)}) collective-permute-start(bf16[128,256]{1,0:T(8,128)(2,1)S(1)} %slice.99), channel_id=1, source_target_pairs={{0,3},{1,0},{2,1},{3,2},{4,7},{5,4},{6,5},{7,6},{8,11},{9,8},{10,9... | collective-permute-start | bytes 196616 | tf_op jit(solution)/shard_map/ppermute | solution.py:657
  256.5 10.7 %collective-permute-start.37 = (bf16[128,256]{1,0:T(8,128)(2,1)S(1)}, bf16[128,256]{1,0:T(8,128)(2,1)S(1)}, u32[]{:S(2)}, u32[]{:S(2)}) collective-permute-start(bf16[128,256]{1,0:T(8,128)(2,1)S(1)} %slice.99), channel_id=1, source_target_pairs={{0,2},{1,3},{2,0},{3,1},{4,6},{5,7},{6,4},{7,5},{8,10},{9,11},{10,... | collective-permute-start | bytes 196616 | tf_op jit(solution)/shard_map/ppermute | solution.py:657
  263.2 6.1 %collective-permute-start.38 = (bf16[128,256]{1,0:T(8,128)(2,1)S(1)}, bf16[128,256]{1,0:T(8,128)(2,1)S(1)}, u32[]{:S(2)}, u32[]{:S(2)}) collective-permute-start(bf16[128,256]{1,0:T(8,128)(2,1)S(1)} %slice.99), channel_id=1, source_target_pairs={{0,1},{1,2},{2,3},{3,0},{4,5},{5,6},{6,7},{7,4},{8,9},{9,10},{10,1... | collective-permute-start | bytes 196616 | tf_op jit(solution)/shard_map/ppermute | solution.py:657
Sparse Core Ops, SparseCore 0:
  12.6 38.3 all-gather.1
  133.4 34.3 reduce-scatter.4
  171.2 44.8 reduce-scatter.2

commit v3 on v2

--- a/solution.py
+++ b/solution.py
@@ -251,11 +251,8 @@
     square_ref[...] = as_row(jnp.sum(gated * gated, axis=1, keepdims=True))
 
 
-def gradient_kernel(width, near, place_ref, *refs):
-    near_refs, refs = refs[:near], refs[near:]
-    weights_ref, scaled_ref, window_ref, cot_ref, grad_ref, along_ref = refs
+def gradient_kernel(width, cot_ref, weights_ref, scaled_ref, window_ref, grad_ref, along_ref):
     step = pl.program_id(0)
-    pick_block(place_ref[0], near_refs, cot_ref)
     window = window_ref[pl.ds(pl.multiple_of(step * Q, Q), Q + 2 * HALO), :]
     live = (window[HALO : HALO + Q] > 0).astype(F32)
     grad = dot(cot_ref[...], weights_ref[...]) * widen(live, width)
@@ -286,6 +283,7 @@
     grad_ref,
     proj_ref,
     part_ref,
+    out_ref,
     sum_x_ref,
     sum_bc_ref,
     sum_head_ref,
@@ -312,6 +310,7 @@
 
     window = window_ref[pl.ds(pl.multiple_of(step * Q, Q), Q + 2 * HALO), :]
     seg, from_prev, same_last, passes, bias = block_masks(window, seg_row_ref[0:1, :])
+    live = (seg[:, 0:1] > 0).astype(F32)
     stat = stat_ref[...].T
     gate_inverse = lax.rsqrt(stat[:, 0:1] / full_inner + EPS)
     along = stat[:, 1:2] * (gate_inverse * gate_inverse * gate_inverse / full_inner)
@@ -326,6 +325,7 @@
     gated = mixed * opened
     normal = gated * gate_inverse
     sum_gate = jnp.sum(grad_out * normal, axis=0, keepdims=True)
+    out_ref[...] = (normal * gain * live).astype(BF16)
     grad_gated = grad_out * gain * gate_inverse - gated * along
     grad_z = grad_gated * mixed * (gate * (1.0 + z_proj * (1.0 - gate)))
     dy = grad_gated * opened
@@ -455,6 +455,10 @@
     sum_gain_ref[0:1, :] += jnp.sum(part * (hidden * inverse), axis=0, keepdims=True)
 
 
+def cost(micros):
+    return pl.CostEstimate(flops=int(micros * 1e9), bytes_accessed=1 << 20, transcendentals=0)
+
+
 def whole(shape):
     return pl.BlockSpec(shape, lambda i: (0,) * len(shape))
 
@@ -525,36 +529,63 @@
             pltpu.VMEM((N, width), F32),
         ],
         compiler_params=pltpu.CompilerParams(vmem_limit_bytes=VMEM_LIMIT),
+        cost_estimate=cost(20),
         name="forward",
     )(place, *near, window, seg_row, weights, kernel_x, kernel_bc, head, channel)
 
 
-def run_gradient(place, near, weights, scaled, window):
-    features = near[0].shape[1]
-    length, width = scaled.shape
+def run_gradient(cot, weights, scaled, window):
+    length, features = cot.shape
+    width = scaled.shape[1]
     return pl.pallas_call(
-        functools.partial(gradient_kernel, width, len(near)),
+        functools.partial(gradient_kernel, width),
         grid=(length // Q,),
         in_specs=[
-            scalar(),
-            *[whole(block.shape) for block in near],
+            pl.BlockSpec((Q, features), lambda i: (i, 0)),
             pl.BlockSpec((features, width), lambda i: (0, 0)),
             pl.BlockSpec((Q, width), lambda i: (i, 0)),
             whole(window.shape),
         ],
         out_specs=[
-            pl.BlockSpec((Q, features), lambda i: (i, 0)),
             pl.BlockSpec((Q, width), lambda i: (i, 0)),
             pl.BlockSpec((8, Q), lambda i: (0, i)),
         ],
         out_shape=[
-            jax.ShapeDtypeStruct((length, features), BF16),
             jax.ShapeDtypeStruct((length, width), F32),
             jax.ShapeDtypeStruct((8, length), F32),
         ],
         compiler_params=pltpu.CompilerParams(vmem_limit_bytes=VMEM_LIMIT),
+        cost_estimate=cost(5),
         name="out_gradient",
-    )(place, *near, weights, scaled, window)
+    )(cot, weights, scaled, window)
+
+
+def weights_kernel(width, cot_ref, normed_ref, tokens_ref, grads_ref, first_ref, second_ref):
+    tokens = tokens_ref[...]
+    first_ref[:, :width] = dot_tn(cot_ref[...], normed_ref[...]).astype(BF16)
+    first_ref[:, width:] = dot_tn(tokens, grads_ref[:, 2 * width :]).astype(BF16)
+    second_ref[...] = dot_tn(tokens, grads_ref[:, : 2 * width]).astype(BF16)
+
+
+def run_weights(cot, normed, tokens, grads):
+    length, features = tokens.shape
+    width = normed.shape[1]
+    columns = [grads.shape[1] - width, 2 * width]
+    return pl.pallas_call(
+        functools.partial(weights_kernel, width),
+        grid=(features // Q,),
+        in_specs=[
+            pl.BlockSpec((length, Q), lambda i: (0, i)),
+            whole(normed.shape),
+            pl.BlockSpec((length, Q), lambda i: (0, i)),
+            whole(grads.shape),
+        ],
+        out_specs=[pl.BlockSpec((Q, count), lambda i: (i, 0)) for count in columns],
+        out_shape=[jax.ShapeDtypeStruct((features, count), BF16) for count in columns],
+        compiler_params=pltpu.CompilerParams(vmem_limit_bytes=VMEM_LIMIT),
+        cost_estimate=cost(7),
+        name="weight_gradients",
+    )(cot, normed, tokens, grads)
 
 
 def run_backward(
@@ -597,8 +628,8 @@
             pl.BlockSpec((1, N, width), lambda i: (blocks - 1 - i, 0, 0)),
             rows(width),
         ],
-        out_specs=[rows(total), rows(features)] + [whole(shape) for shape in sums],
-        out_shape=[made(total, BF16), made(features, BF16)]
+        out_specs=[rows(total), rows(features), rows(width)] + [whole(shape) for shape in sums],
+        out_shape=[made(total, BF16), made(features, BF16), made(width, BF16)]
         + [jax.ShapeDtypeStruct(shape, F32) for shape in sums],
         scratch_shapes=[
             pltpu.VMEM((Q + HALO, width), F32),
@@ -607,6 +638,7 @@
             pltpu.VMEM((8, LANES), F32),
         ],
         compiler_params=pltpu.CompilerParams(vmem_limit_bytes=VMEM_LIMIT),
+        cost_estimate=cost(27),
         name="backward",
     )(
         stat, hidden, window, seg_row, weights, kernel_x, kernel_bc, head, channel,
@@ -649,6 +681,29 @@
         right = lax.ppermute(send_right, axis, [(i, i + 1) for i in range(step)])
         left = lax.ppermute(send_left, axis, [(n - 1 - i, n - 2 - i) for i in range(step)])
     return block(place).astype(F32) + right.astype(F32) + left.astype(F32)
+
+
+def cube_scatter(part, axis, upward):
+    n = lax.axis_size(axis)
+    if n & (n - 1):
+        return lax.psum_scatter(part, axis, scatter_dimension=0, tiled=True).astype(F32)
+    place = lax.axis_index(axis)
+    rows, columns = part.shape
+    bits = list(range(n.bit_length() - 1))
+    order = bits if upward else bits[:1] + bits[:0:-1]
+    left = bits[::-1]
+    part = part.reshape((2,) * len(bits) + (rows // n, columns))
+    for bit in order:
+        dim = left.index(bit)
+        mine = (place >> bit) & 1
+        keep = lax.dynamic_index_in_dim(part, mine, dim, keepdims=False)
+        send = lax.dynamic_index_in_dim(part, 1 - mine, dim, keepdims=False)
+        other = lax.ppermute(send, axis, [(i, i ^ (1 << bit)) for i in range(n)])
+        part = keep.astype(F32) + other.astype(F32)
+        left.remove(bit)
+        if left:
+            part = part.astype(BF16)
+    return part
 
 
 def around(values, axis):
@@ -713,8 +768,8 @@
     seg_full = lax.dynamic_slice_in_dim(
         jnp.concatenate(seg_stack + seg_stack), (n - axis_place) * count, n * count, 0
     )
-    cot_local, _, _ = lax.optimization_barrier((cotangent[0], near_hidden[0], near_hidden[-1]))
-    near_cot = line_gather(cot_local, "tensor")
+    cot_local, _ = lax.optimization_barrier((cotangent[0], weights))
+    cot_full = lax.all_gather(cot_local, "tensor", axis=0, tiled=True)
 
     window = jnp.broadcast_to(
         jnp.pad(seg_full, (HALO, HALO), constant_values=-1)[:, None],
@@ -732,27 +787,23 @@
     ) = run_forward(
         heads, size, place, near_hidden, window, seg_row, weights, kernel_x, kernel_bc, head, channel
     )
-    out_sum = line_scatter(out_part, "tensor")
-    cot_full, grad_out, along = run_gradient(place, near_cot, weights, scaled, window)
+    out_part, _ = lax.optimization_barrier((out_part, cot_full))
+    out_sum = lax.psum_scatter(out_part, "tensor", scatter_dimension=0, tiled=True)
+    grad_out, along = run_gradient(cot_full, weights, scaled, window)
     stat = sum_around(jnp.stack([square[0], along[0]]), "tensor")
     stat_full = jnp.pad(stat, ((0, 6), (0, 0)))
     out_scale = lax.rsqrt(stat[0] / full_inner + EPS) * (seg_full > 0).astype(F32)
-    normed_out = (scaled.astype(F32) * out_scale[:, None]).astype(BF16)
-    grad_w_out = lax.psum_scatter(
-        dot_tn(cot_full, normed_out).astype(BF16), "dp", scatter_dimension=0, tiled=True
-    )
-
-    grads, in_part, sum_x, sum_bc, sum_head, sum_gain = run_backward(
+
+    grads, in_part, normed_out, sum_x, sum_bc, sum_head, sum_gain = run_backward(
         heads, size, full_inner, stat_full, hidden_full, window, seg_row, weights, kernel_x,
         kernel_bc, head, channel, z_proj, mixed, x_proj, pre, bcdt, pre_bc, states, grad_out,
     )
     in_sum = line_scatter(in_part, "tensor")
 
-    sum_weights = lax.psum_scatter(
-        dot_tn(tokens, grads).astype(BF16), "dp", scatter_dimension=0, tiled=True
-    )
-    sum_bc_weights = sum_weights[:, 2 * width : 2 * width + 2 * N]
-    grad_bc = sum(part.astype(F32) for part in around(sum_bc_weights, "tensor"))
+    first, second = run_weights(cot_full, normed_out, tokens, grads)
+    first = cube_scatter(first, "dp", True)
+    second = cube_scatter(second, "dp", False)
+    grad_bc = sum_around(first[:, width : width + 2 * N], "tensor")
     own = jnp.concatenate([sum_x.reshape(-1, LANES), sum_head])
     both = jnp.concatenate([sum_gain[0].reshape(-1, LANES), sum_bc.reshape(-1, LANES)])
     both = sum_around(both, "tensor")
@@ -770,7 +821,7 @@
     local = hidden_local.shape[0]
     hidden_rows = hidden_local.astype(F32)
     scale_here = lax.dynamic_slice_in_dim(out_scale, axis_place * local, local, 0)[:, None]
-    layer_out = (hidden_rows + out_sum * scale_here).astype(BF16)
+    layer_out = (hidden_rows + out_sum.astype(F32) * scale_here).astype(BF16)
 
     inverse = lax.rsqrt(jnp.mean(hidden_rows * hidden_rows, axis=1, keepdims=True) + EPS)
     unit = hidden_rows * inverse
@@ -780,15 +831,14 @@
         + inverse * (grad_scaled - unit * jnp.mean(grad_scaled * unit, axis=1, keepdims=True))
     ).astype(BF16)
 
-    sum_weights = sum_weights.astype(F32)
     return (
         layer_out[None],
         grad_hidden[None],
         grad_norm_gain,
-        sum_weights[:, width : 2 * width],
-        sum_weights[:, :width],
+        second[:, width:],
+        second[:, :width],
         grad_bc,
-        sum_weights[:, 2 * width + 2 * N : 2 * width + 2 * N + heads],
+        first[:, width + 2 * N : width + 2 * N + heads],
         sum_x[0:CONV],
         sum_x[CONV],
         sum_bc[0:CONV],
@@ -797,7 +847,7 @@
         sum_head[1, :heads],
         jnp.sum(sum_x[CONV + 2].reshape(heads, size), axis=1),
         sum_x[CONV + 1],
-        grad_w_out.astype(F32),
+        first[:, :width],
     )
 
 

time: 279 us -> 282 us (1.011)
  waiting for transfers between devices: 81.5 us -> 106 us
  starting transfers between devices: 72.8 us -> 55.3 us
  matrix products: 11.5 us -> 0 us
  Pallas kernels: 54.3 us -> 62.3 us
  other arithmetic: 23.1 us -> 17.8 us
  local copies, waits for them, and re-layouts: 19.9 us -> 24.9 us
    all_gather x1, waiting for transfers between devices: 0.01 us -> 24 us  [shards(): weights = lax.all_gather(packed, 'dp', axis=0, tiled=True)]
    ppermute x6 -> x3, waiting for transfers between devices: 39.9 us -> 56.4 us  [line_gather(): lax.ppermute(left, axis, [(i, i - 1) for i in range(1, n - step + 1)])]
    ppermute x6 -> x3, starting transfers between devices: 25.9 us -> 11 us  [line_scatter(): right = lax.ppermute(send_right, axis, [(i, i + 1) for i in range(step)])]
    dot_general x2 -> x0, matrix products: 11.5 us -> none  [dot_tn(): lax.dot_general(a, b, (((0,), (0,)), ((), ())), preferred_element_type=F32)]
    ppermute x6 -> x3, waiting for transfers between devices: 15.9 us -> 5.06 us  [line_scatter(): right = lax.ppermute(send_right, axis, [(i, i + 1) for i in range(step)])]
    ppermute x6 -> x3, waiting for transfers between devices: 10.5 us -> 0.01 us  [line_gather(): lax.ppermute(right, axis, [(i, i + 1) for i in range(step - 1, n - 1)])]
    pallas_call x1 -> x2, Pallas kernels: 6.06 us -> 13.2 us  [the longest x1 8.31 us: run_weights(): pl.pallas_call(functools.partial(weights_kernel, width), grid=(features /...]
    convert_element_type x4 -> x2, other arithmetic: 7.71 us -> 2.4 us  [line_scatter(): send_right = (send_right.astype(F32) + right.astype(F32)).astype(part.dtype)]
  transfers between devices with their start and end apart: 42 -> 36, of which waited for: 19 -> 11; matrix products, arithmetic and copies ran while one was open for 15% -> 11% of each run, Pallas kernels for 17% -> 20%
where the time goes in v3:
time: 282 us; the launch traced here: 281 us
  waiting for transfers between devices  106 us (38%)
  Pallas kernels  62.3 us (22%)
  starting transfers between devices  55.3 us (20%)
  local copies, waits for them, and re-layouts  24.9 us (9%)
  other arithmetic  17.8 us (6%)
  between operations  14.4 us (5%)
    ppermute x3, waiting for transfers between devices, line_gather(): lax.ppermute(left, axis, [(i, i - 1) for i in range(1, n - step + 1)])  56.4 us
    pallas_call x1, Pallas kernels, run_backward(): pl.pallas_call(functools.partial(backward_kernel, heads, size, full_inner...  27.8 us
    all_gather x1, waiting for transfers between devices, shards(): weights = lax.all_gather(packed, 'dp', axis=0, tiled=True)  24 us
    ppermute x12, starting transfers between devices, around(): lax.ppermute(values, axis, [(i, (i - k) % n) for i in range(n)])  23.2 us
    pallas_call x1, Pallas kernels, run_forward(): pl.pallas_call(functools.partial(forward_kernel, heads, size, len(near)),...  21.3 us
    ppermute x3, starting transfers between devices, line_scatter(): right = lax.ppermute(send_right, axis, [(i, i + 1) for i in range(step)])  11 us
    ppermute x12, waiting for transfers between devices, around(): lax.ppermute(values, axis, [(i, (i - k) % n) for i in range(n)])  10.3 us
    pallas_call x1, Pallas kernels, run_weights(): pl.pallas_call(functools.partial(weights_kernel, width), grid=(features /...  8.31 us
  transfers between devices with their start and end apart: 36, of which 11 were waited for; matrix products, arithmetic and copies ran while one was open for 11% of the time, Pallas kernels for 20%

profile of v3, /device:TPU:0, one launch (start us, length us, event | category | flops | bytes accessed | tf_op | source)
XLA Modules:
  0.0 280.9 jit_solution(4391111815776553597)
XLA Ops:
  7.3 0.8 pad_maximum_fusion.5
  8.2 0.9 constant_dynamic-update-slice_fusion.4
  9.1 0.9 constant_dynamic-update-slice_fusion.3
  10.1 0.9 constant_dynamic-update-slice_fusion.2
  11.0 0.8 constant_dynamic-update-slice_fusion.1
  11.9 0.8 copy-done.10
  12.7 1.3 collective-permute-start.3
  14.0 5.6 %collective-permute-start = (bf16[256,1024]{1,0:T(8,128)(2,1)}, bf16[256,1024]{1,0:T(8,128)(2,1)S(1)}, u32[]{:S(2)}, u32[]{:S(2)}) collective-permute-start(bf16[256,1024]{1,0:T(8,128)(2,1)} %bitcast.72), channel_id=1, source_target_pairs={{0,1},{1,2},{2,3},{4,5},{5,6},{6,7},{8,9},{9,10},{10,11},{12,13},{... | collective-permute-start | bytes 1572872 | tf_op jit(solution)/shard_map/ppermute | solution.py:658
  19.6 2.0 collective-permute-start.8
  21.6 1.1 collective-permute-start.7
  22.8 2.8 %collective-permute-start.6 = (s32[256]{0:T(256)}, s32[256]{0:T(256)S(1)}, u32[]{:S(2)}, u32[]{:S(2)}) collective-permute-start(s32[256]{0:T(256)} %bitcast.85), channel_id=1, source_target_pairs={{0,3},{1,0},{2,1},{3,2},{4,7},{5,4},{6,5},{7,6},{8,11},{9,8},{10,9... | collective-permute-start | bytes 3080 | tf_op jit(solution)/shard_map/ppermute | solution.py:712
  27.1 24.0 %all-gather.3.cloned.1.call-done.refs_9_.weights_ref = bf16[1024,1920]{1,0:T(8,128)(2,1)} async-done(((bf16[128,1920]{1,0:T(8,128)(2,1)}), bf16[1024,1920]{1,0:T(8,128)(2,1)}) %all-gather.3.cloned.1.call-update) | async-done | bytes 3932176 | tf_op jit(solution)/shard_map/all_gather | solution.py:765
  51.9 1.3 collective-permute-start.4
  54.3 22.1 %collective-permute-done.4.refs_5_ = bf16[256,1024]{1,0:T(8,128)(2,1)S(1)} collective-permute-done((bf16[256,1024]{1,0:T(8,128)(2,1)S(1)}, bf16[256,1024]{1,0:T(8,128)(2,1)S(1)}, u32[]{:S(2)}, u32[]{:S(2)}) %collective-permute-start.4) | collective-permute-done | bytes 524320 | tf_op jit(solution)/shard_map/ppermute | solution.py:659
  76.3 1.3 collective-permute-start.5
  78.6 34.3 %collective-permute-done.5.refs_6_ = bf16[256,1024]{1,0:T(8,128)(2,1)S(1)} collective-permute-done((bf16[256,1024]{1,0:T(8,128)(2,1)S(1)}, bf16[256,1024]{1,0:T(8,128)(2,1)S(1)}, u32[]{:S(2)}, u32[]{:S(2)}) %collective-permute-start.5) | collective-permute-done | bytes 524320 | tf_op jit(solution)/shard_map/ppermute | solution.py:659
  112.9 1.0 broadcast_in_dim.37.refs_7_.window_ref
  113.9 21.3 %forward.1 = (bf16[1024,1024]{1,0:T(8,128)(2,1)}, bf16[1024,1024]{1,0:T(8,128)(2,1)}, f32[1024,512]{1,0:T(8,128)}, f32[1024,512]{1,0:T(8,128)}, f32[1024,512]{1,...) custom-call(s32[1]{0:T(128)} %bitcast.1.place_ref, ...), custom_call_target="tpu_custom_call" | custom-call | flops 20000000000 | bytes 1048576 | tf_op jit(solution)/shard_map/forward/pallas_call | solution.py:482
  135.3 1.2 copy-done.1
  136.5 4.9 %out_gradient.1 = (f32[1024,512]{1,0:T(8,128)}, f32[8,1024]{1,0:T(8,128)S(1)}) custom-call(bf16[1024,1024]{1,0:T(8,128)(2,1)} %all-gather.5.cloned.1.call-done.cot_ref, bf16[1024,1920]{1,0:T(8,128)(2,1)} %all-gather.3.cloned.1.call-done.refs_9_.weights_ref, bf16[1024,512]{1,0:T(8,128)(2,1)S(1)} %copy-done.1, s32[1040,128]{1,0:T(8,128)S(1)} %copy-done), custom_call_target="tpu_custom_call" | custom-call | flops 5000000000 | bytes 1048576 | tf_op jit(solution)/shard_map/out_gradient/pallas_call | solution.py:540
  141.4 2.5 collective-permute-start.10
  143.9 2.5 collective-permute-start.11
  146.4 1.3 collective-permute-start.9
  148.3 1.1 collective-permute-done.11
  150.1 27.8 %backward.1 = (bf16[1024,1408]{1,0:T(8,128)(2,1)}, bf16[1024,1024]{1,0:T(8,128)(2,1)}, bf16[1024,512]{1,0:T(8,128)(2,1)S(1)}, f32[8,512]{1,0:T(8,128)S(1)}, f32[...) custom-call(f32[8,1024]{1,0:T(8,128)S(1)} %pad.19.stat_ref, ...), custom_call_target="tpu_custom_call" | custom-call | flops 27000000512 | bytes 1048576 | tf_op jit(solution)/shard_map/backward/pallas_call | solution.py:609
  178.0 3.7 %collective-permute-start.20 = (f32[24,128]{1,0:T(8,128)S(1)}, f32[24,128]{1,0:T(8,128)S(1)}, u32[]{:S(2)}, u32[]{:S(2)}) collective-permute-start(f32[24,128]{1,0:T(8,128)S(1)} %pad_maximum_fusion.2), channel_id=1, source_target_pairs={{0,1},{1,2},{2,3},{3,0},{4,5},{5,6},{6,7},{7,4},{8,9},{9,10},{10,1... | collective-permute-start | bytes 36872 | tf_op jit(solution)/shard_map/ppermute | solution.py:712
  181.9 8.3 %weight_gradients.1 = (bf16[1024,896]{1,0:T(8,128)(2,1)}, bf16[1024,1024]{1,0:T(8,128)(2,1)}) custom-call(bf16[1024,1024]{1,0:T(8,128)(2,1)} %all-gather.5.cloned.1.call-done.cot_ref, bf16[1024,512]{1,0:T(8,128)(2,1)S(1)} %get-tuple-element.63.normed_ref, bf16[1024,1024]{1,0:T(8,128)(2,1)} %get-tuple-element.64.tokens_ref, ...), custom_call_target="tpu_custom_call" | custom-call | flops 7000000000 | bytes 1048576 | tf_op jit(solution)/shard_map/weight_gradients/pallas_call | solution.py:574
  190.4 1.8 constant_dynamic-slice_fusion.1
  192.2 1.0 copy.50
  193.7 1.5 collective-permute-start.22
  195.3 1.0 constant_dynamic-slice_fusion.3
  196.3 3.7 %collective-permute-start.12 = (bf16[256,1024]{1,0:T(8,128)(2,1)}, bf16[256,1024]{1,0:T(8,128)(2,1)S(1)}, u32[]{:S(2)}, u32[]{:S(2)}) collective-permute-start(bf16[256,1024]{1,0:T(8,128)(2,1)} %get-tuple-element.102), channel_id=1, source_target_pairs={{0,1},{4,5},{8,9},{12,13},{16,17},{20,21},{24,25},{28,29}} | collective-permute-start | bytes 1572872 | tf_op jit(solution)/shard_map/ppermute | solution.py:681
  200.0 1.5 collective-permute-start.15
  202.1 1.0 dynamic-slice_bitcast_fusion
  203.8 1.7 collective-permute-done.23
  206.7 0.8 reshape_squeeze.7
  208.1 1.3 slice.92
  210.0 1.3 dynamic_slice.81
  211.2 1.2 slice_bitcast_fusion.3
  212.5 1.3 slice_bitcast_fusion.4
  214.0 2.1 collective-permute-start.13
  216.1 1.5 fusion.1
  218.2 1.5 fusion
  219.8 1.4 collective-permute-start.25
  221.2 5.1 %collective-permute-done.13 = bf16[256,1024]{1,0:T(8,128)(2,1)S(1)} collective-permute-done((bf16[256,1024]{1,0:T(8,128)(2,1)S(1)}, bf16[256,1024]{1,0:T(8,128)(2,1)S(1)}, u32[]{:S(2)}, u32[]{:S(2)}) %collective-permute-start.13) | collective-permute-done | bytes 524320 | tf_op jit(solution)/shard_map/ppermute | solution.py:681
  226.2 2.2 add_convert_fusion.2
  228.4 5.2 %collective-permute-start.14 = (bf16[256,1024]{1,0:T(8,128)(2,1)}, bf16[256,1024]{1,0:T(8,128)(2,1)}, u32[]{:S(2)}, u32[]{:S(2)}) collective-permute-start(bf16[256,1024]{1,0:T(8,128)(2,1)} %get-tuple-element.100), channel_id=1, source_target_pairs={{0,1},{1,2},{2,3},{4,5},{5,6},{6,7},{8,9},{9,10},{10,11},{12,13},{... | collective-permute-start | bytes 1572872 | tf_op jit(solution)/shard_map/ppermute | solution.py:681
  234.5 1.2 collective-permute-start.29
  235.9 0.8 collective-permute-start.26
  236.7 3.8 %collective-permute-done.29 = bf16[128,896]{1,0:T(8,128)(2,1)S(1)} collective-permute-done((bf16[128,896]{1,0:T(8,128)(2,1)S(1)}, bf16[128,896]{1,0:T(8,128)(2,1)S(1)}, u32[]{:S(2)}, u32[]{:S(2)}) %collective-permute-start.29) | collective-permute-done | bytes 229408 | tf_op jit(solution)/shard_map/ppermute | solution.py:701
  241.3 2.2 collective-permute-start.31
  243.5 4.8 %collective-permute-start.30 = (f32[128,256]{1,0:T(8,128)}, f32[128,256]{1,0:T(8,128)}, u32[]{:S(2)}, u32[]{:S(2)}) collective-permute-start(f32[128,256]{1,0:T(8,128)} %slice.103), channel_id=1, source_target_pairs={{0,3},{1,0},{2,1},{3,2},{4,7},{5,4},{6,5},{7,6},{8,11},{9,8},{10,9... | collective-permute-start | bytes 393224 | tf_op jit(solution)/shard_map/ppermute | solution.py:712
  248.3 1.0 add_convert_fusion
  249.3 0.7 slice.113
  250.7 7.0 %collective-permute-done.31 = f32[128,256]{1,0:T(8,128)S(1)} collective-permute-done((f32[128,256]{1,0:T(8,128)}, f32[128,256]{1,0:T(8,128)S(1)}, u32[]{:S(2)}, u32[]{:S(2)}) %collective-permute-start.31) | collective-permute-done | bytes 131104 | tf_op jit(solution)/shard_map/ppermute | solution.py:712
  257.7 1.3 collective-permute-start.17
  259.0 1.4 collective-permute-done.30
  260.5 1.7 add_add_fusion
  262.1 1.1 convert_add_fusion.5
  263.3 0.8 fusion.18
  264.1 4.9 %collective-permute-done.17 = bf16[256,1024]{1,0:T(8,128)(2,1)S(1)} collective-permute-done((bf16[256,1024]{1,0:T(8,128)(2,1)}, bf16[256,1024]{1,0:T(8,128)(2,1)S(1)}, u32[]{:S(2)}, u32[]{:S(2)}) %collective-permute-start.17) | collective-permute-done | bytes 524320 | tf_op jit(solution)/shard_map/ppermute | solution.py:682
  269.0 0.8 copy-done.9
  269.8 1.5 fusion.4
  271.3 3.0 %fusion.14 = (bf16[1,256,1024]{2,1,0:T(8,128)(2,1)}, bf16[1,256,1024]{2,1,0:T(8,128)(2,1)}) fusion(bf16[256,1024]{1,0:T(8,128)(2,1)} %copy-done.9, bf16[256,1024]{1,0:T(8,128)(2,1)} %collective-permute-done.14, f32[256]{0:T(256)S(1)} %broadcast_multiply_fusion, f32[1024]{0:T(1024)S(1)} %bitcast.81, f32[256]{0:T(256)S(1)} %copy-done.12, ...), kind=kLoop, calls=%fused_computation.29 | loop fusion | flops 4718592 | bytes 4201476 | tf_op jit(solution)/shard_map/broadcast_in_dim | solution.py:836
  (141 shorter events, 13.8 us)
Async XLA Ops:
  7.2 46.8 %copy-start.3 = (bf16[1,256,1024]{2,1,0:T(8,128)(2,1)S(1)}, bf16[1,256,1024]{2,1,0:T(8,128)(2,1)}, u32[]{:S(2)}) copy-start(bf16[1,256,1024]{2,1,0:T(8,128)(2,1)} %param.17) | copy-start | bytes 1572868
  7.2 46.8 %copy-start.14 = (s32[1,256]{1,0:T(1,128)S(1)}, s32[1,256]{1,0:T(1,128)}, u32[]{:S(2)}) copy-start(s32[1,256]{1,0:T(1,128)} %param.18) | copy-start | bytes 3076
  7.2 44.7 %copy-start.16 = (f32[512]{0:T(512)S(1)}, f32[512]{0:T(512)}, u32[]{:S(2)}) copy-start(f32[512]{0:T(512)} %param.26) | copy-start | bytes 6148
  7.2 44.7 %copy-start.13 = (f32[4,512]{1,0:T(4,128)S(1)}, f32[4,512]{1,0:T(4,128)}, u32[]{:S(2)}) copy-start(f32[4,512]{1,0:T(4,128)} %param.25) | copy-start | bytes 24580
  7.2 46.9 %copy-start.17 = (f32[8]{0:T(128)S(1)}, f32[8]{0:T(128)}, u32[]{:S(2)}) copy-start(f32[8]{0:T(128)} %param.30) | copy-start | bytes 100
  7.2 46.9 %copy-start.18 = (f32[8]{0:T(128)S(1)}, f32[8]{0:T(128)}, u32[]{:S(2)}) copy-start(f32[8]{0:T(128)} %param.29) | copy-start | bytes 100
  7.2 43.9 %all-gather.3.cloned.1.call-start = ((), (), s32[]{:S(2)}) async-start(), calls=%async_computation.1 | async-start | bytes 4423680 | tf_op jit(solution)/shard_map/all_gather | solution.py:765
  11.8 0.8 copy-start.10
  12.7 122.6 %all-gather.5.cloned.1.call-start = ((), (), s32[]{:S(2)}) async-start(), calls=%async_computation.2 | async-start | bytes 2621440 | tf_op jit(solution)/shard_map/all_gather | solution.py:772
  12.7 39.2 %collective-permute-start.3 = (bf16[256,1024]{1,0:T(8,128)(2,1)}, bf16[256,1024]{1,0:T(8,128)(2,1)S(1)}, u32[]{:S(2)}, u32[]{:S(2)}) collective-permute-start(bf16[256,1024]{1,0:T(8,128)(2,1)} %bitcast.71), channel_id=1, source_target_pairs={{1,0},{2,1},{3,2},{5,4},{6,5},{7,6},{9,8},{10,9},{11,10},{13,12},{... | collective-permute-start | bytes 1572872 | tf_op jit(solution)/shard_map/ppermute | solution.py:659
  14.0 39.2 %collective-permute-start = (bf16[256,1024]{1,0:T(8,128)(2,1)}, bf16[256,1024]{1,0:T(8,128)(2,1)S(1)}, u32[]{:S(2)}, u32[]{:S(2)}) collective-permute-start(bf16[256,1024]{1,0:T(8,128)(2,1)} %bitcast.72), channel_id=1, source_target_pairs={{0,1},{1,2},{2,3},{4,5},{5,6},{6,7},{8,9},{9,10},{10,11},{12,13},{... | collective-permute-start | bytes 1572872 | tf_op jit(solution)/shard_map/ppermute | solution.py:658
  19.6 58.7 %collective-permute-start.8 = (s32[256]{0:T(256)}, s32[256]{0:T(256)S(1)}, u32[]{:S(2)}, u32[]{:S(2)}) collective-permute-start(s32[256]{0:T(256)} %bitcast.83), channel_id=1, source_target_pairs={{0,1},{1,2},{2,3},{3,0},{4,5},{5,6},{6,7},{7,4},{8,9},{9,10},{10,1... | collective-permute-start | bytes 3080 | tf_op jit(solution)/shard_map/ppermute | solution.py:712
  21.6 32.6 %collective-permute-start.7 = (s32[256]{0:T(256)}, s32[256]{0:T(256)S(1)}, u32[]{:S(2)}, u32[]{:S(2)}) collective-permute-start(s32[256]{0:T(256)} %bitcast.84), channel_id=1, source_target_pairs={{0,2},{1,3},{2,0},{3,1},{4,6},{5,7},{6,4},{7,5},{8,10},{9,11},{10,... | collective-permute-start | bytes 3080 | tf_op jit(solution)/shard_map/ppermute | solution.py:712
  22.8 31.4 %collective-permute-start.6 = (s32[256]{0:T(256)}, s32[256]{0:T(256)S(1)}, u32[]{:S(2)}, u32[]{:S(2)}) collective-permute-start(s32[256]{0:T(256)} %bitcast.85), channel_id=1, source_target_pairs={{0,3},{1,0},{2,1},{3,2},{4,7},{5,4},{6,5},{7,6},{8,11},{9,8},{10,9... | collective-permute-start | bytes 3080 | tf_op jit(solution)/shard_map/ppermute | solution.py:712
  51.2 220.2 %reduce-scatter.2.cloned.1.call-start = ((), (), s32[]{:S(2)}) async-start(), calls=%async_computation.3 | async-start | bytes 2621440 | tf_op jit(solution)/shard_map/reduce_scatter | solution.py:791
  51.9 62.0 %copy-start.19 = (bf16[256,1024]{1,0:T(8,128)(2,1)}, bf16[256,1024]{1,0:T(8,128)(2,1)S(1)}, u32[]{:S(2)}) copy-start(bf16[256,1024]{1,0:T(8,128)(2,1)S(1)} %collective-permute-done.3.refs_4_) | copy-start | bytes 1572868
  51.9 24.4 %collective-permute-start.4 = (bf16[256,1024]{1,0:T(8,128)(2,1)S(1)}, bf16[256,1024]{1,0:T(8,128)(2,1)S(1)}, u32[]{:S(2)}, u32[]{:S(2)}) collective-permute-start(bf16[256,1024]{1,0:T(8,128)(2,1)S(1)} %collective-permute-done.3.refs_4_), channel_id=1, source_target_pairs={{1,0},{2,1},{5,4},{6,5},{9,8},{10,9},{13,12},{14,13},{17,16},{18,1... | collective-permute-start | bytes 1572872 | tf_op jit(solution)/shard_map/ppermute | solution.py:659
  53.3 24.4 %collective-permute-start.1 = (bf16[256,1024]{1,0:T(8,128)(2,1)S(1)}, bf16[256,1024]{1,0:T(8,128)(2,1)S(1)}, u32[]{:S(2)}, u32[]{:S(2)}) collective-permute-start(bf16[256,1024]{1,0:T(8,128)(2,1)S(1)} %collective-permute-done.refs_2_), channel_id=1, source_target_pairs={{1,2},{2,3},{5,6},{6,7},{9,10},{10,11},{13,14},{14,15},{17,18},{18... | collective-permute-start | bytes 1572872 | tf_op jit(solution)/shard_map/ppermute | solution.py:658
  76.3 37.6 %copy-start.20 = (bf16[256,1024]{1,0:T(8,128)(2,1)}, bf16[256,1024]{1,0:T(8,128)(2,1)S(1)}, u32[]{:S(2)}) copy-start(bf16[256,1024]{1,0:T(8,128)(2,1)S(1)} %collective-permute-done.4.refs_5_) | copy-start | bytes 1572868
  76.3 36.5 %collective-permute-start.5 = (bf16[256,1024]{1,0:T(8,128)(2,1)S(1)}, bf16[256,1024]{1,0:T(8,128)(2,1)S(1)}, u32[]{:S(2)}, u32[]{:S(2)}) collective-permute-start(bf16[256,1024]{1,0:T(8,128)(2,1)S(1)} %collective-permute-done.4.refs_5_), channel_id=1, source_target_pairs={{1,0},{5,4},{9,8},{13,12},{17,16},{21,20},{25,24},{29,28}} | collective-permute-start | bytes 1572872 | tf_op jit(solution)/shard_map/ppermute | solution.py:659
  77.6 35.2 %collective-permute-start.2 = (bf16[256,1024]{1,0:T(8,128)(2,1)S(1)}, bf16[256,1024]{1,0:T(8,128)(2,1)S(1)}, u32[]{:S(2)}, u32[]{:S(2)}) collective-permute-start(bf16[256,1024]{1,0:T(8,128)(2,1)S(1)} %collective-permute-done.1.refs_1_), channel_id=1, source_target_pairs={{2,3},{6,7},{10,11},{14,15},{18,19},{22,23},{26,27},{30,31}} | collective-permute-start | bytes 1572872 | tf_op jit(solution)/shard_map/ppermute | solution.py:658
  112.9 1.0 copy-start.21
  113.9 21.3 %copy-start = (s32[1040,128]{1,0:T(8,128)S(1)}, s32[1040,128]{1,0:T(8,128)}, u32[]{:S(2)}) copy-start(s32[1040,128]{1,0:T(8,128)} %broadcast_in_dim.37.refs_7_.window_ref) | copy-start | bytes 1597444
  135.3 1.2 copy-start.1
  141.4 6.9 %collective-permute-start.10 = (f32[2,1024]{1,0:T(2,128)S(1)}, f32[2,1024]{1,0:T(2,128)S(1)}, u32[]{:S(2)}, u32[]{:S(2)}) collective-permute-start(f32[2,1024]{1,0:T(2,128)S(1)} %pad_maximum_fusion.4), channel_id=1, source_target_pairs={{0,2},{1,3},{2,0},{3,1},{4,6},{5,7},{6,4},{7,5},{8,10},{9,11},{10,... | collective-permute-start | bytes 24584 | tf_op jit(solution)/shard_map/ppermute | solution.py:712
  143.9 5.4 %collective-permute-start.11 = (f32[2,1024]{1,0:T(2,128)S(1)}, f32[2,1024]{1,0:T(2,128)S(1)}, u32[]{:S(2)}, u32[]{:S(2)}) collective-permute-start(f32[2,1024]{1,0:T(2,128)S(1)} %pad_maximum_fusion.4), channel_id=1, source_target_pairs={{0,1},{1,2},{2,3},{3,0},{4,5},{5,6},{6,7},{7,4},{8,9},{9,10},{10,1... | collective-permute-start | bytes 24584 | tf_op jit(solution)/shard_map/ppermute | solution.py:712
  146.4 3.7 %collective-permute-start.9 = (f32[2,1024]{1,0:T(2,128)S(1)}, f32[2,1024]{1,0:T(2,128)S(1)}, u32[]{:S(2)}, u32[]{:S(2)}) collective-permute-start(f32[2,1024]{1,0:T(2,128)S(1)} %pad_maximum_fusion.4), channel_id=1, source_target_pairs={{0,3},{1,0},{2,1},{3,2},{4,7},{5,4},{6,5},{7,6},{8,11},{9,8},{10,9... | collective-permute-start | bytes 24584 | tf_op jit(solution)/shard_map/ppermute | solution.py:712
  177.9 12.4 %collective-permute-start.19 = (f32[24,128]{1,0:T(8,128)S(1)}, f32[24,128]{1,0:T(8,128)S(1)}, u32[]{:S(2)}, u32[]{:S(2)}) collective-permute-start(f32[24,128]{1,0:T(8,128)S(1)} %pad_maximum_fusion.2), channel_id=1, source_target_pairs={{0,2},{1,3},{2,0},{3,1},{4,6},{5,7},{6,4},{7,5},{8,10},{9,11},{10,... | collective-permute-start | bytes 36872 | tf_op jit(solution)/shard_map/ppermute | solution.py:712
  178.0 12.3 %collective-permute-start.20 = (f32[24,128]{1,0:T(8,128)S(1)}, f32[24,128]{1,0:T(8,128)S(1)}, u32[]{:S(2)}, u32[]{:S(2)}) collective-permute-start(f32[24,128]{1,0:T(8,128)S(1)} %pad_maximum_fusion.2), channel_id=1, source_target_pairs={{0,1},{1,2},{2,3},{3,0},{4,5},{5,6},{6,7},{7,4},{8,9},{9,10},{10,1... | collective-permute-start | bytes 36872 | tf_op jit(solution)/shard_map/ppermute | solution.py:712
  181.6 8.6 %collective-permute-start.18 = (f32[24,128]{1,0:T(8,128)S(1)}, f32[24,128]{1,0:T(8,128)S(1)}, u32[]{:S(2)}, u32[]{:S(2)}) collective-permute-start(f32[24,128]{1,0:T(8,128)S(1)} %pad_maximum_fusion.2), channel_id=1, source_target_pairs={{0,3},{1,0},{2,1},{3,2},{4,7},{5,4},{6,5},{7,6},{8,11},{9,8},{10,9... | collective-permute-start | bytes 36872 | tf_op jit(solution)/shard_map/ppermute | solution.py:712
  190.3 3.4 %collective-permute-start.21 = (f32[64,128]{1,0:T(8,128)S(1)}, f32[64,128]{1,0:T(8,128)S(1)}, u32[]{:S(2)}, u32[]{:S(2)}) collective-permute-start(f32[64,128]{1,0:T(8,128)S(1)} %pad_maximum_fusion), channel_id=1, source_target_pairs={{0,4},{4,0},{8,12},{12,8},{16,20},{20,16},{24,28},{28,24},{1,5},{5... | collective-permute-start | bytes 98312 | tf_op jit(solution)/shard_map/ppermute | solution.py:726
  190.4 4.9 %copy-start.2 = (bf16[1024,1024]{1,0:T(8,128)(2,1)S(1)}, bf16[1024,1024]{1,0:T(8,128)(2,1)}, u32[]{:S(2)}) copy-start(bf16[1024,1024]{1,0:T(8,128)(2,1)} %get-tuple-element.57) | copy-start | bytes 6291460
  192.2 9.9 %copy-start.5 = (bf16[1024,1024]{1,0:T(8,128)(2,1)S(1)}, bf16[1024,1024]{1,0:T(8,128)(2,1)}, u32[]{:S(2)}) copy-start(bf16[1024,1024]{1,0:T(8,128)(2,1)} %get-tuple-element.66) | copy-start | bytes 6291460
  193.2 22.8 %collective-permute-start.27 = (bf16[2,2,128,896]{3,2,0,1:T(8,128)(2,1)}, bf16[2,2,128,896]{3,2,0,1:T(8,128)(2,1)}, u32[]{:S(2)}, u32[]{:S(2)}) collective-permute-start(bf16[2,2,128,896]{3,2,0,1:T(8,128)(2,1)} %bitcast.70), channel_id=1, source_target_pairs={{0,4},{4,0},{8,12},{12,8},{16,20},{20,16},{24,28},{28,24},{1,5},{5... | collective-permute-start | bytes 2752520 | tf_op jit(solution)/shard_map/ppermute | solution.py:701
  193.7 7.8 %collective-permute-start.22 = (f32[64,128]{1,0:T(8,128)S(1)}, f32[64,128]{1,0:T(8,128)S(1)}, u32[]{:S(2)}, u32[]{:S(2)}) collective-permute-start(f32[64,128]{1,0:T(8,128)S(1)} %fusion.17), channel_id=1, source_target_pairs={{0,8},{4,12},{8,0},{12,4},{16,24},{20,28},{24,16},{28,20},{1,9},{5... | collective-permute-start | bytes 98312 | tf_op jit(solution)/shard_map/ppermute | solution.py:726
  196.3 17.5 %collective-permute-start.12 = (bf16[256,1024]{1,0:T(8,128)(2,1)}, bf16[256,1024]{1,0:T(8,128)(2,1)S(1)}, u32[]{:S(2)}, u32[]{:S(2)}) collective-permute-start(bf16[256,1024]{1,0:T(8,128)(2,1)} %get-tuple-element.102), channel_id=1, source_target_pairs={{0,1},{4,5},{8,9},{12,13},{16,17},{20,21},{24,25},{28,29}} | collective-permute-start | bytes 1572872 | tf_op jit(solution)/shard_map/ppermute | solution.py:681
  200.0 21.1 %collective-permute-start.15 = (bf16[256,1024]{1,0:T(8,128)(2,1)}, bf16[256,1024]{1,0:T(8,128)(2,1)}, u32[]{:S(2)}, u32[]{:S(2)}) collective-permute-start(bf16[256,1024]{1,0:T(8,128)(2,1)} %get-tuple-element.103), channel_id=1, source_target_pairs={{3,2},{7,6},{11,10},{15,14},{19,18},{23,22},{27,26},{31,30}} | collective-permute-start | bytes 1572872 | tf_op jit(solution)/shard_map/ppermute | solution.py:682
  201.5 4.0 %collective-permute-start.23 = (f32[64,128]{1,0:T(8,128)S(1)}, f32[64,128]{1,0:T(8,128)S(1)}, u32[]{:S(2)}, u32[]{:S(2)}) collective-permute-start(f32[64,128]{1,0:T(8,128)S(1)} %add.221), channel_id=1, source_target_pairs={{0,16},{4,20},{8,24},{12,28},{16,0},{20,4},{24,8},{28,12},{1,17},{... | collective-permute-start | bytes 98312 | tf_op jit(solution)/shard_map/ppermute | solution.py:726
  203.2 15.0 %collective-permute-start.24 = (bf16[2,2,128,1024]{3,2,1,0:T(8,128)(2,1)}, bf16[2,2,128,1024]{3,2,1,0:T(8,128)(2,1)}, u32[]{:S(2)}, u32[]{:S(2)}) collective-permute-start(bf16[2,2,128,1024]{3,2,1,0:T(8,128)(2,1)} %dynamic-slice_bitcast_fusion), channel_id=1, source_target_pairs={{0,4},{4,0},{8,12},{12,8},{16,20},{20,16},{24,28},{28,24},{1,5},{5... | collective-permute-start | bytes 3145736 | tf_op jit(solution)/shard_map/ppermute | solution.py:701
  205.5 1.2 copy-start.11
  214.0 4.2 %copy-start.6 = (bf16[1024,1024]{1,0:T(8,128)(2,1)S(1)}, bf16[1024,1024]{1,0:T(8,128)(2,1)}, u32[]{:S(2)}) copy-start(bf16[1024,1024]{1,0:T(8,128)(2,1)} %get-tuple-element.66) | copy-start | bytes 6291460
  214.0 12.2 %collective-permute-start.13 = (bf16[256,1024]{1,0:T(8,128)(2,1)S(1)}, bf16[256,1024]{1,0:T(8,128)(2,1)S(1)}, u32[]{:S(2)}, u32[]{:S(2)}) collective-permute-start(bf16[256,1024]{1,0:T(8,128)(2,1)S(1)} %add_convert_fusion.3), channel_id=1, source_target_pairs={{0,1},{1,2},{4,5},{5,6},{8,9},{9,10},{12,13},{13,14},{16,17},{17,1... | collective-permute-start | bytes 1572872 | tf_op jit(solution)/shard_map/ppermute | solution.py:681
  217.6 16.7 %collective-permute-start.28 = (bf16[2,128,896]{2,1,0:T(8,128)(2,1)S(1)}, bf16[2,128,896]{2,1,0:T(8,128)(2,1)S(1)}, u32[]{:S(2)}, u32[]{:S(2)}) collective-permute-start(bf16[2,128,896]{2,1,0:T(8,128)(2,1)S(1)} %dynamic-slice_bitcast_fusion.2), channel_id=1, source_target_pairs={{0,8},{4,12},{8,0},{12,4},{16,24},{20,28},{24,16},{28,20},{1,9},{5... | collective-permute-start | bytes 1376264 | tf_op jit(solution)/shard_map/ppermute | solution.py:701
  219.8 15.9 %collective-permute-start.25 = (bf16[2,128,1024]{2,1,0:T(8,128)(2,1)S(1)}, bf16[2,128,1024]{2,1,0:T(8,128)(2,1)S(1)}, u32[]{:S(2)}, u32[]{:S(2)}) collective-permute-start(bf16[2,128,1024]{2,1,0:T(8,128)(2,1)S(1)} %dynamic-slice_bitcast_fusion.1), channel_id=1, source_target_pairs={{0,16},{4,20},{8,24},{12,28},{16,0},{20,4},{24,8},{28,12},{1,17},{... | collective-permute-start | bytes 1572872 | tf_op jit(solution)/shard_map/ppermute | solution.py:701
  228.4 35.7 %collective-permute-start.14 = (bf16[256,1024]{1,0:T(8,128)(2,1)}, bf16[256,1024]{1,0:T(8,128)(2,1)}, u32[]{:S(2)}, u32[]{:S(2)}) collective-permute-start(bf16[256,1024]{1,0:T(8,128)(2,1)} %get-tuple-element.100), channel_id=1, source_target_pairs={{0,1},{1,2},{2,3},{4,5},{5,6},{6,7},{8,9},{9,10},{10,11},{12,13},{... | collective-permute-start | bytes 1572872 | tf_op jit(solution)/shard_map/ppermute | solution.py:681
  233.6 9.9 %collective-permute-start.16 = (bf16[256,1024]{1,0:T(8,128)(2,1)S(1)}, bf16[256,1024]{1,0:T(8,128)(2,1)S(1)}, u32[]{:S(2)}, u32[]{:S(2)}) collective-permute-start(bf16[256,1024]{1,0:T(8,128)(2,1)S(1)} %get-tuple-element.101), channel_id=1, source_target_pairs={{3,2},{2,1},{7,6},{6,5},{11,10},{10,9},{15,14},{14,13},{19,18},{18... | collective-permute-start | bytes 1572872 | tf_op jit(solution)/shard_map/ppermute | solution.py:682
  234.5 6.1 %collective-permute-start.29 = (bf16[128,896]{1,0:T(8,128)(2,1)S(1)}, bf16[128,896]{1,0:T(8,128)(2,1)S(1)}, u32[]{:S(2)}, u32[]{:S(2)}) collective-permute-start(bf16[128,896]{1,0:T(8,128)(2,1)S(1)} %dynamic-slice_bitcast_fusion.4), channel_id=1, source_target_pairs={{0,16},{4,20},{8,24},{12,28},{16,0},{20,4},{24,8},{28,12},{1,17},{... | collective-permute-start | bytes 688136 | tf_op jit(solution)/shard_map/ppermute | solution.py:701
  235.9 12.4 %copy-start.7 = (bf16[2,128,1024]{2,1,0:T(8,128)(2,1)}, bf16[2,128,1024]{2,1,0:T(8,128)(2,1)S(1)}, u32[]{:S(2)}) copy-start(bf16[2,128,1024]{2,1,0:T(8,128)(2,1)S(1)} %fusion.11) | copy-start | bytes 1572868
  235.9 26.2 %collective-permute-start.26 = (bf16[128,1024]{1,0:T(8,128)(2,1)S(1)}, bf16[128,1024]{1,0:T(8,128)(2,1)}, u32[]{:S(2)}, u32[]{:S(2)}) collective-permute-start(bf16[128,1024]{1,0:T(8,128)(2,1)S(1)} %dynamic-slice_bitcast_fusion.3), channel_id=1, source_target_pairs={{0,8},{4,12},{8,0},{12,4},{16,24},{20,28},{24,16},{28,20},{1,9},{5... | collective-permute-start | bytes 786440 | tf_op jit(solution)/shard_map/ppermute | solution.py:701
  241.3 16.4 %collective-permute-start.31 = (f32[128,256]{1,0:T(8,128)}, f32[128,256]{1,0:T(8,128)S(1)}, u32[]{:S(2)}, u32[]{:S(2)}) collective-permute-start(f32[128,256]{1,0:T(8,128)} %slice.103), channel_id=1, source_target_pairs={{0,2},{1,3},{2,0},{3,1},{4,6},{5,7},{6,4},{7,5},{8,10},{9,11},{10,... | collective-permute-start | bytes 393224 | tf_op jit(solution)/shard_map/ppermute | solution.py:712
  243.5 15.6 %collective-permute-start.32 = (f32[128,256]{1,0:T(8,128)}, f32[128,256]{1,0:T(8,128)}, u32[]{:S(2)}, u32[]{:S(2)}) collective-permute-start(f32[128,256]{1,0:T(8,128)} %slice.103), channel_id=1, source_target_pairs={{0,1},{1,2},{2,3},{3,0},{4,5},{5,6},{6,7},{7,4},{8,9},{9,10},{10,1... | collective-permute-start | bytes 393224 | tf_op jit(solution)/shard_map/ppermute | solution.py:712
  243.5 16.9 %collective-permute-start.30 = (f32[128,256]{1,0:T(8,128)}, f32[128,256]{1,0:T(8,128)}, u32[]{:S(2)}, u32[]{:S(2)}) collective-permute-start(f32[128,256]{1,0:T(8,128)} %slice.103), channel_id=1, source_target_pairs={{0,3},{1,0},{2,1},{3,2},{4,7},{5,4},{6,5},{7,6},{8,11},{9,8},{10,9... | collective-permute-start | bytes 393224 | tf_op jit(solution)/shard_map/ppermute | solution.py:712
  249.3 20.5 %copy-start.4 = (bf16[1,256,1024]{2,1,0:T(8,128)(2,1)S(1)}, bf16[1,256,1024]{2,1,0:T(8,128)(2,1)}, u32[]{:S(2)}) copy-start(bf16[1,256,1024]{2,1,0:T(8,128)(2,1)} %param.17) | copy-start | bytes 1572868
  249.3 20.5 %copy-start.12 = (f32[256]{0:T(256)S(1)}, f32[256]{0:T(256)}, u32[]{:S(2)}) copy-start(f32[256]{0:T(256)} %add_rsqrt_fusion) | copy-start | bytes 3076
  257.7 11.3 %collective-permute-start.17 = (bf16[256,1024]{1,0:T(8,128)(2,1)}, bf16[256,1024]{1,0:T(8,128)(2,1)S(1)}, u32[]{:S(2)}, u32[]{:S(2)}) collective-permute-start(bf16[256,1024]{1,0:T(8,128)(2,1)} %add_convert_fusion), channel_id=1, source_target_pairs={{3,2},{2,1},{1,0},{7,6},{6,5},{5,4},{11,10},{10,9},{9,8},{15,14},{... | collective-permute-start | bytes 1572872 | tf_op jit(solution)/shard_map/ppermute | solution.py:682
  262.1 9.2 %copy-start.8 = (bf16[1,256,1024]{2,1,0:T(8,128)(2,1)S(1)}, bf16[1,256,1024]{2,1,0:T(8,128)(2,1)}, u32[]{:S(2)}) copy-start(bf16[1,256,1024]{2,1,0:T(8,128)(2,1)} %param.19) | copy-start | bytes 1572868
  262.1 9.2 %copy-start.15 = (f32[256]{0:T(256)S(1)}, f32[256]{0:T(256)}, u32[]{:S(2)}) copy-start(f32[256]{0:T(256)} %dynamic_slice.73) | copy-start | bytes 3076
  269.0 0.8 copy-start.9
Sparse Core Ops, SparseCore 0:
  12.8 38.3 all-gather.2
  52.7 55.9 all-gather.4
  148.4 42.0 reduce-scatter.1

commit v4 on v3

--- a/solution.py
+++ b/solution.py
@@ -125,22 +125,29 @@
             block[...] = ref[...]
 
 
+def project_kernel(heads, size, near, place_ref, *refs):
+    near_refs, refs = refs[:near], refs[near:]
+    weights_ref, hidden_ref, tokens_ref, z_ref, x_ref, bcdt_ref, gain_ref = refs
+    width = heads * size
+
+    @pl.when(pl.program_id(0) == 0)
+    def _():
+        tail_columns = weights_ref[:, 3 * width + 2 * N :].astype(F32).T
+        gain_ref[...] = jnp.broadcast_to(tail_columns[heads : heads + 1], gain_ref.shape)
+
+    pick_block(place_ref[0], near_refs, hidden_ref)
+    hidden = hidden_ref[...].astype(F32)
+    inverse = lax.rsqrt(jnp.mean(hidden * hidden, axis=1, keepdims=True) + EPS)
+    tokens = (hidden * inverse * gain_ref[0:1, :]).astype(BF16)
+    tokens_ref[...] = tokens
+    x_ref[...] = dot(tokens, weights_ref[:, width : 2 * width])
+    z_ref[...] = dot(tokens, weights_ref[:, 2 * width : 3 * width])
+    bcdt_ref[...] = dot(tokens, weights_ref[:, 3 * width :])
+
+
 def forward_kernel(
     heads,
     size,
-    near,
-    place_ref,
-    *refs,
-):
-    near_refs, refs = refs[:near], refs[near:]
-    forward_body(heads, size, place_ref[0], near_refs, *refs)
-
-
-def forward_body(
-    heads,
-    size,
-    place,
-    near_refs,
     window_ref,
     seg_row_ref,
     weights_ref,
@@ -148,51 +155,34 @@
     kernel_bc_ref,
     head_ref,
     channel_ref,
-    hidden_ref,
-    tokens_ref,
     z_ref,
+    x_ref,
+    bcdt_ref,
     mixed_ref,
-    x_ref,
     pre_ref,
-    bcdt_ref,
     pre_bc_ref,
     state_ref,
     scaled_ref,
     part_ref,
     square_ref,
-    gain_ref,
     x_buffer,
     bc_buffer,
     carry,
 ):
     step = pl.program_id(0)
     width = heads * size
-    rest = 2 * N + LANES
 
     @pl.when(step == 0)
     def _():
         x_buffer[0:HALO, :] = jnp.zeros((HALO, width), F32)
         bc_buffer[0:HALO, :] = jnp.zeros((HALO, 2 * N), F32)
         carry[...] = jnp.zeros((N, width), F32)
-        tail_columns = weights_ref[:, 3 * width + 2 * N :].astype(F32).T
-        gain_ref[...] = jnp.broadcast_to(tail_columns[heads : heads + 1], gain_ref.shape)
-
-    pick_block(place, near_refs, hidden_ref)
+
     window = window_ref[pl.ds(pl.multiple_of(step * Q, Q), Q + 2 * HALO), :]
     seg, from_prev, same_last, passes, bias = block_masks(window, seg_row_ref[0:1, :])
-
-    hidden = hidden_ref[...].astype(F32)
-    inverse = lax.rsqrt(jnp.mean(hidden * hidden, axis=1, keepdims=True) + EPS)
-    tokens = (hidden * inverse * gain_ref[0:1, :]).astype(BF16)
-    tokens_ref[...] = tokens
-    x_proj = dot(tokens, weights_ref[:, width : 2 * width])
-    z_proj = dot(tokens, weights_ref[:, 2 * width : 3 * width])
-    bcdt = dot(tokens, weights_ref[:, 3 * width : 3 * width + rest])
-    z_ref[...] = z_proj
-    x_ref[...] = x_proj
-    bcdt_ref[...] = bcdt
-
-    x_buffer[HALO : HALO + Q, :] = x_proj
+    z_proj = z_ref[...]
+    bcdt = bcdt_ref[...]
+    x_buffer[HALO : HALO + Q, :] = x_ref[...]
     bc_buffer[HALO : HALO + Q, :] = bcdt[:, : 2 * N]
     pre = conv_forward(
         x_buffer, window, seg, kernel_x_ref[...], kernel_x_ref[CONV : CONV + 1, :], width
@@ -247,12 +237,15 @@
     gated = mixed * (z_proj * sigmoid(z_proj))
     scaled = (gated * channel_ref[0:1, :]).astype(BF16)
     scaled_ref[...] = scaled
-    part_ref[...] = dot_nt(scaled, weights_ref[:, :width]).astype(BF16)
+    part_ref[...] = dot_nt(scaled, weights_ref[...]).astype(BF16)
     square_ref[...] = as_row(jnp.sum(gated * gated, axis=1, keepdims=True))
 
 
-def gradient_kernel(width, cot_ref, weights_ref, scaled_ref, window_ref, grad_ref, along_ref):
+def gradient_kernel(width, near, place_ref, *refs):
+    near_refs, refs = refs[:near], refs[near:]
+    weights_ref, scaled_ref, window_ref, cot_ref, grad_ref, along_ref = refs
     step = pl.program_id(0)
+    pick_block(place_ref[0], near_refs, cot_ref)
     window = window_ref[pl.ds(pl.multiple_of(step * Q, Q), Q + 2 * HALO), :]
     live = (window[HALO : HALO + Q] > 0).astype(F32)
     grad = dot(cot_ref[...], weights_ref[...]) * widen(live, width)
@@ -467,10 +460,11 @@
     return pl.BlockSpec(memory_space=pltpu.SMEM)
 
 
-def run_forward(heads, size, place, near, window, seg_row, weights, kernel_x, kernel_bc, head, channel):
-    length, features = seg_row.shape[1], near[0].shape[1]
+def run_project(heads, size, place, near, weights):
+    features = near[0].shape[1]
+    blocks = len(near) // 2 + 1
+    length = blocks * Q
     width = heads * size
-    blocks = length // Q
     rest = 2 * N + LANES
 
     def rows(columns):
@@ -480,32 +474,15 @@
         return jax.ShapeDtypeStruct((length, columns), dtype)
 
     return pl.pallas_call(
-        functools.partial(forward_kernel, heads, size, len(near)),
+        functools.partial(project_kernel, heads, size, len(near)),
         grid=(blocks,),
-        in_specs=[
-            scalar(),
-            *[whole(block.shape) for block in near],
-            whole(window.shape),
-            pl.BlockSpec((8, Q), lambda i: (0, i)),
-            whole(weights.shape),
-            whole(kernel_x.shape),
-            whole(kernel_bc.shape),
-            whole(head.shape),
-            whole(channel.shape),
-        ],
+        in_specs=[scalar(), *[whole(block.shape) for block in near], whole(weights.shape)],
         out_specs=[
             rows(features),
             rows(features),
             rows(width),
             rows(width),
-            rows(width),
-            rows(width),
             rows(rest),
-            rows(2 * N),
-            pl.BlockSpec((1, N, width), lambda i: (i, 0, 0)),
-            rows(width),
-            rows(features),
-            pl.BlockSpec((8, Q), lambda i: (0, i)),
             whole((8, features)),
         ],
         out_shape=[
@@ -513,15 +490,61 @@
             made(features, BF16),
             made(width, F32),
             made(width, F32),
+            made(rest, F32),
+            jax.ShapeDtypeStruct((8, features), F32),
+        ],
+        compiler_params=pltpu.CompilerParams(vmem_limit_bytes=VMEM_LIMIT),
+        cost_estimate=cost(8),
+        name="project",
+    )(place, *near, weights)
+
+
+def run_forward(
+    heads, size, window, seg_row, weights, kernel_x, kernel_bc, head, channel, z_proj, x_proj, bcdt
+):
+    length, features = seg_row.shape[1], weights.shape[0]
+    width = heads * size
+    blocks = length // Q
+
+    def rows(columns):
+        return pl.BlockSpec((Q, columns), lambda i: (i, 0))
+
+    def made(columns, dtype):
+        return jax.ShapeDtypeStruct((length, columns), dtype)
+
+    across = pl.BlockSpec((8, Q), lambda i: (0, i))
+    return pl.pallas_call(
+        functools.partial(forward_kernel, heads, size),
+        grid=(blocks,),
+        in_specs=[
+            whole(window.shape),
+            across,
+            whole((features, width)),
+            whole(kernel_x.shape),
+            whole(kernel_bc.shape),
+            whole(head.shape),
+            whole(channel.shape),
+            rows(width),
+            rows(width),
+            rows(bcdt.shape[1]),
+        ],
+        out_specs=[
+            rows(width),
+            rows(width),
+            rows(2 * N),
+            pl.BlockSpec((1, N, width), lambda i: (i, 0, 0)),
+            rows(width),
+            rows(features),
+            across,
+        ],
+        out_shape=[
             made(width, F32),
             made(width, F32),
-            made(rest, F32),
             made(2 * N, F32),
             jax.ShapeDtypeStruct((blocks, N, width), F32),
             made(width, BF16),
             made(features, BF16),
             jax.ShapeDtypeStruct((8, length), F32),
-            jax.ShapeDtypeStruct((8, features), F32),
         ],
         scratch_shapes=[
             pltpu.VMEM((Q + HALO, width), F32),
@@ -529,35 +552,38 @@
             pltpu.VMEM((N, width), F32),
         ],
         compiler_params=pltpu.CompilerParams(vmem_limit_bytes=VMEM_LIMIT),
-        cost_estimate=cost(20),
+        cost_estimate=cost(14),
         name="forward",
-    )(place, *near, window, seg_row, weights, kernel_x, kernel_bc, head, channel)
-
-
-def run_gradient(cot, weights, scaled, window):
-    length, features = cot.shape
-    width = scaled.shape[1]
+    )(window, seg_row, weights, kernel_x, kernel_bc, head, channel, z_proj, x_proj, bcdt)
+
+
+def run_gradient(place, near, weights, scaled, window):
+    features = near[0].shape[1]
+    length, width = scaled.shape
     return pl.pallas_call(
-        functools.partial(gradient_kernel, width),
+        functools.partial(gradient_kernel, width, len(near)),
         grid=(length // Q,),
         in_specs=[
-            pl.BlockSpec((Q, features), lambda i: (i, 0)),
-            pl.BlockSpec((features, width), lambda i: (0, 0)),
+            scalar(),
+            *[whole(block.shape) for block in near],
+            whole((features, width)),
             pl.BlockSpec((Q, width), lambda i: (i, 0)),
             whole(window.shape),
         ],
         out_specs=[
+            pl.BlockSpec((Q, features), lambda i: (i, 0)),
             pl.BlockSpec((Q, width), lambda i: (i, 0)),
             pl.BlockSpec((8, Q), lambda i: (0, i)),
         ],
         out_shape=[
+            jax.ShapeDtypeStruct((length, features), BF16),
             jax.ShapeDtypeStruct((length, width), F32),
             jax.ShapeDtypeStruct((8, length), F32),
         ],
         compiler_params=pltpu.CompilerParams(vmem_limit_bytes=VMEM_LIMIT),
         cost_estimate=cost(5),
         name="out_gradient",
-    )(cot, weights, scaled, window)
+    )(place, *near, weights, scaled, window)
 
 
 def weights_kernel(width, cot_ref, normed_ref, tokens_ref, grads_ref, first_ref, second_ref):
@@ -660,27 +686,6 @@
         from_left.append(right)
         from_right.append(left)
     return from_left[::-1] + [block] + from_right
-
-
-def line_scatter(part, axis):
-    n = lax.axis_size(axis)
-    place = lax.axis_index(axis)
-    count = part.shape[0] // n
-
-    def block(index):
-        start = jnp.clip(index, 0, n - 1) * count
-        return lax.dynamic_slice_in_dim(part, start, count, 0)
-
-    right = left = None
-    for step in range(1, n):
-        send_right = block(n - step + place)
-        send_left = block(step + place - n)
-        if step > 1:
-            send_right = (send_right.astype(F32) + right.astype(F32)).astype(part.dtype)
-            send_left = (send_left.astype(F32) + left.astype(F32)).astype(part.dtype)
-        right = lax.ppermute(send_right, axis, [(i, i + 1) for i in range(step)])
-        left = lax.ppermute(send_left, axis, [(n - 1 - i, n - 2 - i) for i in range(step)])
-    return block(place).astype(F32) + right.astype(F32) + left.astype(F32)
 
 
 def cube_scatter(part, axis, upward):
@@ -768,8 +773,8 @@
     seg_full = lax.dynamic_slice_in_dim(
         jnp.concatenate(seg_stack + seg_stack), (n - axis_place) * count, n * count, 0
     )
-    cot_local, _ = lax.optimization_barrier((cotangent[0], weights))
-    cot_full = lax.all_gather(cot_local, "tensor", axis=0, tiled=True)
+    cot_local, _, _ = lax.optimization_barrier((cotangent[0], near_hidden[0], near_hidden[-1]))
+    near_cot = line_gather(cot_local, "tensor")
 
     window = jnp.broadcast_to(
         jnp.pad(seg_full, (HALO, HALO), constant_values=-1)[:, None],
@@ -781,15 +786,17 @@
     head = pad_lanes(jnp.stack([dt_bias, a_log]))
     channel = jnp.stack([gate_gain, jnp.repeat(d_skip, size)])
 
-    (
-        hidden_full, tokens, z_proj, mixed, x_proj, pre, bcdt, pre_bc, states, scaled, out_part,
-        square, gain,
-    ) = run_forward(
-        heads, size, place, near_hidden, window, seg_row, weights, kernel_x, kernel_bc, head, channel
-    )
-    out_part, _ = lax.optimization_barrier((out_part, cot_full))
+    hidden_full, tokens, z_proj, x_proj, bcdt, gain = run_project(
+        heads, size, place, near_hidden, weights
+    )
+    bcdt, _, _ = lax.optimization_barrier((bcdt, near_cot[n - 2], near_cot[n]))
+    mixed, pre, pre_bc, states, scaled, out_part, square = run_forward(
+        heads, size, window, seg_row, weights, kernel_x, kernel_bc, head, channel, z_proj, x_proj,
+        bcdt,
+    )
+    cot_full, grad_out, along = run_gradient(place, near_cot, weights, scaled, window)
+    out_part, _ = lax.optimization_barrier((out_part, along))
     out_sum = lax.psum_scatter(out_part, "tensor", scatter_dimension=0, tiled=True)
-    grad_out, along = run_gradient(cot_full, weights, scaled, window)
     stat = sum_around(jnp.stack([square[0], along[0]]), "tensor")
     stat_full = jnp.pad(stat, ((0, 6), (0, 0)))
     out_scale = lax.rsqrt(stat[0] / full_inner + EPS) * (seg_full > 0).astype(F32)
@@ -798,21 +805,23 @@
         heads, size, full_inner, stat_full, hidden_full, window, seg_row, weights, kernel_x,
         kernel_bc, head, channel, z_proj, mixed, x_proj, pre, bcdt, pre_bc, states, grad_out,
     )
-    in_sum = line_scatter(in_part, "tensor")
+    in_sum = lax.psum_scatter(in_part, "tensor", scatter_dimension=0, tiled=True)
 
     first, second = run_weights(cot_full, normed_out, tokens, grads)
     first = cube_scatter(first, "dp", True)
     second = cube_scatter(second, "dp", False)
-    grad_bc = sum_around(first[:, width : width + 2 * N], "tensor")
     own = jnp.concatenate([sum_x.reshape(-1, LANES), sum_head])
     both = jnp.concatenate([sum_gain[0].reshape(-1, LANES), sum_bc.reshape(-1, LANES)])
-    both = sum_around(both, "tensor")
     small = sum_pairwise(jnp.concatenate([own, both]), "dp")
-    cuts = [sum_x.size // LANES, 8, features // LANES]
-    sum_x = small[: cuts[0]].reshape(8, width)
-    sum_head = small[cuts[0] : cuts[0] + 8]
-    sum_gain = small[cuts[0] + 8 : cuts[0] + 8 + cuts[2]].reshape(features)
-    sum_bc = small[cuts[0] + 8 + cuts[2] :].reshape(8, 2 * N)
+    sum_x = small[: own.shape[0] - 8].reshape(8, width)
+    sum_head = small[own.shape[0] - 8 : own.shape[0]]
+    grad_bc = first[:, width : width + 2 * N]
+    shared = jnp.concatenate([small[own.shape[0] :], grad_bc.reshape(-1, LANES)])
+    shared = sum_around(shared, "tensor")
+    gain_rows = features // LANES
+    sum_gain = shared[:gain_rows].reshape(features)
+    sum_bc = shared[gain_rows : both.shape[0]].reshape(8, 2 * N)
+    grad_bc = shared[both.shape[0] :].reshape(grad_bc.shape)
     local_features = norm_gain.shape[0]
     grad_norm_gain = lax.dynamic_slice_in_dim(
         sum_gain, lax.axis_index("dp") * local_features, local_features, 0
@@ -825,7 +834,7 @@
 
     inverse = lax.rsqrt(jnp.mean(hidden_rows * hidden_rows, axis=1, keepdims=True) + EPS)
     unit = hidden_rows * inverse
-    grad_scaled = in_sum * gain[0:1]
+    grad_scaled = in_sum.astype(F32) * gain[0:1]
     grad_hidden = (
         cotangent[0].astype(F32)
         + inverse * (grad_scaled - unit * jnp.mean(grad_scaled * unit, axis=1, keepdims=True))

time: 282 us -> 258 us (0.915)
  waiting for transfers between devices: 106 us -> 96.3 us
  local copies, waits for them, and re-layouts: 24.9 us -> 17.5 us
  other arithmetic: 17.8 us -> 12.3 us
  starting transfers between devices: 55.3 us -> 51.6 us
    reduce_scatter x1, waiting for transfers between devices: 0.02 us -> 32.2 us  [shards(): lax.psum_scatter(out_part, 'tensor', scatter_dimension=0, tiled=True)]
    all_gather x1, waiting for transfers between devices: 24 us -> 0.02 us  [shards(): weights = lax.all_gather(packed, 'dp', axis=0, tiled=True)]
    ppermute x3 -> x6, waiting for transfers between devices: 56.4 us -> 39.9 us  [line_gather(): lax.ppermute(left, axis, [(i, i - 1) for i in range(1, n - step + 1)])]
    ppermute x6 -> x0, starting transfers between devices: 14.4 us -> none  [the longest x3 11 us: line_scatter(): right = lax.ppermute(send_right, axis, [(i, i + 1) for i in range(step)])]
    ppermute x6, waiting for transfers between devices: 3.86 us -> 14.4 us  [cube_scatter(): other = lax.ppermute(send, axis, [(i, i ^ 1 << bit) for i in range(n)])]
    ppermute x6 -> x0, waiting for transfers between devices: 9.95 us -> none  [the longest x3 5.06 us: line_scatter(): right = lax.ppermute(send_right, axis, [(i, i + 1) for i in range(step)])]
    ppermute x12 -> x9, waiting for transfers between devices: 10.3 us -> 3.02 us  [around(): lax.ppermute(values, axis, [(i, (i - k) % n) for i in range(n)])]
    ppermute x3 -> x6, starting transfers between devices: 6.98 us -> 13 us  [line_gather(): lax.ppermute(right, axis, [(i, i + 1) for i in range(step - 1, n - 1)])]
  transfers between devices with their start and end apart: 36 -> 33, of which waited for: 11 -> 15; matrix products, arithmetic and copies ran while one was open for 11% -> 8% of each run, Pallas kernels for 20% -> 12%
where the time goes in v4:
time: 258 us; the launch traced here: 257 us
  waiting for transfers between devices  96.3 us (37%)
  Pallas kernels  64.6 us (25%)
  starting transfers between devices  51.6 us (20%)
  local copies, waits for them, and re-layouts  17.5 us (7%)
  between operations  14.3 us (6%)
  other arithmetic  12.3 us (5%)
    ppermute x6, waiting for transfers between devices, line_gather(): lax.ppermute(left, axis, [(i, i - 1) for i in range(1, n - step + 1)])  39.9 us
    reduce_scatter x1, waiting for transfers between devices, shards(): lax.psum_scatter(out_part, 'tensor', scatter_dimension=0, tiled=True)  32.2 us
    pallas_call x1, Pallas kernels, run_backward(): pl.pallas_call(functools.partial(backward_kernel, heads, size, full_inner...  27.4 us
    ppermute x9, starting transfers between devices, around(): lax.ppermute(values, axis, [(i, (i - k) % n) for i in range(n)])  22.4 us
    ppermute x6, waiting for transfers between devices, cube_scatter(): other = lax.ppermute(send, axis, [(i, i ^ 1 << bit) for i in range(n)])  14.4 us
    pallas_call x1, Pallas kernels, run_forward(): pl.pallas_call(functools.partial(forward_kernel, heads, size), grid=(bloc...  13.9 us
    ppermute x6, starting transfers between devices, line_gather(): lax.ppermute(right, axis, [(i, i + 1) for i in range(step - 1, n - 1)])  13 us
    pallas_call x1, Pallas kernels, run_weights(): pl.pallas_call(functools.partial(weights_kernel, width), grid=(features /...  8.44 us
  transfers between devices with their start and end apart: 33, of which 15 were waited for; matrix products, arithmetic and copies ran while one was open for 8% of the time, Pallas kernels for 12%

profile of v4, /device:TPU:0, one launch (start us, length us, event | category | flops | bytes accessed | tf_op | source)
XLA Modules:
  0.0 256.6 jit_solution(17856950294031902772)
XLA Ops:
  7.2 0.7 pad_maximum_fusion.5
  8.1 0.9 constant_dynamic-update-slice_fusion.4
  9.0 0.9 constant_dynamic-update-slice_fusion.3
  9.9 0.9 constant_dynamic-update-slice_fusion.2
  10.8 0.8 constant_dynamic-update-slice_fusion.1
  11.7 0.8 copy-done.5
  12.6 1.3 collective-permute-start.6
  13.9 5.6 %collective-permute-start.3 = (bf16[256,1024]{1,0:T(8,128)(2,1)}, bf16[256,1024]{1,0:T(8,128)(2,1)S(1)}, u32[]{:S(2)}, u32[]{:S(2)}) collective-permute-start(bf16[256,1024]{1,0:T(8,128)(2,1)} %bitcast.72), channel_id=1, source_target_pairs={{0,1},{1,2},{2,3},{4,5},{5,6},{6,7},{8,9},{9,10},{10,11},{12,13},{... | collective-permute-start | bytes 1572872 | tf_op jit(solution)/shard_map/ppermute | solution.py:684
  19.5 10.2 %collective-permute-done.6.refs_4_ = bf16[256,1024]{1,0:T(8,128)(2,1)S(1)} collective-permute-done((bf16[256,1024]{1,0:T(8,128)(2,1)}, bf16[256,1024]{1,0:T(8,128)(2,1)S(1)}, u32[]{:S(2)}, u32[]{:S(2)}) %collective-permute-start.6) | collective-permute-done | bytes 524320 | tf_op jit(solution)/shard_map/ppermute | solution.py:685
  29.6 1.3 collective-permute-start.7
  30.9 0.7 collective-permute-start.4
  31.6 13.1 %collective-permute-done.7.refs_5_ = bf16[256,1024]{1,0:T(8,128)(2,1)S(1)} collective-permute-done((bf16[256,1024]{1,0:T(8,128)(2,1)S(1)}, bf16[256,1024]{1,0:T(8,128)(2,1)S(1)}, u32[]{:S(2)}, u32[]{:S(2)}) %collective-permute-start.7) | collective-permute-done | bytes 524320 | tf_op jit(solution)/shard_map/ppermute | solution.py:685
  44.7 1.3 collective-permute-start.8
  46.0 0.7 collective-permute-start.5
  46.7 2.7 %collective-permute-start.2 = (s32[256]{0:T(256)}, s32[256]{0:T(256)S(1)}, u32[]{:S(2)}, u32[]{:S(2)}) collective-permute-start(s32[256]{0:T(256)} %bitcast.86), channel_id=1, source_target_pairs={{0,1},{1,2},{2,3},{3,0},{4,5},{5,6},{6,7},{7,4},{8,9},{9,10},{10,1... | collective-permute-start | bytes 3080 | tf_op jit(solution)/shard_map/ppermute | solution.py:717
  49.4 3.1 %collective-permute-start.1 = (s32[256]{0:T(256)}, s32[256]{0:T(256)S(1)}, u32[]{:S(2)}, u32[]{:S(2)}) collective-permute-start(s32[256]{0:T(256)} %bitcast.87), channel_id=1, source_target_pairs={{0,2},{1,3},{2,0},{3,1},{4,6},{5,7},{6,4},{7,5},{8,10},{9,11},{10,... | collective-permute-start | bytes 3080 | tf_op jit(solution)/shard_map/ppermute | solution.py:717
  52.6 2.8 %collective-permute-start = (s32[256]{0:T(256)}, s32[256]{0:T(256)S(1)}, u32[]{:S(2)}, u32[]{:S(2)}) collective-permute-start(s32[256]{0:T(256)} %bitcast.88), channel_id=1, source_target_pairs={{0,3},{1,0},{2,1},{3,2},{4,7},{5,4},{6,5},{7,6},{8,11},{9,8},{10,9... | collective-permute-start | bytes 3080 | tf_op jit(solution)/shard_map/ppermute | solution.py:717
  55.4 0.7 broadcast_in_dim.41
  56.2 0.7 pad_maximum_fusion.6.channel_ref
  56.9 0.7 pad_maximum_fusion.3.kernel_bc_ref
  57.6 1.4 collective-permute-done.8.refs_6_
  59.1 1.3 collective-permute-start.10
  60.4 4.6 %collective-permute-start.9 = (bf16[256,1024]{1,0:T(8,128)(2,1)}, bf16[256,1024]{1,0:T(8,128)(2,1)S(1)}, u32[]{:S(2)}, u32[]{:S(2)}) collective-permute-start(bf16[256,1024]{1,0:T(8,128)(2,1)} %bitcast.79), channel_id=1, source_target_pairs={{0,1},{1,2},{2,3},{4,5},{5,6},{6,7},{8,9},{9,10},{10,11},{12,13},{... | collective-permute-start | bytes 1572872 | tf_op jit(solution)/shard_map/ppermute | solution.py:684
  65.0 0.7 constant_dynamic-update-slice_fusion
  65.6 0.7 pad_maximum_fusion.2.kernel_x_ref
  67.1 5.6 %collective-permute-done.10.refs_4_ = bf16[256,1024]{1,0:T(8,128)(2,1)S(1)} collective-permute-done((bf16[256,1024]{1,0:T(8,128)(2,1)}, bf16[256,1024]{1,0:T(8,128)(2,1)S(1)}, u32[]{:S(2)}, u32[]{:S(2)}) %collective-permute-start.10) | collective-permute-done | bytes 524320 | tf_op jit(solution)/shard_map/ppermute | solution.py:685
  72.6 1.3 collective-permute-start.13
  74.0 0.7 collective-permute-start.11
  74.7 0.7 constant_dynamic-update-slice_fusion.7
  75.5 9.6 %collective-permute-done.13.refs_5_ = bf16[256,1024]{1,0:T(8,128)(2,1)} collective-permute-done((bf16[256,1024]{1,0:T(8,128)(2,1)S(1)}, bf16[256,1024]{1,0:T(8,128)(2,1)}, u32[]{:S(2)}, u32[]{:S(2)}) %collective-permute-start.13) | collective-permute-done | bytes 524320 | tf_op jit(solution)/shard_map/ppermute | solution.py:685
  85.2 1.3 collective-permute-start.14
  86.5 0.7 collective-permute-start.12
  87.2 8.4 %project.1 = (bf16[1024,1024]{1,0:T(8,128)(2,1)}, bf16[1024,1024]{1,0:T(8,128)(2,1)}, f32[1024,512]{1,0:T(8,128)}, f32[1024,512]{1,0:T(8,128)}, f32[1024,384]{1,0:T(8,128)}, /*index=5*/f32[8,1024]{1,0:T(8,128)S(1)}) custom-call(s32[1]{0:T(128)} %bitcast.8.place_ref, bf16[256,1024]{1,0:T(8,128)(2,1)S(1)} %collective-permute-done.5.refs_0_, ...), custom_call_target="tpu_custom_call" | custom-call | flops 8000000000 | bytes 1048576 | tf_op jit(solution)/shard_map/project/pallas_call | solution.py:476
  95.9 13.9 %forward.1 = (f32[1024,512]{1,0:T(8,128)}, f32[1024,512]{1,0:T(8,128)}, f32[1024,256]{1,0:T(8,128)S(1)}, f32[4,128,512]{2,1,0:T(8,128)}, bf16[1024,512]{1,0:T(8,...) custom-call(s32[1040,128]{1,0:T(8,128)S(1)} %broadcast_in_dim.36.window_ref.refs_9_, ...), custom_call_target="tpu_custom_call" | custom-call | flops 14000000000 | bytes 1048576 | tf_op jit(solution)/shard_map/forward/pallas_call | solution.py:516
  109.8 6.4 %out_gradient.1 = (bf16[1024,1024]{1,0:T(8,128)(2,1)}, f32[1024,512]{1,0:T(8,128)}, f32[8,1024]{1,0:T(8,128)S(1)}) custom-call(s32[1]{0:T(128)} %bitcast.8.place_ref, bf16[256,1024]{1,0:T(8,128)(2,1)S(1)} %collective-permute-done.12.refs_0_, bf16[256,1024]{1,0:T(8,128)(2,1)S(1)} %collective-permute-done.11.refs_1_, ...), custom_call_target="tpu_custom_call" | custom-call | flops 5000000000 | bytes 1048576 | tf_op jit(solution)/shard_map/out_gradient/pallas_call | solution.py:563
  116.3 5.4 %collective-permute-start.16 = (f32[2,1024]{1,0:T(2,128)S(1)}, f32[2,1024]{1,0:T(2,128)S(1)}, u32[]{:S(2)}, u32[]{:S(2)}) collective-permute-start(f32[2,1024]{1,0:T(2,128)S(1)} %pad_maximum_fusion.4), channel_id=1, source_target_pairs={{0,2},{1,3},{2,0},{3,1},{4,6},{5,7},{6,4},{7,5},{8,10},{9,11},{10,... | collective-permute-start | bytes 24584 | tf_op jit(solution)/shard_map/ppermute | solution.py:717
  121.7 3.8 %collective-permute-start.15 = (f32[2,1024]{1,0:T(2,128)S(1)}, f32[2,1024]{1,0:T(2,128)S(1)}, u32[]{:S(2)}, u32[]{:S(2)}) collective-permute-start(f32[2,1024]{1,0:T(2,128)S(1)} %pad_maximum_fusion.4), channel_id=1, source_target_pairs={{0,3},{1,0},{2,1},{3,2},{4,7},{5,4},{6,5},{7,6},{8,11},{9,8},{10,9... | collective-permute-start | bytes 24584 | tf_op jit(solution)/shard_map/ppermute | solution.py:717
  125.5 1.6 collective-permute-done.17
  127.2 27.4 %backward.1 = (bf16[1024,1408]{1,0:T(8,128)(2,1)}, bf16[1024,1024]{1,0:T(8,128)(2,1)}, bf16[1024,512]{1,0:T(8,128)(2,1)S(1)}, f32[8,512]{1,0:T(8,128)S(1)}, f32[...) custom-call(f32[8,1024]{1,0:T(8,128)S(1)} %pad.19.stat_ref, ...), custom_call_target="tpu_custom_call" | custom-call | flops 27000000512 | bytes 1048576 | tf_op jit(solution)/shard_map/backward/pallas_call | solution.py:635
  154.7 1.0 copy-done.3
  155.9 8.4 %weight_gradients.1 = (bf16[1024,896]{1,0:T(8,128)(2,1)}, bf16[1024,1024]{1,0:T(8,128)(2,1)}) custom-call(bf16[1024,1024]{1,0:T(8,128)(2,1)} %get-tuple-element.66.cot_ref, bf16[1024,512]{1,0:T(8,128)(2,1)S(1)} %get-tuple-element.67.normed_ref, bf16[1024,1024]{1,0:T(8,128)(2,1)} %get-tuple-element.68.tokens_ref, bf16[1024,1408]{1,0:T(8,128)(2,1)} %get-tuple-element.69.grads_ref), custom_call_target="tpu_custom_call" | custom-call | flops 7000000000 | bytes 1048576 | tf_op jit(solution)/shard_map/weight_gradients/pallas_call | solution.py:600
  164.3 1.8 constant_dynamic-slice_fusion.1
  167.0 1.8 collective-permute-done.18
  168.8 1.3 collective-permute-start.19
  170.1 2.6 collective-permute-done.19
  172.7 1.4 collective-permute-start.20
  174.3 2.3 collective-permute-done.20
  176.9 1.4 collective-permute-start.22
  180.2 2.0 fusion
  182.2 5.8 %collective-permute-done.22 = bf16[2,128,896]{2,1,0:T(8,128)(2,1)S(1)} collective-permute-done((bf16[2,128,896]{2,1,0:T(8,128)(2,1)S(1)}, bf16[2,128,896]{2,1,0:T(8,128)(2,1)S(1)}, u32[]{:S(2)}, u32[]{:S(2)}) %collective-permute-start.22) | collective-permute-done | bytes 458784 | tf_op jit(solution)/shard_map/ppermute | solution.py:706
  188.2 1.5 collective-permute-start.23
  189.7 0.8 dynamic-slice_bitcast_fusion.1
  191.7 5.2 %collective-permute-done.23 = bf16[128,896]{1,0:T(8,128)(2,1)S(1)} collective-permute-done((bf16[128,896]{1,0:T(8,128)(2,1)S(1)}, bf16[128,896]{1,0:T(8,128)(2,1)S(1)}, u32[]{:S(2)}, u32[]{:S(2)}) %collective-permute-start.23) | collective-permute-done | bytes 229408 | tf_op jit(solution)/shard_map/ppermute | solution.py:706
  197.5 3.9 %collective-permute-start.26 = (f32[280,128]{1,0:T(8,128)S(1)}, f32[280,128]{1,0:T(8,128)}, u32[]{:S(2)}, u32[]{:S(2)}) collective-permute-start(f32[280,128]{1,0:T(8,128)S(1)} %pad_maximum_fusion), channel_id=1, source_target_pairs={{0,1},{1,2},{2,3},{3,0},{4,5},{5,6},{6,7},{7,4},{8,9},{9,10},{10,1... | collective-permute-start | bytes 430088 | tf_op jit(solution)/shard_map/ppermute | solution.py:717
  201.4 3.4 %collective-permute-done.28 = bf16[2,128,1024]{2,1,0:T(8,128)(2,1)S(1)} collective-permute-done((bf16[2,128,1024]{2,1,0:T(8,128)(2,1)}, bf16[2,128,1024]{2,1,0:T(8,128)(2,1)S(1)}, u32[]{:S(2)}, u32[]{:S(2)}) %collective-permute-start.28) | collective-permute-done | bytes 524320 | tf_op jit(solution)/shard_map/ppermute | solution.py:706
  205.1 1.4 collective-permute-start.29
  206.5 0.7 slice.123
  207.9 1.2 collective-permute-done.25
  209.3 1.1 add_add_fusion
  210.5 0.7 reshape.103
  213.0 0.8 fusion.18
  213.8 1.4 fusion.4
  215.2 32.2 %reduce-scatter.3.cloned.1.call-done = bf16[256,1024]{1,0:T(8,128)(2,1)} async-done(((bf16[1024,1024]{1,0:T(8,128)(2,1)}), bf16[256,1024]{1,0:T(8,128)(2,1)}) %reduce-scatter.3.cloned.1.call-update) | async-done | bytes 524304 | tf_op jit(solution)/shard_map/reduce_scatter | solution.py:799
  247.4 2.7 %fusion.14 = (bf16[1,256,1024]{2,1,0:T(8,128)(2,1)}, bf16[1,256,1024]{2,1,0:T(8,128)(2,1)}) fusion(bf16[256,1024]{1,0:T(8,128)(2,1)} %reduce-scatter.5.cloned.1.call-done, f32[256]{0:T(256)S(1)} %broadcast_multiply_fusion, f32[1024]{0:T(1024)S(1)} %bitcast.82, f32[256]{0:T(256)S(1)} %add_rsqrt_fusion, bf16[1,256,1024]{2,1,0:T(8,128)(2,1)S(1)} %copy-done.6, ...), kind=kLoop, calls=%fused_computation.25 | loop fusion | flops 3670016 | bytes 3152896 | tf_op jit(solution)/shard_map/broadcast_in_dim | solution.py:845
  (113 shorter events, 9.9 us)
Async XLA Ops:
  7.2 80.0 %all-gather.2.cloned.1.call-start = ((), (), s32[]{:S(2)}) async-start(), calls=%async_computation.2 | async-start | bytes 4423680 | tf_op jit(solution)/shard_map/all_gather | solution.py:770
  11.7 0.8 copy-start.5
  12.5 201.3 %reduce-scatter.5.cloned.1.call-start = ((), (), s32[]{:S(2)}) async-start(), calls=%async_computation.4 | async-start | bytes 2621440 | tf_op jit(solution)/shard_map/reduce_scatter | solution.py:808
  12.6 17.1 %collective-permute-start.6 = (bf16[256,1024]{1,0:T(8,128)(2,1)}, bf16[256,1024]{1,0:T(8,128)(2,1)S(1)}, u32[]{:S(2)}, u32[]{:S(2)}) collective-permute-start(bf16[256,1024]{1,0:T(8,128)(2,1)} %bitcast.71), channel_id=1, source_target_pairs={{1,0},{2,1},{3,2},{5,4},{6,5},{7,6},{9,8},{10,9},{11,10},{13,12},{... | collective-permute-start | bytes 1572872 | tf_op jit(solution)/shard_map/ppermute | solution.py:685
  13.9 17.1 %collective-permute-start.3 = (bf16[256,1024]{1,0:T(8,128)(2,1)}, bf16[256,1024]{1,0:T(8,128)(2,1)S(1)}, u32[]{:S(2)}, u32[]{:S(2)}) collective-permute-start(bf16[256,1024]{1,0:T(8,128)(2,1)} %bitcast.72), channel_id=1, source_target_pairs={{0,1},{1,2},{2,3},{4,5},{5,6},{6,7},{8,9},{9,10},{10,11},{12,13},{... | collective-permute-start | bytes 1572872 | tf_op jit(solution)/shard_map/ppermute | solution.py:684
  29.6 23.0 %copy-start.7 = (bf16[256,1024]{1,0:T(8,128)(2,1)}, bf16[256,1024]{1,0:T(8,128)(2,1)S(1)}, u32[]{:S(2)}) copy-start(bf16[256,1024]{1,0:T(8,128)(2,1)S(1)} %collective-permute-done.6.refs_4_) | copy-start | bytes 1572868
  29.6 15.1 %collective-permute-start.7 = (bf16[256,1024]{1,0:T(8,128)(2,1)S(1)}, bf16[256,1024]{1,0:T(8,128)(2,1)S(1)}, u32[]{:S(2)}, u32[]{:S(2)}) collective-permute-start(bf16[256,1024]{1,0:T(8,128)(2,1)S(1)} %collective-permute-done.6.refs_4_), channel_id=1, source_target_pairs={{1,0},{2,1},{5,4},{6,5},{9,8},{10,9},{13,12},{14,13},{17,16},{18,1... | collective-permute-start | bytes 1572872 | tf_op jit(solution)/shard_map/ppermute | solution.py:685
  30.9 15.1 %collective-permute-start.4 = (bf16[256,1024]{1,0:T(8,128)(2,1)S(1)}, bf16[256,1024]{1,0:T(8,128)(2,1)S(1)}, u32[]{:S(2)}, u32[]{:S(2)}) collective-permute-start(bf16[256,1024]{1,0:T(8,128)(2,1)S(1)} %collective-permute-done.3.refs_2_), channel_id=1, source_target_pairs={{1,2},{2,3},{5,6},{6,7},{9,10},{10,11},{13,14},{14,15},{17,18},{18... | collective-permute-start | bytes 1572872 | tf_op jit(solution)/shard_map/ppermute | solution.py:684
  44.7 14.3 %copy-start.8 = (bf16[256,1024]{1,0:T(8,128)(2,1)}, bf16[256,1024]{1,0:T(8,128)(2,1)S(1)}, u32[]{:S(2)}) copy-start(bf16[256,1024]{1,0:T(8,128)(2,1)S(1)} %collective-permute-done.7.refs_5_) | copy-start | bytes 1572868
  44.7 14.3 %collective-permute-start.8 = (bf16[256,1024]{1,0:T(8,128)(2,1)S(1)}, bf16[256,1024]{1,0:T(8,128)(2,1)S(1)}, u32[]{:S(2)}, u32[]{:S(2)}) collective-permute-start(bf16[256,1024]{1,0:T(8,128)(2,1)S(1)} %collective-permute-done.7.refs_5_), channel_id=1, source_target_pairs={{1,0},{5,4},{9,8},{13,12},{17,16},{21,20},{25,24},{29,28}} | collective-permute-start | bytes 1572872 | tf_op jit(solution)/shard_map/ppermute | solution.py:685
  46.0 13.0 %collective-permute-start.5 = (bf16[256,1024]{1,0:T(8,128)(2,1)S(1)}, bf16[256,1024]{1,0:T(8,128)(2,1)S(1)}, u32[]{:S(2)}, u32[]{:S(2)}) collective-permute-start(bf16[256,1024]{1,0:T(8,128)(2,1)S(1)} %collective-permute-done.4.refs_1_), channel_id=1, source_target_pairs={{2,3},{6,7},{10,11},{14,15},{18,19},{22,23},{26,27},{30,31}} | collective-permute-start | bytes 1572872 | tf_op jit(solution)/shard_map/ppermute | solution.py:684
  46.7 27.9 %collective-permute-start.2 = (s32[256]{0:T(256)}, s32[256]{0:T(256)S(1)}, u32[]{:S(2)}, u32[]{:S(2)}) collective-permute-start(s32[256]{0:T(256)} %bitcast.86), channel_id=1, source_target_pairs={{0,1},{1,2},{2,3},{3,0},{4,5},{5,6},{6,7},{7,4},{8,9},{9,10},{10,1... | collective-permute-start | bytes 3080 | tf_op jit(solution)/shard_map/ppermute | solution.py:717
  49.4 17.6 %collective-permute-start.1 = (s32[256]{0:T(256)}, s32[256]{0:T(256)S(1)}, u32[]{:S(2)}, u32[]{:S(2)}) collective-permute-start(s32[256]{0:T(256)} %bitcast.87), channel_id=1, source_target_pairs={{0,2},{1,3},{2,0},{3,1},{4,6},{5,7},{6,4},{7,5},{8,10},{9,11},{10,... | collective-permute-start | bytes 3080 | tf_op jit(solution)/shard_map/ppermute | solution.py:717
  52.6 14.5 %collective-permute-start = (s32[256]{0:T(256)}, s32[256]{0:T(256)S(1)}, u32[]{:S(2)}, u32[]{:S(2)}) collective-permute-start(s32[256]{0:T(256)} %bitcast.88), channel_id=1, source_target_pairs={{0,3},{1,0},{2,1},{3,2},{4,7},{5,4},{6,5},{7,6},{8,11},{9,8},{10,9... | collective-permute-start | bytes 3080 | tf_op jit(solution)/shard_map/ppermute | solution.py:717
  59.1 14.9 %copy-start.9 = (bf16[256,1024]{1,0:T(8,128)(2,1)}, bf16[256,1024]{1,0:T(8,128)(2,1)S(1)}, u32[]{:S(2)}) copy-start(bf16[256,1024]{1,0:T(8,128)(2,1)S(1)} %collective-permute-done.8.refs_6_) | copy-start | bytes 1572868
  59.1 13.6 %collective-permute-start.10 = (bf16[256,1024]{1,0:T(8,128)(2,1)}, bf16[256,1024]{1,0:T(8,128)(2,1)S(1)}, u32[]{:S(2)}, u32[]{:S(2)}) collective-permute-start(bf16[256,1024]{1,0:T(8,128)(2,1)} %bitcast.78), channel_id=1, source_target_pairs={{1,0},{2,1},{3,2},{5,4},{6,5},{7,6},{9,8},{10,9},{11,10},{13,12},{... | collective-permute-start | bytes 1572872 | tf_op jit(solution)/shard_map/ppermute | solution.py:685
  60.4 13.6 %collective-permute-start.9 = (bf16[256,1024]{1,0:T(8,128)(2,1)}, bf16[256,1024]{1,0:T(8,128)(2,1)S(1)}, u32[]{:S(2)}, u32[]{:S(2)}) collective-permute-start(bf16[256,1024]{1,0:T(8,128)(2,1)} %bitcast.79), channel_id=1, source_target_pairs={{0,1},{1,2},{2,3},{4,5},{5,6},{6,7},{8,9},{9,10},{10,11},{12,13},{... | collective-permute-start | bytes 1572872 | tf_op jit(solution)/shard_map/ppermute | solution.py:684
  72.6 13.8 %copy-start.10 = (bf16[256,1024]{1,0:T(8,128)(2,1)}, bf16[256,1024]{1,0:T(8,128)(2,1)S(1)}, u32[]{:S(2)}) copy-start(bf16[256,1024]{1,0:T(8,128)(2,1)S(1)} %collective-permute-done.10.refs_4_) | copy-start | bytes 1572868
  72.6 12.5 %collective-permute-start.13 = (bf16[256,1024]{1,0:T(8,128)(2,1)S(1)}, bf16[256,1024]{1,0:T(8,128)(2,1)}, u32[]{:S(2)}, u32[]{:S(2)}) collective-permute-start(bf16[256,1024]{1,0:T(8,128)(2,1)S(1)} %collective-permute-done.10.refs_4_), channel_id=1, source_target_pairs={{1,0},{2,1},{5,4},{6,5},{9,8},{10,9},{13,12},{14,13},{17,16},{18,1... | collective-permute-start | bytes 1572872 | tf_op jit(solution)/shard_map/ppermute | solution.py:685
  74.0 12.5 %collective-permute-start.11 = (bf16[256,1024]{1,0:T(8,128)(2,1)S(1)}, bf16[256,1024]{1,0:T(8,128)(2,1)S(1)}, u32[]{:S(2)}, u32[]{:S(2)}) collective-permute-start(bf16[256,1024]{1,0:T(8,128)(2,1)S(1)} %collective-permute-done.9.refs_2_), channel_id=1, source_target_pairs={{1,2},{2,3},{5,6},{6,7},{9,10},{10,11},{13,14},{14,15},{17,18},{18... | collective-permute-start | bytes 1572872 | tf_op jit(solution)/shard_map/ppermute | solution.py:684
  85.2 24.6 %collective-permute-start.14 = (bf16[256,1024]{1,0:T(8,128)(2,1)}, bf16[256,1024]{1,0:T(8,128)(2,1)}, u32[]{:S(2)}, u32[]{:S(2)}) collective-permute-start(bf16[256,1024]{1,0:T(8,128)(2,1)} %collective-permute-done.13.refs_5_), channel_id=1, source_target_pairs={{1,0},{5,4},{9,8},{13,12},{17,16},{21,20},{25,24},{29,28}} | collective-permute-start | bytes 1572872 | tf_op jit(solution)/shard_map/ppermute | solution.py:685
  86.5 23.3 %collective-permute-start.12 = (bf16[256,1024]{1,0:T(8,128)(2,1)S(1)}, bf16[256,1024]{1,0:T(8,128)(2,1)S(1)}, u32[]{:S(2)}, u32[]{:S(2)}) collective-permute-start(bf16[256,1024]{1,0:T(8,128)(2,1)S(1)} %collective-permute-done.11.refs_1_), channel_id=1, source_target_pairs={{2,3},{6,7},{10,11},{14,15},{18,19},{22,23},{26,27},{30,31}} | collective-permute-start | bytes 1572872 | tf_op jit(solution)/shard_map/ppermute | solution.py:684
  95.8 13.9 %copy-start = (s32[1040,128]{1,0:T(8,128)}, s32[1040,128]{1,0:T(8,128)S(1)}, u32[]{:S(2)}) copy-start(s32[1040,128]{1,0:T(8,128)S(1)} %broadcast_in_dim.36.window_ref.refs_9_) | copy-start | bytes 1597444
  109.8 6.5 %copy-start.2 = (f32[1024,256]{1,0:T(8,128)}, f32[1024,256]{1,0:T(8,128)S(1)}, u32[]{:S(2)}) copy-start(f32[1024,256]{1,0:T(8,128)S(1)} %get-tuple-element.57.pre_bc_ref) | copy-start | bytes 3145732
  109.8 17.4 %copy-start.1 = (s32[1040,128]{1,0:T(8,128)S(1)}, s32[1040,128]{1,0:T(8,128)}, u32[]{:S(2)}) copy-start(s32[1040,128]{1,0:T(8,128)} %copy-done) | copy-start | bytes 1597444
  116.3 9.2 %collective-permute-start.16 = (f32[2,1024]{1,0:T(2,128)S(1)}, f32[2,1024]{1,0:T(2,128)S(1)}, u32[]{:S(2)}, u32[]{:S(2)}) collective-permute-start(f32[2,1024]{1,0:T(2,128)S(1)} %pad_maximum_fusion.4), channel_id=1, source_target_pairs={{0,2},{1,3},{2,0},{3,1},{4,6},{5,7},{6,4},{7,5},{8,10},{9,11},{10,... | collective-permute-start | bytes 24584 | tf_op jit(solution)/shard_map/ppermute | solution.py:717
  121.7 5.4 %collective-permute-start.17 = (f32[2,1024]{1,0:T(2,128)S(1)}, f32[2,1024]{1,0:T(2,128)S(1)}, u32[]{:S(2)}, u32[]{:S(2)}) collective-permute-start(f32[2,1024]{1,0:T(2,128)S(1)} %pad_maximum_fusion.4), channel_id=1, source_target_pairs={{0,1},{1,2},{2,3},{3,0},{4,5},{5,6},{6,7},{7,4},{8,9},{9,10},{10,1... | collective-permute-start | bytes 24584 | tf_op jit(solution)/shard_map/ppermute | solution.py:717
  121.7 5.4 %collective-permute-start.15 = (f32[2,1024]{1,0:T(2,128)S(1)}, f32[2,1024]{1,0:T(2,128)S(1)}, u32[]{:S(2)}, u32[]{:S(2)}) collective-permute-start(f32[2,1024]{1,0:T(2,128)S(1)} %pad_maximum_fusion.4), channel_id=1, source_target_pairs={{0,3},{1,0},{2,1},{3,2},{4,7},{5,4},{6,5},{7,6},{8,11},{9,8},{10,9... | collective-permute-start | bytes 24584 | tf_op jit(solution)/shard_map/ppermute | solution.py:717
  154.6 1.0 copy-start.3
  154.6 92.8 %reduce-scatter.3.cloned.1.call-start = ((), (), s32[]{:S(2)}) async-start(), calls=%async_computation.3 | async-start | bytes 2621440 | tf_op jit(solution)/shard_map/reduce_scatter | solution.py:799
  164.3 2.4 copy-start.4
  166.1 10.5 %collective-permute-start.21 = (bf16[2,2,128,896]{3,2,0,1:T(8,128)(2,1)S(1)}, bf16[2,2,128,896]{3,2,0,1:T(8,128)(2,1)S(1)}, u32[]{:S(2)}, u32[]{:S(2)}) collective-permute-start(bf16[2,2,128,896]{3,2,0,1:T(8,128)(2,1)S(1)} %bitcast.77), channel_id=1, source_target_pairs={{0,4},{4,0},{8,12},{12,8},{16,20},{20,16},{24,28},{28,24},{1,5},{5... | collective-permute-start | bytes 2752520 | tf_op jit(solution)/shard_map/ppermute | solution.py:706
  166.2 2.5 collective-permute-start.18
  166.8 13.4 %collective-permute-start.27 = (bf16[2,2,128,1024]{3,2,1,0:T(8,128)(2,1)S(1)}, bf16[2,2,128,1024]{3,2,1,0:T(8,128)(2,1)}, u32[]{:S(2)}, u32[]{:S(2)}) collective-permute-start(bf16[2,2,128,1024]{3,2,1,0:T(8,128)(2,1)S(1)} %dynamic-slice_bitcast_fusion), channel_id=1, source_target_pairs={{0,4},{4,0},{8,12},{12,8},{16,20},{20,16},{24,28},{28,24},{1,5},{5... | collective-permute-start | bytes 3145736 | tf_op jit(solution)/shard_map/ppermute | solution.py:706
  168.8 3.9 %collective-permute-start.19 = (f32[64,128]{1,0:T(8,128)S(1)}, f32[64,128]{1,0:T(8,128)S(1)}, u32[]{:S(2)}, u32[]{:S(2)}) collective-permute-start(f32[64,128]{1,0:T(8,128)S(1)} %fusion.17), channel_id=1, source_target_pairs={{0,8},{4,12},{8,0},{12,4},{16,24},{20,28},{24,16},{28,20},{1,9},{5... | collective-permute-start | bytes 98312 | tf_op jit(solution)/shard_map/ppermute | solution.py:731
  172.7 3.9 %collective-permute-start.20 = (f32[64,128]{1,0:T(8,128)S(1)}, f32[64,128]{1,0:T(8,128)S(1)}, u32[]{:S(2)}, u32[]{:S(2)}) collective-permute-start(f32[64,128]{1,0:T(8,128)S(1)} %add.135), channel_id=1, source_target_pairs={{0,16},{4,20},{8,24},{12,28},{16,0},{20,4},{24,8},{28,12},{1,17},{... | collective-permute-start | bytes 98312 | tf_op jit(solution)/shard_map/ppermute | solution.py:731
  176.9 11.1 %collective-permute-start.22 = (bf16[2,128,896]{2,1,0:T(8,128)(2,1)S(1)}, bf16[2,128,896]{2,1,0:T(8,128)(2,1)S(1)}, u32[]{:S(2)}, u32[]{:S(2)}) collective-permute-start(bf16[2,128,896]{2,1,0:T(8,128)(2,1)S(1)} %dynamic-slice_bitcast_fusion.2), channel_id=1, source_target_pairs={{0,8},{4,12},{8,0},{12,4},{16,24},{20,28},{24,16},{28,20},{1,9},{5... | collective-permute-start | bytes 1376264 | tf_op jit(solution)/shard_map/ppermute | solution.py:706
  188.2 8.6 %collective-permute-start.23 = (bf16[128,896]{1,0:T(8,128)(2,1)S(1)}, bf16[128,896]{1,0:T(8,128)(2,1)S(1)}, u32[]{:S(2)}, u32[]{:S(2)}) collective-permute-start(bf16[128,896]{1,0:T(8,128)(2,1)S(1)} %dynamic-slice_bitcast_fusion.4), channel_id=1, source_target_pairs={{0,16},{4,20},{8,24},{12,28},{16,0},{20,4},{24,8},{28,12},{1,17},{... | collective-permute-start | bytes 688136 | tf_op jit(solution)/shard_map/ppermute | solution.py:706
  190.5 14.3 %collective-permute-start.28 = (bf16[2,128,1024]{2,1,0:T(8,128)(2,1)}, bf16[2,128,1024]{2,1,0:T(8,128)(2,1)S(1)}, u32[]{:S(2)}, u32[]{:S(2)}) collective-permute-start(bf16[2,128,1024]{2,1,0:T(8,128)(2,1)} %dynamic-slice_bitcast_fusion.1), channel_id=1, source_target_pairs={{0,16},{4,20},{8,24},{12,28},{16,0},{20,4},{24,8},{28,12},{1,17},{... | collective-permute-start | bytes 1572872 | tf_op jit(solution)/shard_map/ppermute | solution.py:706
  196.9 12.2 %collective-permute-start.25 = (f32[280,128]{1,0:T(8,128)S(1)}, f32[280,128]{1,0:T(8,128)}, u32[]{:S(2)}, u32[]{:S(2)}) collective-permute-start(f32[280,128]{1,0:T(8,128)S(1)} %pad_maximum_fusion), channel_id=1, source_target_pairs={{0,2},{1,3},{2,0},{3,1},{4,6},{5,7},{6,4},{7,5},{8,10},{9,11},{10,... | collective-permute-start | bytes 430088 | tf_op jit(solution)/shard_map/ppermute | solution.py:717
  197.5 11.6 %collective-permute-start.26 = (f32[280,128]{1,0:T(8,128)S(1)}, f32[280,128]{1,0:T(8,128)}, u32[]{:S(2)}, u32[]{:S(2)}) collective-permute-start(f32[280,128]{1,0:T(8,128)S(1)} %pad_maximum_fusion), channel_id=1, source_target_pairs={{0,1},{1,2},{2,3},{3,0},{4,5},{5,6},{6,7},{7,4},{8,9},{9,10},{10,1... | collective-permute-start | bytes 430088 | tf_op jit(solution)/shard_map/ppermute | solution.py:717
  201.4 7.9 %collective-permute-start.24 = (f32[280,128]{1,0:T(8,128)S(1)}, f32[280,128]{1,0:T(8,128)}, u32[]{:S(2)}, u32[]{:S(2)}) collective-permute-start(f32[280,128]{1,0:T(8,128)S(1)} %pad_maximum_fusion), channel_id=1, source_target_pairs={{0,3},{1,0},{2,1},{3,2},{4,7},{5,4},{6,5},{7,6},{8,11},{9,8},{10,9... | collective-permute-start | bytes 430088 | tf_op jit(solution)/shard_map/ppermute | solution.py:717
  205.1 7.8 %collective-permute-start.29 = (bf16[128,1024]{1,0:T(8,128)(2,1)S(1)}, bf16[128,1024]{1,0:T(8,128)(2,1)S(1)}, u32[]{:S(2)}, u32[]{:S(2)}) collective-permute-start(bf16[128,1024]{1,0:T(8,128)(2,1)S(1)} %dynamic-slice_bitcast_fusion.3), channel_id=1, source_target_pairs={{0,8},{4,12},{8,0},{12,4},{16,24},{20,28},{24,16},{28,20},{1,9},{5... | collective-permute-start | bytes 786440 | tf_op jit(solution)/shard_map/ppermute | solution.py:706
  207.9 39.5 %copy-start.6 = (bf16[1,256,1024]{2,1,0:T(8,128)(2,1)S(1)}, bf16[1,256,1024]{2,1,0:T(8,128)(2,1)}, u32[]{:S(2)}) copy-start(bf16[1,256,1024]{2,1,0:T(8,128)(2,1)} %param.19) | copy-start | bytes 1572868
Sparse Core Ops, SparseCore 0:
  12.6 38.3 all-gather.1
  154.7 46.1 reduce-scatter.4
  203.3 44.0 reduce-scatter.2

commit v5 on v4

--- a/solution.py
+++ b/solution.py
@@ -275,7 +275,8 @@
     state_ref,
     grad_ref,
     proj_ref,
-    part_ref,
+    left_ref,
+    right_ref,
     out_ref,
     sum_x_ref,
     sum_bc_ref,
@@ -442,7 +443,8 @@
     )
     proj_ref[...] = grads
     part = dot_nt(grads, weights_ref[:, width:])
-    part_ref[...] = part.astype(BF16)
+    left_ref[...] = part[:, : part.shape[1] // 2].astype(BF16)
+    right_ref[...] = part[:, part.shape[1] // 2 :].astype(BF16)
     hidden = hidden_ref[...].astype(F32)
     inverse = lax.rsqrt(jnp.mean(hidden * hidden, axis=1, keepdims=True) + EPS)
     sum_gain_ref[0:1, :] += jnp.sum(part * (hidden * inverse), axis=0, keepdims=True)
@@ -654,8 +656,9 @@
             pl.BlockSpec((1, N, width), lambda i: (blocks - 1 - i, 0, 0)),
             rows(width),
         ],
-        out_specs=[rows(total), rows(features), rows(width)] + [whole(shape) for shape in sums],
-        out_shape=[made(total, BF16), made(features, BF16), made(width, BF16)]
+        out_specs=[rows(total), rows(features // 2), rows(features // 2), rows(width)]
+        + [whole(shape) for shape in sums],
+        out_shape=[made(total, BF16), made(features // 2, BF16), made(features // 2, BF16), made(width, BF16)]
         + [jax.ShapeDtypeStruct(shape, F32) for shape in sums],
         scratch_shapes=[
             pltpu.VMEM((Q + HALO, width), F32),
@@ -672,26 +675,66 @@
     )
 
 
+def finish_kernel(left_ref, right_ref, hidden_ref, cot_ref, gain_ref, out_ref):
+    grad = jnp.concatenate([left_ref[...], right_ref[...]], axis=1).astype(F32)
+    grad = grad * gain_ref[0:1, :]
+    hidden = hidden_ref[...].astype(F32)
+    inverse = lax.rsqrt(jnp.mean(hidden * hidden, axis=1, keepdims=True) + EPS)
+    unit = hidden * inverse
+    along = jnp.mean(grad * unit, axis=1, keepdims=True)
+    out_ref[...] = (cot_ref[...].astype(F32) + inverse * (grad - unit * along)).astype(BF16)
+
+
+def run_finish(in_sums, hidden, cot, gain):
+    length, features = hidden.shape
+    rows = pl.BlockSpec((length // 2, features), lambda i: (i, 0))
+    halves = pl.BlockSpec((length // 2, features // 2), lambda i: (i, 0))
+    return pl.pallas_call(
+        finish_kernel,
+        grid=(2,),
+        in_specs=[halves, halves, rows, rows, whole(gain.shape)],
+        out_specs=rows,
+        out_shape=jax.ShapeDtypeStruct(hidden.shape, BF16),
+        compiler_params=pltpu.CompilerParams(vmem_limit_bytes=VMEM_LIMIT),
+        name="finish",
+    )(*in_sums, hidden, cot, gain)
+
+
 def pad_lanes(values):
     return jnp.pad(values, ((0, 0), (0, LANES - values.shape[1])))
 
 
+def after(value, *others):
+    return lax.optimization_barrier((value, *others))[0]
+
+
+def line_step(right, left, step, axis):
+    n = lax.axis_size(axis)
+    return (
+        lax.ppermute(right, axis, [(i, i + 1) for i in range(step - 1, n - 1)]),
+        lax.ppermute(left, axis, [(i, i - 1) for i in range(1, n - step + 1)]),
+    )
+
+
+def line_order(block, moved):
+    return [pair[0] for pair in moved[::-1]] + [block] + [pair[1] for pair in moved]
+
+
 def line_gather(block, axis):
-    n = lax.axis_size(axis)
-    from_left, from_right = [], []
     right = left = block
-    for step in range(1, n):
-        right = lax.ppermute(right, axis, [(i, i + 1) for i in range(step - 1, n - 1)])
-        left = lax.ppermute(left, axis, [(i, i - 1) for i in range(1, n - step + 1)])
-        from_left.append(right)
-        from_right.append(left)
-    return from_left[::-1] + [block] + from_right
+    moved = []
+    for step in range(1, lax.axis_size(axis)):
+        right, left = line_step(right, left, step, axis)
+        moved.append((right, left))
+    return line_order(block, moved)
 
 
 def cube_scatter(part, axis, upward):
     n = lax.axis_size(axis)
     if n & (n - 1):
-        return lax.psum_scatter(part, axis, scatter_dimension=0, tiled=True).astype(F32)
+        part = lax.psum_scatter(part, axis, scatter_dimension=0, tiled=True).astype(F32)
+        return part, part
+    first = None
     place = lax.axis_index(axis)
     rows, columns = part.shape
     bits = list(range(n.bit_length() - 1))
@@ -704,11 +747,12 @@
         keep = lax.dynamic_index_in_dim(part, mine, dim, keepdims=False)
         send = lax.dynamic_index_in_dim(part, 1 - mine, dim, keepdims=False)
         other = lax.ppermute(send, axis, [(i, i ^ (1 << bit)) for i in range(n)])
+        first = other if first is None else first
         part = keep.astype(F32) + other.astype(F32)
         left.remove(bit)
         if left:
             part = part.astype(BF16)
-    return part
+    return part, first
 
 
 def around(values, axis):
@@ -773,9 +817,6 @@
     seg_full = lax.dynamic_slice_in_dim(
         jnp.concatenate(seg_stack + seg_stack), (n - axis_place) * count, n * count, 0
     )
-    cot_local, _, _ = lax.optimization_barrier((cotangent[0], near_hidden[0], near_hidden[-1]))
-    near_cot = line_gather(cot_local, "tensor")
-
     window = jnp.broadcast_to(
         jnp.pad(seg_full, (HALO, HALO), constant_values=-1)[:, None],
         (seg_full.shape[0] + 2 * HALO, LANES),
@@ -789,30 +830,43 @@
     hidden_full, tokens, z_proj, x_proj, bcdt, gain = run_project(
         heads, size, place, near_hidden, weights
     )
-    bcdt, _, _ = lax.optimization_barrier((bcdt, near_cot[n - 2], near_cot[n]))
+    right = left = after(cotangent[0], near_hidden[0], near_hidden[-1])
+    moved = []
+    right, left = line_step(right, left, 1, "tensor")
+    moved.append((right, left))
+    bcdt = after(bcdt, right, left)
+    right, left = line_step(after(right, gain), after(left, gain), 2, "tensor")
+    moved.append((right, left))
     mixed, pre, pre_bc, states, scaled, out_part, square = run_forward(
         heads, size, window, seg_row, weights, kernel_x, kernel_bc, head, channel, z_proj, x_proj,
         bcdt,
     )
+    for step in range(3, n):
+        right, left = line_step(after(right, square), after(left, square), step, "tensor")
+        moved.append((right, left))
+    near_cot = line_order(cotangent[0], moved)
     cot_full, grad_out, along = run_gradient(place, near_cot, weights, scaled, window)
-    out_part, _ = lax.optimization_barrier((out_part, along))
-    out_sum = lax.psum_scatter(out_part, "tensor", scatter_dimension=0, tiled=True)
+    out_sum = lax.psum_scatter(
+        after(out_part, along), "tensor", scatter_dimension=0, tiled=True
+    )
     stat = sum_around(jnp.stack([square[0], along[0]]), "tensor")
     stat_full = jnp.pad(stat, ((0, 6), (0, 0)))
     out_scale = lax.rsqrt(stat[0] / full_inner + EPS) * (seg_full > 0).astype(F32)
 
-    grads, in_part, normed_out, sum_x, sum_bc, sum_head, sum_gain = run_backward(
+    grads, *in_parts, normed_out, sum_x, sum_bc, sum_head, sum_gain = run_backward(
         heads, size, full_inner, stat_full, hidden_full, window, seg_row, weights, kernel_x,
         kernel_bc, head, channel, z_proj, mixed, x_proj, pre, bcdt, pre_bc, states, grad_out,
     )
-    in_sum = lax.psum_scatter(in_part, "tensor", scatter_dimension=0, tiled=True)
-
-    first, second = run_weights(cot_full, normed_out, tokens, grads)
-    first = cube_scatter(first, "dp", True)
-    second = cube_scatter(second, "dp", False)
+    in_sums = [
+        lax.psum_scatter(half, "tensor", scatter_dimension=0, tiled=True)
+        for half in in_parts
+    ]
+    first, second = run_weights(cot_full, normed_out, tokens, after(grads, out_sum))
+    first, _ = cube_scatter(first, "dp", True)
+    second, arrived = cube_scatter(second, "dp", False)
     own = jnp.concatenate([sum_x.reshape(-1, LANES), sum_head])
     both = jnp.concatenate([sum_gain[0].reshape(-1, LANES), sum_bc.reshape(-1, LANES)])
-    small = sum_pairwise(jnp.concatenate([own, both]), "dp")
+    small = sum_pairwise(after(jnp.concatenate([own, both]), arrived), "dp")
     sum_x = small[: own.shape[0] - 8].reshape(8, width)
     sum_head = small[own.shape[0] - 8 : own.shape[0]]
     grad_bc = first[:, width : width + 2 * N]
@@ -832,13 +886,7 @@
     scale_here = lax.dynamic_slice_in_dim(out_scale, axis_place * local, local, 0)[:, None]
     layer_out = (hidden_rows + out_sum.astype(F32) * scale_here).astype(BF16)
 
-    inverse = lax.rsqrt(jnp.mean(hidden_rows * hidden_rows, axis=1, keepdims=True) + EPS)
-    unit = hidden_rows * inverse
-    grad_scaled = in_sum.astype(F32) * gain[0:1]
-    grad_hidden = (
-        cotangent[0].astype(F32)
-        + inverse * (grad_scaled - unit * jnp.mean(grad_scaled * unit, axis=1, keepdims=True))
-    ).astype(BF16)
+    grad_hidden = run_finish(in_sums, hidden_local, cotangent[0], after(gain, shared))
 
     return (
         layer_out[None],

time: 258 us -> 237 us (0.919)
  waiting for transfers between devices: 96.3 us -> 79.5 us
  starting transfers between devices: 51.6 us -> 44.3 us
  local copies, waits for them, and re-layouts: 17.5 us -> 21.6 us
    reduce_scatter x2 -> x3, waiting for transfers between devices: 32.2 us -> 9.6 us  [the longest x1 9.6 us: shards(): lax.psum_scatter(after(out_part, along), 'tensor', scatter_dimension=0, t...]
    ppermute x9, starting transfers between devices: 22.4 us -> 15.6 us  [around(): lax.ppermute(values, axis, [(i, (i - k) % n) for i in range(n)])]
    ppermute x9, waiting for transfers between devices: 3.02 us -> 7.49 us  [around(): lax.ppermute(values, axis, [(i, (i - k) % n) for i in range(n)])]
    unnamed x34 -> x46, local copies, waits for them, and re-layouts: 7.43 us -> 11.4 us
    ppermute x3, waiting for transfers between devices: 6.72 us -> 10.7 us  [sum_pairwise(): lax.ppermute(values, axis, [(i, i ^ bit) for i in range(n)])]
  transfers between devices with their start and end apart: 33 -> 34, of which waited for: 15 -> 15; matrix products, arithmetic and copies ran while one was open for 8% -> 9% of each run, Pallas kernels for 12% -> 25%
where the time goes in v5:
time: 237 us; the launch traced here: 236 us
  waiting for transfers between devices  79.5 us (34%)
  Pallas kernels  64.9 us (27%)
  starting transfers between devices  44.3 us (19%)
  local copies, waits for them, and re-layouts  21.6 us (9%)
  between operations  14.3 us (6%)
  other arithmetic  11 us (5%)
    ppermute x6, waiting for transfers between devices, line_step(): lax.ppermute(left, axis, [(i, i - 1) for i in range(1, n - step + 1)])  38 us
    pallas_call x1, Pallas kernels, run_backward(): pl.pallas_call(functools.partial(backward_kernel, heads, size, full_inner...  27.2 us
    ppermute x9, starting transfers between devices, around(): lax.ppermute(values, axis, [(i, (i - k) % n) for i in range(n)])  15.6 us
    pallas_call x1, Pallas kernels, run_forward(): pl.pallas_call(functools.partial(forward_kernel, heads, size), grid=(bloc...  13.8 us
    ppermute x6, waiting for transfers between devices, cube_scatter(): other = lax.ppermute(send, axis, [(i, i ^ 1 << bit) for i in range(n)])  13.2 us
    ppermute x6, starting transfers between devices, line_step(): lax.ppermute(right, axis, [(i, i + 1) for i in range(step - 1, n - 1)])  12.9 us
    unnamed x46, local copies, waits for them, and re-layouts  11.4 us
    ppermute x3, waiting for transfers between devices, sum_pairwise(): lax.ppermute(values, axis, [(i, i ^ bit) for i in range(n)])  10.7 us
  transfers between devices with their start and end apart: 34, of which 15 were waited for; matrix products, arithmetic and copies ran while one was open for 9% of the time, Pallas kernels for 25%

profile of v5, /device:TPU:0, one launch (start us, length us, event | category | flops | bytes accessed | tf_op | source)
XLA Modules:
  0.0 235.6 jit_solution(3722953653466467348)
XLA Ops:
  7.2 0.7 pad_maximum_fusion.5
  8.1 0.9 constant_dynamic-update-slice_fusion.4
  9.0 0.9 constant_dynamic-update-slice_fusion.3
  9.9 0.9 constant_dynamic-update-slice_fusion.2
  10.8 0.8 constant_dynamic-update-slice_fusion.1
  11.7 0.8 copy-done.10
  12.6 1.3 collective-permute-start.6
  13.9 5.6 %collective-permute-start.3 = (bf16[256,1024]{1,0:T(8,128)(2,1)}, bf16[256,1024]{1,0:T(8,128)(2,1)S(1)}, u32[]{:S(2)}, u32[]{:S(2)}) collective-permute-start(bf16[256,1024]{1,0:T(8,128)(2,1)} %bitcast.66), channel_id=1, source_target_pairs={{0,1},{1,2},{2,3},{4,5},{5,6},{6,7},{8,9},{9,10},{10,11},{12,13},{... | collective-permute-start | bytes 1572872 | tf_op jit(solution)/shard_map/ppermute | solution.py:714
  19.5 2.0 collective-permute-start.2
  21.5 1.1 collective-permute-start.1
  22.6 2.8 %collective-permute-start = (s32[256]{0:T(256)}, s32[256]{0:T(256)S(1)}, u32[]{:S(2)}, u32[]{:S(2)}) collective-permute-start(s32[256]{0:T(256)} %bitcast.81), channel_id=1, source_target_pairs={{0,3},{1,0},{2,1},{3,2},{4,7},{5,4},{6,5},{7,6},{8,11},{9,8},{10,9... | collective-permute-start | bytes 3080 | tf_op jit(solution)/shard_map/ppermute | solution.py:761
  25.5 0.7 broadcast_in_dim.39
  26.3 0.7 pad_maximum_fusion.6.channel_ref
  27.0 0.7 pad_maximum_fusion.3.kernel_bc_ref
  27.7 2.0 collective-permute-done.6.refs_4_
  29.6 1.3 collective-permute-start.7
  32.3 0.7 pad_maximum_fusion.2.kernel_x_ref
  33.8 11.0 %collective-permute-done.7.refs_5_ = bf16[256,1024]{1,0:T(8,128)(2,1)S(1)} collective-permute-done((bf16[256,1024]{1,0:T(8,128)(2,1)S(1)}, bf16[256,1024]{1,0:T(8,128)(2,1)S(1)}, u32[]{:S(2)}, u32[]{:S(2)}) %collective-permute-start.7) | collective-permute-done | bytes 524320 | tf_op jit(solution)/shard_map/ppermute | solution.py:715
  44.7 1.3 collective-permute-start.8
  46.0 0.7 collective-permute-start.5
  47.6 11.4 %collective-permute-done.8.refs_6_ = bf16[256,1024]{1,0:T(8,128)(2,1)S(1)} collective-permute-done((bf16[256,1024]{1,0:T(8,128)(2,1)S(1)}, bf16[256,1024]{1,0:T(8,128)(2,1)S(1)}, u32[]{:S(2)}, u32[]{:S(2)}) %collective-permute-start.8) | collective-permute-done | bytes 524320 | tf_op jit(solution)/shard_map/ppermute | solution.py:715
  59.0 1.3 collective-permute-start.10
  60.3 4.6 %collective-permute-start.9 = (bf16[256,1024]{1,0:T(8,128)(2,1)}, bf16[256,1024]{1,0:T(8,128)(2,1)S(1)}, u32[]{:S(2)}, u32[]{:S(2)}) collective-permute-start(bf16[256,1024]{1,0:T(8,128)(2,1)} %bitcast.70), channel_id=1, source_target_pairs={{0,1},{1,2},{2,3},{4,5},{5,6},{6,7},{8,9},{9,10},{10,11},{12,13},{... | collective-permute-start | bytes 1572872 | tf_op jit(solution)/shard_map/ppermute | solution.py:714
  65.0 8.4 %project.1 = (bf16[1024,1024]{1,0:T(8,128)(2,1)}, bf16[1024,1024]{1,0:T(8,128)(2,1)}, f32[1024,512]{1,0:T(8,128)}, f32[1024,512]{1,0:T(8,128)}, f32[1024,384]{1,0:T(8,128)}, /*index=5*/f32[8,1024]{1,0:T(8,128)S(1)}) custom-call(s32[1]{0:T(128)} %bitcast.8.place_ref, bf16[256,1024]{1,0:T(8,128)(2,1)S(1)} %collective-permute-done.5.refs_0_, ...), custom_call_target="tpu_custom_call" | custom-call | flops 8000000000 | bytes 1048576 | tf_op jit(solution)/shard_map/project/pallas_call | solution.py:478
  74.6 1.3 collective-permute-start.13
  76.1 13.8 %forward.1 = (f32[1024,512]{1,0:T(8,128)}, f32[1024,512]{1,0:T(8,128)}, f32[1024,256]{1,0:T(8,128)S(1)}, f32[4,128,512]{2,1,0:T(8,128)}, bf16[1024,512]{1,0:T(8,...) custom-call(s32[1040,128]{1,0:T(8,128)S(1)} %broadcast_in_dim.34.window_ref.refs_9_, ...), custom_call_target="tpu_custom_call" | custom-call | flops 14000000000 | bytes 1048576 | tf_op jit(solution)/shard_map/forward/pallas_call | solution.py:518
  89.9 1.0 copy-done.7
  90.8 0.7 collective-permute-start.12
  91.5 1.3 collective-permute-start.14
  92.8 13.7 %collective-permute-done.14.refs_6_ = bf16[256,1024]{1,0:T(8,128)(2,1)S(1)} collective-permute-done((bf16[256,1024]{1,0:T(8,128)(2,1)S(1)}, bf16[256,1024]{1,0:T(8,128)(2,1)S(1)}, u32[]{:S(2)}, u32[]{:S(2)}) %collective-permute-start.14) | collective-permute-done | bytes 524320 | tf_op jit(solution)/shard_map/ppermute | solution.py:715
  106.5 0.8 copy-done.16
  107.3 6.0 %out_gradient.1 = (bf16[1024,1024]{1,0:T(8,128)(2,1)}, f32[1024,512]{1,0:T(8,128)}, f32[8,1024]{1,0:T(8,128)S(1)}) custom-call(s32[1]{0:T(128)} %bitcast.8.place_ref, bf16[256,1024]{1,0:T(8,128)(2,1)S(1)} %collective-permute-done.12.refs_0_, bf16[256,1024]{1,0:T(8,128)(2,1)S(1)} %collective-permute-done.11.refs_1_, ...), custom_call_target="tpu_custom_call" | custom-call | flops 5000000000 | bytes 1048576 | tf_op jit(solution)/shard_map/out_gradient/pallas_call | solution.py:565
  113.5 2.5 %collective-permute-start.17 = (f32[2,1024]{1,0:T(2,128)S(1)}, f32[2,1024]{1,0:T(2,128)S(1)}, u32[]{:S(2)}, u32[]{:S(2)}) collective-permute-start(f32[2,1024]{1,0:T(2,128)S(1)} %pad_maximum_fusion.4), channel_id=1, source_target_pairs={{0,1},{1,2},{2,3},{3,0},{4,5},{5,6},{6,7},{7,4},{8,9},{9,10},{10,1... | collective-permute-start | bytes 24584 | tf_op jit(solution)/shard_map/ppermute | solution.py:761
  116.0 1.3 collective-permute-start.15
  118.0 1.0 collective-permute-done.17
  119.0 0.7 collective-permute-done.15
  119.7 27.2 %backward.1 = (bf16[1024,1408]{1,0:T(8,128)(2,1)}, bf16[1024,512]{1,0:T(8,128)(2,1)}, bf16[1024,512]{1,0:T(8,128)(2,1)}, bf16[1024,512]{1,0:T(8,128)(2,1)}, f32[...) custom-call(f32[8,1024]{1,0:T(8,128)S(1)} %pad.19.stat_ref, ...), custom_call_target="tpu_custom_call" | custom-call | flops 27000000512 | bytes 1048576 | tf_op jit(solution)/shard_map/backward/pallas_call | solution.py:637
  147.1 9.6 %reduce-scatter.4.cloned.1.call-done = bf16[256,1024]{1,0:T(8,128)(2,1)} async-done(((bf16[1024,1024]{1,0:T(8,128)(2,1)}), bf16[256,1024]{1,0:T(8,128)(2,1)}) %reduce-scatter.4.cloned.1.call-update) | async-done | bytes 524304 | tf_op jit(solution)/shard_map/reduce_scatter | solution.py:849
  156.7 1.2 copy-done.6
  157.9 8.3 %weight_gradients.1 = (bf16[1024,896]{1,0:T(8,128)(2,1)}, bf16[1024,1024]{1,0:T(8,128)(2,1)}) custom-call(bf16[1024,1024]{1,0:T(8,128)(2,1)} %get-tuple-element.79.cot_ref, bf16[1024,512]{1,0:T(8,128)(2,1)S(1)} %copy-done.6, bf16[1024,1024]{1,0:T(8,128)(2,1)} %get-tuple-element.81.tokens_ref, bf16[1024,1408]{1,0:T(8,128)(2,1)} %get-tuple-element.83.grads_ref), custom_call_target="tpu_custom_call" | custom-call | flops 7000000000 | bytes 1048576 | tf_op jit(solution)/shard_map/weight_gradients/pallas_call | solution.py:602
  166.1 1.8 constant_dynamic-slice_fusion.1
  167.9 1.0 copy.50
  169.9 1.9 collective-permute-done.22
  171.8 1.5 fusion.1
  173.4 1.6 collective-permute-start.23
  174.9 1.0 fusion.4
  176.7 1.6 fusion
  178.3 8.4 %collective-permute-done.20 = f32[64,128]{1,0:T(8,128)S(1)} collective-permute-done((f32[64,128]{1,0:T(8,128)S(1)}, f32[64,128]{1,0:T(8,128)S(1)}, u32[]{:S(2)}, u32[]{:S(2)}) %collective-permute-start.20) | collective-permute-done | bytes 32800 | tf_op jit(solution)/shard_map/ppermute | solution.py:775
  186.7 1.5 collective-permute-start.21
  188.8 2.1 collective-permute-done.21
  191.1 1.6 collective-permute-start.24
  195.2 11.3 %collective-permute-done.24 = bf16[128,896]{1,0:T(8,128)(2,1)S(1)} collective-permute-done((bf16[128,896]{1,0:T(8,128)(2,1)S(1)}, bf16[128,896]{1,0:T(8,128)(2,1)S(1)}, u32[]{:S(2)}, u32[]{:S(2)}) %collective-permute-start.24) | collective-permute-done | bytes 229408 | tf_op jit(solution)/shard_map/ppermute | solution.py:749
  206.6 1.8 collective-permute-start.26
  208.8 3.3 %collective-permute-start.25 = (f32[280,128]{1,0:T(8,128)S(1)}, f32[280,128]{1,0:T(8,128)}, u32[]{:S(2)}, u32[]{:S(2)}) collective-permute-start(f32[280,128]{1,0:T(8,128)S(1)} %pad_maximum_fusion), channel_id=1, source_target_pairs={{0,3},{1,0},{2,1},{3,2},{4,7},{5,4},{6,5},{7,6},{8,11},{9,8},{10,9... | collective-permute-start | bytes 430088 | tf_op jit(solution)/shard_map/ppermute | solution.py:761
  212.2 1.2 fusion.2
  213.5 1.5 collective-permute-start.29
  215.0 0.7 slice.119
  216.4 5.2 %collective-permute-done.26 = f32[280,128]{1,0:T(8,128)S(1)} collective-permute-done((f32[280,128]{1,0:T(8,128)S(1)}, f32[280,128]{1,0:T(8,128)S(1)}, u32[]{:S(2)}, u32[]{:S(2)}) %collective-permute-start.26) | collective-permute-done | bytes 143392 | tf_op jit(solution)/shard_map/ppermute | solution.py:761
  221.5 1.0 add_add_fusion
  222.6 0.7 reshape.91
  224.5 0.9 copy-done.4
  225.4 0.9 copy-done.5
  226.4 1.3 finish.1
  228.3 0.8 fusion.7
  (124 shorter events, 13.7 us)
Async XLA Ops:
  7.2 57.8 %all-gather.2.cloned.1.call-start = ((), (), s32[]{:S(2)}) async-start(), calls=%async_computation.3 | async-start | bytes 4423680 | tf_op jit(solution)/shard_map/all_gather | solution.py:814
  11.7 0.8 copy-start.10
  12.5 144.1 %reduce-scatter.4.cloned.1.call-start = ((), (), s32[]{:S(2)}) async-start(), calls=%async_computation.4 | async-start | bytes 2621440 | tf_op jit(solution)/shard_map/reduce_scatter | solution.py:849
  12.6 17.1 %collective-permute-start.6 = (bf16[256,1024]{1,0:T(8,128)(2,1)}, bf16[256,1024]{1,0:T(8,128)(2,1)S(1)}, u32[]{:S(2)}, u32[]{:S(2)}) collective-permute-start(bf16[256,1024]{1,0:T(8,128)(2,1)} %bitcast.65), channel_id=1, source_target_pairs={{1,0},{2,1},{3,2},{5,4},{6,5},{7,6},{9,8},{10,9},{11,10},{13,12},{... | collective-permute-start | bytes 1572872 | tf_op jit(solution)/shard_map/ppermute | solution.py:715
  13.9 17.1 %collective-permute-start.3 = (bf16[256,1024]{1,0:T(8,128)(2,1)}, bf16[256,1024]{1,0:T(8,128)(2,1)S(1)}, u32[]{:S(2)}, u32[]{:S(2)}) collective-permute-start(bf16[256,1024]{1,0:T(8,128)(2,1)} %bitcast.66), channel_id=1, source_target_pairs={{0,1},{1,2},{2,3},{4,5},{5,6},{6,7},{8,9},{9,10},{10,11},{12,13},{... | collective-permute-start | bytes 1572872 | tf_op jit(solution)/shard_map/ppermute | solution.py:714
  19.5 27.3 %collective-permute-start.2 = (s32[256]{0:T(256)}, s32[256]{0:T(256)S(1)}, u32[]{:S(2)}, u32[]{:S(2)}) collective-permute-start(s32[256]{0:T(256)} %bitcast.79), channel_id=1, source_target_pairs={{0,1},{1,2},{2,3},{3,0},{4,5},{5,6},{6,7},{7,4},{8,9},{9,10},{10,1... | collective-permute-start | bytes 3080 | tf_op jit(solution)/shard_map/ppermute | solution.py:761
  21.5 12.2 %collective-permute-start.1 = (s32[256]{0:T(256)}, s32[256]{0:T(256)S(1)}, u32[]{:S(2)}, u32[]{:S(2)}) collective-permute-start(s32[256]{0:T(256)} %bitcast.80), channel_id=1, source_target_pairs={{0,2},{1,3},{2,0},{3,1},{4,6},{5,7},{6,4},{7,5},{8,10},{9,11},{10,... | collective-permute-start | bytes 3080 | tf_op jit(solution)/shard_map/ppermute | solution.py:761
  22.6 11.1 %collective-permute-start = (s32[256]{0:T(256)}, s32[256]{0:T(256)S(1)}, u32[]{:S(2)}, u32[]{:S(2)}) collective-permute-start(s32[256]{0:T(256)} %bitcast.81), channel_id=1, source_target_pairs={{0,3},{1,0},{2,1},{3,2},{4,7},{5,4},{6,5},{7,6},{8,11},{9,8},{10,9... | collective-permute-start | bytes 3080 | tf_op jit(solution)/shard_map/ppermute | solution.py:761
  29.6 35.3 %copy-start.12 = (bf16[256,1024]{1,0:T(8,128)(2,1)}, bf16[256,1024]{1,0:T(8,128)(2,1)S(1)}, u32[]{:S(2)}) copy-start(bf16[256,1024]{1,0:T(8,128)(2,1)S(1)} %collective-permute-done.6.refs_4_) | copy-start | bytes 1572868
  29.6 15.1 %collective-permute-start.7 = (bf16[256,1024]{1,0:T(8,128)(2,1)S(1)}, bf16[256,1024]{1,0:T(8,128)(2,1)S(1)}, u32[]{:S(2)}, u32[]{:S(2)}) collective-permute-start(bf16[256,1024]{1,0:T(8,128)(2,1)S(1)} %collective-permute-done.6.refs_4_), channel_id=1, source_target_pairs={{1,0},{2,1},{5,4},{6,5},{9,8},{10,9},{13,12},{14,13},{17,16},{18,1... | collective-permute-start | bytes 1572872 | tf_op jit(solution)/shard_map/ppermute | solution.py:715
  30.9 15.1 %collective-permute-start.4 = (bf16[256,1024]{1,0:T(8,128)(2,1)S(1)}, bf16[256,1024]{1,0:T(8,128)(2,1)S(1)}, u32[]{:S(2)}, u32[]{:S(2)}) collective-permute-start(bf16[256,1024]{1,0:T(8,128)(2,1)S(1)} %collective-permute-done.3.refs_2_), channel_id=1, source_target_pairs={{1,2},{2,3},{5,6},{6,7},{9,10},{10,11},{13,14},{14,15},{17,18},{18... | collective-permute-start | bytes 1572872 | tf_op jit(solution)/shard_map/ppermute | solution.py:714
  44.7 14.3 %copy-start.13 = (bf16[256,1024]{1,0:T(8,128)(2,1)}, bf16[256,1024]{1,0:T(8,128)(2,1)S(1)}, u32[]{:S(2)}) copy-start(bf16[256,1024]{1,0:T(8,128)(2,1)S(1)} %collective-permute-done.7.refs_5_) | copy-start | bytes 1572868
  44.7 14.3 %collective-permute-start.8 = (bf16[256,1024]{1,0:T(8,128)(2,1)S(1)}, bf16[256,1024]{1,0:T(8,128)(2,1)S(1)}, u32[]{:S(2)}, u32[]{:S(2)}) collective-permute-start(bf16[256,1024]{1,0:T(8,128)(2,1)S(1)} %collective-permute-done.7.refs_5_), channel_id=1, source_target_pairs={{1,0},{5,4},{9,8},{13,12},{17,16},{21,20},{25,24},{29,28}} | collective-permute-start | bytes 1572872 | tf_op jit(solution)/shard_map/ppermute | solution.py:715
  46.0 13.0 %collective-permute-start.5 = (bf16[256,1024]{1,0:T(8,128)(2,1)S(1)}, bf16[256,1024]{1,0:T(8,128)(2,1)S(1)}, u32[]{:S(2)}, u32[]{:S(2)}) collective-permute-start(bf16[256,1024]{1,0:T(8,128)(2,1)S(1)} %collective-permute-done.4.refs_1_), channel_id=1, source_target_pairs={{2,3},{6,7},{10,11},{14,15},{18,19},{22,23},{26,27},{30,31}} | collective-permute-start | bytes 1572872 | tf_op jit(solution)/shard_map/ppermute | solution.py:714
  59.0 1.3 copy-start.14
  59.0 14.4 %collective-permute-start.10 = (bf16[256,1024]{1,0:T(8,128)(2,1)}, bf16[256,1024]{1,0:T(8,128)(2,1)}, u32[]{:S(2)}, u32[]{:S(2)}) collective-permute-start(bf16[256,1024]{1,0:T(8,128)(2,1)} %bitcast.69), channel_id=1, source_target_pairs={{1,0},{2,1},{3,2},{5,4},{6,5},{7,6},{9,8},{10,9},{11,10},{13,12},{... | collective-permute-start | bytes 1572872 | tf_op jit(solution)/shard_map/ppermute | solution.py:715
  60.3 13.6 %collective-permute-start.9 = (bf16[256,1024]{1,0:T(8,128)(2,1)}, bf16[256,1024]{1,0:T(8,128)(2,1)S(1)}, u32[]{:S(2)}, u32[]{:S(2)}) collective-permute-start(bf16[256,1024]{1,0:T(8,128)(2,1)} %bitcast.70), channel_id=1, source_target_pairs={{0,1},{1,2},{2,3},{4,5},{5,6},{6,7},{8,9},{9,10},{10,11},{12,13},{... | collective-permute-start | bytes 1572872 | tf_op jit(solution)/shard_map/ppermute | solution.py:714
  73.9 17.0 %collective-permute-start.11 = (bf16[256,1024]{1,0:T(8,128)(2,1)S(1)}, bf16[256,1024]{1,0:T(8,128)(2,1)S(1)}, u32[]{:S(2)}, u32[]{:S(2)}) collective-permute-start(bf16[256,1024]{1,0:T(8,128)(2,1)S(1)} %collective-permute-done.9.refs_2_), channel_id=1, source_target_pairs={{1,2},{2,3},{5,6},{6,7},{9,10},{10,11},{13,14},{14,15},{17,18},{18... | collective-permute-start | bytes 1572872 | tf_op jit(solution)/shard_map/ppermute | solution.py:714
  74.6 16.3 %collective-permute-start.13 = (bf16[256,1024]{1,0:T(8,128)(2,1)}, bf16[256,1024]{1,0:T(8,128)(2,1)S(1)}, u32[]{:S(2)}, u32[]{:S(2)}) collective-permute-start(bf16[256,1024]{1,0:T(8,128)(2,1)} %collective-permute-done.10.refs_4_), channel_id=1, source_target_pairs={{1,0},{2,1},{5,4},{6,5},{9,8},{10,9},{13,12},{14,13},{17,16},{18,1... | collective-permute-start | bytes 1572872 | tf_op jit(solution)/shard_map/ppermute | solution.py:715
  76.1 13.8 %copy-start.1 = (s32[1040,128]{1,0:T(8,128)}, s32[1040,128]{1,0:T(8,128)S(1)}, u32[]{:S(2)}) copy-start(s32[1040,128]{1,0:T(8,128)S(1)} %broadcast_in_dim.34.window_ref.refs_9_) | copy-start | bytes 1597444
  89.9 1.0 copy-start.7
  90.8 15.7 %copy-start.15 = (bf16[256,1024]{1,0:T(8,128)(2,1)}, bf16[256,1024]{1,0:T(8,128)(2,1)S(1)}, u32[]{:S(2)}) copy-start(bf16[256,1024]{1,0:T(8,128)(2,1)S(1)} %collective-permute-done.13.refs_5_) | copy-start | bytes 1572868
  90.8 2.0 collective-permute-start.12
  91.5 15.0 %collective-permute-start.14 = (bf16[256,1024]{1,0:T(8,128)(2,1)S(1)}, bf16[256,1024]{1,0:T(8,128)(2,1)S(1)}, u32[]{:S(2)}, u32[]{:S(2)}) collective-permute-start(bf16[256,1024]{1,0:T(8,128)(2,1)S(1)} %collective-permute-done.13.refs_5_), channel_id=1, source_target_pairs={{1,0},{5,4},{9,8},{13,12},{17,16},{21,20},{25,24},{29,28}} | collective-permute-start | bytes 1572872 | tf_op jit(solution)/shard_map/ppermute | solution.py:715
  106.5 0.8 copy-start.16
  113.3 6.4 %copy-start.2 = (s32[1040,128]{1,0:T(8,128)S(1)}, s32[1040,128]{1,0:T(8,128)}, u32[]{:S(2)}) copy-start(s32[1040,128]{1,0:T(8,128)} %copy-done.1) | copy-start | bytes 1597444
  113.3 111.2 %reduce-scatter.6.cloned.1.call-start = ((), (), s32[]{:S(2)}) async-start(), calls=%async_computation.5 | async-start | bytes 1310720 | tf_op jit(solution)/shard_map/reduce_scatter | solution.py:861
  113.4 4.6 %collective-permute-start.16 = (f32[2,1024]{1,0:T(2,128)S(1)}, f32[2,1024]{1,0:T(2,128)S(1)}, u32[]{:S(2)}, u32[]{:S(2)}) collective-permute-start(f32[2,1024]{1,0:T(2,128)S(1)} %pad_maximum_fusion.4), channel_id=1, source_target_pairs={{0,2},{1,3},{2,0},{3,1},{4,6},{5,7},{6,4},{7,5},{8,10},{9,11},{10,... | collective-permute-start | bytes 24584 | tf_op jit(solution)/shard_map/ppermute | solution.py:761
  113.5 5.5 %collective-permute-start.17 = (f32[2,1024]{1,0:T(2,128)S(1)}, f32[2,1024]{1,0:T(2,128)S(1)}, u32[]{:S(2)}, u32[]{:S(2)}) collective-permute-start(f32[2,1024]{1,0:T(2,128)S(1)} %pad_maximum_fusion.4), channel_id=1, source_target_pairs={{0,1},{1,2},{2,3},{3,0},{4,5},{5,6},{6,7},{7,4},{8,9},{9,10},{10,1... | collective-permute-start | bytes 24584 | tf_op jit(solution)/shard_map/ppermute | solution.py:761
  116.0 3.7 %collective-permute-start.15 = (f32[2,1024]{1,0:T(2,128)S(1)}, f32[2,1024]{1,0:T(2,128)S(1)}, u32[]{:S(2)}, u32[]{:S(2)}) collective-permute-start(f32[2,1024]{1,0:T(2,128)S(1)} %pad_maximum_fusion.4), channel_id=1, source_target_pairs={{0,3},{1,0},{2,1},{3,2},{4,7},{5,4},{6,5},{7,6},{8,11},{9,8},{10,9... | collective-permute-start | bytes 24584 | tf_op jit(solution)/shard_map/ppermute | solution.py:761
  147.0 77.5 %reduce-scatter.8.cloned.1.call-start = ((), (), s32[]{:S(2)}) async-start(), calls=%async_computation.6 | async-start | bytes 1310720 | tf_op jit(solution)/shard_map/reduce_scatter | solution.py:861
  156.6 1.2 copy-start.6
  166.1 2.8 %copy-start.8 = (bf16[1024,1024]{1,0:T(8,128)(2,1)S(1)}, bf16[1024,1024]{1,0:T(8,128)(2,1)}, u32[]{:S(2)}) copy-start(bf16[1024,1024]{1,0:T(8,128)(2,1)} %get-tuple-element.84) | copy-start | bytes 6291460
  168.9 2.8 %collective-permute-start.22 = (bf16[2,2,128,896]{3,2,0,1:T(8,128)(2,1)}, bf16[2,2,128,896]{3,2,0,1:T(8,128)(2,1)}, u32[]{:S(2)}, u32[]{:S(2)}) collective-permute-start(bf16[2,2,128,896]{3,2,0,1:T(8,128)(2,1)} %bitcast.64), channel_id=1, source_target_pairs={{0,4},{4,0},{8,12},{12,8},{16,20},{20,16},{24,28},{28,24},{1,5},{5... | collective-permute-start | bytes 2752520 | tf_op jit(solution)/shard_map/ppermute | solution.py:749
  169.0 5.9 %collective-permute-start.18 = (bf16[2,2,128,1024]{3,2,1,0:T(8,128)(2,1)S(1)}, bf16[2,2,128,1024]{3,2,1,0:T(8,128)(2,1)}, u32[]{:S(2)}, u32[]{:S(2)}) collective-permute-start(bf16[2,2,128,1024]{3,2,1,0:T(8,128)(2,1)S(1)} %dynamic-slice_bitcast_fusion), channel_id=1, source_target_pairs={{0,4},{4,0},{8,12},{12,8},{16,20},{20,16},{24,28},{28,24},{1,5},{5... | collective-permute-start | bytes 3145736 | tf_op jit(solution)/shard_map/ppermute | solution.py:749
  169.8 5.1 %copy-start = (bf16[1,256,1024]{2,1,0:T(8,128)(2,1)S(1)}, bf16[1,256,1024]{2,1,0:T(8,128)(2,1)}, u32[]{:S(2)}) copy-start(bf16[1,256,1024]{2,1,0:T(8,128)(2,1)} %param.17) | copy-start | bytes 1572868
  169.8 5.1 %copy-start.11 = (bf16[256,1024]{1,0:T(8,128)(2,1)S(1)}, bf16[256,1024]{1,0:T(8,128)(2,1)}, u32[]{:S(2)}) copy-start(bf16[256,1024]{1,0:T(8,128)(2,1)} %reduce-scatter.4.cloned.1.call-done) | copy-start | bytes 1572868
  171.8 5.0 %copy-start.9 = (bf16[1024,1024]{1,0:T(8,128)(2,1)S(1)}, bf16[1024,1024]{1,0:T(8,128)(2,1)}, u32[]{:S(2)}) copy-start(bf16[1024,1024]{1,0:T(8,128)(2,1)} %get-tuple-element.84) | copy-start | bytes 6291460
  173.4 17.6 %collective-permute-start.23 = (bf16[2,128,896]{2,1,0:T(8,128)(2,1)S(1)}, bf16[2,128,896]{2,1,0:T(8,128)(2,1)S(1)}, u32[]{:S(2)}, u32[]{:S(2)}) collective-permute-start(bf16[2,128,896]{2,1,0:T(8,128)(2,1)S(1)} %dynamic-slice_bitcast_fusion.2), channel_id=1, source_target_pairs={{0,8},{4,12},{8,0},{12,4},{16,24},{20,28},{24,16},{28,20},{1,9},{5... | collective-permute-start | bytes 1376264 | tf_op jit(solution)/shard_map/ppermute | solution.py:749
  174.9 1.2 collective-permute-start.19
  176.1 10.6 %collective-permute-start.20 = (f32[64,128]{1,0:T(8,128)S(1)}, f32[64,128]{1,0:T(8,128)S(1)}, u32[]{:S(2)}, u32[]{:S(2)}) collective-permute-start(f32[64,128]{1,0:T(8,128)S(1)} %add.120), channel_id=1, source_target_pairs={{0,8},{4,12},{8,0},{12,4},{16,24},{20,28},{24,16},{28,20},{1,9},{5... | collective-permute-start | bytes 98312 | tf_op jit(solution)/shard_map/ppermute | solution.py:775
  186.7 4.3 %collective-permute-start.21 = (f32[64,128]{1,0:T(8,128)S(1)}, f32[64,128]{1,0:T(8,128)S(1)}, u32[]{:S(2)}, u32[]{:S(2)}) collective-permute-start(f32[64,128]{1,0:T(8,128)S(1)} %add.121), channel_id=1, source_target_pairs={{0,16},{4,20},{8,24},{12,28},{16,0},{20,4},{24,8},{28,12},{1,17},{... | collective-permute-start | bytes 98312 | tf_op jit(solution)/shard_map/ppermute | solution.py:775
  188.2 23.9 %collective-permute-start.28 = (bf16[2,128,1024]{2,1,0:T(8,128)(2,1)S(1)}, bf16[2,128,1024]{2,1,0:T(8,128)(2,1)}, u32[]{:S(2)}, u32[]{:S(2)}) collective-permute-start(bf16[2,128,1024]{2,1,0:T(8,128)(2,1)S(1)} %dynamic-slice_bitcast_fusion.1), channel_id=1, source_target_pairs={{0,16},{4,20},{8,24},{12,28},{16,0},{20,4},{24,8},{28,12},{1,17},{... | collective-permute-start | bytes 1572872 | tf_op jit(solution)/shard_map/ppermute | solution.py:749
  191.1 15.3 %collective-permute-start.24 = (bf16[128,896]{1,0:T(8,128)(2,1)S(1)}, bf16[128,896]{1,0:T(8,128)(2,1)S(1)}, u32[]{:S(2)}, u32[]{:S(2)}) collective-permute-start(bf16[128,896]{1,0:T(8,128)(2,1)S(1)} %dynamic-slice_bitcast_fusion.4), channel_id=1, source_target_pairs={{0,16},{4,20},{8,24},{12,28},{16,0},{20,4},{24,8},{28,12},{1,17},{... | collective-permute-start | bytes 688136 | tf_op jit(solution)/shard_map/ppermute | solution.py:749
  206.5 17.9 %copy-start.3 = (bf16[1,256,1024]{2,1,0:T(8,128)(2,1)S(1)}, bf16[1,256,1024]{2,1,0:T(8,128)(2,1)}, u32[]{:S(2)}) copy-start(bf16[1,256,1024]{2,1,0:T(8,128)(2,1)} %param.19) | copy-start | bytes 1572868
  206.6 15.0 %collective-permute-start.26 = (f32[280,128]{1,0:T(8,128)S(1)}, f32[280,128]{1,0:T(8,128)S(1)}, u32[]{:S(2)}, u32[]{:S(2)}) collective-permute-start(f32[280,128]{1,0:T(8,128)S(1)} %pad_maximum_fusion), channel_id=1, source_target_pairs={{0,2},{1,3},{2,0},{3,1},{4,6},{5,7},{6,4},{7,5},{8,10},{9,11},{10,... | collective-permute-start | bytes 430088 | tf_op jit(solution)/shard_map/ppermute | solution.py:761
  208.4 13.2 %collective-permute-start.27 = (f32[280,128]{1,0:T(8,128)S(1)}, f32[280,128]{1,0:T(8,128)}, u32[]{:S(2)}, u32[]{:S(2)}) collective-permute-start(f32[280,128]{1,0:T(8,128)S(1)} %pad_maximum_fusion), channel_id=1, source_target_pairs={{0,1},{1,2},{2,3},{3,0},{4,5},{5,6},{6,7},{7,4},{8,9},{9,10},{10,1... | collective-permute-start | bytes 430088 | tf_op jit(solution)/shard_map/ppermute | solution.py:761
  208.8 12.7 %collective-permute-start.25 = (f32[280,128]{1,0:T(8,128)S(1)}, f32[280,128]{1,0:T(8,128)}, u32[]{:S(2)}, u32[]{:S(2)}) collective-permute-start(f32[280,128]{1,0:T(8,128)S(1)} %pad_maximum_fusion), channel_id=1, source_target_pairs={{0,3},{1,0},{2,1},{3,2},{4,7},{5,4},{6,5},{7,6},{8,11},{9,8},{10,9... | collective-permute-start | bytes 430088 | tf_op jit(solution)/shard_map/ppermute | solution.py:761
  213.5 14.8 %collective-permute-start.29 = (bf16[128,1024]{1,0:T(8,128)(2,1)S(1)}, bf16[128,1024]{1,0:T(8,128)(2,1)S(1)}, u32[]{:S(2)}, u32[]{:S(2)}) collective-permute-start(bf16[128,1024]{1,0:T(8,128)(2,1)S(1)} %dynamic-slice_bitcast_fusion.3), channel_id=1, source_target_pairs={{0,8},{4,12},{8,0},{12,4},{16,24},{20,28},{24,16},{28,20},{1,9},{5... | collective-permute-start | bytes 786440 | tf_op jit(solution)/shard_map/ppermute | solution.py:749
  224.5 1.0 copy-start.4
  225.4 0.9 copy-start.5
Sparse Core Ops, SparseCore 0:
  12.6 38.3 all-gather.1
  113.4 43.1 reduce-scatter.3
  159.0 26.4 reduce-scatter.5
  187.7 29.8 reduce-scatter.7

commit v6 on v5

--- a/solution.py
+++ b/solution.py
@@ -275,8 +275,7 @@
     state_ref,
     grad_ref,
     proj_ref,
-    left_ref,
-    right_ref,
+    part_ref,
     out_ref,
     sum_x_ref,
     sum_bc_ref,
@@ -443,8 +442,7 @@
     )
     proj_ref[...] = grads
     part = dot_nt(grads, weights_ref[:, width:])
-    left_ref[...] = part[:, : part.shape[1] // 2].astype(BF16)
-    right_ref[...] = part[:, part.shape[1] // 2 :].astype(BF16)
+    part_ref[...] = part.astype(BF16)
     hidden = hidden_ref[...].astype(F32)
     inverse = lax.rsqrt(jnp.mean(hidden * hidden, axis=1, keepdims=True) + EPS)
     sum_gain_ref[0:1, :] += jnp.sum(part * (hidden * inverse), axis=0, keepdims=True)
@@ -656,9 +654,9 @@
             pl.BlockSpec((1, N, width), lambda i: (blocks - 1 - i, 0, 0)),
             rows(width),
         ],
-        out_specs=[rows(total), rows(features // 2), rows(features // 2), rows(width)]
+        out_specs=[rows(total), rows(features), rows(width)]
         + [whole(shape) for shape in sums],
-        out_shape=[made(total, BF16), made(features // 2, BF16), made(features // 2, BF16), made(width, BF16)]
+        out_shape=[made(total, BF16), made(features, BF16), made(width, BF16)]
         + [jax.ShapeDtypeStruct(shape, F32) for shape in sums],
         scratch_shapes=[
             pltpu.VMEM((Q + HALO, width), F32),
@@ -667,7 +665,7 @@
             pltpu.VMEM((8, LANES), F32),
         ],
         compiler_params=pltpu.CompilerParams(vmem_limit_bytes=VMEM_LIMIT),
-        cost_estimate=cost(27),
+        cost_estimate=cost(2),
         name="backward",
     )(
         stat, hidden, window, seg_row, weights, kernel_x, kernel_bc, head, channel,
@@ -675,9 +673,8 @@
     )
 
 
-def finish_kernel(left_ref, right_ref, hidden_ref, cot_ref, gain_ref, out_ref):
-    grad = jnp.concatenate([left_ref[...], right_ref[...]], axis=1).astype(F32)
-    grad = grad * gain_ref[0:1, :]
+def finish_kernel(sum_ref, hidden_ref, cot_ref, gain_ref, out_ref):
+    grad = sum_ref[...].astype(F32) * gain_ref[0:1, :]
     hidden = hidden_ref[...].astype(F32)
     inverse = lax.rsqrt(jnp.mean(hidden * hidden, axis=1, keepdims=True) + EPS)
     unit = hidden * inverse
@@ -685,19 +682,18 @@
     out_ref[...] = (cot_ref[...].astype(F32) + inverse * (grad - unit * along)).astype(BF16)
 
 
-def run_finish(in_sums, hidden, cot, gain):
+def run_finish(in_sum, hidden, cot, gain):
     length, features = hidden.shape
     rows = pl.BlockSpec((length // 2, features), lambda i: (i, 0))
-    halves = pl.BlockSpec((length // 2, features // 2), lambda i: (i, 0))
     return pl.pallas_call(
         finish_kernel,
         grid=(2,),
-        in_specs=[halves, halves, rows, rows, whole(gain.shape)],
+        in_specs=[rows, rows, rows, whole(gain.shape)],
         out_specs=rows,
         out_shape=jax.ShapeDtypeStruct(hidden.shape, BF16),
         compiler_params=pltpu.CompilerParams(vmem_limit_bytes=VMEM_LIMIT),
         name="finish",
-    )(*in_sums, hidden, cot, gain)
+    )(in_sum, hidden, cot, gain)
 
 
 def pad_lanes(values):
@@ -729,30 +725,50 @@
     return line_order(block, moved)
 
 
-def cube_scatter(part, axis, upward):
+def cube_scatter(first, second, small, axis):
     n = lax.axis_size(axis)
     if n & (n - 1):
-        part = lax.psum_scatter(part, axis, scatter_dimension=0, tiled=True).astype(F32)
-        return part, part
-    first = None
+        sums = [
+            lax.psum_scatter(part, axis, scatter_dimension=0, tiled=True).astype(F32)
+            for part in (first, second)
+        ]
+        return (*sums, lax.psum(small, axis), sums)
     place = lax.axis_index(axis)
-    rows, columns = part.shape
     bits = list(range(n.bit_length() - 1))
-    order = bits if upward else bits[:1] + bits[:0:-1]
-    left = bits[::-1]
-    part = part.reshape((2,) * len(bits) + (rows // n, columns))
-    for bit in order:
-        dim = left.index(bit)
-        mine = (place >> bit) & 1
-        keep = lax.dynamic_index_in_dim(part, mine, dim, keepdims=False)
-        send = lax.dynamic_index_in_dim(part, 1 - mine, dim, keepdims=False)
-        other = lax.ppermute(send, axis, [(i, i ^ (1 << bit)) for i in range(n)])
-        first = other if first is None else first
-        part = keep.astype(F32) + other.astype(F32)
-        left.remove(bit)
-        if left:
-            part = part.astype(BF16)
-    return part, first
+    orders = [bits, bits[:1] + bits[:0:-1]]
+    parts = [part.reshape((2,) * len(bits) + (-1, part.shape[1])) for part in (first, second)]
+    left = [bits[::-1], bits[::-1]]
+    came = [None, None]
+    for step in range(len(bits)):
+        for index in range(2):
+            part = parts[index]
+            bit = orders[index][step]
+            dim = left[index].index(bit)
+            mine = (place >> bit) & 1
+            keep = lax.dynamic_index_in_dim(part, mine, dim, keepdims=False)
+            send = lax.dynamic_index_in_dim(part, 1 - mine, dim, keepdims=False)
+            pairs = [(i, i ^ (1 << bit)) for i in range(n)]
+            if index == 0:
+                columns = part.shape[-1]
+                rows = send.size // columns
+                extra = -(-small.size // (16 * columns)) * 16
+                small = lax.reduce_precision(small, 8, 7)
+                rider = jnp.pad(
+                    small.astype(BF16).reshape(-1), (0, extra * columns - small.size)
+                ).reshape(extra, columns)
+                moved = lax.ppermute(
+                    jnp.concatenate([send.reshape(rows, columns), rider]), axis, pairs
+                )
+                other = moved[:rows].reshape(send.shape)
+                rider = moved[rows:].reshape(-1)[: small.size].reshape(small.shape)
+                small = small + rider.astype(F32)
+            else:
+                moved = other = lax.ppermute(send, axis, pairs)
+            came[index] = moved
+            part = keep.astype(F32) + other.astype(F32)
+            left[index] = [other_bit for other_bit in left[index] if other_bit != bit]
+            parts[index] = part.astype(BF16) if left[index] else part
+    return (*parts, small, came)
 
 
 def around(values, axis):
@@ -764,17 +780,6 @@
 
 def sum_around(values, axis):
     return functools.reduce(jnp.add, around(values, axis))
-
-
-def sum_pairwise(values, axis):
-    n = lax.axis_size(axis)
-    if n & (n - 1):
-        return lax.psum(values, axis)
-    bit = 1
-    while bit < n:
-        values = values + lax.ppermute(values, axis, [(i, i ^ bit) for i in range(n)])
-        bit *= 2
-    return values
 
 
 def shards(
@@ -847,26 +852,21 @@
     near_cot = line_order(cotangent[0], moved)
     cot_full, grad_out, along = run_gradient(place, near_cot, weights, scaled, window)
     out_sum = lax.psum_scatter(
-        after(out_part, along), "tensor", scatter_dimension=0, tiled=True
+        out_part, "tensor", scatter_dimension=0, tiled=True
     )
     stat = sum_around(jnp.stack([square[0], along[0]]), "tensor")
     stat_full = jnp.pad(stat, ((0, 6), (0, 0)))
     out_scale = lax.rsqrt(stat[0] / full_inner + EPS) * (seg_full > 0).astype(F32)
 
-    grads, *in_parts, normed_out, sum_x, sum_bc, sum_head, sum_gain = run_backward(
+    grads, in_part, normed_out, sum_x, sum_bc, sum_head, sum_gain = run_backward(
         heads, size, full_inner, stat_full, hidden_full, window, seg_row, weights, kernel_x,
         kernel_bc, head, channel, z_proj, mixed, x_proj, pre, bcdt, pre_bc, states, grad_out,
     )
-    in_sums = [
-        lax.psum_scatter(half, "tensor", scatter_dimension=0, tiled=True)
-        for half in in_parts
-    ]
+    in_sum = lax.psum_scatter(in_part, "tensor", scatter_dimension=0, tiled=True)
     first, second = run_weights(cot_full, normed_out, tokens, after(grads, out_sum))
-    first, _ = cube_scatter(first, "dp", True)
-    second, arrived = cube_scatter(second, "dp", False)
     own = jnp.concatenate([sum_x.reshape(-1, LANES), sum_head])
     both = jnp.concatenate([sum_gain[0].reshape(-1, LANES), sum_bc.reshape(-1, LANES)])
-    small = sum_pairwise(after(jnp.concatenate([own, both]), arrived), "dp")
+    first, second, small, came = cube_scatter(first, second, jnp.concatenate([own, both]), "dp")
     sum_x = small[: own.shape[0] - 8].reshape(8, width)
     sum_head = small[own.shape[0] - 8 : own.shape[0]]
     grad_bc = first[:, width : width + 2 * N]
@@ -886,7 +886,7 @@
     scale_here = lax.dynamic_slice_in_dim(out_scale, axis_place * local, local, 0)[:, None]
     layer_out = (hidden_rows + out_sum.astype(F32) * scale_here).astype(BF16)
 
-    grad_hidden = run_finish(in_sums, hidden_local, cotangent[0], after(gain, shared))
+    grad_hidden = run_finish(in_sum, hidden_local, cotangent[0], after(gain, came[1]))
 
     return (
         layer_out[None],

time: 237 us -> 266 us (1.12)
  waiting for transfers between devices: 79.5 us -> 110 us
  starting transfers between devices: 44.3 us -> 39.9 us
  local copies, waits for them, and re-layouts: 21.6 us -> 24.5 us
    ppermute x6, waiting for transfers between devices: 38 us -> 78.3 us  [line_step(): lax.ppermute(left, axis, [(i, i - 1) for i in range(1, n - step + 1)])]
    ppermute x9 -> x6, waiting for transfers between devices: 23.8 us -> 16.1 us  [the longest x3 10.6 us: cube_scatter(): lax.ppermute(jnp.concatenate([send.reshape(rows, columns), rider]), axis,...]
    ppermute x9, waiting for transfers between devices: 7.49 us -> 2.33 us  [around(): lax.ppermute(values, axis, [(i, (i - k) % n) for i in range(n)])]
    ppermute x9 -> x6, starting transfers between devices: 7.9 us -> 2.92 us  [the longest x3 2.07 us: cube_scatter(): moved = other = lax.ppermute(send, axis, pairs)]
    reduce_scatter x3 -> x2, waiting for transfers between devices: 9.6 us -> 13.1 us  [the longest x1 13 us: shards(): lax.psum_scatter(in_part, 'tensor', scatter_dimension=0, tiled=True)]
    unnamed x46 -> x44, local copies, waits for them, and re-layouts: 11.4 us -> 11.6 us
  transfers between devices with their start and end apart: 34 -> 30, of which waited for: 15 -> 13; matrix products, arithmetic and copies ran while one was open for 9% -> 8% of each run, Pallas kernels for 25% -> 16%
where the time goes in v6:
time: 266 us; the launch traced here: 265 us
  waiting for transfers between devices  110 us (41%)
  Pallas kernels  65.2 us (25%)
  starting transfers between devices  39.9 us (15%)
  local copies, waits for them, and re-layouts  24.5 us (9%)
  between operations  14.4 us (5%)
  other arithmetic  10.7 us (4%)
    ppermute x6, waiting for transfers between devices, line_step(): lax.ppermute(left, axis, [(i, i - 1) for i in range(1, n - step + 1)])  78.3 us
    pallas_call x1, Pallas kernels, run_backward(): pl.pallas_call(functools.partial(backward_kernel, heads, size, full_inner...  27.4 us
    ppermute x9, starting transfers between devices, around(): lax.ppermute(values, axis, [(i, (i - k) % n) for i in range(n)])  16.2 us
    pallas_call x1, Pallas kernels, run_forward(): pl.pallas_call(functools.partial(forward_kernel, heads, size), grid=(bloc...  13.8 us
    reduce_scatter x1, waiting for transfers between devices, shards(): lax.psum_scatter(in_part, 'tensor', scatter_dimension=0, tiled=True)  13 us
    ppermute x6, starting transfers between devices, line_step(): lax.ppermute(right, axis, [(i, i + 1) for i in range(step - 1, n - 1)])  12.9 us
    unnamed x44, local copies, waits for them, and re-layouts  11.6 us
    ppermute x3, waiting for transfers between devices, cube_scatter(): lax.ppermute(jnp.concatenate([send.reshape(rows, columns), rider]), axis,...  10.6 us
  transfers between devices with their start and end apart: 30, of which 13 were waited for; matrix products, arithmetic and copies ran while one was open for 8% of the time, Pallas kernels for 16%

profile of v6, /device:TPU:0, one launch (start us, length us, event | category | flops | bytes accessed | tf_op | source)
XLA Modules:
  0.0 265.1 jit_solution(5870680290372509959)
XLA Ops:
  7.2 0.7 pad_maximum_fusion.7
  8.1 0.9 constant_dynamic-update-slice_fusion.4
  9.0 0.9 constant_dynamic-update-slice_fusion.3
  9.9 0.9 constant_dynamic-update-slice_fusion.2
  10.8 0.8 constant_dynamic-update-slice_fusion.1
  11.7 0.8 copy-done.9
  12.6 1.3 collective-permute-start.6
  13.9 5.6 %collective-permute-start.3 = (bf16[256,1024]{1,0:T(8,128)(2,1)}, bf16[256,1024]{1,0:T(8,128)(2,1)S(1)}, u32[]{:S(2)}, u32[]{:S(2)}) collective-permute-start(bf16[256,1024]{1,0:T(8,128)(2,1)} %bitcast.73), channel_id=1, source_target_pairs={{0,1},{1,2},{2,3},{4,5},{5,6},{6,7},{8,9},{9,10},{10,11},{12,13},{... | collective-permute-start | bytes 1572872 | tf_op jit(solution)/shard_map/ppermute | solution.py:710
  19.5 2.0 collective-permute-start.2
  21.5 1.1 collective-permute-start.1
  22.6 2.8 %collective-permute-start = (s32[256]{0:T(256)}, s32[256]{0:T(256)S(1)}, u32[]{:S(2)}, u32[]{:S(2)}) collective-permute-start(s32[256]{0:T(256)} %bitcast.96), channel_id=1, source_target_pairs={{0,3},{1,0},{2,1},{3,2},{4,7},{5,4},{6,5},{7,6},{8,11},{9,8},{10,9... | collective-permute-start | bytes 3080 | tf_op jit(solution)/shard_map/ppermute | solution.py:777
  25.5 0.7 broadcast_in_dim.39
  27.0 0.7 pad_maximum_fusion.5.kernel_bc_ref
  27.7 2.0 collective-permute-done.6.refs_4_
  29.7 1.3 collective-permute-start.7
  32.3 0.7 pad_maximum_fusion.4.kernel_x_ref
  33.8 11.0 %collective-permute-done.7.refs_5_ = bf16[256,1024]{1,0:T(8,128)(2,1)S(1)} collective-permute-done((bf16[256,1024]{1,0:T(8,128)(2,1)S(1)}, bf16[256,1024]{1,0:T(8,128)(2,1)S(1)}, u32[]{:S(2)}, u32[]{:S(2)}) %collective-permute-start.7) | collective-permute-done | bytes 524320 | tf_op jit(solution)/shard_map/ppermute | solution.py:711
  44.7 1.3 collective-permute-start.8
  46.0 0.7 collective-permute-start.5
  47.6 11.4 %collective-permute-done.8.refs_6_ = bf16[256,1024]{1,0:T(8,128)(2,1)S(1)} collective-permute-done((bf16[256,1024]{1,0:T(8,128)(2,1)S(1)}, bf16[256,1024]{1,0:T(8,128)(2,1)S(1)}, u32[]{:S(2)}, u32[]{:S(2)}) %collective-permute-start.8) | collective-permute-done | bytes 524320 | tf_op jit(solution)/shard_map/ppermute | solution.py:711
  59.0 0.8 copy-done.13
  59.8 1.3 collective-permute-start.10
  61.1 4.6 %collective-permute-start.9 = (bf16[256,1024]{1,0:T(8,128)(2,1)}, bf16[256,1024]{1,0:T(8,128)(2,1)S(1)}, u32[]{:S(2)}, u32[]{:S(2)}) collective-permute-start(bf16[256,1024]{1,0:T(8,128)(2,1)} %bitcast.77), channel_id=1, source_target_pairs={{0,1},{1,2},{2,3},{4,5},{5,6},{6,7},{8,9},{9,10},{10,11},{12,13},{... | collective-permute-start | bytes 1572872 | tf_op jit(solution)/shard_map/ppermute | solution.py:710
  65.8 8.5 %project.1 = (bf16[1024,1024]{1,0:T(8,128)(2,1)}, bf16[1024,1024]{1,0:T(8,128)(2,1)}, f32[1024,512]{1,0:T(8,128)}, f32[1024,512]{1,0:T(8,128)}, f32[1024,384]{1,0:T(8,128)}, /*index=5*/f32[8,1024]{1,0:T(8,128)S(1)}) custom-call(s32[1]{0:T(128)} %bitcast.8.place_ref, bf16[256,1024]{1,0:T(8,128)(2,1)S(1)} %collective-permute-done.5.refs_0_, ...), custom_call_target="tpu_custom_call" | custom-call | flops 8000000000 | bytes 1048576 | tf_op jit(solution)/shard_map/project/pallas_call | solution.py:476
  74.9 13.8 %forward.1 = (f32[1024,512]{1,0:T(8,128)}, f32[1024,512]{1,0:T(8,128)}, f32[1024,256]{1,0:T(8,128)S(1)}, f32[4,128,512]{2,1,0:T(8,128)}, bf16[1024,512]{1,0:T(8,...) custom-call(s32[1040,128]{1,0:T(8,128)S(1)} %broadcast_in_dim.34.window_ref.refs_9_, ...), custom_call_target="tpu_custom_call" | custom-call | flops 14000000000 | bytes 1048576 | tf_op jit(solution)/shard_map/forward/pallas_call | solution.py:516
  88.7 1.0 copy-done.3
  89.7 1.3 collective-permute-start.13
  91.0 0.7 collective-permute-start.11
  91.7 31.3 %collective-permute-done.13.refs_5_ = bf16[256,1024]{1,0:T(8,128)(2,1)S(1)} collective-permute-done((bf16[256,1024]{1,0:T(8,128)(2,1)}, bf16[256,1024]{1,0:T(8,128)(2,1)S(1)}, u32[]{:S(2)}, u32[]{:S(2)}) %collective-permute-start.13) | collective-permute-done | bytes 524320 | tf_op jit(solution)/shard_map/ppermute | solution.py:711
  123.7 1.3 collective-permute-start.14
  125.0 22.7 %collective-permute-done.14.refs_6_ = bf16[256,1024]{1,0:T(8,128)(2,1)S(1)} collective-permute-done((bf16[256,1024]{1,0:T(8,128)(2,1)S(1)}, bf16[256,1024]{1,0:T(8,128)(2,1)S(1)}, u32[]{:S(2)}, u32[]{:S(2)}) %collective-permute-start.14) | collective-permute-done | bytes 524320 | tf_op jit(solution)/shard_map/ppermute | solution.py:711
  147.8 0.8 copy-done.15
  148.5 6.1 %out_gradient.1 = (bf16[1024,1024]{1,0:T(8,128)(2,1)}, f32[1024,512]{1,0:T(8,128)}, f32[8,1024]{1,0:T(8,128)S(1)}) custom-call(s32[1]{0:T(128)} %bitcast.8.place_ref, bf16[256,1024]{1,0:T(8,128)(2,1)S(1)} %collective-permute-done.12.refs_0_, bf16[256,1024]{1,0:T(8,128)(2,1)S(1)} %collective-permute-done.11.refs_1_, ...), custom_call_target="tpu_custom_call" | custom-call | flops 5000000000 | bytes 1048576 | tf_op jit(solution)/shard_map/out_gradient/pallas_call | solution.py:563
  154.6 2.5 collective-permute-start.16
  157.2 2.5 collective-permute-start.17
  159.7 1.3 collective-permute-start.15
  161.0 1.6 collective-permute-done.17
  162.6 0.7 collective-permute-done.15
  163.4 27.4 %backward.1 = (bf16[1024,1408]{1,0:T(8,128)(2,1)}, bf16[1024,1024]{1,0:T(8,128)(2,1)}, bf16[1024,512]{1,0:T(8,128)(2,1)S(1)}, f32[8,512]{1,0:T(8,128)S(1)}, f32[...) custom-call(f32[8,1024]{1,0:T(8,128)S(1)} %pad.29.stat_ref, ...), custom_call_target="tpu_custom_call" | custom-call | flops 2000000000 | bytes 1048576 | tf_op jit(solution)/shard_map/backward/pallas_call | solution.py:635
  190.9 8.3 %weight_gradients.1 = (bf16[1024,896]{1,0:T(8,128)(2,1)}, bf16[1024,1024]{1,0:T(8,128)(2,1)}) custom-call(bf16[1024,1024]{1,0:T(8,128)(2,1)} %get-tuple-element.70.cot_ref, bf16[1024,512]{1,0:T(8,128)(2,1)S(1)} %get-tuple-element.71.normed_ref, bf16[1024,1024]{1,0:T(8,128)(2,1)} %get-tuple-element.72.tokens_ref, bf16[1024,1408]{1,0:T(8,128)(2,1)} %get-tuple-element.74.grads_ref), custom_call_target="tpu_custom_call" | custom-call | flops 7000000000 | bytes 1048576 | tf_op jit(solution)/shard_map/weight_gradients/pallas_call | solution.py:600
  199.2 1.3 constant_dynamic-slice_fusion.1
  200.4 1.0 pad_maximum_fusion
  201.5 0.9 copy-done.6
  202.4 1.1 dynamic-slice_bitcast_fusion
  203.6 0.7 collective-permute-done.21
  204.3 0.8 slice.152
  205.2 1.3 slice.154
  207.9 1.0 fusion.4
  208.9 1.6 fusion
  210.5 0.8 dynamic-slice_bitcast_fusion.1
  211.4 0.9 collective-permute-start.19
  212.3 7.8 %collective-permute-done.22 = bf16[272,896]{1,0:T(8,128)(2,1)S(1)} collective-permute-done((bf16[272,896]{1,0:T(8,128)(2,1)S(1)}, bf16[272,896]{1,0:T(8,128)(2,1)S(1)}, u32[]{:S(2)}, u32[]{:S(2)}) %collective-permute-start.22) | collective-permute-done | bytes 487456 | tf_op jit(solution)/shard_map/ppermute | solution.py:759
  220.9 5.5 %collective-permute-done.19 = bf16[2,128,1024]{2,1,0:T(8,128)(2,1)} collective-permute-done((bf16[2,128,1024]{2,1,0:T(8,128)(2,1)}, bf16[2,128,1024]{2,1,0:T(8,128)(2,1)}, u32[]{:S(2)}, u32[]{:S(2)}) %collective-permute-start.19) | collective-permute-done | bytes 524320 | tf_op jit(solution)/shard_map/ppermute | solution.py:766
  226.5 1.2 fusion.2
  227.7 1.2 collective-permute-start.20
  228.9 2.1 collective-permute-done.23
  231.8 0.7 slice.176
  232.5 3.6 %collective-permute-start.26 = (f32[280,128]{1,0:T(8,128)S(1)}, f32[280,128]{1,0:T(8,128)S(1)}, u32[]{:S(2)}, u32[]{:S(2)}) collective-permute-start(f32[280,128]{1,0:T(8,128)S(1)} %pad_maximum_fusion.3), channel_id=1, source_target_pairs={{0,1},{1,2},{2,3},{3,0},{4,5},{5,6},{6,7},{7,4},{8,9},{9,10},{10,1... | collective-permute-start | bytes 430088 | tf_op jit(solution)/shard_map/ppermute | solution.py:777
  238.9 1.0 convert_add_fusion.4
  239.9 13.0 %reduce-scatter.5.cloned.1.call-done.sum_ref = bf16[256,1024]{1,0:T(8,128)(2,1)} async-done(((bf16[1024,1024]{1,0:T(8,128)(2,1)}), bf16[256,1024]{1,0:T(8,128)(2,1)}) %reduce-scatter.5.cloned.1.call-update) | async-done | bytes 524304 | tf_op jit(solution)/shard_map/reduce_scatter | solution.py:865
  252.9 1.0 copy-done.5
  254.0 1.3 finish.1
  255.2 0.8 fusion.9
  256.7 0.7 reshape.143
  (129 shorter events, 13.4 us)
Async XLA Ops:
  7.2 58.5 %all-gather.2.cloned.1.call-start = ((), (), s32[]{:S(2)}) async-start(), calls=%async_computation.2 | async-start | bytes 4423680 | tf_op jit(solution)/shard_map/all_gather | solution.py:819
  11.7 0.8 copy-start.9
  12.5 178.3 %reduce-scatter.3.cloned.1.call-start = ((), (), s32[]{:S(2)}) async-start(), calls=%async_computation.3 | async-start | bytes 2621440 | tf_op jit(solution)/shard_map/reduce_scatter | solution.py:854
  12.6 17.1 %collective-permute-start.6 = (bf16[256,1024]{1,0:T(8,128)(2,1)}, bf16[256,1024]{1,0:T(8,128)(2,1)S(1)}, u32[]{:S(2)}, u32[]{:S(2)}) collective-permute-start(bf16[256,1024]{1,0:T(8,128)(2,1)} %bitcast.72), channel_id=1, source_target_pairs={{1,0},{2,1},{3,2},{5,4},{6,5},{7,6},{9,8},{10,9},{11,10},{13,12},{... | collective-permute-start | bytes 1572872 | tf_op jit(solution)/shard_map/ppermute | solution.py:711
  13.9 17.1 %collective-permute-start.3 = (bf16[256,1024]{1,0:T(8,128)(2,1)}, bf16[256,1024]{1,0:T(8,128)(2,1)S(1)}, u32[]{:S(2)}, u32[]{:S(2)}) collective-permute-start(bf16[256,1024]{1,0:T(8,128)(2,1)} %bitcast.73), channel_id=1, source_target_pairs={{0,1},{1,2},{2,3},{4,5},{5,6},{6,7},{8,9},{9,10},{10,11},{12,13},{... | collective-permute-start | bytes 1572872 | tf_op jit(solution)/shard_map/ppermute | solution.py:710
  19.5 27.3 %collective-permute-start.2 = (s32[256]{0:T(256)}, s32[256]{0:T(256)S(1)}, u32[]{:S(2)}, u32[]{:S(2)}) collective-permute-start(s32[256]{0:T(256)} %bitcast.94), channel_id=1, source_target_pairs={{0,1},{1,2},{2,3},{3,0},{4,5},{5,6},{6,7},{7,4},{8,9},{9,10},{10,1... | collective-permute-start | bytes 3080 | tf_op jit(solution)/shard_map/ppermute | solution.py:777
  21.5 12.2 %collective-permute-start.1 = (s32[256]{0:T(256)}, s32[256]{0:T(256)S(1)}, u32[]{:S(2)}, u32[]{:S(2)}) collective-permute-start(s32[256]{0:T(256)} %bitcast.95), channel_id=1, source_target_pairs={{0,2},{1,3},{2,0},{3,1},{4,6},{5,7},{6,4},{7,5},{8,10},{9,11},{10,... | collective-permute-start | bytes 3080 | tf_op jit(solution)/shard_map/ppermute | solution.py:777
  22.6 11.1 %collective-permute-start = (s32[256]{0:T(256)}, s32[256]{0:T(256)S(1)}, u32[]{:S(2)}, u32[]{:S(2)}) collective-permute-start(s32[256]{0:T(256)} %bitcast.96), channel_id=1, source_target_pairs={{0,3},{1,0},{2,1},{3,2},{4,7},{5,4},{6,5},{7,6},{8,11},{9,8},{10,9... | collective-permute-start | bytes 3080 | tf_op jit(solution)/shard_map/ppermute | solution.py:777
  29.6 36.1 %copy-start.11 = (bf16[256,1024]{1,0:T(8,128)(2,1)}, bf16[256,1024]{1,0:T(8,128)(2,1)S(1)}, u32[]{:S(2)}) copy-start(bf16[256,1024]{1,0:T(8,128)(2,1)S(1)} %collective-permute-done.6.refs_4_) | copy-start | bytes 1572868
  29.7 15.1 %collective-permute-start.7 = (bf16[256,1024]{1,0:T(8,128)(2,1)S(1)}, bf16[256,1024]{1,0:T(8,128)(2,1)S(1)}, u32[]{:S(2)}, u32[]{:S(2)}) collective-permute-start(bf16[256,1024]{1,0:T(8,128)(2,1)S(1)} %collective-permute-done.6.refs_4_), channel_id=1, source_target_pairs={{1,0},{2,1},{5,4},{6,5},{9,8},{10,9},{13,12},{14,13},{17,16},{18,1... | collective-permute-start | bytes 1572872 | tf_op jit(solution)/shard_map/ppermute | solution.py:711
  31.0 15.1 %collective-permute-start.4 = (bf16[256,1024]{1,0:T(8,128)(2,1)S(1)}, bf16[256,1024]{1,0:T(8,128)(2,1)S(1)}, u32[]{:S(2)}, u32[]{:S(2)}) collective-permute-start(bf16[256,1024]{1,0:T(8,128)(2,1)S(1)} %collective-permute-done.3.refs_2_), channel_id=1, source_target_pairs={{1,2},{2,3},{5,6},{6,7},{9,10},{10,11},{13,14},{14,15},{17,18},{18... | collective-permute-start | bytes 1572872 | tf_op jit(solution)/shard_map/ppermute | solution.py:710
  44.7 21.0 %copy-start.12 = (bf16[256,1024]{1,0:T(8,128)(2,1)}, bf16[256,1024]{1,0:T(8,128)(2,1)S(1)}, u32[]{:S(2)}) copy-start(bf16[256,1024]{1,0:T(8,128)(2,1)S(1)} %collective-permute-done.7.refs_5_) | copy-start | bytes 1572868
  44.7 14.3 %collective-permute-start.8 = (bf16[256,1024]{1,0:T(8,128)(2,1)S(1)}, bf16[256,1024]{1,0:T(8,128)(2,1)S(1)}, u32[]{:S(2)}, u32[]{:S(2)}) collective-permute-start(bf16[256,1024]{1,0:T(8,128)(2,1)S(1)} %collective-permute-done.7.refs_5_), channel_id=1, source_target_pairs={{1,0},{5,4},{9,8},{13,12},{17,16},{21,20},{25,24},{29,28}} | collective-permute-start | bytes 1572872 | tf_op jit(solution)/shard_map/ppermute | solution.py:711
  46.0 13.0 %collective-permute-start.5 = (bf16[256,1024]{1,0:T(8,128)(2,1)S(1)}, bf16[256,1024]{1,0:T(8,128)(2,1)S(1)}, u32[]{:S(2)}, u32[]{:S(2)}) collective-permute-start(bf16[256,1024]{1,0:T(8,128)(2,1)S(1)} %collective-permute-done.4.refs_1_), channel_id=1, source_target_pairs={{2,3},{6,7},{10,11},{14,15},{18,19},{22,23},{26,27},{30,31}} | collective-permute-start | bytes 1572872 | tf_op jit(solution)/shard_map/ppermute | solution.py:710
  59.0 0.8 copy-start.13
  59.8 14.4 %collective-permute-start.10 = (bf16[256,1024]{1,0:T(8,128)(2,1)}, bf16[256,1024]{1,0:T(8,128)(2,1)}, u32[]{:S(2)}, u32[]{:S(2)}) collective-permute-start(bf16[256,1024]{1,0:T(8,128)(2,1)} %bitcast.76), channel_id=1, source_target_pairs={{1,0},{2,1},{3,2},{5,4},{6,5},{7,6},{9,8},{10,9},{11,10},{13,12},{... | collective-permute-start | bytes 1572872 | tf_op jit(solution)/shard_map/ppermute | solution.py:711
  61.1 13.6 %collective-permute-start.9 = (bf16[256,1024]{1,0:T(8,128)(2,1)}, bf16[256,1024]{1,0:T(8,128)(2,1)S(1)}, u32[]{:S(2)}, u32[]{:S(2)}) collective-permute-start(bf16[256,1024]{1,0:T(8,128)(2,1)} %bitcast.77), channel_id=1, source_target_pairs={{0,1},{1,2},{2,3},{4,5},{5,6},{6,7},{8,9},{9,10},{10,11},{12,13},{... | collective-permute-start | bytes 1572872 | tf_op jit(solution)/shard_map/ppermute | solution.py:710
  74.9 13.8 %copy-start = (s32[1040,128]{1,0:T(8,128)}, s32[1040,128]{1,0:T(8,128)S(1)}, u32[]{:S(2)}) copy-start(s32[1040,128]{1,0:T(8,128)S(1)} %broadcast_in_dim.34.window_ref.refs_9_) | copy-start | bytes 1597444
  88.6 1.0 copy-start.3
  89.6 163.3 %reduce-scatter.5.cloned.1.call-start = ((), (), s32[]{:S(2)}) async-start(), calls=%async_computation.4 | async-start | bytes 2621440 | tf_op jit(solution)/shard_map/reduce_scatter | solution.py:865
  89.7 33.3 %collective-permute-start.13 = (bf16[256,1024]{1,0:T(8,128)(2,1)}, bf16[256,1024]{1,0:T(8,128)(2,1)S(1)}, u32[]{:S(2)}, u32[]{:S(2)}) collective-permute-start(bf16[256,1024]{1,0:T(8,128)(2,1)} %collective-permute-done.10.refs_4_), channel_id=1, source_target_pairs={{1,0},{2,1},{5,4},{6,5},{9,8},{10,9},{13,12},{14,13},{17,16},{18,1... | collective-permute-start | bytes 1572872 | tf_op jit(solution)/shard_map/ppermute | solution.py:711
  91.0 32.0 %collective-permute-start.11 = (bf16[256,1024]{1,0:T(8,128)(2,1)S(1)}, bf16[256,1024]{1,0:T(8,128)(2,1)S(1)}, u32[]{:S(2)}, u32[]{:S(2)}) collective-permute-start(bf16[256,1024]{1,0:T(8,128)(2,1)S(1)} %collective-permute-done.9.refs_2_), channel_id=1, source_target_pairs={{1,2},{2,3},{5,6},{6,7},{9,10},{10,11},{13,14},{14,15},{17,18},{18... | collective-permute-start | bytes 1572872 | tf_op jit(solution)/shard_map/ppermute | solution.py:710
  123.0 24.7 %copy-start.14 = (bf16[256,1024]{1,0:T(8,128)(2,1)}, bf16[256,1024]{1,0:T(8,128)(2,1)S(1)}, u32[]{:S(2)}) copy-start(bf16[256,1024]{1,0:T(8,128)(2,1)S(1)} %collective-permute-done.13.refs_5_) | copy-start | bytes 1572868
  123.0 2.0 collective-permute-start.12
  123.7 24.0 %collective-permute-start.14 = (bf16[256,1024]{1,0:T(8,128)(2,1)S(1)}, bf16[256,1024]{1,0:T(8,128)(2,1)S(1)}, u32[]{:S(2)}, u32[]{:S(2)}) collective-permute-start(bf16[256,1024]{1,0:T(8,128)(2,1)S(1)} %collective-permute-done.13.refs_5_), channel_id=1, source_target_pairs={{1,0},{5,4},{9,8},{13,12},{17,16},{21,20},{25,24},{29,28}} | collective-permute-start | bytes 1572872 | tf_op jit(solution)/shard_map/ppermute | solution.py:711
  147.8 0.8 copy-start.15
  148.5 14.8 %copy-start.1 = (s32[1040,128]{1,0:T(8,128)S(1)}, s32[1040,128]{1,0:T(8,128)}, u32[]{:S(2)}) copy-start(s32[1040,128]{1,0:T(8,128)} %copy-done) | copy-start | bytes 1597444
  154.6 6.4 %collective-permute-start.16 = (f32[2,1024]{1,0:T(2,128)S(1)}, f32[2,1024]{1,0:T(2,128)S(1)}, u32[]{:S(2)}, u32[]{:S(2)}) collective-permute-start(f32[2,1024]{1,0:T(2,128)S(1)} %pad_maximum_fusion.6), channel_id=1, source_target_pairs={{0,2},{1,3},{2,0},{3,1},{4,6},{5,7},{6,4},{7,5},{8,10},{9,11},{10,... | collective-permute-start | bytes 24584 | tf_op jit(solution)/shard_map/ppermute | solution.py:777
  157.2 5.4 %collective-permute-start.17 = (f32[2,1024]{1,0:T(2,128)S(1)}, f32[2,1024]{1,0:T(2,128)S(1)}, u32[]{:S(2)}, u32[]{:S(2)}) collective-permute-start(f32[2,1024]{1,0:T(2,128)S(1)} %pad_maximum_fusion.6), channel_id=1, source_target_pairs={{0,1},{1,2},{2,3},{3,0},{4,5},{5,6},{6,7},{7,4},{8,9},{9,10},{10,1... | collective-permute-start | bytes 24584 | tf_op jit(solution)/shard_map/ppermute | solution.py:777
  159.7 3.7 %collective-permute-start.15 = (f32[2,1024]{1,0:T(2,128)S(1)}, f32[2,1024]{1,0:T(2,128)S(1)}, u32[]{:S(2)}, u32[]{:S(2)}) collective-permute-start(f32[2,1024]{1,0:T(2,128)S(1)} %pad_maximum_fusion.6), channel_id=1, source_target_pairs={{0,3},{1,0},{2,1},{3,2},{4,7},{5,4},{6,5},{7,6},{8,11},{9,8},{10,9... | collective-permute-start | bytes 24584 | tf_op jit(solution)/shard_map/ppermute | solution.py:777
  200.4 1.9 copy-start.6
  201.4 2.9 %collective-permute-start.21 = (bf16[528,896]{1,0:T(8,128)(2,1)}, bf16[528,896]{1,0:T(8,128)(2,1)}, u32[]{:S(2)}, u32[]{:S(2)}) collective-permute-start(bf16[528,896]{1,0:T(8,128)(2,1)} %pad_maximum_fusion), channel_id=1, source_target_pairs={{0,4},{4,0},{8,12},{12,8},{16,20},{20,16},{24,28},{28,24},{1,5},{5... | collective-permute-start | bytes 2838536 | tf_op jit(solution)/shard_map/ppermute | solution.py:759
  203.4 3.0 %copy-start.8 = (bf16[1024,896]{1,0:T(8,128)(2,1)S(1)}, bf16[1024,896]{1,0:T(8,128)(2,1)}, u32[]{:S(2)}) copy-start(bf16[1024,896]{1,0:T(8,128)(2,1)} %get-tuple-element.81) | copy-start | bytes 5505028
  203.4 5.4 %collective-permute-start.18 = (bf16[2,2,128,1024]{3,2,1,0:T(8,128)(2,1)}, bf16[2,2,128,1024]{3,2,1,0:T(8,128)(2,1)}, u32[]{:S(2)}, u32[]{:S(2)}) collective-permute-start(bf16[2,2,128,1024]{3,2,1,0:T(8,128)(2,1)} %dynamic-slice_bitcast_fusion), channel_id=1, source_target_pairs={{0,4},{4,0},{8,12},{12,8},{16,20},{20,16},{24,28},{28,24},{1,5},{5... | collective-permute-start | bytes 3145736 | tf_op jit(solution)/shard_map/ppermute | solution.py:766
  206.5 1.1 copy-start.2
  206.5 1.4 copy-start.10
  206.7 2.2 copy-start.7
  206.8 13.2 %collective-permute-start.22 = (bf16[272,896]{1,0:T(8,128)(2,1)S(1)}, bf16[272,896]{1,0:T(8,128)(2,1)S(1)}, u32[]{:S(2)}, u32[]{:S(2)}) collective-permute-start(bf16[272,896]{1,0:T(8,128)(2,1)S(1)} %pad_maximum_fusion.1), channel_id=1, source_target_pairs={{0,8},{4,12},{8,0},{12,4},{16,24},{20,28},{24,16},{28,20},{1,9},{5... | collective-permute-start | bytes 1462280 | tf_op jit(solution)/shard_map/ppermute | solution.py:759
  211.4 15.1 %collective-permute-start.19 = (bf16[2,128,1024]{2,1,0:T(8,128)(2,1)}, bf16[2,128,1024]{2,1,0:T(8,128)(2,1)}, u32[]{:S(2)}, u32[]{:S(2)}) collective-permute-start(bf16[2,128,1024]{2,1,0:T(8,128)(2,1)} %dynamic-slice_bitcast_fusion.1), channel_id=1, source_target_pairs={{0,16},{4,20},{8,24},{12,28},{16,0},{20,4},{24,8},{28,12},{1,17},{... | collective-permute-start | bytes 1572872 | tf_op jit(solution)/shard_map/ppermute | solution.py:766
  220.5 10.5 %collective-permute-start.23 = (bf16[144,896]{1,0:T(8,128)(2,1)S(1)}, bf16[144,896]{1,0:T(8,128)(2,1)S(1)}, u32[]{:S(2)}, u32[]{:S(2)}) collective-permute-start(bf16[144,896]{1,0:T(8,128)(2,1)S(1)} %pad_maximum_fusion.2), channel_id=1, source_target_pairs={{0,16},{4,20},{8,24},{12,28},{16,0},{20,4},{24,8},{28,12},{1,17},{... | collective-permute-start | bytes 774152 | tf_op jit(solution)/shard_map/ppermute | solution.py:759
  227.7 25.2 %copy-start.4 = (bf16[1,256,1024]{2,1,0:T(8,128)(2,1)S(1)}, bf16[1,256,1024]{2,1,0:T(8,128)(2,1)}, u32[]{:S(2)}) copy-start(bf16[1,256,1024]{2,1,0:T(8,128)(2,1)} %param.19) | copy-start | bytes 1572868
  227.7 11.1 %collective-permute-start.20 = (bf16[128,1024]{1,0:T(8,128)(2,1)S(1)}, bf16[128,1024]{1,0:T(8,128)(2,1)}, u32[]{:S(2)}, u32[]{:S(2)}) collective-permute-start(bf16[128,1024]{1,0:T(8,128)(2,1)S(1)} %dynamic-slice_bitcast_fusion.2), channel_id=1, source_target_pairs={{0,8},{4,12},{8,0},{12,4},{16,24},{20,28},{24,16},{28,20},{1,9},{5... | collective-permute-start | bytes 786440 | tf_op jit(solution)/shard_map/ppermute | solution.py:766
  232.5 23.5 %collective-permute-start.25 = (f32[280,128]{1,0:T(8,128)S(1)}, f32[280,128]{1,0:T(8,128)S(1)}, u32[]{:S(2)}, u32[]{:S(2)}) collective-permute-start(f32[280,128]{1,0:T(8,128)S(1)} %pad_maximum_fusion.3), channel_id=1, source_target_pairs={{0,2},{1,3},{2,0},{3,1},{4,6},{5,7},{6,4},{7,5},{8,10},{9,11},{10,... | collective-permute-start | bytes 430088 | tf_op jit(solution)/shard_map/ppermute | solution.py:777
  232.5 23.5 %collective-permute-start.26 = (f32[280,128]{1,0:T(8,128)S(1)}, f32[280,128]{1,0:T(8,128)S(1)}, u32[]{:S(2)}, u32[]{:S(2)}) collective-permute-start(f32[280,128]{1,0:T(8,128)S(1)} %pad_maximum_fusion.3), channel_id=1, source_target_pairs={{0,1},{1,2},{2,3},{3,0},{4,5},{5,6},{6,7},{7,4},{8,9},{9,10},{10,1... | collective-permute-start | bytes 430088 | tf_op jit(solution)/shard_map/ppermute | solution.py:777
  236.1 19.9 %collective-permute-start.24 = (f32[280,128]{1,0:T(8,128)S(1)}, f32[280,128]{1,0:T(8,128)S(1)}, u32[]{:S(2)}, u32[]{:S(2)}) collective-permute-start(f32[280,128]{1,0:T(8,128)S(1)} %pad_maximum_fusion.3), channel_id=1, source_target_pairs={{0,3},{1,0},{2,1},{3,2},{4,7},{5,4},{6,5},{7,6},{8,11},{9,8},{10,9... | collective-permute-start | bytes 430088 | tf_op jit(solution)/shard_map/ppermute | solution.py:777
  252.9 1.0 copy-start.5
Sparse Core Ops, SparseCore 0:
  12.6 38.3 all-gather.1
  89.8 55.2 reduce-scatter.2
  201.6 51.2 reduce-scatter.4

commit v7 on v6

--- a/solution.py
+++ b/solution.py
@@ -158,13 +158,29 @@
     z_ref,
     x_ref,
     bcdt_ref,
-    mixed_ref,
-    pre_ref,
-    pre_bc_ref,
-    state_ref,
     scaled_ref,
     part_ref,
     square_ref,
+    state_ref,
+    survive_ref,
+    shape_ref,
+    prob_ref,
+    gated_ref,
+    opened_ref,
+    slope_z_ref,
+    inner_ref,
+    carried_ref,
+    x_conv_ref,
+    slope_x_ref,
+    dt_ref,
+    from_start_ref,
+    to_end_ref,
+    weighted_ref,
+    weighted_end_ref,
+    bc_ref,
+    slope_bc_ref,
+    decay_ref,
+    slope_dt_ref,
     x_buffer,
     bc_buffer,
     carry,
@@ -180,7 +196,6 @@
 
     window = window_ref[pl.ds(pl.multiple_of(step * Q, Q), Q + 2 * HALO), :]
     seg, from_prev, same_last, passes, bias = block_masks(window, seg_row_ref[0:1, :])
-    z_proj = z_ref[...]
     bcdt = bcdt_ref[...]
     x_buffer[HALO : HALO + Q, :] = x_ref[...]
     bc_buffer[HALO : HALO + Q, :] = bcdt[:, : 2 * N]
@@ -192,49 +207,72 @@
     )
     x_buffer[0:HALO, :] = x_buffer[Q : Q + HALO, :]
     bc_buffer[0:HALO, :] = bc_buffer[Q : Q + HALO, :]
-    pre_ref[...] = pre
-    pre_bc_ref[...] = pre_bc
-    x_conv = pre * sigmoid(pre)
-    bc_conv = (pre_bc * sigmoid(pre_bc)).astype(BF16)
+    gate_x = sigmoid(pre)
+    x_conv = pre * gate_x
+    x_conv_ref[...] = x_conv
+    slope_x_ref[...] = gate_x * (1.0 + pre * (1.0 - gate_x))
+    gate_bc = sigmoid(pre_bc)
+    bc_conv = (pre_bc * gate_bc).astype(BF16)
+    bc_ref[...] = bc_conv
+    slope_bc_ref[...] = gate_bc * (1.0 + pre_bc * (1.0 - gate_bc))
     b_in = bc_conv[:, :N]
     c_in = bc_conv[:, N:]
 
-    dt = softplus(bcdt[:, 2 * N :] + head_ref[0:1, :])
+    raw = bcdt[:, 2 * N :] + head_ref[0:1, :]
+    slope_dt_ref[...] = sigmoid(raw)
+    dt = softplus(raw)
     decay = -dt * jnp.exp(head_ref[1:2, :])
+    decay_ref[...] = decay
     total = dot_exact(triangle(True).astype(F32), decay)
     total_t = total.T
-    weighted = x_conv * spread(dt, heads, size)
+    dt_wide = spread(dt, heads, size)
+    dt_ref[...] = dt_wide
+    weighted = x_conv * dt_wide
+    weighted_low = weighted.astype(BF16)
+    weighted_ref[...] = weighted_low
     scores = dot_nt(c_in, b_in)
     before = carry[...]
     state_ref[0] = before
 
     per = LANES // size
     lane = lax.broadcasted_iota(jnp.int32, (Q, LANES), 1)
+    none = jnp.zeros((Q, LANES), BF16)
     inner = []
     for first in range(0, heads, per):
-        group = weighted[:, first * size : first * size + LANES]
+        group = weighted_low[:, first * size : first * size + LANES]
         summed = jnp.zeros((Q, LANES), F32)
         for extra in range(per):
             h = first + extra
             shape = jnp.exp(total[:, h : h + 1] - total_t[h : h + 1, :] + bias)
+            prob = (scores * shape).astype(BF16)
+            shape_ref[:, h * Q : (h + 1) * Q] = shape.astype(BF16)
+            prob_ref[:, h * Q : (h + 1) * Q] = prob
             mine = (lane >= extra * size) & (lane < (extra + 1) * size)
-            summed = summed + dot(
-                (scores * shape).astype(BF16), jnp.where(mine, group, 0.0).astype(BF16)
-            )
+            summed = summed + dot(prob, jnp.where(mine, group, none))
         inner.append(summed)
-    scanned = jnp.concatenate(inner, axis=1)
-    scanned = scanned + dot(c_in, before.astype(BF16)) * spread(
-        jnp.exp(total) * from_prev, heads, size
-    )
+    inner = jnp.concatenate(inner, axis=1)
+    inner_ref[...] = inner
+    carried = dot(c_in, before.astype(BF16))
+    carried_ref[...] = carried
+    from_start = spread(jnp.exp(total) * from_prev, heads, size)
+    from_start_ref[...] = from_start
     last = total[Q - 1 : Q, :]
-    to_end = jnp.exp(last - total) * same_last
-    carry[...] = dot_tn(
-        b_in, (weighted * spread(to_end, heads, size)).astype(BF16)
-    ) + before * spread(jnp.exp(last) * passes, heads, size)
-
-    mixed = scanned + channel_ref[1:2, :] * x_conv
-    mixed_ref[...] = mixed
-    gated = mixed * (z_proj * sigmoid(z_proj))
+    to_end = spread(jnp.exp(last - total) * same_last, heads, size)
+    to_end_ref[...] = to_end
+    weighted_end = (weighted * to_end).astype(BF16)
+    weighted_end_ref[...] = weighted_end
+    survive = spread(jnp.exp(last) * passes, heads, size)
+    survive_ref[0] = jnp.broadcast_to(survive, (8, width))
+    carry[...] = dot_tn(b_in, weighted_end) + before * survive
+
+    mixed = inner + carried * from_start + channel_ref[1:2, :] * x_conv
+    z_proj = z_ref[...]
+    gate = sigmoid(z_proj)
+    opened = z_proj * gate
+    opened_ref[...] = opened
+    slope_z_ref[...] = mixed * (gate * (1.0 + z_proj * (1.0 - gate)))
+    gated = mixed * opened
+    gated_ref[...] = gated
     scaled = (gated * channel_ref[0:1, :]).astype(BF16)
     scaled_ref[...] = scaled
     part_ref[...] = dot_nt(scaled, weights_ref[...]).astype(BF16)
@@ -260,20 +298,34 @@
     stat_ref,
     hidden_ref,
     window_ref,
-    seg_row_ref,
     weights_ref,
     kernel_x_ref,
     kernel_bc_ref,
     head_ref,
     channel_ref,
-    z_ref,
-    mixed_ref,
     x_ref,
-    pre_ref,
     bcdt_ref,
-    pre_bc_ref,
+    grad_ref,
     state_ref,
-    grad_ref,
+    survive_ref,
+    shape_ref,
+    prob_ref,
+    gated_ref,
+    opened_ref,
+    slope_z_ref,
+    inner_ref,
+    carried_ref,
+    x_conv_ref,
+    slope_x_ref,
+    dt_ref,
+    from_start_ref,
+    to_end_ref,
+    weighted_ref,
+    weighted_end_ref,
+    bc_ref,
+    slope_bc_ref,
+    decay_ref,
+    slope_dt_ref,
     proj_ref,
     part_ref,
     out_ref,
@@ -302,7 +354,7 @@
         sum_gain_ref[...] = jnp.zeros(sum_gain_ref.shape, F32)
 
     window = window_ref[pl.ds(pl.multiple_of(step * Q, Q), Q + 2 * HALO), :]
-    seg, from_prev, same_last, passes, bias = block_masks(window, seg_row_ref[0:1, :])
+    seg = window[HALO : HALO + Q]
     live = (seg[:, 0:1] > 0).astype(F32)
     stat = stat_ref[...].T
     gate_inverse = lax.rsqrt(stat[:, 0:1] / full_inner + EPS)
@@ -310,55 +362,29 @@
 
     gain = channel_ref[0:1, :]
     skip = channel_ref[1:2, :]
-    z_proj = z_ref[...]
-    mixed = mixed_ref[...]
     grad_out = grad_ref[...]
-    gate = sigmoid(z_proj)
-    opened = z_proj * gate
-    gated = mixed * opened
+    gated = gated_ref[...]
     normal = gated * gate_inverse
     sum_gate = jnp.sum(grad_out * normal, axis=0, keepdims=True)
     out_ref[...] = (normal * gain * live).astype(BF16)
     grad_gated = grad_out * gain * gate_inverse - gated * along
-    grad_z = grad_gated * mixed * (gate * (1.0 + z_proj * (1.0 - gate)))
-    dy = grad_gated * opened
-
-    pre = pre_ref[...]
-    gate_x = sigmoid(pre)
-    x_conv = pre * gate_x
-    pre_bc = pre_bc_ref[...]
-    gate_bc = sigmoid(pre_bc)
-    bc_conv = (pre_bc * gate_bc).astype(BF16)
+    grad_z = (grad_gated * slope_z_ref[...]).astype(BF16)
+    dy = grad_gated * opened_ref[...]
+    dy_low = dy.astype(BF16)
+    dy_start = (dy * from_start_ref[...]).astype(BF16)
+
+    bc_conv = bc_ref[...]
     b_in = bc_conv[:, :N]
     c_in = bc_conv[:, N:]
-    bcdt = bcdt_ref[...]
-    raw = bcdt[:, 2 * N :] + head_ref[0:1, :]
-    dt = softplus(raw)
-    rate = jnp.exp(head_ref[1:2, :])
-    decay = -dt * rate
-    total = dot_exact(triangle(True).astype(F32), decay)
-    total_t = total.T
-    dt_wide = spread(dt, heads, size)
-    weighted = x_conv * dt_wide
-    scores = dot_nt(c_in, b_in)
     before = state_ref[0]
     before_low = before.astype(BF16)
-    last = total[Q - 1 : Q, :]
-    to_end = spread(jnp.exp(last - total) * same_last, heads, size)
-    from_start = spread(jnp.exp(total) * from_prev, heads, size)
-    after = carry[...]
-    after_low = after.astype(BF16)
-
-    dy_low = dy.astype(BF16)
-    weighted_low = weighted.astype(BF16)
-    dy_start = (dy * from_start).astype(BF16)
+    after_low = carry[...].astype(BF16)
+    weighted_low = weighted_ref[...]
+    weighted_end = weighted_end_ref[...]
     grad_c = dot_nt(dy_start, before_low)
-    carried = dot(c_in, before_low)
     returned = dot(b_in, after_low)
-    grad_weighted = to_end * returned
-    weighted_end = (weighted * to_end).astype(BF16)
     grad_b = dot_nt(weighted_end, after_low)
-    new_after = dot_tn(c_in, dy_start) + after * spread(jnp.exp(last) * passes, heads, size)
+    new_after = dot_tn(c_in, dy_start) + carry[...] * survive_ref[0, 0:1, :]
     carry[...] = new_after
 
     per = LANES // size
@@ -373,22 +399,22 @@
         summed = jnp.zeros((Q, LANES), F32)
         for extra in range(per):
             h = first + extra
-            shape = jnp.exp(total[:, h : h + 1] - total_t[h : h + 1, :] + bias)
             mine = (lane >= extra * size) & (lane < (extra + 1) * size)
             dy_mine = jnp.where(mine, dy_group, none)
+            shape = shape_ref[:, h * Q : (h + 1) * Q].astype(F32)
             grad_scores = grad_scores + dot_nt(dy_mine, weighted_group) * shape
-            summed = summed + dot_tn((scores * shape).astype(BF16), dy_mine)
+            summed = summed + dot_tn(prob_ref[:, h * Q : (h + 1) * Q], dy_mine)
         inner.append(summed)
     grad_inner = jnp.concatenate(inner, axis=1)
-    grad_weighted = grad_weighted + grad_inner
+    grad_weighted = to_end_ref[...] * returned + grad_inner
     grad_scores = grad_scores.astype(BF16)
     grad_c = grad_c + dot(grad_scores, b_in)
     grad_b = grad_b + dot_tn(grad_scores, c_in)
 
-    scanned = mixed - skip * x_conv - carried * from_start
+    x_conv = x_conv_ref[...]
     pairs = head_sums(
-        dy_low.astype(F32) * scanned
-        + dy_start.astype(F32) * carried
+        dy_low.astype(F32) * inner_ref[...]
+        + dy_start.astype(F32) * carried_ref[...]
         - weighted_low.astype(F32) * grad_inner
         - weighted_end.astype(F32) * returned,
         heads,
@@ -396,16 +422,15 @@
     )
     grad_decay = dot_exact(triangle(False).astype(F32), pairs) + tail[0:1, :]
     kept = jnp.sum(new_after.astype(BF16).astype(F32) * before, axis=0, keepdims=True)
-    kept = jnp.broadcast_to(kept, (8, width))
-    tail[...] = head_sums(kept, heads, size)
+    tail[...] = head_sums(jnp.broadcast_to(kept, (8, width)), heads, size)
+    rate = jnp.exp(head_ref[1:2, :])
     grad_dt = head_sums(grad_weighted * x_conv, heads, size) - grad_decay * rate
-    grad_raw = grad_dt * sigmoid(raw)
+    grad_raw = grad_dt * slope_dt_ref[...]
     sum_head_ref[0:1, :] += jnp.sum(grad_raw, axis=0, keepdims=True)
-    sum_head_ref[1:2, :] += jnp.sum(grad_decay * decay, axis=0, keepdims=True)
-
-    grad_x = grad_weighted * dt_wide + skip * dy
+    sum_head_ref[1:2, :] += jnp.sum(grad_decay * decay_ref[...], axis=0, keepdims=True)
+
     sum_skip = jnp.sum(dy * x_conv, axis=0, keepdims=True)
-    grad_pre = grad_x * (gate_x * (1.0 + pre * (1.0 - gate_x)))
+    grad_pre = (grad_weighted * dt_ref[...] + skip * dy) * slope_x_ref[...]
     x_buffer[Q : Q + HALO, :] = x_buffer[0:HALO, :]
     x_buffer[0:Q, :] = grad_pre
     grad_proj, taps = conv_backward(
@@ -417,13 +442,11 @@
         [taps[3], taps[2], taps[1], taps[0], sum_bias, sum_gate, sum_skip, blank], axis=0
     )
 
-    grad_pre_bc = jnp.concatenate([grad_b, grad_c], axis=1) * (
-        gate_bc * (1.0 + pre_bc * (1.0 - gate_bc))
-    )
+    grad_pre_bc = jnp.concatenate([grad_b, grad_c], axis=1) * slope_bc_ref[...]
     bc_buffer[Q : Q + HALO, :] = bc_buffer[0:HALO, :]
     bc_buffer[0:Q, :] = grad_pre_bc
     grad_bc, taps_bc = conv_backward(
-        bc_buffer, window, seg, kernel_bc_ref[...], bcdt[:, : 2 * N], 2 * N
+        bc_buffer, window, seg, kernel_bc_ref[...], bcdt_ref[:, : 2 * N], 2 * N
     )
     sum_bias_bc = jnp.sum(grad_pre_bc, axis=0, keepdims=True)
     blank_bc = jnp.zeros((3, 2 * N), F32)
@@ -432,13 +455,7 @@
     )
 
     grads = jnp.concatenate(
-        [
-            grad_proj.astype(BF16),
-            grad_z.astype(BF16),
-            grad_bc.astype(BF16),
-            grad_raw.astype(BF16),
-        ],
-        axis=1,
+        [grad_proj.astype(BF16), grad_z, grad_bc.astype(BF16), grad_raw.astype(BF16)], axis=1
     )
     proj_ref[...] = grads
     part = dot_nt(grads, weights_ref[:, width:])
@@ -446,6 +463,29 @@
     hidden = hidden_ref[...].astype(F32)
     inverse = lax.rsqrt(jnp.mean(hidden * hidden, axis=1, keepdims=True) + EPS)
     sum_gain_ref[0:1, :] += jnp.sum(part * (hidden * inverse), axis=0, keepdims=True)
+
+
+def pack_kernel(heads, out_ref_in, x_ref, z_ref, bc_ref, dt_ref, gain_ref, packed_ref):
+    width = x_ref.shape[1]
+    at = 0
+    for ref in (out_ref_in, x_ref, z_ref, bc_ref):
+        packed_ref[:, at : at + ref.shape[1]] = ref[...]
+        at += ref.shape[1]
+    rows = x_ref.shape[0]
+    packed_ref[:, at:] = jnp.concatenate(
+        [dt_ref[...], gain_ref[...], jnp.zeros((rows, LANES - heads - 1), BF16)], axis=1
+    )
+
+
+def run_pack(heads, *parts):
+    rows = parts[0].shape[0]
+    columns = sum(part.shape[1] for part in parts[:4]) + LANES
+    return pl.pallas_call(
+        functools.partial(pack_kernel, heads),
+        out_shape=jax.ShapeDtypeStruct((rows, columns), BF16),
+        compiler_params=pltpu.CompilerParams(vmem_limit_bytes=VMEM_LIMIT),
+        name="pack",
+    )(*parts)
 
 
 def cost(micros):
@@ -497,6 +537,27 @@
         cost_estimate=cost(8),
         name="project",
     )(place, *near, weights)
+
+
+def saved_rows(heads, size):
+    width = heads * size
+    return (
+        [(heads * Q, BF16)] * 2
+        + [(width, F32)] * 10
+        + [(width, BF16)] * 2
+        + [(2 * N, BF16), (2 * N, F32), (LANES, F32), (LANES, F32)]
+    )
+
+
+def saved_specs(heads, size, place):
+    width = heads * size
+    return [
+        pl.BlockSpec((1, N, width), lambda i: (place(i), 0, 0)),
+        pl.BlockSpec((1, 8, width), lambda i: (place(i), 0, 0)),
+    ] + [
+        pl.BlockSpec((Q, columns), lambda i: (place(i), 0))
+        for columns, _ in saved_rows(heads, size)
+    ]
 
 
 def run_forward(
@@ -528,23 +589,15 @@
             rows(width),
             rows(bcdt.shape[1]),
         ],
-        out_specs=[
-            rows(width),
-            rows(width),
-            rows(2 * N),
-            pl.BlockSpec((1, N, width), lambda i: (i, 0, 0)),
-            rows(width),
-            rows(features),
-            across,
-        ],
+        out_specs=[rows(width), rows(features), across, *saved_specs(heads, size, lambda i: i)],
         out_shape=[
-            made(width, F32),
-            made(width, F32),
-            made(2 * N, F32),
-            jax.ShapeDtypeStruct((blocks, N, width), F32),
             made(width, BF16),
             made(features, BF16),
             jax.ShapeDtypeStruct((8, length), F32),
+            *[
+                jax.ShapeDtypeStruct((blocks,) + shape, F32) for shape in ((N, width), (8, width))
+            ],
+            *[made(columns, dtype) for columns, dtype in saved_rows(heads, size)],
         ],
         scratch_shapes=[
             pltpu.VMEM((Q + HALO, width), F32),
@@ -615,8 +668,8 @@
 
 
 def run_backward(
-    heads, size, full_inner, stat, hidden, window, seg_row, weights, kernel_x, kernel_bc, head, channel,
-    z_proj, mixed, x_proj, pre, bcdt, pre_bc, states, grad_out,
+    heads, size, full_inner, stat, hidden, window, weights, kernel_x, kernel_bc, head, channel,
+    x_proj, bcdt, grad_out, saved,
 ):
     length, features = hidden.shape
     width = heads * size
@@ -639,23 +692,17 @@
             across,
             rows(features),
             whole(window.shape),
-            across,
             whole(weights.shape),
             whole(kernel_x.shape),
             whole(kernel_bc.shape),
             whole(head.shape),
             whole(channel.shape),
             rows(width),
+            rows(rest),
             rows(width),
-            rows(width),
-            rows(width),
-            rows(rest),
-            rows(2 * N),
-            pl.BlockSpec((1, N, width), lambda i: (blocks - 1 - i, 0, 0)),
-            rows(width),
-        ],
-        out_specs=[rows(total), rows(features), rows(width)]
-        + [whole(shape) for shape in sums],
+            *saved_specs(heads, size, lambda i: blocks - 1 - i),
+        ],
+        out_specs=[rows(total), rows(features), rows(width)] + [whole(shape) for shape in sums],
         out_shape=[made(total, BF16), made(features, BF16), made(width, BF16)]
         + [jax.ShapeDtypeStruct(shape, F32) for shape in sums],
         scratch_shapes=[
@@ -665,11 +712,11 @@
             pltpu.VMEM((8, LANES), F32),
         ],
         compiler_params=pltpu.CompilerParams(vmem_limit_bytes=VMEM_LIMIT),
-        cost_estimate=cost(2),
+        cost_estimate=cost(27),
         name="backward",
     )(
-        stat, hidden, window, seg_row, weights, kernel_x, kernel_bc, head, channel,
-        z_proj, mixed, x_proj, pre, bcdt, pre_bc, states, grad_out,
+        stat, hidden, window, weights, kernel_x, kernel_bc, head, channel, x_proj, bcdt, grad_out,
+        *saved,
     )
 
 
@@ -808,10 +855,7 @@
     features = hidden.shape[2]
     hidden_local = hidden[0]
 
-    steps = jnp.pad(
-        jnp.concatenate([w_in_dt, norm_gain[:, None]], axis=1), ((0, 0), (0, LANES - heads - 1))
-    )
-    packed = jnp.concatenate([w_out, w_in_x, w_in_z, w_in_bc, steps], axis=1)
+    packed = run_pack(heads, w_out, w_in_x, w_in_z, w_in_bc, w_in_dt, norm_gain[:, None])
     n = lax.axis_size("tensor")
     axis_place = lax.axis_index("tensor")
     place = axis_place[None]
@@ -842,7 +886,7 @@
     bcdt = after(bcdt, right, left)
     right, left = line_step(after(right, gain), after(left, gain), 2, "tensor")
     moved.append((right, left))
-    mixed, pre, pre_bc, states, scaled, out_part, square = run_forward(
+    scaled, out_part, square, *saved = run_forward(
         heads, size, window, seg_row, weights, kernel_x, kernel_bc, head, channel, z_proj, x_proj,
         bcdt,
     )
@@ -852,18 +896,18 @@
     near_cot = line_order(cotangent[0], moved)
     cot_full, grad_out, along = run_gradient(place, near_cot, weights, scaled, window)
     out_sum = lax.psum_scatter(
-        out_part, "tensor", scatter_dimension=0, tiled=True
+        after(out_part, along), "tensor", scatter_dimension=0, tiled=True
     )
     stat = sum_around(jnp.stack([square[0], along[0]]), "tensor")
     stat_full = jnp.pad(stat, ((0, 6), (0, 0)))
     out_scale = lax.rsqrt(stat[0] / full_inner + EPS) * (seg_full > 0).astype(F32)
 
     grads, in_part, normed_out, sum_x, sum_bc, sum_head, sum_gain = run_backward(
-        heads, size, full_inner, stat_full, hidden_full, window, seg_row, weights, kernel_x,
-        kernel_bc, head, channel, z_proj, mixed, x_proj, pre, bcdt, pre_bc, states, grad_out,
+        heads, size, full_inner, stat_full, hidden_full, window, weights, kernel_x, kernel_bc, head,
+        channel, x_proj, bcdt, grad_out, saved,
     )
     in_sum = lax.psum_scatter(in_part, "tensor", scatter_dimension=0, tiled=True)
-    first, second = run_weights(cot_full, normed_out, tokens, after(grads, out_sum))
+    first, second = run_weights(cot_full, normed_out, tokens, grads)
     own = jnp.concatenate([sum_x.reshape(-1, LANES), sum_head])
     both = jnp.concatenate([sum_gain[0].reshape(-1, LANES), sum_bc.reshape(-1, LANES)])
     first, second, small, came = cube_scatter(first, second, jnp.concatenate([own, both]), "dp")

time: 266 us -> 234 us (0.88)
  waiting for transfers between devices: 110 us -> 78 us
    ppermute x6, waiting for transfers between devices: 78.3 us -> 40.6 us  [line_step(): lax.ppermute(left, axis, [(i, i - 1) for i in range(1, n - step + 1)])]
    ppermute x9, waiting for transfers between devices: 2.33 us -> 13.8 us  [around(): lax.ppermute(values, axis, [(i, (i - k) % n) for i in range(n)])]
    ppermute x3, waiting for transfers between devices: 5.53 us -> 0.14 us  [cube_scatter(): moved = other = lax.ppermute(send, axis, pairs)]
    reduce_scatter x1, waiting for transfers between devices: 13 us -> 7.68 us  [shards(): lax.psum_scatter(in_part, 'tensor', scatter_dimension=0, tiled=True)]
    pallas_call x1, Pallas kernels: 13.8 us -> 18 us  [run_forward(): pl.pallas_call(functools.partial(forward_kernel, heads, size), grid=(bloc...]
    ppermute x6, starting transfers between devices: 12.9 us -> 9.18 us  [line_step(): lax.ppermute(right, axis, [(i, i + 1) for i in range(step - 1, n - 1)])]
    pallas_call x1, Pallas kernels: 27.4 us -> 24.5 us  [run_backward(): pl.pallas_call(functools.partial(backward_kernel, heads, size, full_inner...]
    ppermute x3, waiting for transfers between devices: 10.6 us -> 13.4 us  [cube_scatter(): lax.ppermute(jnp.concatenate([send.reshape(rows, columns), rider]), axis,...]
  transfers between devices with their start and end apart: 30 -> 30, of which waited for: 13 -> 16; matrix products, arithmetic and copies ran while one was open for 8% -> 10% of each run, Pallas kernels for 16% -> 26%
where the time goes in v7:
time: 234 us; the launch traced here: 231 us
  waiting for transfers between devices  78 us (33%)
  Pallas kernels  67.3 us (29%)
  starting transfers between devices  37.8 us (16%)
  local copies, waits for them, and re-layouts  24.8 us (11%)
  between operations  14.3 us (6%)
  other arithmetic  9.1 us (4%)
    ppermute x6, waiting for transfers between devices, line_step(): lax.ppermute(left, axis, [(i, i - 1) for i in range(1, n - step + 1)])  40.6 us
    pallas_call x1, Pallas kernels, run_backward(): pl.pallas_call(functools.partial(backward_kernel, heads, size, full_inner...  24.5 us
    pallas_call x1, Pallas kernels, run_forward(): pl.pallas_call(functools.partial(forward_kernel, heads, size), grid=(bloc...  18 us
    ppermute x9, starting transfers between devices, around(): lax.ppermute(values, axis, [(i, (i - k) % n) for i in range(n)])  13.9 us
    ppermute x9, waiting for transfers between devices, around(): lax.ppermute(values, axis, [(i, (i - k) % n) for i in range(n)])  13.8 us
    ppermute x3, waiting for transfers between devices, cube_scatter(): lax.ppermute(jnp.concatenate([send.reshape(rows, columns), rider]), axis,...  13.4 us
    unnamed x47, local copies, waits for them, and re-layouts  12 us
    ppermute x6, starting transfers between devices, line_step(): lax.ppermute(right, axis, [(i, i + 1) for i in range(step - 1, n - 1)])  9.18 us
  transfers between devices with their start and end apart: 30, of which 16 were waited for; matrix products, arithmetic and copies ran while one was open for 10% of the time, Pallas kernels for 26%

profile of v7, /device:TPU:0, one launch (start us, length us, event | category | flops | bytes accessed | tf_op | source)
XLA Modules:
  0.0 231.3 jit_solution(2975274930317288979)
XLA Ops:
  7.2 0.8 copy.38.dt_ref
  8.0 0.8 copy.39.gain_ref
  8.8 0.9 copy-done.3
  9.7 0.9 copy-done.4
  10.6 0.9 copy-done.5
  11.5 0.8 copy-done.6
  12.4 0.9 pack.1
  13.3 5.0 %collective-permute-start.3 = (bf16[256,1024]{1,0:T(8,128)(2,1)}, bf16[256,1024]{1,0:T(8,128)(2,1)S(1)}, u32[]{:S(2)}, u32[]{:S(2)}) collective-permute-start(bf16[256,1024]{1,0:T(8,128)(2,1)} %bitcast.72), channel_id=1, source_target_pairs={{0,1},{1,2},{2,3},{4,5},{5,6},{6,7},{8,9},{9,10},{10,11},{12,13},{... | collective-permute-start | bytes 1572872 | tf_op jit(solution)/shard_map/ppermute | solution.py:757
  18.3 1.3 collective-permute-start.6
  19.6 4.7 %collective-permute-start = (s32[256]{0:T(256)}, s32[256]{0:T(256)S(1)}, u32[]{:S(2)}, u32[]{:S(2)}) collective-permute-start(s32[256]{0:T(256)} %bitcast.94), channel_id=1, source_target_pairs={{0,3},{1,0},{2,1},{3,2},{4,7},{5,4},{6,5},{7,6},{8,11},{9,8},{10,9... | collective-permute-start | bytes 3080 | tf_op jit(solution)/shard_map/ppermute | solution.py:824
  24.3 1.0 collective-permute-start.2
  25.3 0.7 broadcast_in_dim.39
  26.8 0.7 pad_maximum_fusion.5.kernel_bc_ref
  27.5 2.3 collective-permute-done.3.refs_2_
  30.5 3.3 %collective-permute-done.6.refs_4_ = bf16[256,1024]{1,0:T(8,128)(2,1)S(1)} collective-permute-done((bf16[256,1024]{1,0:T(8,128)(2,1)}, bf16[256,1024]{1,0:T(8,128)(2,1)S(1)}, u32[]{:S(2)}, u32[]{:S(2)}) %collective-permute-start.6) | collective-permute-done | bytes 524320 | tf_op jit(solution)/shard_map/ppermute | solution.py:758
  33.8 1.3 collective-permute-start.7
  35.8 0.7 pad_maximum_fusion.4.kernel_x_ref
  37.3 0.7 collective-permute-start.5
  38.0 10.5 %collective-permute-done.7.refs_5_ = bf16[256,1024]{1,0:T(8,128)(2,1)S(1)} collective-permute-done((bf16[256,1024]{1,0:T(8,128)(2,1)S(1)}, bf16[256,1024]{1,0:T(8,128)(2,1)S(1)}, u32[]{:S(2)}, u32[]{:S(2)}) %collective-permute-start.7) | collective-permute-done | bytes 524320 | tf_op jit(solution)/shard_map/ppermute | solution.py:758
  48.4 1.3 collective-permute-start.8
  50.6 11.6 %collective-permute-done.8.refs_6_ = bf16[256,1024]{1,0:T(8,128)(2,1)S(1)} collective-permute-done((bf16[256,1024]{1,0:T(8,128)(2,1)S(1)}, bf16[256,1024]{1,0:T(8,128)(2,1)S(1)}, u32[]{:S(2)}, u32[]{:S(2)}) %collective-permute-start.8) | collective-permute-done | bytes 524320 | tf_op jit(solution)/shard_map/ppermute | solution.py:758
  62.2 0.8 copy-done.17
  63.0 1.5 collective-permute-start.9
  64.5 1.3 collective-permute-start.10
  65.9 8.4 %project.1 = (bf16[1024,1024]{1,0:T(8,128)(2,1)}, bf16[1024,1024]{1,0:T(8,128)(2,1)}, f32[1024,512]{1,0:T(8,128)}, f32[1024,512]{1,0:T(8,128)}, f32[1024,384]{1,0:T(8,128)}, /*index=5*/f32[8,1024]{1,0:T(8,128)S(1)}) custom-call(s32[1]{0:T(128)} %bitcast.8.place_ref, bf16[256,1024]{1,0:T(8,128)(2,1)S(1)} %collective-permute-done.5.refs_0_, ...), custom_call_target="tpu_custom_call" | custom-call | flops 8000000000 | bytes 1048576 | tf_op jit(solution)/shard_map/project/pallas_call | solution.py:516
  74.3 3.3 %collective-permute-done.10.refs_4_ = bf16[256,1024]{1,0:T(8,128)(2,1)} collective-permute-done((bf16[256,1024]{1,0:T(8,128)(2,1)}, bf16[256,1024]{1,0:T(8,128)(2,1)}, u32[]{:S(2)}, u32[]{:S(2)}) %collective-permute-start.10) | collective-permute-done | bytes 524320 | tf_op jit(solution)/shard_map/ppermute | solution.py:758
  78.3 1.3 collective-permute-start.13
  79.6 1.0 broadcast_in_dim.34.window_ref.refs_9_
  80.6 18.0 %forward.1 = (bf16[1024,512]{1,0:T(8,128)(2,1)}, bf16[1024,1024]{1,0:T(8,128)(2,1)}, f32[8,1024]{1,0:T(8,128)S(1)}, f32[4,128,512]{2,1,0:T(8,128)}, f32[4,8,512]...) custom-call(s32[1040,128]{1,0:T(8,128)} %broadcast_in_dim.34.window_, ...), custom_call_target="tpu_custom_call" | custom-call | flops 14000000000 | bytes 1048576 | tf_op jit(solution)/shard_map/forward/pallas_call | solution.py:577
  98.6 0.8 copy-done.8
  100.1 1.3 collective-permute-start.14
  101.4 11.9 %collective-permute-done.14.refs_6_ = bf16[256,1024]{1,0:T(8,128)(2,1)S(1)} collective-permute-done((bf16[256,1024]{1,0:T(8,128)(2,1)S(1)}, bf16[256,1024]{1,0:T(8,128)(2,1)S(1)}, u32[]{:S(2)}, u32[]{:S(2)}) %collective-permute-start.14) | collective-permute-done | bytes 524320 | tf_op jit(solution)/shard_map/ppermute | solution.py:758
  113.4 0.8 copy-done.18
  114.1 6.0 %out_gradient.1 = (bf16[1024,1024]{1,0:T(8,128)(2,1)}, f32[1024,512]{1,0:T(8,128)}, f32[8,1024]{1,0:T(8,128)S(1)}) custom-call(s32[1]{0:T(128)} %bitcast.8.place_ref, bf16[256,1024]{1,0:T(8,128)(2,1)S(1)} %collective-permute-done.12.refs_0_, bf16[256,1024]{1,0:T(8,128)(2,1)S(1)} %collective-permute-done.11.refs_1_, ...), custom_call_target="tpu_custom_call" | custom-call | flops 5000000000 | bytes 1048576 | tf_op jit(solution)/shard_map/out_gradient/pallas_call | solution.py:616
  120.2 2.5 %collective-permute-start.16 = (f32[2,1024]{1,0:T(2,128)S(1)}, f32[2,1024]{1,0:T(2,128)S(1)}, u32[]{:S(2)}, u32[]{:S(2)}) collective-permute-start(f32[2,1024]{1,0:T(2,128)S(1)} %pad_maximum_fusion.6), channel_id=1, source_target_pairs={{0,2},{1,3},{2,0},{3,1},{4,6},{5,7},{6,4},{7,5},{8,10},{9,11},{10,... | collective-permute-start | bytes 24584 | tf_op jit(solution)/shard_map/ppermute | solution.py:824
  122.8 1.3 collective-permute-start.15
  124.3 1.4 collective-permute-done.17
  125.7 0.7 collective-permute-done.15
  126.5 24.5 %backward.1 = (bf16[1024,1408]{1,0:T(8,128)(2,1)}, bf16[1024,1024]{1,0:T(8,128)(2,1)}, bf16[1024,512]{1,0:T(8,128)(2,1)}, f32[8,512]{1,0:T(8,128)S(1)}, f32[8,25...) custom-call(f32[8,1024]{1,0:T(8,128)S(1)} %pad.24.stat_ref, ...), custom_call_target="tpu_custom_call" | custom-call | flops 27000000512 | bytes 1048576 | tf_op jit(solution)/shard_map/backward/pallas_call | solution.py:688
  151.1 1.2 copy-done.7
  152.3 8.3 %weight_gradients.1 = (bf16[1024,896]{1,0:T(8,128)(2,1)}, bf16[1024,1024]{1,0:T(8,128)(2,1)}) custom-call(bf16[1024,1024]{1,0:T(8,128)(2,1)} %get-tuple-element.103.cot_ref, bf16[1024,512]{1,0:T(8,128)(2,1)S(1)} %copy-done.7, bf16[1024,1024]{1,0:T(8,128)(2,1)} %get-tuple-element.105.tokens_ref, bf16[1024,1408]{1,0:T(8,128)(2,1)} %get-tuple-element.106.grads_ref), custom_call_target="tpu_custom_call" | custom-call | flops 7000000000 | bytes 1048576 | tf_op jit(solution)/shard_map/weight_gradients/pallas_call | solution.py:653
  160.6 1.4 constant_dynamic-slice_fusion.1
  162.0 1.0 pad_maximum_fusion
  163.0 1.0 dynamic-slice_bitcast_fusion
  164.6 1.1 collective-permute-done.21
  166.4 1.6 collective-permute-start.22
  168.1 1.6 fusion
  169.8 1.6 collective-permute-start.19
  171.4 8.2 %collective-permute-done.22 = bf16[272,896]{1,0:T(8,128)(2,1)S(1)} collective-permute-done((bf16[272,896]{1,0:T(8,128)(2,1)S(1)}, bf16[272,896]{1,0:T(8,128)(2,1)S(1)}, u32[]{:S(2)}, u32[]{:S(2)}) %collective-permute-start.22) | collective-permute-done | bytes 487456 | tf_op jit(solution)/shard_map/ppermute | solution.py:806
  179.6 0.8 copy-done.13
  180.5 1.1 slice.157
  181.8 1.6 collective-permute-start.23
  183.7 1.4 collective-permute-start.20
  185.1 4.1 %collective-permute-done.23 = bf16[144,896]{1,0:T(8,128)(2,1)S(1)} collective-permute-done((bf16[144,896]{1,0:T(8,128)(2,1)S(1)}, bf16[144,896]{1,0:T(8,128)(2,1)S(1)}, u32[]{:S(2)}, u32[]{:S(2)}) %collective-permute-start.23) | collective-permute-done | bytes 258080 | tf_op jit(solution)/shard_map/ppermute | solution.py:806
  189.5 1.9 collective-permute-start.26
  191.4 1.9 collective-permute-start.25
  194.4 0.7 slice.176
  197.7 0.8 fusion.9
  198.5 2.7 %collective-permute-done.26 = f32[280,128]{1,0:T(8,128)S(1)} collective-permute-done((f32[280,128]{1,0:T(8,128)S(1)}, f32[280,128]{1,0:T(8,128)S(1)}, u32[]{:S(2)}, u32[]{:S(2)}) %collective-permute-start.26) | collective-permute-done | bytes 143392 | tf_op jit(solution)/shard_map/ppermute | solution.py:824
  201.2 8.8 %collective-permute-done.25 = f32[280,128]{1,0:T(8,128)S(1)} collective-permute-done((f32[280,128]{1,0:T(8,128)S(1)}, f32[280,128]{1,0:T(8,128)S(1)}, u32[]{:S(2)}, u32[]{:S(2)}) %collective-permute-start.25) | collective-permute-done | bytes 143392 | tf_op jit(solution)/shard_map/ppermute | solution.py:824
  212.8 2.1 fusion.4
  214.8 7.7 %reduce-scatter.5.cloned.1.call-done.sum_ref = bf16[256,1024]{1,0:T(8,128)(2,1)} async-done(((bf16[1024,1024]{1,0:T(8,128)(2,1)}), bf16[256,1024]{1,0:T(8,128)(2,1)}) %reduce-scatter.5.cloned.1.call-update) | async-done | bytes 524304 | tf_op jit(solution)/shard_map/reduce_scatter | solution.py:909
  222.5 1.0 copy-done.2
  223.5 1.3 finish.1
  (131 shorter events, 14.3 us)
Async XLA Ops:
  7.2 58.7 %all-gather.2.cloned.1.call-start = ((), (), s32[]{:S(2)}) async-start(), calls=%async_computation.2 | async-start | bytes 4423680 | tf_op jit(solution)/shard_map/all_gather | solution.py:863
  8.8 0.9 copy-start.3
  9.7 0.9 copy-start.4
  10.6 0.9 copy-start.5
  11.5 0.8 copy-start.6
  13.3 199.5 %reduce-scatter.3.cloned.1.call-start = ((), (), s32[]{:S(2)}) async-start(), calls=%async_computation.3 | async-start | bytes 2621440 | tf_op jit(solution)/shard_map/reduce_scatter | solution.py:898
  13.3 16.5 %collective-permute-start.3 = (bf16[256,1024]{1,0:T(8,128)(2,1)}, bf16[256,1024]{1,0:T(8,128)(2,1)S(1)}, u32[]{:S(2)}, u32[]{:S(2)}) collective-permute-start(bf16[256,1024]{1,0:T(8,128)(2,1)} %bitcast.72), channel_id=1, source_target_pairs={{0,1},{1,2},{2,3},{4,5},{5,6},{6,7},{8,9},{9,10},{10,11},{12,13},{... | collective-permute-start | bytes 1572872 | tf_op jit(solution)/shard_map/ppermute | solution.py:757
  18.3 15.5 %collective-permute-start.6 = (bf16[256,1024]{1,0:T(8,128)(2,1)}, bf16[256,1024]{1,0:T(8,128)(2,1)S(1)}, u32[]{:S(2)}, u32[]{:S(2)}) collective-permute-start(bf16[256,1024]{1,0:T(8,128)(2,1)} %bitcast.73), channel_id=1, source_target_pairs={{1,0},{2,1},{3,2},{5,4},{6,5},{7,6},{9,8},{10,9},{11,10},{13,12},{... | collective-permute-start | bytes 1572872 | tf_op jit(solution)/shard_map/ppermute | solution.py:758
  19.6 17.6 %collective-permute-start = (s32[256]{0:T(256)}, s32[256]{0:T(256)S(1)}, u32[]{:S(2)}, u32[]{:S(2)}) collective-permute-start(s32[256]{0:T(256)} %bitcast.94), channel_id=1, source_target_pairs={{0,3},{1,0},{2,1},{3,2},{4,7},{5,4},{6,5},{7,6},{8,11},{9,8},{10,9... | collective-permute-start | bytes 3080 | tf_op jit(solution)/shard_map/ppermute | solution.py:824
  24.3 12.9 %collective-permute-start.1 = (s32[256]{0:T(256)}, s32[256]{0:T(256)S(1)}, u32[]{:S(2)}, u32[]{:S(2)}) collective-permute-start(s32[256]{0:T(256)} %bitcast.95), channel_id=1, source_target_pairs={{0,2},{1,3},{2,0},{3,1},{4,6},{5,7},{6,4},{7,5},{8,10},{9,11},{10,... | collective-permute-start | bytes 3080 | tf_op jit(solution)/shard_map/ppermute | solution.py:824
  24.3 25.4 %collective-permute-start.2 = (s32[256]{0:T(256)}, s32[256]{0:T(256)S(1)}, u32[]{:S(2)}, u32[]{:S(2)}) collective-permute-start(s32[256]{0:T(256)} %bitcast.96), channel_id=1, source_target_pairs={{0,1},{1,2},{2,3},{3,0},{4,5},{5,6},{6,7},{7,4},{8,9},{9,10},{10,1... | collective-permute-start | bytes 3080 | tf_op jit(solution)/shard_map/ppermute | solution.py:824
  29.8 7.5 %collective-permute-start.4 = (bf16[256,1024]{1,0:T(8,128)(2,1)S(1)}, bf16[256,1024]{1,0:T(8,128)(2,1)S(1)}, u32[]{:S(2)}, u32[]{:S(2)}) collective-permute-start(bf16[256,1024]{1,0:T(8,128)(2,1)S(1)} %collective-permute-done.3.refs_2_), channel_id=1, source_target_pairs={{1,2},{2,3},{5,6},{6,7},{9,10},{10,11},{13,14},{14,15},{17,18},{18... | collective-permute-start | bytes 1572872 | tf_op jit(solution)/shard_map/ppermute | solution.py:757
  33.8 32.0 %copy-start.14 = (bf16[256,1024]{1,0:T(8,128)(2,1)}, bf16[256,1024]{1,0:T(8,128)(2,1)S(1)}, u32[]{:S(2)}) copy-start(bf16[256,1024]{1,0:T(8,128)(2,1)S(1)} %collective-permute-done.6.refs_4_) | copy-start | bytes 1572868
  33.8 14.6 %collective-permute-start.7 = (bf16[256,1024]{1,0:T(8,128)(2,1)S(1)}, bf16[256,1024]{1,0:T(8,128)(2,1)S(1)}, u32[]{:S(2)}, u32[]{:S(2)}) collective-permute-start(bf16[256,1024]{1,0:T(8,128)(2,1)S(1)} %collective-permute-done.6.refs_4_), channel_id=1, source_target_pairs={{1,0},{2,1},{5,4},{6,5},{9,8},{10,9},{13,12},{14,13},{17,16},{18,1... | collective-permute-start | bytes 1572872 | tf_op jit(solution)/shard_map/ppermute | solution.py:758
  37.3 13.4 %collective-permute-start.5 = (bf16[256,1024]{1,0:T(8,128)(2,1)S(1)}, bf16[256,1024]{1,0:T(8,128)(2,1)S(1)}, u32[]{:S(2)}, u32[]{:S(2)}) collective-permute-start(bf16[256,1024]{1,0:T(8,128)(2,1)S(1)} %collective-permute-done.4.refs_1_), channel_id=1, source_target_pairs={{2,3},{6,7},{10,11},{14,15},{18,19},{22,23},{26,27},{30,31}} | collective-permute-start | bytes 1572872 | tf_op jit(solution)/shard_map/ppermute | solution.py:757
  48.4 13.8 %copy-start.15 = (bf16[256,1024]{1,0:T(8,128)(2,1)}, bf16[256,1024]{1,0:T(8,128)(2,1)S(1)}, u32[]{:S(2)}) copy-start(bf16[256,1024]{1,0:T(8,128)(2,1)S(1)} %collective-permute-done.7.refs_5_) | copy-start | bytes 1572868
  48.4 13.8 %collective-permute-start.8 = (bf16[256,1024]{1,0:T(8,128)(2,1)S(1)}, bf16[256,1024]{1,0:T(8,128)(2,1)S(1)}, u32[]{:S(2)}, u32[]{:S(2)}) collective-permute-start(bf16[256,1024]{1,0:T(8,128)(2,1)S(1)} %collective-permute-done.7.refs_5_), channel_id=1, source_target_pairs={{1,0},{5,4},{9,8},{13,12},{17,16},{21,20},{25,24},{29,28}} | collective-permute-start | bytes 1572872 | tf_op jit(solution)/shard_map/ppermute | solution.py:758
  62.2 0.8 copy-start.17
  63.0 11.2 %collective-permute-start.9 = (bf16[256,1024]{1,0:T(8,128)(2,1)}, bf16[256,1024]{1,0:T(8,128)(2,1)S(1)}, u32[]{:S(2)}, u32[]{:S(2)}) collective-permute-start(bf16[256,1024]{1,0:T(8,128)(2,1)} %bitcast.76), channel_id=1, source_target_pairs={{0,1},{1,2},{2,3},{4,5},{5,6},{6,7},{8,9},{9,10},{10,11},{12,13},{... | collective-permute-start | bytes 1572872 | tf_op jit(solution)/shard_map/ppermute | solution.py:757
  64.5 13.0 %collective-permute-start.10 = (bf16[256,1024]{1,0:T(8,128)(2,1)}, bf16[256,1024]{1,0:T(8,128)(2,1)}, u32[]{:S(2)}, u32[]{:S(2)}) collective-permute-start(bf16[256,1024]{1,0:T(8,128)(2,1)} %bitcast.77), channel_id=1, source_target_pairs={{1,0},{2,1},{3,2},{5,4},{6,5},{7,6},{9,8},{10,9},{11,10},{13,12},{... | collective-permute-start | bytes 1572872 | tf_op jit(solution)/shard_map/ppermute | solution.py:758
  77.6 21.8 %collective-permute-start.11 = (bf16[256,1024]{1,0:T(8,128)(2,1)S(1)}, bf16[256,1024]{1,0:T(8,128)(2,1)S(1)}, u32[]{:S(2)}, u32[]{:S(2)}) collective-permute-start(bf16[256,1024]{1,0:T(8,128)(2,1)S(1)} %collective-permute-done.9.refs_2_), channel_id=1, source_target_pairs={{1,2},{2,3},{5,6},{6,7},{9,10},{10,11},{13,14},{14,15},{17,18},{18... | collective-permute-start | bytes 1572872 | tf_op jit(solution)/shard_map/ppermute | solution.py:757
  78.3 21.8 %collective-permute-start.13 = (bf16[256,1024]{1,0:T(8,128)(2,1)}, bf16[256,1024]{1,0:T(8,128)(2,1)S(1)}, u32[]{:S(2)}, u32[]{:S(2)}) collective-permute-start(bf16[256,1024]{1,0:T(8,128)(2,1)} %collective-permute-done.10.refs_4_), channel_id=1, source_target_pairs={{1,0},{2,1},{5,4},{6,5},{9,8},{10,9},{13,12},{14,13},{17,16},{18,1... | collective-permute-start | bytes 1572872 | tf_op jit(solution)/shard_map/ppermute | solution.py:758
  98.6 0.8 copy-start.8
  99.4 2.0 collective-permute-start.12
  100.1 13.3 %copy-start.16 = (bf16[256,1024]{1,0:T(8,128)(2,1)}, bf16[256,1024]{1,0:T(8,128)(2,1)S(1)}, u32[]{:S(2)}) copy-start(bf16[256,1024]{1,0:T(8,128)(2,1)S(1)} %collective-permute-done.13.refs_5_) | copy-start | bytes 1572868
  100.1 13.3 %collective-permute-start.14 = (bf16[256,1024]{1,0:T(8,128)(2,1)S(1)}, bf16[256,1024]{1,0:T(8,128)(2,1)S(1)}, u32[]{:S(2)}, u32[]{:S(2)}) collective-permute-start(bf16[256,1024]{1,0:T(8,128)(2,1)S(1)} %collective-permute-done.13.refs_5_), channel_id=1, source_target_pairs={{1,0},{5,4},{9,8},{13,12},{17,16},{21,20},{25,24},{29,28}} | collective-permute-start | bytes 1572872 | tf_op jit(solution)/shard_map/ppermute | solution.py:758
  113.4 0.8 copy-start.18
  120.1 6.3 %copy-start.9 = (f32[1024,128]{1,0:T(8,128)S(1)}, f32[1024,128]{1,0:T(8,128)}, u32[]{:S(2)}) copy-start(f32[1024,128]{1,0:T(8,128)} %copy-done.8) | copy-start | bytes 1572868
  120.2 5.5 %collective-permute-start.17 = (f32[2,1024]{1,0:T(2,128)S(1)}, f32[2,1024]{1,0:T(2,128)S(1)}, u32[]{:S(2)}, u32[]{:S(2)}) collective-permute-start(f32[2,1024]{1,0:T(2,128)S(1)} %pad_maximum_fusion.6), channel_id=1, source_target_pairs={{0,1},{1,2},{2,3},{3,0},{4,5},{5,6},{6,7},{7,4},{8,9},{9,10},{10,1... | collective-permute-start | bytes 24584 | tf_op jit(solution)/shard_map/ppermute | solution.py:824
  120.2 5.4 %collective-permute-start.16 = (f32[2,1024]{1,0:T(2,128)S(1)}, f32[2,1024]{1,0:T(2,128)S(1)}, u32[]{:S(2)}, u32[]{:S(2)}) collective-permute-start(f32[2,1024]{1,0:T(2,128)S(1)} %pad_maximum_fusion.6), channel_id=1, source_target_pairs={{0,2},{1,3},{2,0},{3,1},{4,6},{5,7},{6,4},{7,5},{8,10},{9,11},{10,... | collective-permute-start | bytes 24584 | tf_op jit(solution)/shard_map/ppermute | solution.py:824
  122.8 3.7 %collective-permute-start.15 = (f32[2,1024]{1,0:T(2,128)S(1)}, f32[2,1024]{1,0:T(2,128)S(1)}, u32[]{:S(2)}, u32[]{:S(2)}) collective-permute-start(f32[2,1024]{1,0:T(2,128)S(1)} %pad_maximum_fusion.6), channel_id=1, source_target_pairs={{0,3},{1,0},{2,1},{3,2},{4,7},{5,4},{6,5},{7,6},{8,11},{9,8},{10,9... | collective-permute-start | bytes 24584 | tf_op jit(solution)/shard_map/ppermute | solution.py:824
  124.1 98.4 %reduce-scatter.5.cloned.1.call-start = ((), (), s32[]{:S(2)}) async-start(), calls=%async_computation.4 | async-start | bytes 2621440 | tf_op jit(solution)/shard_map/reduce_scatter | solution.py:909
  151.0 1.2 copy-start.7
  160.6 2.4 %copy-start.10 = (bf16[1024,1024]{1,0:T(8,128)(2,1)S(1)}, bf16[1024,1024]{1,0:T(8,128)(2,1)}, u32[]{:S(2)}) copy-start(bf16[1024,1024]{1,0:T(8,128)(2,1)} %get-tuple-element.107) | copy-start | bytes 6291460
  163.0 2.7 %collective-permute-start.21 = (bf16[528,896]{1,0:T(8,128)(2,1)}, bf16[528,896]{1,0:T(8,128)(2,1)S(1)}, u32[]{:S(2)}, u32[]{:S(2)}) collective-permute-start(bf16[528,896]{1,0:T(8,128)(2,1)} %pad_maximum_fusion), channel_id=1, source_target_pairs={{0,4},{4,0},{8,12},{12,8},{16,20},{20,16},{24,28},{28,24},{1,5},{5... | collective-permute-start | bytes 2838536 | tf_op jit(solution)/shard_map/ppermute | solution.py:806
  164.1 4.1 %collective-permute-start.18 = (bf16[2,2,128,1024]{3,2,1,0:T(8,128)(2,1)}, bf16[2,2,128,1024]{3,2,1,0:T(8,128)(2,1)}, u32[]{:S(2)}, u32[]{:S(2)}) collective-permute-start(bf16[2,2,128,1024]{3,2,1,0:T(8,128)(2,1)} %dynamic-slice_bitcast_fusion), channel_id=1, source_target_pairs={{0,4},{4,0},{8,12},{12,8},{16,20},{20,16},{24,28},{28,24},{1,5},{5... | collective-permute-start | bytes 3145736 | tf_op jit(solution)/shard_map/ppermute | solution.py:813
  164.6 1.5 copy-start.12
  166.1 2.0 copy-start.11
  166.4 13.1 %collective-permute-start.22 = (bf16[272,896]{1,0:T(8,128)(2,1)S(1)}, bf16[272,896]{1,0:T(8,128)(2,1)S(1)}, u32[]{:S(2)}, u32[]{:S(2)}) collective-permute-start(bf16[272,896]{1,0:T(8,128)(2,1)S(1)} %pad_maximum_fusion.1), channel_id=1, source_target_pairs={{0,8},{4,12},{8,0},{12,4},{16,24},{20,28},{24,16},{28,20},{1,9},{5... | collective-permute-start | bytes 1462280 | tf_op jit(solution)/shard_map/ppermute | solution.py:806
  169.8 13.7 %collective-permute-start.19 = (bf16[2,128,1024]{2,1,0:T(8,128)(2,1)S(1)}, bf16[2,128,1024]{2,1,0:T(8,128)(2,1)S(1)}, u32[]{:S(2)}, u32[]{:S(2)}) collective-permute-start(bf16[2,128,1024]{2,1,0:T(8,128)(2,1)S(1)} %dynamic-slice_bitcast_fusion.1), channel_id=1, source_target_pairs={{0,16},{4,20},{8,24},{12,28},{16,0},{20,4},{24,8},{28,12},{1,17},{... | collective-permute-start | bytes 1572872 | tf_op jit(solution)/shard_map/ppermute | solution.py:813
  179.6 0.8 copy-start.13
  181.8 7.5 %collective-permute-start.23 = (bf16[144,896]{1,0:T(8,128)(2,1)S(1)}, bf16[144,896]{1,0:T(8,128)(2,1)S(1)}, u32[]{:S(2)}, u32[]{:S(2)}) collective-permute-start(bf16[144,896]{1,0:T(8,128)(2,1)S(1)} %pad_maximum_fusion.2), channel_id=1, source_target_pairs={{0,16},{4,20},{8,24},{12,28},{16,0},{20,4},{24,8},{28,12},{1,17},{... | collective-permute-start | bytes 774152 | tf_op jit(solution)/shard_map/ppermute | solution.py:806
  183.7 13.9 %collective-permute-start.20 = (bf16[128,1024]{1,0:T(8,128)(2,1)S(1)}, bf16[128,1024]{1,0:T(8,128)(2,1)S(1)}, u32[]{:S(2)}, u32[]{:S(2)}) collective-permute-start(bf16[128,1024]{1,0:T(8,128)(2,1)S(1)} %dynamic-slice_bitcast_fusion.2), channel_id=1, source_target_pairs={{0,8},{4,12},{8,0},{12,4},{16,24},{20,28},{24,16},{28,20},{1,9},{5... | collective-permute-start | bytes 786440 | tf_op jit(solution)/shard_map/ppermute | solution.py:813
  189.5 23.3 %copy-start = (bf16[1,256,1024]{2,1,0:T(8,128)(2,1)S(1)}, bf16[1,256,1024]{2,1,0:T(8,128)(2,1)}, u32[]{:S(2)}) copy-start(bf16[1,256,1024]{2,1,0:T(8,128)(2,1)} %param.17) | copy-start | bytes 1572868
  189.5 11.8 %collective-permute-start.26 = (f32[280,128]{1,0:T(8,128)S(1)}, f32[280,128]{1,0:T(8,128)S(1)}, u32[]{:S(2)}, u32[]{:S(2)}) collective-permute-start(f32[280,128]{1,0:T(8,128)S(1)} %pad_maximum_fusion.3), channel_id=1, source_target_pairs={{0,1},{1,2},{2,3},{3,0},{4,5},{5,6},{6,7},{7,4},{8,9},{9,10},{10,1... | collective-permute-start | bytes 430088 | tf_op jit(solution)/shard_map/ppermute | solution.py:824
  191.4 18.7 %collective-permute-start.25 = (f32[280,128]{1,0:T(8,128)S(1)}, f32[280,128]{1,0:T(8,128)S(1)}, u32[]{:S(2)}, u32[]{:S(2)}) collective-permute-start(f32[280,128]{1,0:T(8,128)S(1)} %pad_maximum_fusion.3), channel_id=1, source_target_pairs={{0,2},{1,3},{2,0},{3,1},{4,6},{5,7},{6,4},{7,5},{8,10},{9,11},{10,... | collective-permute-start | bytes 430088 | tf_op jit(solution)/shard_map/ppermute | solution.py:824
  193.2 17.0 %collective-permute-start.24 = (f32[280,128]{1,0:T(8,128)S(1)}, f32[280,128]{1,0:T(8,128)S(1)}, u32[]{:S(2)}, u32[]{:S(2)}) collective-permute-start(f32[280,128]{1,0:T(8,128)S(1)} %pad_maximum_fusion.3), channel_id=1, source_target_pairs={{0,3},{1,0},{2,1},{3,2},{4,7},{5,4},{6,5},{7,6},{8,11},{9,8},{10,9... | collective-permute-start | bytes 430088 | tf_op jit(solution)/shard_map/ppermute | solution.py:824
  197.7 24.8 %copy-start.1 = (bf16[1,256,1024]{2,1,0:T(8,128)(2,1)S(1)}, bf16[1,256,1024]{2,1,0:T(8,128)(2,1)}, u32[]{:S(2)}) copy-start(bf16[1,256,1024]{2,1,0:T(8,128)(2,1)} %param.19) | copy-start | bytes 1572868
  222.5 1.0 copy-start.2
Sparse Core Ops, SparseCore 0:
  13.4 38.3 all-gather.1
  124.2 43.5 reduce-scatter.2
  170.2 52.2 reduce-scatter.4

commit v8 on v7

--- a/solution.py
+++ b/solution.py
@@ -279,11 +279,8 @@
     square_ref[...] = as_row(jnp.sum(gated * gated, axis=1, keepdims=True))
 
 
-def gradient_kernel(width, near, place_ref, *refs):
-    near_refs, refs = refs[:near], refs[near:]
-    weights_ref, scaled_ref, window_ref, cot_ref, grad_ref, along_ref = refs
+def gradient_kernel(width, cot_ref, weights_ref, scaled_ref, window_ref, grad_ref, along_ref):
     step = pl.program_id(0)
-    pick_block(place_ref[0], near_refs, cot_ref)
     window = window_ref[pl.ds(pl.multiple_of(step * Q, Q), Q + 2 * HALO), :]
     live = (window[HALO : HALO + Q] > 0).astype(F32)
     grad = dot(cot_ref[...], weights_ref[...]) * widen(live, width)
@@ -465,24 +462,31 @@
     sum_gain_ref[0:1, :] += jnp.sum(part * (hidden * inverse), axis=0, keepdims=True)
 
 
-def pack_kernel(heads, out_ref_in, x_ref, z_ref, bc_ref, dt_ref, gain_ref, packed_ref):
-    width = x_ref.shape[1]
+def pack_kernel(*refs):
+    *parts, packed, sems = refs
     at = 0
-    for ref in (out_ref_in, x_ref, z_ref, bc_ref):
-        packed_ref[:, at : at + ref.shape[1]] = ref[...]
-        at += ref.shape[1]
-    rows = x_ref.shape[0]
-    packed_ref[:, at:] = jnp.concatenate(
-        [dt_ref[...], gain_ref[...], jnp.zeros((rows, LANES - heads - 1), BF16)], axis=1
-    )
-
-
-def run_pack(heads, *parts):
+    copies = []
+    for index, part in enumerate(parts):
+        columns = part.shape[1]
+        copies.append(
+            pltpu.make_async_copy(part, packed.at[:, pl.ds(at, columns)], sems.at[index])
+        )
+        at += columns
+    for copy in copies:
+        copy.start()
+    for copy in copies:
+        copy.wait()
+
+
+def run_pack(*parts):
     rows = parts[0].shape[0]
-    columns = sum(part.shape[1] for part in parts[:4]) + LANES
+    columns = sum(part.shape[1] for part in parts)
     return pl.pallas_call(
-        functools.partial(pack_kernel, heads),
+        pack_kernel,
+        in_specs=[pl.BlockSpec(memory_space=pl.ANY)] * len(parts),
+        out_specs=pl.BlockSpec(memory_space=pl.ANY),
         out_shape=jax.ShapeDtypeStruct((rows, columns), BF16),
+        scratch_shapes=[pltpu.SemaphoreType.DMA((len(parts),))],
         compiler_params=pltpu.CompilerParams(vmem_limit_bytes=VMEM_LIMIT),
         name="pack",
     )(*parts)
@@ -610,61 +614,68 @@
     )(window, seg_row, weights, kernel_x, kernel_bc, head, channel, z_proj, x_proj, bcdt)
 
 
-def run_gradient(place, near, weights, scaled, window):
-    features = near[0].shape[1]
-    length, width = scaled.shape
+def run_gradient(cot, weights, scaled, window):
+    length, features = cot.shape
+    width = scaled.shape[1]
     return pl.pallas_call(
-        functools.partial(gradient_kernel, width, len(near)),
+        functools.partial(gradient_kernel, width),
         grid=(length // Q,),
         in_specs=[
-            scalar(),
-            *[whole(block.shape) for block in near],
+            pl.BlockSpec((Q, features), lambda i: (i, 0)),
             whole((features, width)),
             pl.BlockSpec((Q, width), lambda i: (i, 0)),
             whole(window.shape),
         ],
         out_specs=[
-            pl.BlockSpec((Q, features), lambda i: (i, 0)),
             pl.BlockSpec((Q, width), lambda i: (i, 0)),
             pl.BlockSpec((8, Q), lambda i: (0, i)),
         ],
         out_shape=[
-            jax.ShapeDtypeStruct((length, features), BF16),
             jax.ShapeDtypeStruct((length, width), F32),
             jax.ShapeDtypeStruct((8, length), F32),
         ],
         compiler_params=pltpu.CompilerParams(vmem_limit_bytes=VMEM_LIMIT),
         cost_estimate=cost(5),
         name="out_gradient",
-    )(place, *near, weights, scaled, window)
-
-
-def weights_kernel(width, cot_ref, normed_ref, tokens_ref, grads_ref, first_ref, second_ref):
-    tokens = tokens_ref[...]
-    first_ref[:, :width] = dot_tn(cot_ref[...], normed_ref[...]).astype(BF16)
-    first_ref[:, width:] = dot_tn(tokens, grads_ref[:, 2 * width :]).astype(BF16)
-    second_ref[...] = dot_tn(tokens, grads_ref[:, : 2 * width]).astype(BF16)
+    )(cot, weights, scaled, window)
+
+
+def first_kernel(width, cot_ref, normed_ref, tokens_ref, grads_ref, sum_ref):
+    sum_ref[:, :width] = dot_tn(cot_ref[...], normed_ref[...]).astype(BF16)
+    sum_ref[:, width:] = dot_tn(tokens_ref[...], grads_ref[...]).astype(BF16)
+
+
+def second_kernel(tokens_ref, grads_ref, sum_ref):
+    sum_ref[...] = dot_tn(tokens_ref[...], grads_ref[...]).astype(BF16)
 
 
 def run_weights(cot, normed, tokens, grads):
     length, features = tokens.shape
     width = normed.shape[1]
-    columns = [grads.shape[1] - width, 2 * width]
-    return pl.pallas_call(
-        functools.partial(weights_kernel, width),
+    rest = grads.shape[1] - 2 * width
+    params = pltpu.CompilerParams(vmem_limit_bytes=VMEM_LIMIT)
+    strip = pl.BlockSpec((length, Q), lambda i: (0, i))
+    second = pl.pallas_call(
+        second_kernel,
         grid=(features // Q,),
-        in_specs=[
-            pl.BlockSpec((length, Q), lambda i: (0, i)),
-            whole(normed.shape),
-            pl.BlockSpec((length, Q), lambda i: (0, i)),
-            whole(grads.shape),
-        ],
-        out_specs=[pl.BlockSpec((Q, count), lambda i: (i, 0)) for count in columns],
-        out_shape=[jax.ShapeDtypeStruct((features, count), BF16) for count in columns],
-        compiler_params=pltpu.CompilerParams(vmem_limit_bytes=VMEM_LIMIT),
-        cost_estimate=cost(7),
-        name="weight_gradients",
-    )(cot, normed, tokens, grads)
+        in_specs=[strip, pl.BlockSpec((length, 2 * width), lambda i: (0, 0))],
+        out_specs=pl.BlockSpec((Q, 2 * width), lambda i: (i, 0)),
+        out_shape=jax.ShapeDtypeStruct((features, 2 * width), BF16),
+        compiler_params=params,
+        cost_estimate=cost(4),
+        name="weight_gradients_xz",
+    )(tokens, grads)
+    first = pl.pallas_call(
+        functools.partial(first_kernel, width),
+        grid=(features // Q,),
+        in_specs=[strip, whole(normed.shape), strip, whole((length, rest))],
+        out_specs=pl.BlockSpec((Q, width + rest), lambda i: (i, 0)),
+        out_shape=jax.ShapeDtypeStruct((features, width + rest), BF16),
+        compiler_params=params,
+        cost_estimate=cost(4),
+        name="weight_gradients_out",
+    )(cot, normed, tokens, grads[:, 2 * width :])
+    return first, second
 
 
 def run_backward(
@@ -712,7 +723,7 @@
             pltpu.VMEM((8, LANES), F32),
         ],
         compiler_params=pltpu.CompilerParams(vmem_limit_bytes=VMEM_LIMIT),
-        cost_estimate=cost(27),
+        cost_estimate=cost(2),
         name="backward",
     )(
         stat, hidden, window, weights, kernel_x, kernel_bc, head, channel, x_proj, bcdt, grad_out,
@@ -829,6 +840,11 @@
     return functools.reduce(jnp.add, around(values, axis))
 
 
+def sum_around_low(values, axis):
+    low = around(lax.reduce_precision(values, 8, 7).astype(BF16), axis)
+    return functools.reduce(jnp.add, [share.astype(F32) for share in low])
+
+
 def shards(
     hidden,
     seg_ids,
@@ -855,7 +871,10 @@
     features = hidden.shape[2]
     hidden_local = hidden[0]
 
-    packed = run_pack(heads, w_out, w_in_x, w_in_z, w_in_bc, w_in_dt, norm_gain[:, None])
+    steps = jnp.pad(
+        jnp.concatenate([w_in_dt, norm_gain[:, None]], axis=1), ((0, 0), (0, LANES - heads - 1))
+    )
+    packed = run_pack(w_out, w_in_x, w_in_z, w_in_bc, steps)
     n = lax.axis_size("tensor")
     axis_place = lax.axis_index("tensor")
     place = axis_place[None]
@@ -879,24 +898,16 @@
     hidden_full, tokens, z_proj, x_proj, bcdt, gain = run_project(
         heads, size, place, near_hidden, weights
     )
-    right = left = after(cotangent[0], near_hidden[0], near_hidden[-1])
-    moved = []
-    right, left = line_step(right, left, 1, "tensor")
-    moved.append((right, left))
-    bcdt = after(bcdt, right, left)
-    right, left = line_step(after(right, gain), after(left, gain), 2, "tensor")
-    moved.append((right, left))
+    cot_full = lax.all_gather(
+        after(cotangent[0], near_hidden[0], near_hidden[-1]), "tensor", axis=0, tiled=True
+    )
     scaled, out_part, square, *saved = run_forward(
         heads, size, window, seg_row, weights, kernel_x, kernel_bc, head, channel, z_proj, x_proj,
         bcdt,
     )
-    for step in range(3, n):
-        right, left = line_step(after(right, square), after(left, square), step, "tensor")
-        moved.append((right, left))
-    near_cot = line_order(cotangent[0], moved)
-    cot_full, grad_out, along = run_gradient(place, near_cot, weights, scaled, window)
+    grad_out, along = run_gradient(cot_full, weights, scaled, window)
     out_sum = lax.psum_scatter(
-        after(out_part, along), "tensor", scatter_dimension=0, tiled=True
+        out_part, "tensor", scatter_dimension=0, tiled=True
     )
     stat = sum_around(jnp.stack([square[0], along[0]]), "tensor")
     stat_full = jnp.pad(stat, ((0, 6), (0, 0)))
@@ -907,7 +918,7 @@
         channel, x_proj, bcdt, grad_out, saved,
     )
     in_sum = lax.psum_scatter(in_part, "tensor", scatter_dimension=0, tiled=True)
-    first, second = run_weights(cot_full, normed_out, tokens, grads)
+    first, second = run_weights(cot_full, normed_out, tokens, after(grads, out_sum))
     own = jnp.concatenate([sum_x.reshape(-1, LANES), sum_head])
     both = jnp.concatenate([sum_gain[0].reshape(-1, LANES), sum_bc.reshape(-1, LANES)])
     first, second, small, came = cube_scatter(first, second, jnp.concatenate([own, both]), "dp")
@@ -915,7 +926,7 @@
     sum_head = small[own.shape[0] - 8 : own.shape[0]]
     grad_bc = first[:, width : width + 2 * N]
     shared = jnp.concatenate([small[own.shape[0] :], grad_bc.reshape(-1, LANES)])
-    shared = sum_around(shared, "tensor")
+    shared = sum_around_low(shared, "tensor")
     gain_rows = features // LANES
     sum_gain = shared[:gain_rows].reshape(features)
     sum_bc = shared[gain_rows : both.shape[0]].reshape(8, 2 * N)

time: 234 us -> 230 us (0.983)
  starting transfers between devices: 37.8 us -> 34.4 us
  local copies, waits for them, and re-layouts: 24.8 us -> 21.8 us
    all_gather x0 -> x1, waiting for transfers between devices: none -> 19.7 us  [shards(): lax.all_gather(after(cotangent[0], near_hidden[0], near_hidden[-1]), 'ten...]
    ppermute x6 -> x3, waiting for transfers between devices: 40.6 us -> 24.7 us  [line_step(): lax.ppermute(left, axis, [(i, i - 1) for i in range(1, n - step + 1)])]
    reduce_scatter x1, waiting for transfers between devices: 0.01 us -> 8.98 us  [shards(): lax.psum_scatter(out_part, 'tensor', scatter_dimension=0, tiled=True)]
    ppermute x9, waiting for transfers between devices: 13.8 us -> 7.6 us  [around(): lax.ppermute(values, axis, [(i, (i - k) % n) for i in range(n)])]
    unnamed x47 -> x50, local copies, waits for them, and re-layouts: 12 us -> 7.57 us
    ppermute x3, waiting for transfers between devices: 0.14 us -> 4.57 us  [cube_scatter(): moved = other = lax.ppermute(send, axis, pairs)]
    ppermute x6 -> x3, starting transfers between devices: 7.73 us -> 3.85 us  [line_step(): lax.ppermute(left, axis, [(i, i - 1) for i in range(1, n - step + 1)])]
    ppermute x3, waiting for transfers between devices: 13.4 us -> 9.72 us  [cube_scatter(): lax.ppermute(jnp.concatenate([send.reshape(rows, columns), rider]), axis,...]
  transfers between devices with their start and end apart: 30 -> 25, of which waited for: 16 -> 13; matrix products, arithmetic and copies ran while one was open for 10% -> 8% of each run, Pallas kernels for 26% -> 27%
where the time goes in v8:
time: 230 us; the launch traced here: 229 us
  waiting for transfers between devices  80.1 us (35%)
  Pallas kernels  69.5 us (30%)
  starting transfers between devices  34.4 us (15%)
  local copies, waits for them, and re-layouts  21.8 us (9%)
  between operations  14.4 us (6%)
  other arithmetic  8.41 us (4%)
    ppermute x3, waiting for transfers between devices, line_step(): lax.ppermute(left, axis, [(i, i - 1) for i in range(1, n - step + 1)])  24.7 us
    pallas_call x1, Pallas kernels, run_backward(): pl.pallas_call(functools.partial(backward_kernel, heads, size, full_inner...  24.1 us
    all_gather x1, waiting for transfers between devices, shards(): lax.all_gather(after(cotangent[0], near_hidden[0], near_hidden[-1]), 'ten...  19.7 us
    pallas_call x1, Pallas kernels, run_forward(): pl.pallas_call(functools.partial(forward_kernel, heads, size), grid=(bloc...  18.1 us
    ppermute x9, starting transfers between devices, around(): lax.ppermute(values, axis, [(i, (i - k) % n) for i in range(n)])  17.5 us
    ppermute x3, waiting for transfers between devices, cube_scatter(): lax.ppermute(jnp.concatenate([send.reshape(rows, columns), rider]), axis,...  9.72 us
    reduce_scatter x1, waiting for transfers between devices, shards(): lax.psum_scatter(out_part, 'tensor', scatter_dimension=0, tiled=True)  8.98 us
    pallas_call x1, Pallas kernels, run_project(): pl.pallas_call(functools.partial(project_kernel, heads, size, len(near)),...  8.4 us
  transfers between devices with their start and end apart: 25, of which 13 were waited for; matrix products, arithmetic and copies ran while one was open for 8% of the time, Pallas kernels for 27%

profile of v8, /device:TPU:0, one launch (start us, length us, event | category | flops | bytes accessed | tf_op | source)
XLA Modules:
  0.0 228.6 jit_solution(13074745910517409584)
XLA Ops:
  7.3 0.7 pad_maximum_fusion.6
  8.2 0.9 copy-done.4
  9.0 0.9 copy-done.5
  10.0 0.9 copy-done.6
  10.9 0.8 copy-done.7
  11.7 0.8 pack.1
  12.6 1.3 collective-permute-start.6
  13.9 5.6 %collective-permute-start.3 = (bf16[256,1024]{1,0:T(8,128)(2,1)}, bf16[256,1024]{1,0:T(8,128)(2,1)S(1)}, u32[]{:S(2)}, u32[]{:S(2)}) collective-permute-start(bf16[256,1024]{1,0:T(8,128)(2,1)} %bitcast.75), channel_id=1, source_target_pairs={{0,1},{1,2},{2,3},{4,5},{5,6},{6,7},{8,9},{9,10},{10,11},{12,13},{... | collective-permute-start | bytes 1572872 | tf_op jit(solution)/shard_map/ppermute | solution.py:768
  19.5 10.2 %collective-permute-done.6.refs_4_ = bf16[256,1024]{1,0:T(8,128)(2,1)S(1)} collective-permute-done((bf16[256,1024]{1,0:T(8,128)(2,1)}, bf16[256,1024]{1,0:T(8,128)(2,1)S(1)}, u32[]{:S(2)}, u32[]{:S(2)}) %collective-permute-start.6) | collective-permute-done | bytes 524320 | tf_op jit(solution)/shard_map/ppermute | solution.py:769
  29.7 1.3 collective-permute-start.7
  31.0 0.7 collective-permute-start.4
  31.7 13.1 %collective-permute-done.7.refs_5_ = bf16[256,1024]{1,0:T(8,128)(2,1)S(1)} collective-permute-done((bf16[256,1024]{1,0:T(8,128)(2,1)S(1)}, bf16[256,1024]{1,0:T(8,128)(2,1)S(1)}, u32[]{:S(2)}, u32[]{:S(2)}) %collective-permute-start.7) | collective-permute-done | bytes 524320 | tf_op jit(solution)/shard_map/ppermute | solution.py:769
  44.8 1.3 collective-permute-start.8
  46.1 0.7 collective-permute-start.5
  46.8 2.7 %collective-permute-start.2 = (s32[256]{0:T(256)}, s32[256]{0:T(256)S(1)}, u32[]{:S(2)}, u32[]{:S(2)}) collective-permute-start(s32[256]{0:T(256)} %bitcast.92), channel_id=1, source_target_pairs={{0,1},{1,2},{2,3},{3,0},{4,5},{5,6},{6,7},{7,4},{8,9},{9,10},{10,1... | collective-permute-start | bytes 3080 | tf_op jit(solution)/shard_map/ppermute | solution.py:835
  49.5 3.1 %collective-permute-start.1 = (s32[256]{0:T(256)}, s32[256]{0:T(256)S(1)}, u32[]{:S(2)}, u32[]{:S(2)}) collective-permute-start(s32[256]{0:T(256)} %bitcast.93), channel_id=1, source_target_pairs={{0,2},{1,3},{2,0},{3,1},{4,6},{5,7},{6,4},{7,5},{8,10},{9,11},{10,... | collective-permute-start | bytes 3080 | tf_op jit(solution)/shard_map/ppermute | solution.py:835
  52.6 2.8 %collective-permute-start = (s32[256]{0:T(256)}, s32[256]{0:T(256)S(1)}, u32[]{:S(2)}, u32[]{:S(2)}) collective-permute-start(s32[256]{0:T(256)} %bitcast.94), channel_id=1, source_target_pairs={{0,3},{1,0},{2,1},{3,2},{4,7},{5,4},{6,5},{7,6},{8,11},{9,8},{10,9... | collective-permute-start | bytes 3080 | tf_op jit(solution)/shard_map/ppermute | solution.py:835
  55.5 0.7 broadcast_in_dim.39
  56.3 0.7 pad_maximum_fusion.7.channel_ref
  57.0 0.7 pad_maximum_fusion.4.kernel_bc_ref
  57.7 1.4 collective-permute-done.8.refs_6_
  59.9 8.4 %project.1 = (bf16[1024,1024]{1,0:T(8,128)(2,1)}, bf16[1024,1024]{1,0:T(8,128)(2,1)}, f32[1024,512]{1,0:T(8,128)}, f32[1024,512]{1,0:T(8,128)}, f32[1024,384]{1,0:T(8,128)}, /*index=5*/f32[8,1024]{1,0:T(8,128)S(1)}) custom-call(s32[1]{0:T(128)} %bitcast.8.place_ref, bf16[256,1024]{1,0:T(8,128)(2,1)S(1)} %collective-permute-done.5.refs_0_, ...), custom_call_target="tpu_custom_call" | custom-call | flops 8000000000 | bytes 1048576 | tf_op jit(solution)/shard_map/project/pallas_call | solution.py:520
  68.3 1.0 broadcast_in_dim.34.window_ref
  69.4 18.1 %forward.1 = (bf16[1024,512]{1,0:T(8,128)(2,1)}, bf16[1024,1024]{1,0:T(8,128)(2,1)}, f32[8,1024]{1,0:T(8,128)S(1)}, f32[4,128,512]{2,1,0:T(8,128)}, f32[4,8,512]...) custom-call(s32[1040,128]{1,0:T(8,128)} %broadcast_in_dim.34.window_, ...), custom_call_target="tpu_custom_call" | custom-call | flops 14000000000 | bytes 1048576 | tf_op jit(solution)/shard_map/forward/pallas_call | solution.py:581
  87.6 19.7 %all-gather.5.cloned.1.call-done.cot_ref = bf16[1024,1024]{1,0:T(8,128)(2,1)} async-done(((bf16[256,1024]{1,0:T(8,128)(2,1)}), bf16[1024,1024]{1,0:T(8,128)(2,1)}) %all-gather.5.cloned.1.call-update) | async-done | bytes 2097168 | tf_op jit(solution)/shard_map/all_gather | solution.py:901
  107.3 5.0 %out_gradient.1 = (f32[1024,512]{1,0:T(8,128)}, f32[8,1024]{1,0:T(8,128)S(1)}) custom-call(bf16[1024,1024]{1,0:T(8,128)(2,1)} %all-gather.5.cloned.1.call-done.cot_ref, bf16[1024,1920]{1,0:T(8,128)(2,1)} %all-gather.3.cloned.1.call-done.refs_7_.weights_ref, bf16[1024,512]{1,0:T(8,128)(2,1)S(1)} %copy-done.9, s32[1040,128]{1,0:T(8,128)S(1)} %copy-done), custom_call_target="tpu_custom_call" | custom-call | flops 5000000000 | bytes 1048576 | tf_op jit(solution)/shard_map/out_gradient/pallas_call | solution.py:620
  112.3 1.1 collective-permute-start.10
  113.4 0.7 collective-permute-start.11
  114.1 3.2 %collective-permute-start.9 = (f32[2,1024]{1,0:T(2,128)S(1)}, f32[2,1024]{1,0:T(2,128)S(1)}, u32[]{:S(2)}, u32[]{:S(2)}) collective-permute-start(f32[2,1024]{1,0:T(2,128)S(1)} %pad_maximum_fusion.5), channel_id=1, source_target_pairs={{0,3},{1,0},{2,1},{3,2},{4,7},{5,4},{6,5},{7,6},{8,11},{9,8},{10,9... | collective-permute-start | bytes 24584 | tf_op jit(solution)/shard_map/ppermute | solution.py:835
  117.2 1.8 collective-permute-done.11
  119.1 24.1 %backward.1 = (bf16[1024,1408]{1,0:T(8,128)(2,1)}, bf16[1024,1024]{1,0:T(8,128)(2,1)}, bf16[1024,512]{1,0:T(8,128)(2,1)}, f32[8,512]{1,0:T(8,128)S(1)}, f32[8,25...) custom-call(f32[8,1024]{1,0:T(8,128)S(1)} %pad.29.stat_ref, ...), custom_call_target="tpu_custom_call" | custom-call | flops 2000000000 | bytes 1048576 | tf_op jit(solution)/shard_map/backward/pallas_call | solution.py:699
  143.3 9.0 %reduce-scatter.3.cloned.1.call-done = bf16[256,1024]{1,0:T(8,128)(2,1)} async-done(((bf16[1024,1024]{1,0:T(8,128)(2,1)}), bf16[256,1024]{1,0:T(8,128)(2,1)}) %reduce-scatter.3.cloned.1.call-update) | async-done | bytes 524304 | tf_op jit(solution)/shard_map/reduce_scatter | solution.py:909
  152.2 1.2 slice.124.grads_ref
  153.5 1.2 copy-done.8
  154.7 5.7 %weight_gradients_out.1 = bf16[1024,896]{1,0:T(8,128)(2,1)} custom-call(bf16[1024,1024]{1,0:T(8,128)(2,1)} %all-gather.5.cloned.1.call-done.cot_ref, bf16[1024,512]{1,0:T(8,128)(2,1)S(1)} %copy-done.8, bf16[1024,1024]{1,0:T(8,128)(2,1)} %get-tuple-element.89.tokens_ref, bf16[1024,384]{1,0:T(8,128)(2,1)S(1)} %slice.124.grads_ref), custom_call_target="tpu_custom_call" | custom-call | flops 4000000000 | bytes 1048576 | tf_op jit(solution)/shard_map/weight_gradients_out/pallas_call | solution.py:668
  160.4 1.3 constant_dynamic-slice_fusion.1
  161.6 1.0 pad_maximum_fusion
  162.7 6.1 %weight_gradients_xz.1 = bf16[1024,1024]{1,0:T(8,128)(2,1)} custom-call(bf16[1024,1024]{1,0:T(8,128)(2,1)} %get-tuple-element.89.tokens_ref, bf16[1024,1408]{1,0:T(8,128)(2,1)} %get-tuple-element.91.grads_ref), custom_call_target="tpu_custom_call" | custom-call | flops 4000000000 | bytes 1048576 | tf_op jit(solution)/shard_map/weight_gradients_xz/pallas_call | solution.py:658
  168.8 2.3 dynamic-slice_bitcast_fusion
  171.9 0.7 copy-done.11
  173.0 1.5 collective-permute-start.16
  174.5 1.0 fusion.4
  175.6 1.6 fusion
  177.2 0.8 dynamic-slice_bitcast_fusion.1
  178.1 1.5 collective-permute-start.13
  179.5 7.1 %collective-permute-done.16 = bf16[272,896]{1,0:T(8,128)(2,1)S(1)} collective-permute-done((bf16[272,896]{1,0:T(8,128)(2,1)S(1)}, bf16[272,896]{1,0:T(8,128)(2,1)S(1)}, u32[]{:S(2)}, u32[]{:S(2)}) %collective-permute-start.16) | collective-permute-done | bytes 487456 | tf_op jit(solution)/shard_map/ppermute | solution.py:817
  187.0 1.5 collective-permute-start.17
  188.6 4.6 %collective-permute-done.13 = bf16[2,128,1024]{2,1,0:T(8,128)(2,1)} collective-permute-done((bf16[2,128,1024]{2,1,0:T(8,128)(2,1)}, bf16[2,128,1024]{2,1,0:T(8,128)(2,1)}, u32[]{:S(2)}, u32[]{:S(2)}) %collective-permute-start.13) | collective-permute-done | bytes 524320 | tf_op jit(solution)/shard_map/ppermute | solution.py:824
  193.1 1.2 fusion.2
  194.4 0.8 collective-permute-start.14
  195.2 2.6 %collective-permute-done.17 = bf16[144,896]{1,0:T(8,128)(2,1)S(1)} collective-permute-done((bf16[144,896]{1,0:T(8,128)(2,1)S(1)}, bf16[144,896]{1,0:T(8,128)(2,1)S(1)}, u32[]{:S(2)}, u32[]{:S(2)}) %collective-permute-start.17) | collective-permute-done | bytes 258080 | tf_op jit(solution)/shard_map/ppermute | solution.py:817
  198.1 1.8 collective-permute-start.19
  199.9 1.2 collective-permute-start.18
  201.1 0.8 collective-permute-start.20
  203.0 0.7 slice.180
  205.1 0.7 copy.46
  205.7 3.4 %collective-permute-done.19 = bf16[280,128]{1,0:T(8,128)(2,1)S(1)} collective-permute-done((bf16[280,128]{1,0:T(8,128)(2,1)S(1)}, bf16[280,128]{1,0:T(8,128)(2,1)S(1)}, u32[]{:S(2)}, u32[]{:S(2)}) %collective-permute-start.19) | collective-permute-done | bytes 71712 | tf_op jit(solution)/shard_map/ppermute | solution.py:835
  209.1 1.3 collective-permute-done.18
  210.4 1.1 collective-permute-done.20
  211.6 0.7 reshape.143
  214.1 0.8 fusion.10
  214.9 4.8 %reduce-scatter.5.cloned.1.call-done.sum_ref = bf16[256,1024]{1,0:T(8,128)(2,1)} async-done(((bf16[1024,1024]{1,0:T(8,128)(2,1)}), bf16[256,1024]{1,0:T(8,128)(2,1)}) %reduce-scatter.5.cloned.1.call-update) | async-done | bytes 524304 | tf_op jit(solution)/shard_map/reduce_scatter | solution.py:920
  219.7 1.0 copy-done.3
  220.8 1.3 finish.1
  (129 shorter events, 7.3 us)
Async XLA Ops:
  7.2 52.0 %copy-start.14 = (s32[1,256]{1,0:T(1,128)S(1)}, s32[1,256]{1,0:T(1,128)}, u32[]{:S(2)}) copy-start(s32[1,256]{1,0:T(1,128)} %param.18) | copy-start | bytes 3076
  7.2 52.0 %copy-start.15 = (f32[512]{0:T(512)S(1)}, f32[512]{0:T(512)}, u32[]{:S(2)}) copy-start(f32[512]{0:T(512)} %param.26) | copy-start | bytes 6148
  7.2 52.0 %copy-start.13 = (f32[4,512]{1,0:T(4,128)S(1)}, f32[4,512]{1,0:T(4,128)}, u32[]{:S(2)}) copy-start(f32[4,512]{1,0:T(4,128)} %param.25) | copy-start | bytes 24580
  7.2 52.0 %copy-start.16 = (f32[8]{0:T(128)S(1)}, f32[8]{0:T(128)}, u32[]{:S(2)}) copy-start(f32[8]{0:T(128)} %param.30) | copy-start | bytes 100
  7.2 52.0 %copy-start.17 = (f32[8]{0:T(128)S(1)}, f32[8]{0:T(128)}, u32[]{:S(2)}) copy-start(f32[8]{0:T(128)} %param.29) | copy-start | bytes 100
  7.2 52.3 %all-gather.3.cloned.1.call-start = ((), (), s32[]{:S(2)}) async-start(), calls=%async_computation.2 | async-start | bytes 4423680 | tf_op jit(solution)/shard_map/all_gather | solution.py:882
  8.1 0.9 copy-start.4
  9.0 0.9 copy-start.5
  10.0 0.9 copy-start.6
  10.9 0.8 copy-start.7
  12.6 94.7 %all-gather.5.cloned.1.call-start = ((), (), s32[]{:S(2)}) async-start(), calls=%async_computation.4 | async-start | bytes 2621440 | tf_op jit(solution)/shard_map/all_gather | solution.py:901
  12.6 17.1 %collective-permute-start.6 = (bf16[256,1024]{1,0:T(8,128)(2,1)}, bf16[256,1024]{1,0:T(8,128)(2,1)S(1)}, u32[]{:S(2)}, u32[]{:S(2)}) collective-permute-start(bf16[256,1024]{1,0:T(8,128)(2,1)} %bitcast.74), channel_id=1, source_target_pairs={{1,0},{2,1},{3,2},{5,4},{6,5},{7,6},{9,8},{10,9},{11,10},{13,12},{... | collective-permute-start | bytes 1572872 | tf_op jit(solution)/shard_map/ppermute | solution.py:769
  13.9 17.1 %collective-permute-start.3 = (bf16[256,1024]{1,0:T(8,128)(2,1)}, bf16[256,1024]{1,0:T(8,128)(2,1)S(1)}, u32[]{:S(2)}, u32[]{:S(2)}) collective-permute-start(bf16[256,1024]{1,0:T(8,128)(2,1)} %bitcast.75), channel_id=1, source_target_pairs={{0,1},{1,2},{2,3},{4,5},{5,6},{6,7},{8,9},{9,10},{10,11},{12,13},{... | collective-permute-start | bytes 1572872 | tf_op jit(solution)/shard_map/ppermute | solution.py:768
  29.7 29.9 %copy-start.18 = (bf16[256,1024]{1,0:T(8,128)(2,1)}, bf16[256,1024]{1,0:T(8,128)(2,1)S(1)}, u32[]{:S(2)}) copy-start(bf16[256,1024]{1,0:T(8,128)(2,1)S(1)} %collective-permute-done.6.refs_4_) | copy-start | bytes 1572868
  29.7 15.1 %collective-permute-start.7 = (bf16[256,1024]{1,0:T(8,128)(2,1)S(1)}, bf16[256,1024]{1,0:T(8,128)(2,1)S(1)}, u32[]{:S(2)}, u32[]{:S(2)}) collective-permute-start(bf16[256,1024]{1,0:T(8,128)(2,1)S(1)} %collective-permute-done.6.refs_4_), channel_id=1, source_target_pairs={{1,0},{2,1},{5,4},{6,5},{9,8},{10,9},{13,12},{14,13},{17,16},{18,1... | collective-permute-start | bytes 1572872 | tf_op jit(solution)/shard_map/ppermute | solution.py:769
  31.0 15.1 %collective-permute-start.4 = (bf16[256,1024]{1,0:T(8,128)(2,1)S(1)}, bf16[256,1024]{1,0:T(8,128)(2,1)S(1)}, u32[]{:S(2)}, u32[]{:S(2)}) collective-permute-start(bf16[256,1024]{1,0:T(8,128)(2,1)S(1)} %collective-permute-done.3.refs_2_), channel_id=1, source_target_pairs={{1,2},{2,3},{5,6},{6,7},{9,10},{10,11},{13,14},{14,15},{17,18},{18... | collective-permute-start | bytes 1572872 | tf_op jit(solution)/shard_map/ppermute | solution.py:768
  44.8 14.8 %copy-start.19 = (bf16[256,1024]{1,0:T(8,128)(2,1)}, bf16[256,1024]{1,0:T(8,128)(2,1)S(1)}, u32[]{:S(2)}) copy-start(bf16[256,1024]{1,0:T(8,128)(2,1)S(1)} %collective-permute-done.7.refs_5_) | copy-start | bytes 1572868
  44.8 14.3 %collective-permute-start.8 = (bf16[256,1024]{1,0:T(8,128)(2,1)S(1)}, bf16[256,1024]{1,0:T(8,128)(2,1)S(1)}, u32[]{:S(2)}, u32[]{:S(2)}) collective-permute-start(bf16[256,1024]{1,0:T(8,128)(2,1)S(1)} %collective-permute-done.7.refs_5_), channel_id=1, source_target_pairs={{1,0},{5,4},{9,8},{13,12},{17,16},{21,20},{25,24},{29,28}} | collective-permute-start | bytes 1572872 | tf_op jit(solution)/shard_map/ppermute | solution.py:769
  46.1 13.0 %collective-permute-start.5 = (bf16[256,1024]{1,0:T(8,128)(2,1)S(1)}, bf16[256,1024]{1,0:T(8,128)(2,1)S(1)}, u32[]{:S(2)}, u32[]{:S(2)}) collective-permute-start(bf16[256,1024]{1,0:T(8,128)(2,1)S(1)} %collective-permute-done.4.refs_1_), channel_id=1, source_target_pairs={{2,3},{6,7},{10,11},{14,15},{18,19},{22,23},{26,27},{30,31}} | collective-permute-start | bytes 1572872 | tf_op jit(solution)/shard_map/ppermute | solution.py:768
  46.8 12.6 %collective-permute-start.2 = (s32[256]{0:T(256)}, s32[256]{0:T(256)S(1)}, u32[]{:S(2)}, u32[]{:S(2)}) collective-permute-start(s32[256]{0:T(256)} %bitcast.92), channel_id=1, source_target_pairs={{0,1},{1,2},{2,3},{3,0},{4,5},{5,6},{6,7},{7,4},{8,9},{9,10},{10,1... | collective-permute-start | bytes 3080 | tf_op jit(solution)/shard_map/ppermute | solution.py:835
  49.5 9.8 %collective-permute-start.1 = (s32[256]{0:T(256)}, s32[256]{0:T(256)S(1)}, u32[]{:S(2)}, u32[]{:S(2)}) collective-permute-start(s32[256]{0:T(256)} %bitcast.93), channel_id=1, source_target_pairs={{0,2},{1,3},{2,0},{3,1},{4,6},{5,7},{6,4},{7,5},{8,10},{9,11},{10,... | collective-permute-start | bytes 3080 | tf_op jit(solution)/shard_map/ppermute | solution.py:835
  52.6 6.7 %collective-permute-start = (s32[256]{0:T(256)}, s32[256]{0:T(256)S(1)}, u32[]{:S(2)}, u32[]{:S(2)}) collective-permute-start(s32[256]{0:T(256)} %bitcast.94), channel_id=1, source_target_pairs={{0,3},{1,0},{2,1},{3,2},{4,7},{5,4},{6,5},{7,6},{8,11},{9,8},{10,9... | collective-permute-start | bytes 3080 | tf_op jit(solution)/shard_map/ppermute | solution.py:835
  59.1 0.8 copy-start.20
  59.1 93.1 %reduce-scatter.3.cloned.1.call-start = ((), (), s32[]{:S(2)}) async-start(), calls=%async_computation.3 | async-start | bytes 2621440 | tf_op jit(solution)/shard_map/reduce_scatter | solution.py:909
  87.5 19.8 %copy-start = (s32[1040,128]{1,0:T(8,128)S(1)}, s32[1040,128]{1,0:T(8,128)}, u32[]{:S(2)}) copy-start(s32[1040,128]{1,0:T(8,128)} %broadcast_in_dim.34.window_ref) | copy-start | bytes 1597444
  87.5 19.8 %copy-start.9 = (bf16[1024,512]{1,0:T(8,128)(2,1)S(1)}, bf16[1024,512]{1,0:T(8,128)(2,1)}, u32[]{:S(2)}) copy-start(bf16[1024,512]{1,0:T(8,128)(2,1)} %get-tuple-element.63.scaled_ref) | copy-start | bytes 3145732
  87.5 132.2 %reduce-scatter.5.cloned.1.call-start = ((), (), s32[]{:S(2)}) async-start(), calls=%async_computation.5 | async-start | bytes 2621440 | tf_op jit(solution)/shard_map/reduce_scatter | solution.py:920
  112.3 4.9 %collective-permute-start.10 = (f32[2,1024]{1,0:T(2,128)S(1)}, f32[2,1024]{1,0:T(2,128)S(1)}, u32[]{:S(2)}, u32[]{:S(2)}) collective-permute-start(f32[2,1024]{1,0:T(2,128)S(1)} %pad_maximum_fusion.5), channel_id=1, source_target_pairs={{0,2},{1,3},{2,0},{3,1},{4,6},{5,7},{6,4},{7,5},{8,10},{9,11},{10,... | collective-permute-start | bytes 24584 | tf_op jit(solution)/shard_map/ppermute | solution.py:835
  113.4 5.6 %collective-permute-start.11 = (f32[2,1024]{1,0:T(2,128)S(1)}, f32[2,1024]{1,0:T(2,128)S(1)}, u32[]{:S(2)}, u32[]{:S(2)}) collective-permute-start(f32[2,1024]{1,0:T(2,128)S(1)} %pad_maximum_fusion.5), channel_id=1, source_target_pairs={{0,1},{1,2},{2,3},{3,0},{4,5},{5,6},{6,7},{7,4},{8,9},{9,10},{10,1... | collective-permute-start | bytes 24584 | tf_op jit(solution)/shard_map/ppermute | solution.py:835
  114.1 5.0 %collective-permute-start.9 = (f32[2,1024]{1,0:T(2,128)S(1)}, f32[2,1024]{1,0:T(2,128)S(1)}, u32[]{:S(2)}, u32[]{:S(2)}) collective-permute-start(f32[2,1024]{1,0:T(2,128)S(1)} %pad_maximum_fusion.5), channel_id=1, source_target_pairs={{0,3},{1,0},{2,1},{3,2},{4,7},{5,4},{6,5},{7,6},{8,11},{9,8},{10,9... | collective-permute-start | bytes 24584 | tf_op jit(solution)/shard_map/ppermute | solution.py:835
  153.5 1.2 copy-start.8
  162.7 9.1 %collective-permute-start.15 = (bf16[528,896]{1,0:T(8,128)(2,1)}, bf16[528,896]{1,0:T(8,128)(2,1)S(1)}, u32[]{:S(2)}, u32[]{:S(2)}) collective-permute-start(bf16[528,896]{1,0:T(8,128)(2,1)} %pad_maximum_fusion), channel_id=1, source_target_pairs={{0,4},{4,0},{8,12},{12,8},{16,20},{20,16},{24,28},{28,24},{1,5},{5... | collective-permute-start | bytes 2838536 | tf_op jit(solution)/shard_map/ppermute | solution.py:817
  171.0 1.5 copy-start.11
  171.1 4.5 %collective-permute-start.12 = (bf16[2,2,128,1024]{3,2,1,0:T(8,128)(2,1)}, bf16[2,2,128,1024]{3,2,1,0:T(8,128)(2,1)}, u32[]{:S(2)}, u32[]{:S(2)}) collective-permute-start(bf16[2,2,128,1024]{3,2,1,0:T(8,128)(2,1)} %dynamic-slice_bitcast_fusion), channel_id=1, source_target_pairs={{0,4},{4,0},{8,12},{12,8},{16,20},{20,16},{24,28},{28,24},{1,5},{5... | collective-permute-start | bytes 3145736 | tf_op jit(solution)/shard_map/ppermute | solution.py:824
  172.5 2.0 copy-start.2
  172.8 1.8 copy-start.12
  172.9 2.7 %copy-start.10 = (bf16[1024,1024]{1,0:T(8,128)(2,1)S(1)}, bf16[1024,1024]{1,0:T(8,128)(2,1)}, u32[]{:S(2)}) copy-start(bf16[1024,1024]{1,0:T(8,128)(2,1)} %weight_gradients_xz.1) | copy-start | bytes 6291460
  173.0 13.6 %collective-permute-start.16 = (bf16[272,896]{1,0:T(8,128)(2,1)S(1)}, bf16[272,896]{1,0:T(8,128)(2,1)S(1)}, u32[]{:S(2)}, u32[]{:S(2)}) collective-permute-start(bf16[272,896]{1,0:T(8,128)(2,1)S(1)} %pad_maximum_fusion.1), channel_id=1, source_target_pairs={{0,8},{4,12},{8,0},{12,4},{16,24},{20,28},{24,16},{28,20},{1,9},{5... | collective-permute-start | bytes 1462280 | tf_op jit(solution)/shard_map/ppermute | solution.py:817
  178.1 15.1 %collective-permute-start.13 = (bf16[2,128,1024]{2,1,0:T(8,128)(2,1)}, bf16[2,128,1024]{2,1,0:T(8,128)(2,1)}, u32[]{:S(2)}, u32[]{:S(2)}) collective-permute-start(bf16[2,128,1024]{2,1,0:T(8,128)(2,1)} %dynamic-slice_bitcast_fusion.1), channel_id=1, source_target_pairs={{0,16},{4,20},{8,24},{12,28},{16,0},{20,4},{24,8},{28,12},{1,17},{... | collective-permute-start | bytes 1572872 | tf_op jit(solution)/shard_map/ppermute | solution.py:824
  187.0 10.8 %collective-permute-start.17 = (bf16[144,896]{1,0:T(8,128)(2,1)S(1)}, bf16[144,896]{1,0:T(8,128)(2,1)S(1)}, u32[]{:S(2)}, u32[]{:S(2)}) collective-permute-start(bf16[144,896]{1,0:T(8,128)(2,1)S(1)} %pad_maximum_fusion.2), channel_id=1, source_target_pairs={{0,16},{4,20},{8,24},{12,28},{16,0},{20,4},{24,8},{28,12},{1,17},{... | collective-permute-start | bytes 774152 | tf_op jit(solution)/shard_map/ppermute | solution.py:817
  194.4 19.6 %collective-permute-start.14 = (bf16[128,1024]{1,0:T(8,128)(2,1)S(1)}, bf16[128,1024]{1,0:T(8,128)(2,1)S(1)}, u32[]{:S(2)}, u32[]{:S(2)}) collective-permute-start(bf16[128,1024]{1,0:T(8,128)(2,1)S(1)} %dynamic-slice_bitcast_fusion.2), channel_id=1, source_target_pairs={{0,8},{4,12},{8,0},{12,4},{16,24},{20,28},{24,16},{28,20},{1,9},{5... | collective-permute-start | bytes 786440 | tf_op jit(solution)/shard_map/ppermute | solution.py:824
  198.0 21.7 %copy-start.1 = (bf16[1,256,1024]{2,1,0:T(8,128)(2,1)S(1)}, bf16[1,256,1024]{2,1,0:T(8,128)(2,1)}, u32[]{:S(2)}) copy-start(bf16[1,256,1024]{2,1,0:T(8,128)(2,1)} %param.19) | copy-start | bytes 1572868
  198.1 11.0 %collective-permute-start.19 = (bf16[280,128]{1,0:T(8,128)(2,1)S(1)}, bf16[280,128]{1,0:T(8,128)(2,1)S(1)}, u32[]{:S(2)}, u32[]{:S(2)}) collective-permute-start(bf16[280,128]{1,0:T(8,128)(2,1)S(1)} %fusion.5), channel_id=1, source_target_pairs={{0,2},{1,3},{2,0},{3,1},{4,6},{5,7},{6,4},{7,5},{8,10},{9,11},{10,... | collective-permute-start | bytes 215048 | tf_op jit(solution)/shard_map/ppermute | solution.py:835
  199.9 10.5 %collective-permute-start.18 = (bf16[280,128]{1,0:T(8,128)(2,1)S(1)}, bf16[280,128]{1,0:T(8,128)(2,1)S(1)}, u32[]{:S(2)}, u32[]{:S(2)}) collective-permute-start(bf16[280,128]{1,0:T(8,128)(2,1)S(1)} %fusion.5), channel_id=1, source_target_pairs={{0,3},{1,0},{2,1},{3,2},{4,7},{5,4},{6,5},{7,6},{8,11},{9,8},{10,9... | collective-permute-start | bytes 215048 | tf_op jit(solution)/shard_map/ppermute | solution.py:835
  201.1 10.5 %collective-permute-start.20 = (bf16[280,128]{1,0:T(8,128)(2,1)S(1)}, bf16[280,128]{1,0:T(8,128)(2,1)S(1)}, u32[]{:S(2)}, u32[]{:S(2)}) collective-permute-start(bf16[280,128]{1,0:T(8,128)(2,1)S(1)} %fusion.5), channel_id=1, source_target_pairs={{0,1},{1,2},{2,3},{3,0},{4,5},{5,6},{6,7},{7,4},{8,9},{9,10},{10,1... | collective-permute-start | bytes 215048 | tf_op jit(solution)/shard_map/ppermute | solution.py:835
  219.7 1.0 copy-start.3
Sparse Core Ops, SparseCore 0:
  12.7 38.3 all-gather.2
  59.3 47.9 all-gather.4
  109.6 42.6 reduce-scatter.2
  171.8 47.8 reduce-scatter.4

commit v9 on v8

--- a/solution.py
+++ b/solution.py
@@ -324,6 +324,7 @@
     decay_ref,
     slope_dt_ref,
     proj_ref,
+    rest_ref,
     part_ref,
     out_ref,
     sum_x_ref,
@@ -454,7 +455,8 @@
     grads = jnp.concatenate(
         [grad_proj.astype(BF16), grad_z, grad_bc.astype(BF16), grad_raw.astype(BF16)], axis=1
     )
-    proj_ref[...] = grads
+    proj_ref[...] = grads[:, : 2 * width]
+    rest_ref[...] = grads[:, 2 * width :]
     part = dot_nt(grads, weights_ref[:, width:])
     part_ref[...] = part.astype(BF16)
     hidden = hidden_ref[...].astype(F32)
@@ -635,7 +637,7 @@
             jax.ShapeDtypeStruct((8, length), F32),
         ],
         compiler_params=pltpu.CompilerParams(vmem_limit_bytes=VMEM_LIMIT),
-        cost_estimate=cost(5),
+        cost_estimate=cost(0),
         name="out_gradient",
     )(cot, weights, scaled, window)
 
@@ -649,10 +651,10 @@
     sum_ref[...] = dot_tn(tokens_ref[...], grads_ref[...]).astype(BF16)
 
 
-def run_weights(cot, normed, tokens, grads):
+def run_weights(cot, normed, tokens, grads, rest_grads):
     length, features = tokens.shape
     width = normed.shape[1]
-    rest = grads.shape[1] - 2 * width
+    rest = rest_grads.shape[1]
     params = pltpu.CompilerParams(vmem_limit_bytes=VMEM_LIMIT)
     strip = pl.BlockSpec((length, Q), lambda i: (0, i))
     second = pl.pallas_call(
@@ -662,7 +664,7 @@
         out_specs=pl.BlockSpec((Q, 2 * width), lambda i: (i, 0)),
         out_shape=jax.ShapeDtypeStruct((features, 2 * width), BF16),
         compiler_params=params,
-        cost_estimate=cost(4),
+        cost_estimate=cost(0),
         name="weight_gradients_xz",
     )(tokens, grads)
     first = pl.pallas_call(
@@ -672,9 +674,9 @@
         out_specs=pl.BlockSpec((Q, width + rest), lambda i: (i, 0)),
         out_shape=jax.ShapeDtypeStruct((features, width + rest), BF16),
         compiler_params=params,
-        cost_estimate=cost(4),
+        cost_estimate=cost(0),
         name="weight_gradients_out",
-    )(cot, normed, tokens, grads[:, 2 * width :])
+    )(cot, normed, tokens, rest_grads)
     return first, second
 
 
@@ -686,7 +688,6 @@
     width = heads * size
     blocks = length // Q
     rest = 2 * N + LANES
-    total = 2 * width + rest
 
     def rows(columns):
         return pl.BlockSpec((Q, columns), lambda i: (blocks - 1 - i, 0))
@@ -713,8 +714,10 @@
             rows(width),
             *saved_specs(heads, size, lambda i: blocks - 1 - i),
         ],
-        out_specs=[rows(total), rows(features), rows(width)] + [whole(shape) for shape in sums],
-        out_shape=[made(total, BF16), made(features, BF16), made(width, BF16)]
+        out_specs=[rows(2 * width), rows(rest), rows(features), rows(width)] + [whole(shape) for shape in sums],
+        out_shape=[
+            made(2 * width, BF16), made(rest, BF16), made(features, BF16), made(width, BF16)
+        ]
         + [jax.ShapeDtypeStruct(shape, F32) for shape in sums],
         scratch_shapes=[
             pltpu.VMEM((Q + HALO, width), F32),
@@ -723,7 +726,7 @@
             pltpu.VMEM((8, LANES), F32),
         ],
         compiler_params=pltpu.CompilerParams(vmem_limit_bytes=VMEM_LIMIT),
-        cost_estimate=cost(2),
+        cost_estimate=cost(0),
         name="backward",
     )(
         stat, hidden, window, weights, kernel_x, kernel_bc, head, channel, x_proj, bcdt, grad_out,
@@ -796,7 +799,7 @@
     orders = [bits, bits[:1] + bits[:0:-1]]
     parts = [part.reshape((2,) * len(bits) + (-1, part.shape[1])) for part in (first, second)]
     left = [bits[::-1], bits[::-1]]
-    came = [None, None]
+    came = []
     for step in range(len(bits)):
         for index in range(2):
             part = parts[index]
@@ -822,7 +825,7 @@
                 small = small + rider.astype(F32)
             else:
                 moved = other = lax.ppermute(send, axis, pairs)
-            came[index] = moved
+            came.append(moved)
             part = keep.astype(F32) + other.astype(F32)
             left[index] = [other_bit for other_bit in left[index] if other_bit != bit]
             parts[index] = part.astype(BF16) if left[index] else part
@@ -913,12 +916,12 @@
     stat_full = jnp.pad(stat, ((0, 6), (0, 0)))
     out_scale = lax.rsqrt(stat[0] / full_inner + EPS) * (seg_full > 0).astype(F32)
 
-    grads, in_part, normed_out, sum_x, sum_bc, sum_head, sum_gain = run_backward(
+    grads, rest_grads, in_part, normed_out, sum_x, sum_bc, sum_head, sum_gain = run_backward(
         heads, size, full_inner, stat_full, hidden_full, window, weights, kernel_x, kernel_bc, head,
         channel, x_proj, bcdt, grad_out, saved,
     )
     in_sum = lax.psum_scatter(in_part, "tensor", scatter_dimension=0, tiled=True)
-    first, second = run_weights(cot_full, normed_out, tokens, after(grads, out_sum))
+    first, second = run_weights(cot_full, after(normed_out, out_sum), tokens, grads, rest_grads)
     own = jnp.concatenate([sum_x.reshape(-1, LANES), sum_head])
     both = jnp.concatenate([sum_gain[0].reshape(-1, LANES), sum_bc.reshape(-1, LANES)])
     first, second, small, came = cube_scatter(first, second, jnp.concatenate([own, both]), "dp")
@@ -941,7 +944,7 @@
     scale_here = lax.dynamic_slice_in_dim(out_scale, axis_place * local, local, 0)[:, None]
     layer_out = (hidden_rows + out_sum.astype(F32) * scale_here).astype(BF16)
 
-    grad_hidden = run_finish(in_sum, hidden_local, cotangent[0], after(gain, came[1]))
+    grad_hidden = run_finish(in_sum, hidden_local, cotangent[0], after(gain, shared))
 
     return (
         layer_out[None],

time: 230 us -> 230 us (level)
    ppermute x3, waiting for transfers between devices: 4.57 us -> 20.2 us  [cube_scatter(): moved = other = lax.ppermute(send, axis, pairs)]
    reduce_scatter x1, waiting for transfers between devices: 8.98 us -> 0.02 us  [shards(): lax.psum_scatter(out_part, 'tensor', scatter_dimension=0, tiled=True)]
    reduce_scatter x1, waiting for transfers between devices: 4.78 us -> 0.01 us  [shards(): lax.psum_scatter(in_part, 'tensor', scatter_dimension=0, tiled=True)]
    ppermute x9, waiting for transfers between devices: 7.6 us -> 3.6 us  [around(): lax.ppermute(values, axis, [(i, (i - k) % n) for i in range(n)])]
  transfers between devices with their start and end apart: 25 -> 25, of which waited for: 13 -> 11; matrix products, arithmetic and copies ran while one was open for 8% -> 10% of each run, Pallas kernels for 27% -> 27%
where the time goes in v9:
time: 230 us; the launch traced here: 229 us
  waiting for transfers between devices  79.8 us (35%)
  Pallas kernels  69.4 us (30%)
  starting transfers between devices  34.5 us (15%)
  local copies, waits for them, and re-layouts  21.3 us (9%)
  between operations  14.5 us (6%)
  other arithmetic  9.7 us (4%)
    ppermute x3, waiting for transfers between devices, line_step(): lax.ppermute(left, axis, [(i, i - 1) for i in range(1, n - step + 1)])  24.7 us
    pallas_call x1, Pallas kernels, run_backward(): pl.pallas_call(functools.partial(backward_kernel, heads, size, full_inner...  24.1 us
    ppermute x3, waiting for transfers between devices, cube_scatter(): moved = other = lax.ppermute(send, axis, pairs)  20.2 us
    all_gather x1, waiting for transfers between devices, shards(): lax.all_gather(after(cotangent[0], near_hidden[0], near_hidden[-1]), 'ten...  19.8 us
    ppermute x9, starting transfers between devices, around(): lax.ppermute(values, axis, [(i, (i - k) % n) for i in range(n)])  18.1 us
    pallas_call x1, Pallas kernels, run_forward(): pl.pallas_call(functools.partial(forward_kernel, heads, size), grid=(bloc...  18 us
    ppermute x3, waiting for transfers between devices, cube_scatter(): lax.ppermute(jnp.concatenate([send.reshape(rows, columns), rider]), axis,...  11.4 us
    pallas_call x1, Pallas kernels, run_project(): pl.pallas_call(functools.partial(project_kernel, heads, size, len(near)),...  8.34 us
  transfers between devices with their start and end apart: 25, of which 11 were waited for; matrix products, arithmetic and copies ran while one was open for 10% of the time, Pallas kernels for 27%

profile of v9, /device:TPU:0, one launch (start us, length us, event | category | flops | bytes accessed | tf_op | source)
XLA Modules:
  0.0 229.1 jit_solution(6417122923451615724)
XLA Ops:
  7.3 0.7 pad_maximum_fusion.6
  8.1 0.9 copy-done.7
  9.0 0.9 copy-done.8
  10.0 0.9 copy-done.9
  10.9 0.8 copy-done.10
  11.7 0.9 pack.1
  12.6 1.3 collective-permute-start.6
  13.9 5.6 %collective-permute-start.3 = (bf16[256,1024]{1,0:T(8,128)(2,1)}, bf16[256,1024]{1,0:T(8,128)(2,1)S(1)}, u32[]{:S(2)}, u32[]{:S(2)}) collective-permute-start(bf16[256,1024]{1,0:T(8,128)(2,1)} %bitcast.75), channel_id=1, source_target_pairs={{0,1},{1,2},{2,3},{4,5},{5,6},{6,7},{8,9},{9,10},{10,11},{12,13},{... | collective-permute-start | bytes 1572872 | tf_op jit(solution)/shard_map/ppermute | solution.py:771
  19.5 10.2 %collective-permute-done.6.refs_4_ = bf16[256,1024]{1,0:T(8,128)(2,1)S(1)} collective-permute-done((bf16[256,1024]{1,0:T(8,128)(2,1)}, bf16[256,1024]{1,0:T(8,128)(2,1)S(1)}, u32[]{:S(2)}, u32[]{:S(2)}) %collective-permute-start.6) | collective-permute-done | bytes 524320 | tf_op jit(solution)/shard_map/ppermute | solution.py:772
  29.7 1.3 collective-permute-start.7
  31.0 0.7 collective-permute-start.4
  31.7 13.1 %collective-permute-done.7.refs_5_ = bf16[256,1024]{1,0:T(8,128)(2,1)S(1)} collective-permute-done((bf16[256,1024]{1,0:T(8,128)(2,1)S(1)}, bf16[256,1024]{1,0:T(8,128)(2,1)S(1)}, u32[]{:S(2)}, u32[]{:S(2)}) %collective-permute-start.7) | collective-permute-done | bytes 524320 | tf_op jit(solution)/shard_map/ppermute | solution.py:772
  44.8 1.3 collective-permute-start.8
  46.1 0.7 collective-permute-start.5
  46.8 2.7 %collective-permute-start.2 = (s32[256]{0:T(256)}, s32[256]{0:T(256)S(1)}, u32[]{:S(2)}, u32[]{:S(2)}) collective-permute-start(s32[256]{0:T(256)} %bitcast.92), channel_id=1, source_target_pairs={{0,1},{1,2},{2,3},{3,0},{4,5},{5,6},{6,7},{7,4},{8,9},{9,10},{10,1... | collective-permute-start | bytes 3080 | tf_op jit(solution)/shard_map/ppermute | solution.py:838
  49.5 3.1 %collective-permute-start.1 = (s32[256]{0:T(256)}, s32[256]{0:T(256)S(1)}, u32[]{:S(2)}, u32[]{:S(2)}) collective-permute-start(s32[256]{0:T(256)} %bitcast.93), channel_id=1, source_target_pairs={{0,2},{1,3},{2,0},{3,1},{4,6},{5,7},{6,4},{7,5},{8,10},{9,11},{10,... | collective-permute-start | bytes 3080 | tf_op jit(solution)/shard_map/ppermute | solution.py:838
  52.7 2.8 %collective-permute-start = (s32[256]{0:T(256)}, s32[256]{0:T(256)S(1)}, u32[]{:S(2)}, u32[]{:S(2)}) collective-permute-start(s32[256]{0:T(256)} %bitcast.94), channel_id=1, source_target_pairs={{0,3},{1,0},{2,1},{3,2},{4,7},{5,4},{6,5},{7,6},{8,11},{9,8},{10,9... | collective-permute-start | bytes 3080 | tf_op jit(solution)/shard_map/ppermute | solution.py:838
  55.5 0.7 broadcast_in_dim.39
  56.3 0.7 pad_maximum_fusion.7.channel_ref
  57.0 0.7 pad_maximum_fusion.4.kernel_bc_ref
  57.7 1.4 collective-permute-done.8.refs_6_
  59.9 8.3 %project.1 = (bf16[1024,1024]{1,0:T(8,128)(2,1)}, bf16[1024,1024]{1,0:T(8,128)(2,1)}, f32[1024,512]{1,0:T(8,128)}, f32[1024,512]{1,0:T(8,128)}, f32[1024,384]{1,0:T(8,128)}, /*index=5*/f32[8,1024]{1,0:T(8,128)S(1)}) custom-call(s32[1]{0:T(128)} %bitcast.8.place_ref, bf16[256,1024]{1,0:T(8,128)(2,1)S(1)} %collective-permute-done.5.refs_0_, ...), custom_call_target="tpu_custom_call" | custom-call | flops 8000000000 | bytes 1048576 | tf_op jit(solution)/shard_map/project/pallas_call | solution.py:522
  68.3 1.0 broadcast_in_dim.34.window_ref
  69.3 18.0 %forward.1 = (bf16[1024,512]{1,0:T(8,128)(2,1)}, bf16[1024,1024]{1,0:T(8,128)(2,1)}, f32[8,1024]{1,0:T(8,128)S(1)}, f32[4,128,512]{2,1,0:T(8,128)}, f32[4,8,512]...) custom-call(s32[1040,128]{1,0:T(8,128)} %broadcast_in_dim.34.window_, ...), custom_call_target="tpu_custom_call" | custom-call | flops 14000000000 | bytes 1048576 | tf_op jit(solution)/shard_map/forward/pallas_call | solution.py:583
  87.4 19.8 %all-gather.5.cloned.1.call-done.cot_ref = bf16[1024,1024]{1,0:T(8,128)(2,1)} async-done(((bf16[256,1024]{1,0:T(8,128)(2,1)}), bf16[1024,1024]{1,0:T(8,128)(2,1)}) %all-gather.5.cloned.1.call-update) | async-done | bytes 2097168 | tf_op jit(solution)/shard_map/all_gather | solution.py:904
  107.3 5.0 %out_gradient.1 = (f32[1024,512]{1,0:T(8,128)}, f32[8,1024]{1,0:T(8,128)S(1)}) custom-call(bf16[1024,1024]{1,0:T(8,128)(2,1)} %all-gather.5.cloned.1.call-done.cot_ref, bf16[1024,1920]{1,0:T(8,128)(2,1)} %all-gather.3.cloned.1.call-done.refs_7_.weights_ref, bf16[1024,512]{1,0:T(8,128)(2,1)S(1)} %copy-done.4, s32[1040,128]{1,0:T(8,128)S(1)} %copy-done), custom_call_target="tpu_custom_call" | custom-call | bytes 1048576 | tf_op jit(solution)/shard_map/out_gradient/pallas_call | solution.py:622
  112.3 1.1 collective-permute-start.10
  113.4 0.7 collective-permute-start.11
  114.0 3.2 %collective-permute-start.9 = (f32[2,1024]{1,0:T(2,128)S(1)}, f32[2,1024]{1,0:T(2,128)S(1)}, u32[]{:S(2)}, u32[]{:S(2)}) collective-permute-start(f32[2,1024]{1,0:T(2,128)S(1)} %pad_maximum_fusion.5), channel_id=1, source_target_pairs={{0,3},{1,0},{2,1},{3,2},{4,7},{5,4},{6,5},{7,6},{8,11},{9,8},{10,9... | collective-permute-start | bytes 24584 | tf_op jit(solution)/shard_map/ppermute | solution.py:838
  117.2 1.8 collective-permute-done.11
  119.0 24.1 %backward.1 = (bf16[1024,1024]{1,0:T(8,128)(2,1)}, bf16[1024,384]{1,0:T(8,128)(2,1)}, bf16[1024,1024]{1,0:T(8,128)(2,1)}, bf16[1024,512]{1,0:T(8,128)(2,1)}, f32...) custom-call(f32[8,1024]{1,0:T(8,128)S(1)} %pad.29.stat_ref, ...), custom_call_target="tpu_custom_call" | custom-call | bytes 1048576 | tf_op jit(solution)/shard_map/backward/pallas_call | solution.py:700
  143.1 6.1 %weight_gradients_xz.1 = bf16[1024,1024]{1,0:T(8,128)(2,1)} custom-call(bf16[1024,1024]{1,0:T(8,128)(2,1)} %get-tuple-element.96.tokens_ref, bf16[1024,1024]{1,0:T(8,128)(2,1)} %get-tuple-element.99.grads_ref), custom_call_target="tpu_custom_call" | custom-call | bytes 1048576 | tf_op jit(solution)/shard_map/weight_gradients_xz/pallas_call | solution.py:660
  149.3 1.3 dynamic-slice_bitcast_fusion
  150.8 2.6 %collective-permute-done.18 = bf16[2,2,128,1024]{3,2,1,0:T(8,128)(2,1)} collective-permute-done((bf16[2,2,128,1024]{3,2,1,0:T(8,128)(2,1)S(1)}, bf16[2,2,128,1024]{3,2,1,0:T(8,128)(2,1)}, u32[]{:S(2)}, u32[]{:S(2)}) %collective-permute-start.18) | collective-permute-done | bytes 1048608 | tf_op jit(solution)/shard_map/ppermute | solution.py:827
  153.5 1.9 fusion
  155.5 5.7 %weight_gradients_out.1 = bf16[1024,896]{1,0:T(8,128)(2,1)} custom-call(bf16[1024,1024]{1,0:T(8,128)(2,1)} %all-gather.5.cloned.1.call-done.cot_ref, bf16[1024,512]{1,0:T(8,128)(2,1)S(1)} %copy-done.3, bf16[1024,1024]{1,0:T(8,128)(2,1)} %get-tuple-element.96.tokens_ref, bf16[1024,384]{1,0:T(8,128)(2,1)S(1)} %copy-done.5), custom_call_target="tpu_custom_call" | custom-call | bytes 1048576 | tf_op jit(solution)/shard_map/weight_gradients_out/pallas_call | solution.py:670
  161.2 1.3 constant_dynamic-slice_fusion.1
  162.4 1.0 pad_maximum_fusion
  163.6 1.6 collective-permute-start.19
  165.4 12.6 %collective-permute-done.19 = bf16[2,128,1024]{2,1,0:T(8,128)(2,1)} collective-permute-done((bf16[2,128,1024]{2,1,0:T(8,128)(2,1)S(1)}, bf16[2,128,1024]{2,1,0:T(8,128)(2,1)}, u32[]{:S(2)}, u32[]{:S(2)}) %collective-permute-start.19) | collective-permute-done | bytes 524320 | tf_op jit(solution)/shard_map/ppermute | solution.py:827
  178.0 1.2 fusion.2
  179.3 0.7 dynamic-slice_bitcast_fusion.2
  180.0 1.5 collective-permute-start.20
  181.5 0.8 slice.152
  182.3 1.3 slice.154
  184.0 0.6 collective-permute-start.13
  184.6 4.9 %collective-permute-done.20 = bf16[128,1024]{1,0:T(8,128)(2,1)} collective-permute-done((bf16[128,1024]{1,0:T(8,128)(2,1)}, bf16[128,1024]{1,0:T(8,128)(2,1)}, u32[]{:S(2)}, u32[]{:S(2)}) %collective-permute-start.20) | collective-permute-done | bytes 262176 | tf_op jit(solution)/shard_map/ppermute | solution.py:827
  189.5 1.0 convert_add_fusion.4
  190.6 0.8 fusion.10
  191.4 7.1 %collective-permute-done.13 = bf16[272,896]{1,0:T(8,128)(2,1)} collective-permute-done((bf16[272,896]{1,0:T(8,128)(2,1)S(1)}, bf16[272,896]{1,0:T(8,128)(2,1)}, u32[]{:S(2)}, u32[]{:S(2)}) %collective-permute-start.13) | collective-permute-done | bytes 487456 | tf_op jit(solution)/shard_map/ppermute | solution.py:820
  198.5 0.8 slice.155
  199.4 1.1 slice.157
  200.7 1.5 collective-permute-start.14
  202.2 1.0 fusion.4
  203.2 4.3 %collective-permute-done.14 = bf16[144,896]{1,0:T(8,128)(2,1)S(1)} collective-permute-done((bf16[144,896]{1,0:T(8,128)(2,1)S(1)}, bf16[144,896]{1,0:T(8,128)(2,1)S(1)}, u32[]{:S(2)}, u32[]{:S(2)}) %collective-permute-start.14) | collective-permute-done | bytes 258080 | tf_op jit(solution)/shard_map/ppermute | solution.py:820
  208.2 3.4 %collective-permute-start.15 = (bf16[280,128]{1,0:T(8,128)(2,1)S(1)}, bf16[280,128]{1,0:T(8,128)(2,1)S(1)}, u32[]{:S(2)}, u32[]{:S(2)}) collective-permute-start(bf16[280,128]{1,0:T(8,128)(2,1)S(1)} %fusion.5), channel_id=1, source_target_pairs={{0,3},{1,0},{2,1},{3,2},{4,7},{5,4},{6,5},{7,6},{8,11},{9,8},{10,9... | collective-permute-start | bytes 215048 | tf_op jit(solution)/shard_map/ppermute | solution.py:838
  213.2 0.7 slice.176
  214.1 0.6 reduce_sum.9
  214.7 0.6 slice.141
  215.3 0.7 copy.46
  216.0 1.8 collective-permute-done.17
  217.8 0.7 reshape.143
  220.3 1.0 copy-done.6
  221.3 1.3 finish.1
  (128 shorter events, 6.6 us)
Async XLA Ops:
  7.2 52.0 %copy-start.14 = (s32[1,256]{1,0:T(1,128)S(1)}, s32[1,256]{1,0:T(1,128)}, u32[]{:S(2)}) copy-start(s32[1,256]{1,0:T(1,128)} %param.18) | copy-start | bytes 3076
  7.2 52.0 %copy-start.15 = (f32[512]{0:T(512)S(1)}, f32[512]{0:T(512)}, u32[]{:S(2)}) copy-start(f32[512]{0:T(512)} %param.26) | copy-start | bytes 6148
  7.2 52.0 %copy-start.13 = (f32[4,512]{1,0:T(4,128)S(1)}, f32[4,512]{1,0:T(4,128)}, u32[]{:S(2)}) copy-start(f32[4,512]{1,0:T(4,128)} %param.25) | copy-start | bytes 24580
  7.2 52.1 %copy-start.16 = (f32[8]{0:T(128)S(1)}, f32[8]{0:T(128)}, u32[]{:S(2)}) copy-start(f32[8]{0:T(128)} %param.30) | copy-start | bytes 100
  7.2 52.1 %copy-start.17 = (f32[8]{0:T(128)S(1)}, f32[8]{0:T(128)}, u32[]{:S(2)}) copy-start(f32[8]{0:T(128)} %param.29) | copy-start | bytes 100
  7.2 52.4 %all-gather.3.cloned.1.call-start = ((), (), s32[]{:S(2)}) async-start(), calls=%async_computation.2 | async-start | bytes 4423680 | tf_op jit(solution)/shard_map/all_gather | solution.py:885
  8.1 0.9 copy-start.7
  9.0 0.9 copy-start.8
  9.9 0.9 copy-start.9
  10.9 0.8 copy-start.10
  12.6 94.7 %all-gather.5.cloned.1.call-start = ((), (), s32[]{:S(2)}) async-start(), calls=%async_computation.4 | async-start | bytes 2621440 | tf_op jit(solution)/shard_map/all_gather | solution.py:904
  12.6 17.1 %collective-permute-start.6 = (bf16[256,1024]{1,0:T(8,128)(2,1)}, bf16[256,1024]{1,0:T(8,128)(2,1)S(1)}, u32[]{:S(2)}, u32[]{:S(2)}) collective-permute-start(bf16[256,1024]{1,0:T(8,128)(2,1)} %bitcast.74), channel_id=1, source_target_pairs={{1,0},{2,1},{3,2},{5,4},{6,5},{7,6},{9,8},{10,9},{11,10},{13,12},{... | collective-permute-start | bytes 1572872 | tf_op jit(solution)/shard_map/ppermute | solution.py:772
  13.9 17.1 %collective-permute-start.3 = (bf16[256,1024]{1,0:T(8,128)(2,1)}, bf16[256,1024]{1,0:T(8,128)(2,1)S(1)}, u32[]{:S(2)}, u32[]{:S(2)}) collective-permute-start(bf16[256,1024]{1,0:T(8,128)(2,1)} %bitcast.75), channel_id=1, source_target_pairs={{0,1},{1,2},{2,3},{4,5},{5,6},{6,7},{8,9},{9,10},{10,11},{12,13},{... | collective-permute-start | bytes 1572872 | tf_op jit(solution)/shard_map/ppermute | solution.py:771
  29.7 29.9 %copy-start.18 = (bf16[256,1024]{1,0:T(8,128)(2,1)}, bf16[256,1024]{1,0:T(8,128)(2,1)S(1)}, u32[]{:S(2)}) copy-start(bf16[256,1024]{1,0:T(8,128)(2,1)S(1)} %collective-permute-done.6.refs_4_) | copy-start | bytes 1572868
  29.7 15.1 %collective-permute-start.7 = (bf16[256,1024]{1,0:T(8,128)(2,1)S(1)}, bf16[256,1024]{1,0:T(8,128)(2,1)S(1)}, u32[]{:S(2)}, u32[]{:S(2)}) collective-permute-start(bf16[256,1024]{1,0:T(8,128)(2,1)S(1)} %collective-permute-done.6.refs_4_), channel_id=1, source_target_pairs={{1,0},{2,1},{5,4},{6,5},{9,8},{10,9},{13,12},{14,13},{17,16},{18,1... | collective-permute-start | bytes 1572872 | tf_op jit(solution)/shard_map/ppermute | solution.py:772
  31.0 15.1 %collective-permute-start.4 = (bf16[256,1024]{1,0:T(8,128)(2,1)S(1)}, bf16[256,1024]{1,0:T(8,128)(2,1)S(1)}, u32[]{:S(2)}, u32[]{:S(2)}) collective-permute-start(bf16[256,1024]{1,0:T(8,128)(2,1)S(1)} %collective-permute-done.3.refs_2_), channel_id=1, source_target_pairs={{1,2},{2,3},{5,6},{6,7},{9,10},{10,11},{13,14},{14,15},{17,18},{18... | collective-permute-start | bytes 1572872 | tf_op jit(solution)/shard_map/ppermute | solution.py:771
  44.8 14.8 %copy-start.19 = (bf16[256,1024]{1,0:T(8,128)(2,1)}, bf16[256,1024]{1,0:T(8,128)(2,1)S(1)}, u32[]{:S(2)}) copy-start(bf16[256,1024]{1,0:T(8,128)(2,1)S(1)} %collective-permute-done.7.refs_5_) | copy-start | bytes 1572868
  44.8 14.3 %collective-permute-start.8 = (bf16[256,1024]{1,0:T(8,128)(2,1)S(1)}, bf16[256,1024]{1,0:T(8,128)(2,1)S(1)}, u32[]{:S(2)}, u32[]{:S(2)}) collective-permute-start(bf16[256,1024]{1,0:T(8,128)(2,1)S(1)} %collective-permute-done.7.refs_5_), channel_id=1, source_target_pairs={{1,0},{5,4},{9,8},{13,12},{17,16},{21,20},{25,24},{29,28}} | collective-permute-start | bytes 1572872 | tf_op jit(solution)/shard_map/ppermute | solution.py:772
  46.1 13.0 %collective-permute-start.5 = (bf16[256,1024]{1,0:T(8,128)(2,1)S(1)}, bf16[256,1024]{1,0:T(8,128)(2,1)S(1)}, u32[]{:S(2)}, u32[]{:S(2)}) collective-permute-start(bf16[256,1024]{1,0:T(8,128)(2,1)S(1)} %collective-permute-done.4.refs_1_), channel_id=1, source_target_pairs={{2,3},{6,7},{10,11},{14,15},{18,19},{22,23},{26,27},{30,31}} | collective-permute-start | bytes 1572872 | tf_op jit(solution)/shard_map/ppermute | solution.py:771
  46.8 12.6 %collective-permute-start.2 = (s32[256]{0:T(256)}, s32[256]{0:T(256)S(1)}, u32[]{:S(2)}, u32[]{:S(2)}) collective-permute-start(s32[256]{0:T(256)} %bitcast.92), channel_id=1, source_target_pairs={{0,1},{1,2},{2,3},{3,0},{4,5},{5,6},{6,7},{7,4},{8,9},{9,10},{10,1... | collective-permute-start | bytes 3080 | tf_op jit(solution)/shard_map/ppermute | solution.py:838
  49.5 9.8 %collective-permute-start.1 = (s32[256]{0:T(256)}, s32[256]{0:T(256)S(1)}, u32[]{:S(2)}, u32[]{:S(2)}) collective-permute-start(s32[256]{0:T(256)} %bitcast.93), channel_id=1, source_target_pairs={{0,2},{1,3},{2,0},{3,1},{4,6},{5,7},{6,4},{7,5},{8,10},{9,11},{10,... | collective-permute-start | bytes 3080 | tf_op jit(solution)/shard_map/ppermute | solution.py:838
  52.7 6.7 %collective-permute-start = (s32[256]{0:T(256)}, s32[256]{0:T(256)S(1)}, u32[]{:S(2)}, u32[]{:S(2)}) collective-permute-start(s32[256]{0:T(256)} %bitcast.94), channel_id=1, source_target_pairs={{0,3},{1,0},{2,1},{3,2},{4,7},{5,4},{6,5},{7,6},{8,11},{9,8},{10,9... | collective-permute-start | bytes 3080 | tf_op jit(solution)/shard_map/ppermute | solution.py:838
  59.1 0.8 copy-start.20
  59.2 96.3 %reduce-scatter.3.cloned.1.call-start = ((), (), s32[]{:S(2)}) async-start(), calls=%async_computation.3 | async-start | bytes 2621440 | tf_op jit(solution)/shard_map/reduce_scatter | solution.py:912
  87.3 19.9 %copy-start = (s32[1040,128]{1,0:T(8,128)S(1)}, s32[1040,128]{1,0:T(8,128)}, u32[]{:S(2)}) copy-start(s32[1040,128]{1,0:T(8,128)} %broadcast_in_dim.34.window_ref) | copy-start | bytes 1597444
  87.3 19.9 %copy-start.4 = (bf16[1024,512]{1,0:T(8,128)(2,1)S(1)}, bf16[1024,512]{1,0:T(8,128)(2,1)}, u32[]{:S(2)}) copy-start(bf16[1024,512]{1,0:T(8,128)(2,1)} %get-tuple-element.64.scaled_ref) | copy-start | bytes 3145732
  87.4 132.9 %reduce-scatter.5.cloned.1.call-start = ((), (), s32[]{:S(2)}) async-start(), calls=%async_computation.5 | async-start | bytes 2621440 | tf_op jit(solution)/shard_map/reduce_scatter | solution.py:923
  112.3 5.0 %collective-permute-start.10 = (f32[2,1024]{1,0:T(2,128)S(1)}, f32[2,1024]{1,0:T(2,128)S(1)}, u32[]{:S(2)}, u32[]{:S(2)}) collective-permute-start(f32[2,1024]{1,0:T(2,128)S(1)} %pad_maximum_fusion.5), channel_id=1, source_target_pairs={{0,2},{1,3},{2,0},{3,1},{4,6},{5,7},{6,4},{7,5},{8,10},{9,11},{10,... | collective-permute-start | bytes 24584 | tf_op jit(solution)/shard_map/ppermute | solution.py:838
  113.4 5.6 %collective-permute-start.11 = (f32[2,1024]{1,0:T(2,128)S(1)}, f32[2,1024]{1,0:T(2,128)S(1)}, u32[]{:S(2)}, u32[]{:S(2)}) collective-permute-start(f32[2,1024]{1,0:T(2,128)S(1)} %pad_maximum_fusion.5), channel_id=1, source_target_pairs={{0,1},{1,2},{2,3},{3,0},{4,5},{5,6},{6,7},{7,4},{8,9},{9,10},{10,1... | collective-permute-start | bytes 24584 | tf_op jit(solution)/shard_map/ppermute | solution.py:838
  114.0 5.0 %collective-permute-start.9 = (f32[2,1024]{1,0:T(2,128)S(1)}, f32[2,1024]{1,0:T(2,128)S(1)}, u32[]{:S(2)}, u32[]{:S(2)}) collective-permute-start(f32[2,1024]{1,0:T(2,128)S(1)} %pad_maximum_fusion.5), channel_id=1, source_target_pairs={{0,3},{1,0},{2,1},{3,2},{4,7},{5,4},{6,5},{7,6},{8,11},{9,8},{10,9... | collective-permute-start | bytes 24584 | tf_op jit(solution)/shard_map/ppermute | solution.py:838
  150.6 4.9 %copy-start.3 = (bf16[1024,512]{1,0:T(8,128)(2,1)S(1)}, bf16[1024,512]{1,0:T(8,128)(2,1)}, u32[]{:S(2)}) copy-start(bf16[1024,512]{1,0:T(8,128)(2,1)} %get-tuple-element.95.normed_ref) | copy-start | bytes 3145732
  150.6 4.9 %copy-start.5 = (bf16[1024,384]{1,0:T(8,128)(2,1)S(1)}, bf16[1024,384]{1,0:T(8,128)(2,1)}, u32[]{:S(2)}) copy-start(bf16[1024,384]{1,0:T(8,128)(2,1)} %get-tuple-element.97.grads_ref) | copy-start | bytes 2359300
  150.6 2.9 %collective-permute-start.18 = (bf16[2,2,128,1024]{3,2,1,0:T(8,128)(2,1)S(1)}, bf16[2,2,128,1024]{3,2,1,0:T(8,128)(2,1)}, u32[]{:S(2)}, u32[]{:S(2)}) collective-permute-start(bf16[2,2,128,1024]{3,2,1,0:T(8,128)(2,1)S(1)} %dynamic-slice_bitcast_fusion), channel_id=1, source_target_pairs={{0,4},{4,0},{8,12},{12,8},{16,20},{20,16},{24,28},{28,24},{1,5},{5... | collective-permute-start | bytes 3145736 | tf_op jit(solution)/shard_map/ppermute | solution.py:827
  163.5 18.0 %collective-permute-start.12 = (bf16[528,896]{1,0:T(8,128)(2,1)}, bf16[528,896]{1,0:T(8,128)(2,1)}, u32[]{:S(2)}, u32[]{:S(2)}) collective-permute-start(bf16[528,896]{1,0:T(8,128)(2,1)} %pad_maximum_fusion), channel_id=1, source_target_pairs={{0,4},{4,0},{8,12},{12,8},{16,20},{20,16},{24,28},{28,24},{1,5},{5... | collective-permute-start | bytes 2838536 | tf_op jit(solution)/shard_map/ppermute | solution.py:820
  163.6 14.4 %collective-permute-start.19 = (bf16[2,128,1024]{2,1,0:T(8,128)(2,1)S(1)}, bf16[2,128,1024]{2,1,0:T(8,128)(2,1)}, u32[]{:S(2)}, u32[]{:S(2)}) collective-permute-start(bf16[2,128,1024]{2,1,0:T(8,128)(2,1)S(1)} %dynamic-slice_bitcast_fusion.1), channel_id=1, source_target_pairs={{0,16},{4,20},{8,24},{12,28},{16,0},{20,4},{24,8},{28,12},{1,17},{... | collective-permute-start | bytes 1572872 | tf_op jit(solution)/shard_map/ppermute | solution.py:827
  165.2 18.3 %copy-start.11 = (bf16[1024,896]{1,0:T(8,128)(2,1)S(1)}, bf16[1024,896]{1,0:T(8,128)(2,1)}, u32[]{:S(2)}) copy-start(bf16[1024,896]{1,0:T(8,128)(2,1)} %weight_gradients_out.1) | copy-start | bytes 5505028
  180.0 9.5 %collective-permute-start.20 = (bf16[128,1024]{1,0:T(8,128)(2,1)}, bf16[128,1024]{1,0:T(8,128)(2,1)}, u32[]{:S(2)}, u32[]{:S(2)}) collective-permute-start(bf16[128,1024]{1,0:T(8,128)(2,1)} %dynamic-slice_bitcast_fusion.2), channel_id=1, source_target_pairs={{0,8},{4,12},{8,0},{12,4},{16,24},{20,28},{24,16},{28,20},{1,9},{5... | collective-permute-start | bytes 786440 | tf_op jit(solution)/shard_map/ppermute | solution.py:827
  184.0 14.6 %collective-permute-start.13 = (bf16[272,896]{1,0:T(8,128)(2,1)S(1)}, bf16[272,896]{1,0:T(8,128)(2,1)}, u32[]{:S(2)}, u32[]{:S(2)}) collective-permute-start(bf16[272,896]{1,0:T(8,128)(2,1)S(1)} %pad_maximum_fusion.1), channel_id=1, source_target_pairs={{0,8},{4,12},{8,0},{12,4},{16,24},{20,28},{24,16},{28,20},{1,9},{5... | collective-permute-start | bytes 1462280 | tf_op jit(solution)/shard_map/ppermute | solution.py:820
  190.6 11.7 %copy-start.2 = (bf16[1,256,1024]{2,1,0:T(8,128)(2,1)S(1)}, bf16[1,256,1024]{2,1,0:T(8,128)(2,1)}, u32[]{:S(2)}) copy-start(bf16[1,256,1024]{2,1,0:T(8,128)(2,1)} %param.17) | copy-start | bytes 1572868
  190.6 11.7 %copy-start.12 = (bf16[256,1024]{1,0:T(8,128)(2,1)S(1)}, bf16[256,1024]{1,0:T(8,128)(2,1)}, u32[]{:S(2)}) copy-start(bf16[256,1024]{1,0:T(8,128)(2,1)} %reduce-scatter.3.cloned.1.call-done) | copy-start | bytes 1572868
  200.7 6.8 %collective-permute-start.14 = (bf16[144,896]{1,0:T(8,128)(2,1)S(1)}, bf16[144,896]{1,0:T(8,128)(2,1)S(1)}, u32[]{:S(2)}, u32[]{:S(2)}) collective-permute-start(bf16[144,896]{1,0:T(8,128)(2,1)S(1)} %pad_maximum_fusion.2), channel_id=1, source_target_pairs={{0,16},{4,20},{8,24},{12,28},{16,0},{20,4},{24,8},{28,12},{1,17},{... | collective-permute-start | bytes 774152 | tf_op jit(solution)/shard_map/ppermute | solution.py:820
  203.2 17.0 %copy-start.1 = (bf16[1,256,1024]{2,1,0:T(8,128)(2,1)S(1)}, bf16[1,256,1024]{2,1,0:T(8,128)(2,1)}, u32[]{:S(2)}) copy-start(bf16[1,256,1024]{2,1,0:T(8,128)(2,1)} %param.19) | copy-start | bytes 1572868
  207.7 8.2 %collective-permute-start.16 = (bf16[280,128]{1,0:T(8,128)(2,1)S(1)}, bf16[280,128]{1,0:T(8,128)(2,1)S(1)}, u32[]{:S(2)}, u32[]{:S(2)}) collective-permute-start(bf16[280,128]{1,0:T(8,128)(2,1)S(1)} %fusion.5), channel_id=1, source_target_pairs={{0,2},{1,3},{2,0},{3,1},{4,6},{5,7},{6,4},{7,5},{8,10},{9,11},{10,... | collective-permute-start | bytes 215048 | tf_op jit(solution)/shard_map/ppermute | solution.py:838
  208.2 7.8 %collective-permute-start.15 = (bf16[280,128]{1,0:T(8,128)(2,1)S(1)}, bf16[280,128]{1,0:T(8,128)(2,1)S(1)}, u32[]{:S(2)}, u32[]{:S(2)}) collective-permute-start(bf16[280,128]{1,0:T(8,128)(2,1)S(1)} %fusion.5), channel_id=1, source_target_pairs={{0,3},{1,0},{2,1},{3,2},{4,7},{5,4},{6,5},{7,6},{8,11},{9,8},{10,9... | collective-permute-start | bytes 215048 | tf_op jit(solution)/shard_map/ppermute | solution.py:838
  211.6 6.1 %collective-permute-start.17 = (bf16[280,128]{1,0:T(8,128)(2,1)S(1)}, bf16[280,128]{1,0:T(8,128)(2,1)S(1)}, u32[]{:S(2)}, u32[]{:S(2)}) collective-permute-start(bf16[280,128]{1,0:T(8,128)(2,1)S(1)} %fusion.5), channel_id=1, source_target_pairs={{0,1},{1,2},{2,3},{3,0},{4,5},{5,6},{6,7},{7,4},{8,9},{9,10},{10,1... | collective-permute-start | bytes 215048 | tf_op jit(solution)/shard_map/ppermute | solution.py:838
  220.3 1.0 copy-start.6
Sparse Core Ops, SparseCore 0:
  12.7 38.3 all-gather.2
  59.3 47.9 all-gather.4
  109.6 42.7 reduce-scatter.2
  165.3 44.2 reduce-scatter.4

commit v10 on v8

--- a/solution.py
+++ b/solution.py
@@ -640,42 +640,32 @@
     )(cot, weights, scaled, window)
 
 
-def first_kernel(width, cot_ref, normed_ref, tokens_ref, grads_ref, sum_ref):
-    sum_ref[:, :width] = dot_tn(cot_ref[...], normed_ref[...]).astype(BF16)
-    sum_ref[:, width:] = dot_tn(tokens_ref[...], grads_ref[...]).astype(BF16)
-
-
-def second_kernel(tokens_ref, grads_ref, sum_ref):
-    sum_ref[...] = dot_tn(tokens_ref[...], grads_ref[...]).astype(BF16)
+def weights_kernel(width, cot_ref, normed_ref, tokens_ref, grads_ref, first_ref, second_ref):
+    tokens = tokens_ref[...]
+    first_ref[:, :width] = dot_tn(cot_ref[...], normed_ref[...]).astype(BF16)
+    first_ref[:, width:] = dot_tn(tokens, grads_ref[:, 2 * width :]).astype(BF16)
+    second_ref[...] = dot_tn(tokens, grads_ref[:, : 2 * width]).astype(BF16)
 
 
 def run_weights(cot, normed, tokens, grads):
     length, features = tokens.shape
     width = normed.shape[1]
-    rest = grads.shape[1] - 2 * width
-    params = pltpu.CompilerParams(vmem_limit_bytes=VMEM_LIMIT)
-    strip = pl.BlockSpec((length, Q), lambda i: (0, i))
-    second = pl.pallas_call(
-        second_kernel,
+    columns = [grads.shape[1] - width, 2 * width]
+    return pl.pallas_call(
+        functools.partial(weights_kernel, width),
         grid=(features // Q,),
-        in_specs=[strip, pl.BlockSpec((length, 2 * width), lambda i: (0, 0))],
-        out_specs=pl.BlockSpec((Q, 2 * width), lambda i: (i, 0)),
-        out_shape=jax.ShapeDtypeStruct((features, 2 * width), BF16),
-        compiler_params=params,
-        cost_estimate=cost(4),
-        name="weight_gradients_xz",
-    )(tokens, grads)
-    first = pl.pallas_call(
-        functools.partial(first_kernel, width),
-        grid=(features // Q,),
-        in_specs=[strip, whole(normed.shape), strip, whole((length, rest))],
-        out_specs=pl.BlockSpec((Q, width + rest), lambda i: (i, 0)),
-        out_shape=jax.ShapeDtypeStruct((features, width + rest), BF16),
-        compiler_params=params,
-        cost_estimate=cost(4),
-        name="weight_gradients_out",
-    )(cot, normed, tokens, grads[:, 2 * width :])
-    return first, second
+        in_specs=[
+            pl.BlockSpec((length, Q), lambda i: (0, i)),
+            whole(normed.shape),
+            pl.BlockSpec((length, Q), lambda i: (0, i)),
+            whole(grads.shape),
+        ],
+        out_specs=[pl.BlockSpec((Q, count), lambda i: (i, 0)) for count in columns],
+        out_shape=[jax.ShapeDtypeStruct((features, count), BF16) for count in columns],
+        compiler_params=pltpu.CompilerParams(vmem_limit_bytes=VMEM_LIMIT),
+        cost_estimate=cost(7),
+        name="weight_gradients",
+    )(cot, normed, tokens, grads)
 
 
 def run_backward(
@@ -796,7 +786,7 @@
     orders = [bits, bits[:1] + bits[:0:-1]]
     parts = [part.reshape((2,) * len(bits) + (-1, part.shape[1])) for part in (first, second)]
     left = [bits[::-1], bits[::-1]]
-    came = [None, None]
+    came = []
     for step in range(len(bits)):
         for index in range(2):
             part = parts[index]
@@ -822,7 +812,7 @@
                 small = small + rider.astype(F32)
             else:
                 moved = other = lax.ppermute(send, axis, pairs)
-            came[index] = moved
+            came.append(moved)
             part = keep.astype(F32) + other.astype(F32)
             left[index] = [other_bit for other_bit in left[index] if other_bit != bit]
             parts[index] = part.astype(BF16) if left[index] else part
@@ -941,7 +931,7 @@
     scale_here = lax.dynamic_slice_in_dim(out_scale, axis_place * local, local, 0)[:, None]
     layer_out = (hidden_rows + out_sum.astype(F32) * scale_here).astype(BF16)
 
-    grad_hidden = run_finish(in_sum, hidden_local, cotangent[0], after(gain, came[1]))
+    grad_hidden = run_finish(in_sum, hidden_local, cotangent[0], after(gain, shared))
 
     return (
         layer_out[None],

time: 230 us -> 225 us (0.978)
  waiting for transfers between devices: 80.1 us -> 72.5 us
  local copies, waits for them, and re-layouts: 21.8 us -> 26.7 us
  Pallas kernels: 69.5 us -> 65.9 us
    reduce_scatter x1, waiting for transfers between devices: 4.78 us -> 0.01 us  [shards(): lax.psum_scatter(in_part, 'tensor', scatter_dimension=0, tiled=True)]
    ppermute x3, waiting for transfers between devices: 4.57 us -> 0.01 us  [cube_scatter(): moved = other = lax.ppermute(send, axis, pairs)]
    pallas_call x2 -> x1, Pallas kernels: 11.8 us -> 8.28 us  [run_weights(): pl.pallas_call(functools.partial(weights_kernel, width), grid=(features /...]
    slice x6, local copies, waits for them, and re-layouts: 0.17 us -> 2.88 us  [cube_scatter(): rider = moved[rows:].reshape(-1)[:small.size].reshape(small.shape)]
    unnamed x50 -> x62, local copies, waits for them, and re-layouts: 7.57 us -> 9.06 us
  transfers between devices with their start and end apart: 25 -> 25, of which waited for: 13 -> 11; matrix products, arithmetic and copies ran while one was open for 8% -> 11% of each run, Pallas kernels for 27% -> 25%
where the time goes in v10:
time: 225 us; the launch traced here: 224 us
  waiting for transfers between devices  72.5 us (32%)
  Pallas kernels  65.9 us (29%)
  starting transfers between devices  34.6 us (15%)
  local copies, waits for them, and re-layouts  26.7 us (12%)
  between operations  14.5 us (6%)
  other arithmetic  9.79 us (4%)
    ppermute x3, waiting for transfers between devices, line_step(): lax.ppermute(left, axis, [(i, i - 1) for i in range(1, n - step + 1)])  24.7 us
    pallas_call x1, Pallas kernels, run_backward(): pl.pallas_call(functools.partial(backward_kernel, heads, size, full_inner...  24.1 us
    all_gather x1, waiting for transfers between devices, shards(): lax.all_gather(after(cotangent[0], near_hidden[0], near_hidden[-1]), 'ten...  19.8 us
    pallas_call x1, Pallas kernels, run_forward(): pl.pallas_call(functools.partial(forward_kernel, heads, size), grid=(bloc...  18 us
    ppermute x9, starting transfers between devices, around(): lax.ppermute(values, axis, [(i, (i - k) % n) for i in range(n)])  17.5 us
    ppermute x3, waiting for transfers between devices, cube_scatter(): lax.ppermute(jnp.concatenate([send.reshape(rows, columns), rider]), axis,...  11.7 us
    unnamed x62, local copies, waits for them, and re-layouts  9.06 us
    reduce_scatter x1, waiting for transfers between devices, shards(): lax.psum_scatter(out_part, 'tensor', scatter_dimension=0, tiled=True)  8.99 us
  transfers between devices with their start and end apart: 25, of which 11 were waited for; matrix products, arithmetic and copies ran while one was open for 11% of the time, Pallas kernels for 25%

profile of v10, /device:TPU:0, one launch (start us, length us, event | category | flops | bytes accessed | tf_op | source)
XLA Modules:
  0.0 223.9 jit_solution(69794499247755008)
XLA Ops:
  7.3 0.7 pad_maximum_fusion.6
  8.1 0.9 copy-done.4
  9.0 0.9 copy-done.5
  10.0 0.9 copy-done.6
  10.9 0.8 copy-done.7
  11.7 0.9 pack.1
  12.6 1.3 collective-permute-start.6
  13.9 5.6 %collective-permute-start.3 = (bf16[256,1024]{1,0:T(8,128)(2,1)}, bf16[256,1024]{1,0:T(8,128)(2,1)S(1)}, u32[]{:S(2)}, u32[]{:S(2)}) collective-permute-start(bf16[256,1024]{1,0:T(8,128)(2,1)} %bitcast.75), channel_id=1, source_target_pairs={{0,1},{1,2},{2,3},{4,5},{5,6},{6,7},{8,9},{9,10},{10,11},{12,13},{... | collective-permute-start | bytes 1572872 | tf_op jit(solution)/shard_map/ppermute | solution.py:758
  19.5 10.2 %collective-permute-done.6.refs_4_ = bf16[256,1024]{1,0:T(8,128)(2,1)S(1)} collective-permute-done((bf16[256,1024]{1,0:T(8,128)(2,1)}, bf16[256,1024]{1,0:T(8,128)(2,1)S(1)}, u32[]{:S(2)}, u32[]{:S(2)}) %collective-permute-start.6) | collective-permute-done | bytes 524320 | tf_op jit(solution)/shard_map/ppermute | solution.py:759
  29.7 1.3 collective-permute-start.7
  31.0 0.7 collective-permute-start.4
  31.7 13.1 %collective-permute-done.7.refs_5_ = bf16[256,1024]{1,0:T(8,128)(2,1)S(1)} collective-permute-done((bf16[256,1024]{1,0:T(8,128)(2,1)S(1)}, bf16[256,1024]{1,0:T(8,128)(2,1)S(1)}, u32[]{:S(2)}, u32[]{:S(2)}) %collective-permute-start.7) | collective-permute-done | bytes 524320 | tf_op jit(solution)/shard_map/ppermute | solution.py:759
  44.8 1.3 collective-permute-start.8
  46.1 0.7 collective-permute-start.5
  46.8 2.7 %collective-permute-start.2 = (s32[256]{0:T(256)}, s32[256]{0:T(256)S(1)}, u32[]{:S(2)}, u32[]{:S(2)}) collective-permute-start(s32[256]{0:T(256)} %bitcast.92), channel_id=1, source_target_pairs={{0,1},{1,2},{2,3},{3,0},{4,5},{5,6},{6,7},{7,4},{8,9},{9,10},{10,1... | collective-permute-start | bytes 3080 | tf_op jit(solution)/shard_map/ppermute | solution.py:825
  49.5 3.1 %collective-permute-start.1 = (s32[256]{0:T(256)}, s32[256]{0:T(256)S(1)}, u32[]{:S(2)}, u32[]{:S(2)}) collective-permute-start(s32[256]{0:T(256)} %bitcast.93), channel_id=1, source_target_pairs={{0,2},{1,3},{2,0},{3,1},{4,6},{5,7},{6,4},{7,5},{8,10},{9,11},{10,... | collective-permute-start | bytes 3080 | tf_op jit(solution)/shard_map/ppermute | solution.py:825
  52.7 2.8 %collective-permute-start = (s32[256]{0:T(256)}, s32[256]{0:T(256)S(1)}, u32[]{:S(2)}, u32[]{:S(2)}) collective-permute-start(s32[256]{0:T(256)} %bitcast.94), channel_id=1, source_target_pairs={{0,3},{1,0},{2,1},{3,2},{4,7},{5,4},{6,5},{7,6},{8,11},{9,8},{10,9... | collective-permute-start | bytes 3080 | tf_op jit(solution)/shard_map/ppermute | solution.py:825
  55.5 0.7 broadcast_in_dim.39
  56.3 0.7 pad_maximum_fusion.7.channel_ref
  57.0 0.7 pad_maximum_fusion.4.kernel_bc_ref
  57.7 1.4 collective-permute-done.8.refs_6_
  60.0 8.4 %project.1 = (bf16[1024,1024]{1,0:T(8,128)(2,1)}, bf16[1024,1024]{1,0:T(8,128)(2,1)}, f32[1024,512]{1,0:T(8,128)}, f32[1024,512]{1,0:T(8,128)}, f32[1024,384]{1,0:T(8,128)}, /*index=5*/f32[8,1024]{1,0:T(8,128)S(1)}) custom-call(s32[1]{0:T(128)} %bitcast.8.place_ref, bf16[256,1024]{1,0:T(8,128)(2,1)S(1)} %collective-permute-done.5.refs_0_, ...), custom_call_target="tpu_custom_call" | custom-call | flops 8000000000 | bytes 1048576 | tf_op jit(solution)/shard_map/project/pallas_call | solution.py:520
  68.3 1.0 broadcast_in_dim.34.window_ref
  69.4 18.0 %forward.1 = (bf16[1024,512]{1,0:T(8,128)(2,1)}, bf16[1024,1024]{1,0:T(8,128)(2,1)}, f32[8,1024]{1,0:T(8,128)S(1)}, f32[4,128,512]{2,1,0:T(8,128)}, f32[4,8,512]...) custom-call(s32[1040,128]{1,0:T(8,128)} %broadcast_in_dim.34.window_, ...), custom_call_target="tpu_custom_call" | custom-call | flops 14000000000 | bytes 1048576 | tf_op jit(solution)/shard_map/forward/pallas_call | solution.py:581
  87.5 19.8 %all-gather.5.cloned.1.call-done.cot_ref = bf16[1024,1024]{1,0:T(8,128)(2,1)} async-done(((bf16[256,1024]{1,0:T(8,128)(2,1)}), bf16[1024,1024]{1,0:T(8,128)(2,1)}) %all-gather.5.cloned.1.call-update) | async-done | bytes 2097168 | tf_op jit(solution)/shard_map/all_gather | solution.py:891
  107.3 5.0 %out_gradient.1 = (f32[1024,512]{1,0:T(8,128)}, f32[8,1024]{1,0:T(8,128)S(1)}) custom-call(bf16[1024,1024]{1,0:T(8,128)(2,1)} %all-gather.5.cloned.1.call-done.cot_ref, bf16[1024,1920]{1,0:T(8,128)(2,1)} %all-gather.3.cloned.1.call-done.refs_7_.weights_ref, bf16[1024,512]{1,0:T(8,128)(2,1)S(1)} %copy-done.9, s32[1040,128]{1,0:T(8,128)S(1)} %copy-done), custom_call_target="tpu_custom_call" | custom-call | flops 5000000000 | bytes 1048576 | tf_op jit(solution)/shard_map/out_gradient/pallas_call | solution.py:620
  112.3 1.1 collective-permute-start.10
  114.0 3.2 %collective-permute-start.9 = (f32[2,1024]{1,0:T(2,128)S(1)}, f32[2,1024]{1,0:T(2,128)S(1)}, u32[]{:S(2)}, u32[]{:S(2)}) collective-permute-start(f32[2,1024]{1,0:T(2,128)S(1)} %pad_maximum_fusion.5), channel_id=1, source_target_pairs={{0,3},{1,0},{2,1},{3,2},{4,7},{5,4},{6,5},{7,6},{8,11},{9,8},{10,9... | collective-permute-start | bytes 24584 | tf_op jit(solution)/shard_map/ppermute | solution.py:825
  117.2 1.8 collective-permute-done.11
  119.0 24.1 %backward.1 = (bf16[1024,1408]{1,0:T(8,128)(2,1)}, bf16[1024,1024]{1,0:T(8,128)(2,1)}, bf16[1024,512]{1,0:T(8,128)(2,1)}, f32[8,512]{1,0:T(8,128)S(1)}, f32[8,25...) custom-call(f32[8,1024]{1,0:T(8,128)S(1)} %pad.29.stat_ref, ...), custom_call_target="tpu_custom_call" | custom-call | flops 2000000000 | bytes 1048576 | tf_op jit(solution)/shard_map/backward/pallas_call | solution.py:689
  143.3 9.0 %reduce-scatter.3.cloned.1.call-done = bf16[256,1024]{1,0:T(8,128)(2,1)} async-done(((bf16[1024,1024]{1,0:T(8,128)(2,1)}), bf16[256,1024]{1,0:T(8,128)(2,1)}) %reduce-scatter.3.cloned.1.call-update) | async-done | bytes 524304 | tf_op jit(solution)/shard_map/reduce_scatter | solution.py:899
  152.3 1.2 copy-done.8
  153.5 8.3 %weight_gradients.1 = (bf16[1024,896]{1,0:T(8,128)(2,1)}, bf16[1024,1024]{1,0:T(8,128)(2,1)}) custom-call(bf16[1024,1024]{1,0:T(8,128)(2,1)} %all-gather.5.cloned.1.call-done.cot_ref, bf16[1024,512]{1,0:T(8,128)(2,1)S(1)} %copy-done.8, bf16[1024,1024]{1,0:T(8,128)(2,1)} %get-tuple-element.96.tokens_ref, bf16[1024,1408]{1,0:T(8,128)(2,1)} %get-tuple-element.98.grads_ref), custom_call_target="tpu_custom_call" | custom-call | flops 7000000000 | bytes 1048576 | tf_op jit(solution)/shard_map/weight_gradients/pallas_call | solution.py:654
  161.8 1.3 constant_dynamic-slice_fusion.1
  163.0 1.0 pad_maximum_fusion
  164.1 0.9 copy-done.10
  165.0 1.1 dynamic-slice_bitcast_fusion
  166.2 0.7 collective-permute-done.12
  166.9 0.8 slice.152
  167.8 1.3 slice.154
  169.5 1.5 collective-permute-start.13
  171.0 1.0 fusion.4
  172.1 1.6 fusion
  173.7 0.8 dynamic-slice_bitcast_fusion.1
  174.5 1.5 collective-permute-start.19
  176.0 6.7 %collective-permute-done.13 = bf16[272,896]{1,0:T(8,128)(2,1)S(1)} collective-permute-done((bf16[272,896]{1,0:T(8,128)(2,1)S(1)}, bf16[272,896]{1,0:T(8,128)(2,1)S(1)}, u32[]{:S(2)}, u32[]{:S(2)}) %collective-permute-start.13) | collective-permute-done | bytes 487456 | tf_op jit(solution)/shard_map/ppermute | solution.py:807
  183.3 1.4 slice.126
  184.7 0.8 convert_bitcast_fusion
  186.1 1.4 reshape.139
  188.3 1.5 collective-permute-start.14
  190.1 1.5 collective-permute-start.20
  191.6 4.3 %collective-permute-done.14 = bf16[144,896]{1,0:T(8,128)(2,1)S(1)} collective-permute-done((bf16[144,896]{1,0:T(8,128)(2,1)S(1)}, bf16[144,896]{1,0:T(8,128)(2,1)S(1)}, u32[]{:S(2)}, u32[]{:S(2)}) %collective-permute-start.14) | collective-permute-done | bytes 258080 | tf_op jit(solution)/shard_map/ppermute | solution.py:807
  195.9 0.7 copy-done.16
  196.7 0.8 convert_add_fusion.7
  197.5 1.0 convert_add_fusion.5
  198.5 1.8 collective-permute-start.16
  200.3 1.2 collective-permute-start.15
  201.5 0.9 collective-permute-start.17
  203.5 0.7 slice.176
  206.2 4.9 %collective-permute-done.16 = bf16[280,128]{1,0:T(8,128)(2,1)S(1)} collective-permute-done((bf16[280,128]{1,0:T(8,128)(2,1)S(1)}, bf16[280,128]{1,0:T(8,128)(2,1)S(1)}, u32[]{:S(2)}, u32[]{:S(2)}) %collective-permute-start.16) | collective-permute-done | bytes 71712 | tf_op jit(solution)/shard_map/ppermute | solution.py:825
  211.7 0.7 reshape.143
  213.6 1.0 copy-done.3
  214.6 1.3 finish.1
  216.5 0.8 fusion.10
  (139 shorter events, 10.4 us)
Async XLA Ops:
  7.2 52.0 %copy-start.20 = (s32[1,256]{1,0:T(1,128)S(1)}, s32[1,256]{1,0:T(1,128)}, u32[]{:S(2)}) copy-start(s32[1,256]{1,0:T(1,128)} %param.18) | copy-start | bytes 3076
  7.2 52.0 %copy-start.21 = (f32[512]{0:T(512)S(1)}, f32[512]{0:T(512)}, u32[]{:S(2)}) copy-start(f32[512]{0:T(512)} %param.26) | copy-start | bytes 6148
  7.2 52.0 %copy-start.19 = (f32[4,512]{1,0:T(4,128)S(1)}, f32[4,512]{1,0:T(4,128)}, u32[]{:S(2)}) copy-start(f32[4,512]{1,0:T(4,128)} %param.25) | copy-start | bytes 24580
  7.2 52.1 %copy-start.22 = (f32[8]{0:T(128)S(1)}, f32[8]{0:T(128)}, u32[]{:S(2)}) copy-start(f32[8]{0:T(128)} %param.30) | copy-start | bytes 100
  7.2 52.1 %copy-start.23 = (f32[8]{0:T(128)S(1)}, f32[8]{0:T(128)}, u32[]{:S(2)}) copy-start(f32[8]{0:T(128)} %param.29) | copy-start | bytes 100
  7.2 52.4 %all-gather.3.cloned.1.call-start = ((), (), s32[]{:S(2)}) async-start(), calls=%async_computation.2 | async-start | bytes 4423680 | tf_op jit(solution)/shard_map/all_gather | solution.py:872
  8.1 0.9 copy-start.4
  9.0 0.9 copy-start.5
  9.9 0.9 copy-start.6
  10.9 0.8 copy-start.7
  12.6 94.7 %all-gather.5.cloned.1.call-start = ((), (), s32[]{:S(2)}) async-start(), calls=%async_computation.4 | async-start | bytes 2621440 | tf_op jit(solution)/shard_map/all_gather | solution.py:891
  12.6 17.1 %collective-permute-start.6 = (bf16[256,1024]{1,0:T(8,128)(2,1)}, bf16[256,1024]{1,0:T(8,128)(2,1)S(1)}, u32[]{:S(2)}, u32[]{:S(2)}) collective-permute-start(bf16[256,1024]{1,0:T(8,128)(2,1)} %bitcast.74), channel_id=1, source_target_pairs={{1,0},{2,1},{3,2},{5,4},{6,5},{7,6},{9,8},{10,9},{11,10},{13,12},{... | collective-permute-start | bytes 1572872 | tf_op jit(solution)/shard_map/ppermute | solution.py:759
  13.9 17.1 %collective-permute-start.3 = (bf16[256,1024]{1,0:T(8,128)(2,1)}, bf16[256,1024]{1,0:T(8,128)(2,1)S(1)}, u32[]{:S(2)}, u32[]{:S(2)}) collective-permute-start(bf16[256,1024]{1,0:T(8,128)(2,1)} %bitcast.75), channel_id=1, source_target_pairs={{0,1},{1,2},{2,3},{4,5},{5,6},{6,7},{8,9},{9,10},{10,11},{12,13},{... | collective-permute-start | bytes 1572872 | tf_op jit(solution)/shard_map/ppermute | solution.py:758
  29.7 29.9 %copy-start.24 = (bf16[256,1024]{1,0:T(8,128)(2,1)}, bf16[256,1024]{1,0:T(8,128)(2,1)S(1)}, u32[]{:S(2)}) copy-start(bf16[256,1024]{1,0:T(8,128)(2,1)S(1)} %collective-permute-done.6.refs_4_) | copy-start | bytes 1572868
  29.7 15.1 %collective-permute-start.7 = (bf16[256,1024]{1,0:T(8,128)(2,1)S(1)}, bf16[256,1024]{1,0:T(8,128)(2,1)S(1)}, u32[]{:S(2)}, u32[]{:S(2)}) collective-permute-start(bf16[256,1024]{1,0:T(8,128)(2,1)S(1)} %collective-permute-done.6.refs_4_), channel_id=1, source_target_pairs={{1,0},{2,1},{5,4},{6,5},{9,8},{10,9},{13,12},{14,13},{17,16},{18,1... | collective-permute-start | bytes 1572872 | tf_op jit(solution)/shard_map/ppermute | solution.py:759
  31.0 15.1 %collective-permute-start.4 = (bf16[256,1024]{1,0:T(8,128)(2,1)S(1)}, bf16[256,1024]{1,0:T(8,128)(2,1)S(1)}, u32[]{:S(2)}, u32[]{:S(2)}) collective-permute-start(bf16[256,1024]{1,0:T(8,128)(2,1)S(1)} %collective-permute-done.3.refs_2_), channel_id=1, source_target_pairs={{1,2},{2,3},{5,6},{6,7},{9,10},{10,11},{13,14},{14,15},{17,18},{18... | collective-permute-start | bytes 1572872 | tf_op jit(solution)/shard_map/ppermute | solution.py:758
  44.8 14.8 %copy-start.25 = (bf16[256,1024]{1,0:T(8,128)(2,1)}, bf16[256,1024]{1,0:T(8,128)(2,1)S(1)}, u32[]{:S(2)}) copy-start(bf16[256,1024]{1,0:T(8,128)(2,1)S(1)} %collective-permute-done.7.refs_5_) | copy-start | bytes 1572868
  44.8 14.3 %collective-permute-start.8 = (bf16[256,1024]{1,0:T(8,128)(2,1)S(1)}, bf16[256,1024]{1,0:T(8,128)(2,1)S(1)}, u32[]{:S(2)}, u32[]{:S(2)}) collective-permute-start(bf16[256,1024]{1,0:T(8,128)(2,1)S(1)} %collective-permute-done.7.refs_5_), channel_id=1, source_target_pairs={{1,0},{5,4},{9,8},{13,12},{17,16},{21,20},{25,24},{29,28}} | collective-permute-start | bytes 1572872 | tf_op jit(solution)/shard_map/ppermute | solution.py:759
  46.1 13.0 %collective-permute-start.5 = (bf16[256,1024]{1,0:T(8,128)(2,1)S(1)}, bf16[256,1024]{1,0:T(8,128)(2,1)S(1)}, u32[]{:S(2)}, u32[]{:S(2)}) collective-permute-start(bf16[256,1024]{1,0:T(8,128)(2,1)S(1)} %collective-permute-done.4.refs_1_), channel_id=1, source_target_pairs={{2,3},{6,7},{10,11},{14,15},{18,19},{22,23},{26,27},{30,31}} | collective-permute-start | bytes 1572872 | tf_op jit(solution)/shard_map/ppermute | solution.py:758
  46.8 12.6 %collective-permute-start.2 = (s32[256]{0:T(256)}, s32[256]{0:T(256)S(1)}, u32[]{:S(2)}, u32[]{:S(2)}) collective-permute-start(s32[256]{0:T(256)} %bitcast.92), channel_id=1, source_target_pairs={{0,1},{1,2},{2,3},{3,0},{4,5},{5,6},{6,7},{7,4},{8,9},{9,10},{10,1... | collective-permute-start | bytes 3080 | tf_op jit(solution)/shard_map/ppermute | solution.py:825
  49.5 9.8 %collective-permute-start.1 = (s32[256]{0:T(256)}, s32[256]{0:T(256)S(1)}, u32[]{:S(2)}, u32[]{:S(2)}) collective-permute-start(s32[256]{0:T(256)} %bitcast.93), channel_id=1, source_target_pairs={{0,2},{1,3},{2,0},{3,1},{4,6},{5,7},{6,4},{7,5},{8,10},{9,11},{10,... | collective-permute-start | bytes 3080 | tf_op jit(solution)/shard_map/ppermute | solution.py:825
  52.7 6.7 %collective-permute-start = (s32[256]{0:T(256)}, s32[256]{0:T(256)S(1)}, u32[]{:S(2)}, u32[]{:S(2)}) collective-permute-start(s32[256]{0:T(256)} %bitcast.94), channel_id=1, source_target_pairs={{0,3},{1,0},{2,1},{3,2},{4,7},{5,4},{6,5},{7,6},{8,11},{9,8},{10,9... | collective-permute-start | bytes 3080 | tf_op jit(solution)/shard_map/ppermute | solution.py:825
  59.1 0.8 copy-start.26
  59.2 93.1 %reduce-scatter.3.cloned.1.call-start = ((), (), s32[]{:S(2)}) async-start(), calls=%async_computation.3 | async-start | bytes 2621440 | tf_op jit(solution)/shard_map/reduce_scatter | solution.py:899
  87.4 19.9 %copy-start = (s32[1040,128]{1,0:T(8,128)S(1)}, s32[1040,128]{1,0:T(8,128)}, u32[]{:S(2)}) copy-start(s32[1040,128]{1,0:T(8,128)} %broadcast_in_dim.34.window_ref) | copy-start | bytes 1597444
  87.4 19.9 %copy-start.9 = (bf16[1024,512]{1,0:T(8,128)(2,1)S(1)}, bf16[1024,512]{1,0:T(8,128)(2,1)}, u32[]{:S(2)}) copy-start(bf16[1024,512]{1,0:T(8,128)(2,1)} %get-tuple-element.65.scaled_ref) | copy-start | bytes 3145732
  87.4 126.1 %reduce-scatter.5.cloned.1.call-start = ((), (), s32[]{:S(2)}) async-start(), calls=%async_computation.5 | async-start | bytes 2621440 | tf_op jit(solution)/shard_map/reduce_scatter | solution.py:910
  112.3 4.9 %collective-permute-start.10 = (f32[2,1024]{1,0:T(2,128)S(1)}, f32[2,1024]{1,0:T(2,128)S(1)}, u32[]{:S(2)}, u32[]{:S(2)}) collective-permute-start(f32[2,1024]{1,0:T(2,128)S(1)} %pad_maximum_fusion.5), channel_id=1, source_target_pairs={{0,2},{1,3},{2,0},{3,1},{4,6},{5,7},{6,4},{7,5},{8,10},{9,11},{10,... | collective-permute-start | bytes 24584 | tf_op jit(solution)/shard_map/ppermute | solution.py:825
  113.4 5.6 %collective-permute-start.11 = (f32[2,1024]{1,0:T(2,128)S(1)}, f32[2,1024]{1,0:T(2,128)S(1)}, u32[]{:S(2)}, u32[]{:S(2)}) collective-permute-start(f32[2,1024]{1,0:T(2,128)S(1)} %pad_maximum_fusion.5), channel_id=1, source_target_pairs={{0,1},{1,2},{2,3},{3,0},{4,5},{5,6},{6,7},{7,4},{8,9},{9,10},{10,1... | collective-permute-start | bytes 24584 | tf_op jit(solution)/shard_map/ppermute | solution.py:825
  114.0 5.0 %collective-permute-start.9 = (f32[2,1024]{1,0:T(2,128)S(1)}, f32[2,1024]{1,0:T(2,128)S(1)}, u32[]{:S(2)}, u32[]{:S(2)}) collective-permute-start(f32[2,1024]{1,0:T(2,128)S(1)} %pad_maximum_fusion.5), channel_id=1, source_target_pairs={{0,3},{1,0},{2,1},{3,2},{4,7},{5,4},{6,5},{7,6},{8,11},{9,8},{10,9... | collective-permute-start | bytes 24584 | tf_op jit(solution)/shard_map/ppermute | solution.py:825
  143.2 24.5 %copy-start.14 = (f32[32,128]{1,0:T(8,128)}, f32[32,128]{1,0:T(8,128)S(1)}, u32[]{:S(2)}) copy-start(f32[32,128]{1,0:T(8,128)S(1)} %reshape.130) | copy-start | bytes 49156
  152.3 1.2 copy-start.8
  163.0 1.9 copy-start.10
  164.0 2.9 %collective-permute-start.12 = (bf16[528,896]{1,0:T(8,128)(2,1)}, bf16[528,896]{1,0:T(8,128)(2,1)}, u32[]{:S(2)}, u32[]{:S(2)}) collective-permute-start(bf16[528,896]{1,0:T(8,128)(2,1)} %pad_maximum_fusion), channel_id=1, source_target_pairs={{0,4},{4,0},{8,12},{12,8},{16,20},{20,16},{24,28},{28,24},{1,5},{5... | collective-permute-start | bytes 2838536 | tf_op jit(solution)/shard_map/ppermute | solution.py:807
  166.0 3.1 %copy-start.12 = (bf16[1024,896]{1,0:T(8,128)(2,1)S(1)}, bf16[1024,896]{1,0:T(8,128)(2,1)}, u32[]{:S(2)}) copy-start(bf16[1024,896]{1,0:T(8,128)(2,1)} %get-tuple-element.99) | copy-start | bytes 5505028
  166.0 6.0 %collective-permute-start.18 = (bf16[2,2,128,1024]{3,2,1,0:T(8,128)(2,1)}, bf16[2,2,128,1024]{3,2,1,0:T(8,128)(2,1)}, u32[]{:S(2)}, u32[]{:S(2)}) collective-permute-start(bf16[2,2,128,1024]{3,2,1,0:T(8,128)(2,1)} %dynamic-slice_bitcast_fusion), channel_id=1, source_target_pairs={{0,4},{4,0},{8,12},{12,8},{16,20},{20,16},{24,28},{28,24},{1,5},{5... | collective-permute-start | bytes 3145736 | tf_op jit(solution)/shard_map/ppermute | solution.py:814
  167.7 1.4 copy-start.17
  169.1 1.9 copy-start.2
  169.1 1.9 copy-start.13
  169.4 2.7 %copy-start.11 = (bf16[1024,1024]{1,0:T(8,128)(2,1)S(1)}, bf16[1024,1024]{1,0:T(8,128)(2,1)}, u32[]{:S(2)}) copy-start(bf16[1024,1024]{1,0:T(8,128)(2,1)} %get-tuple-element.101) | copy-start | bytes 6291460
  169.5 13.2 %collective-permute-start.13 = (bf16[272,896]{1,0:T(8,128)(2,1)S(1)}, bf16[272,896]{1,0:T(8,128)(2,1)S(1)}, u32[]{:S(2)}, u32[]{:S(2)}) collective-permute-start(bf16[272,896]{1,0:T(8,128)(2,1)S(1)} %pad_maximum_fusion.1), channel_id=1, source_target_pairs={{0,8},{4,12},{8,0},{12,4},{16,24},{20,28},{24,16},{28,20},{1,9},{5... | collective-permute-start | bytes 1462280 | tf_op jit(solution)/shard_map/ppermute | solution.py:807
  174.5 15.3 %collective-permute-start.19 = (bf16[2,128,1024]{2,1,0:T(8,128)(2,1)}, bf16[2,128,1024]{2,1,0:T(8,128)(2,1)S(1)}, u32[]{:S(2)}, u32[]{:S(2)}) collective-permute-start(bf16[2,128,1024]{2,1,0:T(8,128)(2,1)} %dynamic-slice_bitcast_fusion.1), channel_id=1, source_target_pairs={{0,16},{4,20},{8,24},{12,28},{16,0},{20,4},{24,8},{28,12},{1,17},{... | collective-permute-start | bytes 1572872 | tf_op jit(solution)/shard_map/ppermute | solution.py:814
  187.5 0.7 copy-start.18
  187.6 9.1 %copy-start.15 = (f32[32,128]{1,0:T(8,128)S(1)}, f32[32,128]{1,0:T(8,128)}, u32[]{:S(2)}) copy-start(f32[32,128]{1,0:T(8,128)} %copy-done.14) | copy-start | bytes 49156
  188.3 7.6 %collective-permute-start.14 = (bf16[144,896]{1,0:T(8,128)(2,1)S(1)}, bf16[144,896]{1,0:T(8,128)(2,1)S(1)}, u32[]{:S(2)}, u32[]{:S(2)}) collective-permute-start(bf16[144,896]{1,0:T(8,128)(2,1)S(1)} %pad_maximum_fusion.2), channel_id=1, source_target_pairs={{0,16},{4,20},{8,24},{12,28},{16,0},{20,4},{24,8},{28,12},{1,17},{... | collective-permute-start | bytes 774152 | tf_op jit(solution)/shard_map/ppermute | solution.py:807
  190.1 23.5 %copy-start.1 = (bf16[1,256,1024]{2,1,0:T(8,128)(2,1)S(1)}, bf16[1,256,1024]{2,1,0:T(8,128)(2,1)}, u32[]{:S(2)}) copy-start(bf16[1,256,1024]{2,1,0:T(8,128)(2,1)} %param.19) | copy-start | bytes 1572868
  190.1 26.3 %collective-permute-start.20 = (bf16[128,1024]{1,0:T(8,128)(2,1)S(1)}, bf16[128,1024]{1,0:T(8,128)(2,1)S(1)}, u32[]{:S(2)}, u32[]{:S(2)}) collective-permute-start(bf16[128,1024]{1,0:T(8,128)(2,1)S(1)} %dynamic-slice_bitcast_fusion.2), channel_id=1, source_target_pairs={{0,8},{4,12},{8,0},{12,4},{16,24},{20,28},{24,16},{28,20},{1,9},{5... | collective-permute-start | bytes 786440 | tf_op jit(solution)/shard_map/ppermute | solution.py:814
  195.9 0.7 copy-start.16
  198.5 12.5 %collective-permute-start.16 = (bf16[280,128]{1,0:T(8,128)(2,1)S(1)}, bf16[280,128]{1,0:T(8,128)(2,1)S(1)}, u32[]{:S(2)}, u32[]{:S(2)}) collective-permute-start(bf16[280,128]{1,0:T(8,128)(2,1)S(1)} %fusion.5), channel_id=1, source_target_pairs={{0,2},{1,3},{2,0},{3,1},{4,6},{5,7},{6,4},{7,5},{8,10},{9,11},{10,... | collective-permute-start | bytes 215048 | tf_op jit(solution)/shard_map/ppermute | solution.py:825
  200.3 10.7 %collective-permute-start.15 = (bf16[280,128]{1,0:T(8,128)(2,1)S(1)}, bf16[280,128]{1,0:T(8,128)(2,1)S(1)}, u32[]{:S(2)}, u32[]{:S(2)}) collective-permute-start(bf16[280,128]{1,0:T(8,128)(2,1)S(1)} %fusion.5), channel_id=1, source_target_pairs={{0,3},{1,0},{2,1},{3,2},{4,7},{5,4},{6,5},{7,6},{8,11},{9,8},{10,9... | collective-permute-start | bytes 215048 | tf_op jit(solution)/shard_map/ppermute | solution.py:825
  201.5 10.1 %collective-permute-start.17 = (bf16[280,128]{1,0:T(8,128)(2,1)S(1)}, bf16[280,128]{1,0:T(8,128)(2,1)S(1)}, u32[]{:S(2)}, u32[]{:S(2)}) collective-permute-start(bf16[280,128]{1,0:T(8,128)(2,1)S(1)} %fusion.5), channel_id=1, source_target_pairs={{0,1},{1,2},{2,3},{3,0},{4,5},{5,6},{6,7},{7,4},{8,9},{9,10},{10,1... | collective-permute-start | bytes 215048 | tf_op jit(solution)/shard_map/ppermute | solution.py:825
  213.6 1.0 copy-start.3
Sparse Core Ops, SparseCore 0:
  12.7 38.3 all-gather.2
  59.3 47.9 all-gather.4
  109.6 42.6 reduce-scatter.2
  164.2 47.8 reduce-scatter.4

commit v11 on v10

--- a/solution.py
+++ b/solution.py
@@ -908,7 +908,7 @@
         channel, x_proj, bcdt, grad_out, saved,
     )
     in_sum = lax.psum_scatter(in_part, "tensor", scatter_dimension=0, tiled=True)
-    first, second = run_weights(cot_full, normed_out, tokens, after(grads, out_sum))
+    first, second = run_weights(cot_full, normed_out, tokens, grads)
     own = jnp.concatenate([sum_x.reshape(-1, LANES), sum_head])
     both = jnp.concatenate([sum_gain[0].reshape(-1, LANES), sum_bc.reshape(-1, LANES)])
     first, second, small, came = cube_scatter(first, second, jnp.concatenate([own, both]), "dp")

time: 225 us -> 218 us (0.969)
  starting transfers between devices: 34.6 us -> 29.5 us
    ppermute x3, waiting for transfers between devices: 0.01 us -> 10.2 us  [line_step(): lax.ppermute(right, axis, [(i, i + 1) for i in range(step - 1, n - 1)])]
    reduce_scatter x1, waiting for transfers between devices: 8.99 us -> 0.01 us  [shards(): lax.psum_scatter(out_part, 'tensor', scatter_dimension=0, tiled=True)]
    ppermute x9, starting transfers between devices: 17.5 us -> 12.4 us  [around(): lax.ppermute(values, axis, [(i, (i - k) % n) for i in range(n)])]
    all_gather x1, waiting for transfers between devices: 19.8 us -> 16.1 us  [shards(): lax.all_gather(after(cotangent[0], near_hidden[0], near_hidden[-1]), 'ten...]
    ppermute x3, waiting for transfers between devices: 24.7 us -> 21.8 us  [line_step(): lax.ppermute(left, axis, [(i, i - 1) for i in range(1, n - step + 1)])]
    unnamed x62 -> x66, local copies, waits for them, and re-layouts: 9.06 us -> 7.57 us
  transfers between devices with their start and end apart: 25 -> 25, of which waited for: 11 -> 12; matrix products, arithmetic and copies ran while one was open for 11% -> 12% of each run, Pallas kernels for 25% -> 30%
where the time goes in v11:
time: 218 us; the launch traced here: 215 us
  waiting for transfers between devices  70.9 us (33%)
  Pallas kernels  65.9 us (30%)
  starting transfers between devices  29.5 us (14%)
  local copies, waits for them, and re-layouts  24.6 us (11%)
  between operations  14.5 us (7%)
  other arithmetic  9.3 us (4%)
    pallas_call x1, Pallas kernels, run_backward(): pl.pallas_call(functools.partial(backward_kernel, heads, size, full_inner...  24.2 us
    ppermute x3, waiting for transfers between devices, line_step(): lax.ppermute(left, axis, [(i, i - 1) for i in range(1, n - step + 1)])  21.8 us
    pallas_call x1, Pallas kernels, run_forward(): pl.pallas_call(functools.partial(forward_kernel, heads, size), grid=(bloc...  18 us
    all_gather x1, waiting for transfers between devices, shards(): lax.all_gather(after(cotangent[0], near_hidden[0], near_hidden[-1]), 'ten...  16.1 us
    ppermute x3, waiting for transfers between devices, cube_scatter(): lax.ppermute(jnp.concatenate([send.reshape(rows, columns), rider]), axis,...  13.6 us
    ppermute x9, starting transfers between devices, around(): lax.ppermute(values, axis, [(i, (i - k) % n) for i in range(n)])  12.4 us
    ppermute x3, waiting for transfers between devices, line_step(): lax.ppermute(right, axis, [(i, i + 1) for i in range(step - 1, n - 1)])  10.2 us
    ppermute x9, waiting for transfers between devices, around(): lax.ppermute(values, axis, [(i, (i - k) % n) for i in range(n)])  9.13 us
  transfers between devices with their start and end apart: 25, of which 12 were waited for; matrix products, arithmetic and copies ran while one was open for 12% of the time, Pallas kernels for 30%

profile of v11, /device:TPU:0, one launch (start us, length us, event | category | flops | bytes accessed | tf_op | source)
XLA Modules:
  0.0 214.6 jit_solution(133240551271371615)
XLA Ops:
  7.3 0.7 pad_maximum_fusion.6
  8.1 0.9 copy-done.4
  9.0 0.9 copy-done.5
  10.0 0.9 copy-done.6
  10.9 0.8 copy-done.7
  11.7 0.8 pack.1
  12.6 5.0 %collective-permute-start.3 = (bf16[256,1024]{1,0:T(8,128)(2,1)}, bf16[256,1024]{1,0:T(8,128)(2,1)S(1)}, u32[]{:S(2)}, u32[]{:S(2)}) collective-permute-start(bf16[256,1024]{1,0:T(8,128)(2,1)} %bitcast.74), channel_id=1, source_target_pairs={{0,1},{1,2},{2,3},{4,5},{5,6},{6,7},{8,9},{9,10},{10,11},{12,13},{... | collective-permute-start | bytes 1572872 | tf_op jit(solution)/shard_map/ppermute | solution.py:758
  17.6 1.3 collective-permute-start.6
  18.9 10.2 %collective-permute-done.3.refs_2_ = bf16[256,1024]{1,0:T(8,128)(2,1)S(1)} collective-permute-done((bf16[256,1024]{1,0:T(8,128)(2,1)}, bf16[256,1024]{1,0:T(8,128)(2,1)S(1)}, u32[]{:S(2)}, u32[]{:S(2)}) %collective-permute-start.3) | collective-permute-done | bytes 524320 | tf_op jit(solution)/shard_map/ppermute | solution.py:758
  29.1 0.7 collective-permute-start.4
  29.8 3.4 %collective-permute-done.6.refs_4_ = bf16[256,1024]{1,0:T(8,128)(2,1)S(1)} collective-permute-done((bf16[256,1024]{1,0:T(8,128)(2,1)}, bf16[256,1024]{1,0:T(8,128)(2,1)S(1)}, u32[]{:S(2)}, u32[]{:S(2)}) %collective-permute-start.6) | collective-permute-done | bytes 524320 | tf_op jit(solution)/shard_map/ppermute | solution.py:759
  33.1 1.3 collective-permute-start.7
  34.4 0.7 collective-permute-start.5
  35.1 12.6 %collective-permute-done.7.refs_5_ = bf16[256,1024]{1,0:T(8,128)(2,1)S(1)} collective-permute-done((bf16[256,1024]{1,0:T(8,128)(2,1)S(1)}, bf16[256,1024]{1,0:T(8,128)(2,1)S(1)}, u32[]{:S(2)}, u32[]{:S(2)}) %collective-permute-start.7) | collective-permute-done | bytes 524320 | tf_op jit(solution)/shard_map/ppermute | solution.py:759
  47.7 1.3 collective-permute-start.8
  49.0 1.3 collective-permute-start
  50.3 2.9 %collective-permute-start.1 = (s32[256]{0:T(256)}, s32[256]{0:T(256)S(1)}, u32[]{:S(2)}, u32[]{:S(2)}) collective-permute-start(s32[256]{0:T(256)} %bitcast.93), channel_id=1, source_target_pairs={{0,2},{1,3},{2,0},{3,1},{4,6},{5,7},{6,4},{7,5},{8,10},{9,11},{10,... | collective-permute-start | bytes 3080 | tf_op jit(solution)/shard_map/ppermute | solution.py:825
  53.5 0.7 broadcast_in_dim.39
  54.3 0.7 pad_maximum_fusion.7.channel_ref
  55.0 0.7 pad_maximum_fusion.4.kernel_bc_ref
  55.7 5.8 %collective-permute-done.8.refs_6_ = bf16[256,1024]{1,0:T(8,128)(2,1)S(1)} collective-permute-done((bf16[256,1024]{1,0:T(8,128)(2,1)S(1)}, bf16[256,1024]{1,0:T(8,128)(2,1)S(1)}, u32[]{:S(2)}, u32[]{:S(2)}) %collective-permute-start.8) | collective-permute-done | bytes 524320 | tf_op jit(solution)/shard_map/ppermute | solution.py:759
  62.5 8.4 %project.1 = (bf16[1024,1024]{1,0:T(8,128)(2,1)}, bf16[1024,1024]{1,0:T(8,128)(2,1)}, f32[1024,512]{1,0:T(8,128)}, f32[1024,512]{1,0:T(8,128)}, f32[1024,384]{1,0:T(8,128)}, /*index=5*/f32[8,1024]{1,0:T(8,128)S(1)}) custom-call(s32[1]{0:T(128)} %bitcast.8.place_ref, bf16[256,1024]{1,0:T(8,128)(2,1)S(1)} %collective-permute-done.5.refs_0_, ...), custom_call_target="tpu_custom_call" | custom-call | flops 8000000000 | bytes 1048576 | tf_op jit(solution)/shard_map/project/pallas_call | solution.py:520
  70.9 1.0 broadcast_in_dim.34.window_ref
  71.9 18.0 %forward.1 = (bf16[1024,512]{1,0:T(8,128)(2,1)}, bf16[1024,1024]{1,0:T(8,128)(2,1)}, f32[8,1024]{1,0:T(8,128)S(1)}, f32[4,128,512]{2,1,0:T(8,128)}, f32[4,8,512]...) custom-call(s32[1040,128]{1,0:T(8,128)} %broadcast_in_dim.34.window_, ...), custom_call_target="tpu_custom_call" | custom-call | flops 14000000000 | bytes 1048576 | tf_op jit(solution)/shard_map/forward/pallas_call | solution.py:581
  90.0 16.1 %all-gather.5.cloned.1.call-done.cot_ref = bf16[1024,1024]{1,0:T(8,128)(2,1)} async-done(((bf16[256,1024]{1,0:T(8,128)(2,1)}), bf16[1024,1024]{1,0:T(8,128)(2,1)}) %all-gather.5.cloned.1.call-update) | async-done | bytes 2097168 | tf_op jit(solution)/shard_map/all_gather | solution.py:891
  106.1 4.9 %out_gradient.1 = (f32[1024,512]{1,0:T(8,128)}, f32[8,1024]{1,0:T(8,128)S(1)}) custom-call(bf16[1024,1024]{1,0:T(8,128)(2,1)} %all-gather.5.cloned.1.call-done.cot_ref, bf16[1024,1920]{1,0:T(8,128)(2,1)} %all-gather.3.cloned.1.call-done.refs_7_.weights_ref, bf16[1024,512]{1,0:T(8,128)(2,1)S(1)} %copy-done.9, s32[1040,128]{1,0:T(8,128)S(1)} %copy-done), custom_call_target="tpu_custom_call" | custom-call | flops 5000000000 | bytes 1048576 | tf_op jit(solution)/shard_map/out_gradient/pallas_call | solution.py:620
  111.1 1.7 collective-permute-start.10
  112.8 2.3 %collective-permute-start.9 = (f32[2,1024]{1,0:T(2,128)S(1)}, f32[2,1024]{1,0:T(2,128)S(1)}, u32[]{:S(2)}, u32[]{:S(2)}) collective-permute-start(f32[2,1024]{1,0:T(2,128)S(1)} %pad_maximum_fusion.5), channel_id=1, source_target_pairs={{0,3},{1,0},{2,1},{3,2},{4,7},{5,4},{6,5},{7,6},{8,11},{9,8},{10,9... | collective-permute-start | bytes 24584 | tf_op jit(solution)/shard_map/ppermute | solution.py:825
  115.0 1.6 collective-permute-done.11
  116.6 1.8 collective-permute-done.9
  118.5 24.2 %backward.1 = (bf16[1024,1408]{1,0:T(8,128)(2,1)}, bf16[1024,1024]{1,0:T(8,128)(2,1)}, bf16[1024,512]{1,0:T(8,128)(2,1)}, f32[8,512]{1,0:T(8,128)S(1)}, f32[8,25...) custom-call(f32[8,1024]{1,0:T(8,128)S(1)} %pad.29.stat_ref, ...), custom_call_target="tpu_custom_call" | custom-call | flops 2000000000 | bytes 1048576 | tf_op jit(solution)/shard_map/backward/pallas_call | solution.py:689
  142.8 1.2 copy-done.8
  144.0 8.3 %weight_gradients.1 = (bf16[1024,896]{1,0:T(8,128)(2,1)}, bf16[1024,1024]{1,0:T(8,128)(2,1)}) custom-call(bf16[1024,1024]{1,0:T(8,128)(2,1)} %all-gather.5.cloned.1.call-done.cot_ref, bf16[1024,512]{1,0:T(8,128)(2,1)S(1)} %copy-done.8, bf16[1024,1024]{1,0:T(8,128)(2,1)} %get-tuple-element.95.tokens_ref, bf16[1024,1408]{1,0:T(8,128)(2,1)} %get-tuple-element.96.grads_ref), custom_call_target="tpu_custom_call" | custom-call | flops 7000000000 | bytes 1048576 | tf_op jit(solution)/shard_map/weight_gradients/pallas_call | solution.py:654
  152.3 1.4 constant_dynamic-slice_fusion.1
  153.7 1.0 pad_maximum_fusion
  154.8 1.1 dynamic-slice_bitcast_fusion
  156.4 1.2 collective-permute-done.12
  157.6 0.8 slice.152
  158.5 1.3 slice.154
  160.2 1.5 collective-permute-start.13
  161.9 1.8 fusion
  163.7 1.6 collective-permute-start.19
  165.3 8.1 %collective-permute-done.13 = bf16[272,896]{1,0:T(8,128)(2,1)S(1)} collective-permute-done((bf16[272,896]{1,0:T(8,128)(2,1)S(1)}, bf16[272,896]{1,0:T(8,128)(2,1)S(1)}, u32[]{:S(2)}, u32[]{:S(2)}) %collective-permute-start.13) | collective-permute-done | bytes 487456 | tf_op jit(solution)/shard_map/ppermute | solution.py:807
  173.4 0.6 slice.155
  174.0 1.4 slice.126
  175.4 0.8 convert_bitcast_fusion
  176.2 0.6 pad.32
  176.8 1.4 reshape.139
  179.0 1.6 collective-permute-start.14
  180.8 1.5 collective-permute-start.20
  182.3 4.3 %collective-permute-done.14 = bf16[144,896]{1,0:T(8,128)(2,1)S(1)} collective-permute-done((bf16[144,896]{1,0:T(8,128)(2,1)S(1)}, bf16[144,896]{1,0:T(8,128)(2,1)S(1)}, u32[]{:S(2)}, u32[]{:S(2)}) %collective-permute-start.14) | collective-permute-done | bytes 258080 | tf_op jit(solution)/shard_map/ppermute | solution.py:807
  186.9 0.9 collective-permute-start.17
  187.8 1.9 collective-permute-start.16
  189.7 1.1 collective-permute-start.15
  191.9 0.7 slice.176
  192.6 0.7 copy.46
  193.9 0.6 reduce_sum.9
  194.6 1.0 collective-permute-done.17
  195.5 4.8 %collective-permute-done.16 = bf16[280,128]{1,0:T(8,128)(2,1)S(1)} collective-permute-done((bf16[280,128]{1,0:T(8,128)(2,1)S(1)}, bf16[280,128]{1,0:T(8,128)(2,1)S(1)}, u32[]{:S(2)}, u32[]{:S(2)}) %collective-permute-start.16) | collective-permute-done | bytes 71712 | tf_op jit(solution)/shard_map/ppermute | solution.py:825
  200.4 0.7 reshape.143
  202.9 0.8 fusion.10
  203.7 2.1 fusion.4
  205.8 1.0 copy-done.3
  206.8 1.3 finish.1
  (143 shorter events, 7.7 us)
Async XLA Ops:
  7.2 54.5 %copy-start.22 = (s32[1,256]{1,0:T(1,128)S(1)}, s32[1,256]{1,0:T(1,128)}, u32[]{:S(2)}) copy-start(s32[1,256]{1,0:T(1,128)} %param.18) | copy-start | bytes 3076
  7.2 54.5 %copy-start.23 = (f32[512]{0:T(512)S(1)}, f32[512]{0:T(512)}, u32[]{:S(2)}) copy-start(f32[512]{0:T(512)} %param.26) | copy-start | bytes 6148
  7.2 54.5 %copy-start.21 = (f32[4,512]{1,0:T(4,128)S(1)}, f32[4,512]{1,0:T(4,128)}, u32[]{:S(2)}) copy-start(f32[4,512]{1,0:T(4,128)} %param.25) | copy-start | bytes 24580
  7.2 54.5 %copy-start.24 = (f32[8]{0:T(128)S(1)}, f32[8]{0:T(128)}, u32[]{:S(2)}) copy-start(f32[8]{0:T(128)} %param.30) | copy-start | bytes 100
  7.2 54.5 %copy-start.25 = (f32[8]{0:T(128)S(1)}, f32[8]{0:T(128)}, u32[]{:S(2)}) copy-start(f32[8]{0:T(128)} %param.29) | copy-start | bytes 100
  7.2 54.8 %all-gather.3.cloned.1.call-start = ((), (), s32[]{:S(2)}) async-start(), calls=%async_computation.2 | async-start | bytes 4423680 | tf_op jit(solution)/shard_map/all_gather | solution.py:872
  8.1 0.9 copy-start.4
  9.0 0.9 copy-start.5
  9.9 0.9 copy-start.6
  10.9 0.8 copy-start.7
  12.6 93.5 %all-gather.5.cloned.1.call-start = ((), (), s32[]{:S(2)}) async-start(), calls=%async_computation.4 | async-start | bytes 2621440 | tf_op jit(solution)/shard_map/all_gather | solution.py:891
  12.6 16.4 %collective-permute-start.3 = (bf16[256,1024]{1,0:T(8,128)(2,1)}, bf16[256,1024]{1,0:T(8,128)(2,1)S(1)}, u32[]{:S(2)}, u32[]{:S(2)}) collective-permute-start(bf16[256,1024]{1,0:T(8,128)(2,1)} %bitcast.74), channel_id=1, source_target_pairs={{0,1},{1,2},{2,3},{4,5},{5,6},{6,7},{8,9},{9,10},{10,11},{12,13},{... | collective-permute-start | bytes 1572872 | tf_op jit(solution)/shard_map/ppermute | solution.py:758
  17.6 15.5 %collective-permute-start.6 = (bf16[256,1024]{1,0:T(8,128)(2,1)}, bf16[256,1024]{1,0:T(8,128)(2,1)S(1)}, u32[]{:S(2)}, u32[]{:S(2)}) collective-permute-start(bf16[256,1024]{1,0:T(8,128)(2,1)} %bitcast.75), channel_id=1, source_target_pairs={{1,0},{2,1},{3,2},{5,4},{6,5},{7,6},{9,8},{10,9},{11,10},{13,12},{... | collective-permute-start | bytes 1572872 | tf_op jit(solution)/shard_map/ppermute | solution.py:759
  29.1 5.3 %collective-permute-start.4 = (bf16[256,1024]{1,0:T(8,128)(2,1)S(1)}, bf16[256,1024]{1,0:T(8,128)(2,1)S(1)}, u32[]{:S(2)}, u32[]{:S(2)}) collective-permute-start(bf16[256,1024]{1,0:T(8,128)(2,1)S(1)} %collective-permute-done.3.refs_2_), channel_id=1, source_target_pairs={{1,2},{2,3},{5,6},{6,7},{9,10},{10,11},{13,14},{14,15},{17,18},{18... | collective-permute-start | bytes 1572872 | tf_op jit(solution)/shard_map/ppermute | solution.py:758
  33.1 29.4 %copy-start.26 = (bf16[256,1024]{1,0:T(8,128)(2,1)}, bf16[256,1024]{1,0:T(8,128)(2,1)S(1)}, u32[]{:S(2)}) copy-start(bf16[256,1024]{1,0:T(8,128)(2,1)S(1)} %collective-permute-done.6.refs_4_) | copy-start | bytes 1572868
  33.1 14.6 %collective-permute-start.7 = (bf16[256,1024]{1,0:T(8,128)(2,1)S(1)}, bf16[256,1024]{1,0:T(8,128)(2,1)S(1)}, u32[]{:S(2)}, u32[]{:S(2)}) collective-permute-start(bf16[256,1024]{1,0:T(8,128)(2,1)S(1)} %collective-permute-done.6.refs_4_), channel_id=1, source_target_pairs={{1,0},{2,1},{5,4},{6,5},{9,8},{10,9},{13,12},{14,13},{17,16},{18,1... | collective-permute-start | bytes 1572872 | tf_op jit(solution)/shard_map/ppermute | solution.py:759
  34.4 21.3 %collective-permute-start.5 = (bf16[256,1024]{1,0:T(8,128)(2,1)S(1)}, bf16[256,1024]{1,0:T(8,128)(2,1)S(1)}, u32[]{:S(2)}, u32[]{:S(2)}) collective-permute-start(bf16[256,1024]{1,0:T(8,128)(2,1)S(1)} %collective-permute-done.4.refs_1_), channel_id=1, source_target_pairs={{2,3},{6,7},{10,11},{14,15},{18,19},{22,23},{26,27},{30,31}} | collective-permute-start | bytes 1572872 | tf_op jit(solution)/shard_map/ppermute | solution.py:758
  47.7 14.8 %copy-start.27 = (bf16[256,1024]{1,0:T(8,128)(2,1)}, bf16[256,1024]{1,0:T(8,128)(2,1)S(1)}, u32[]{:S(2)}) copy-start(bf16[256,1024]{1,0:T(8,128)(2,1)S(1)} %collective-permute-done.7.refs_5_) | copy-start | bytes 1572868
  47.7 13.8 %collective-permute-start.8 = (bf16[256,1024]{1,0:T(8,128)(2,1)S(1)}, bf16[256,1024]{1,0:T(8,128)(2,1)S(1)}, u32[]{:S(2)}, u32[]{:S(2)}) collective-permute-start(bf16[256,1024]{1,0:T(8,128)(2,1)S(1)} %collective-permute-done.7.refs_5_), channel_id=1, source_target_pairs={{1,0},{5,4},{9,8},{13,12},{17,16},{21,20},{25,24},{29,28}} | collective-permute-start | bytes 1572872 | tf_op jit(solution)/shard_map/ppermute | solution.py:759
  49.0 12.7 %collective-permute-start = (s32[256]{0:T(256)}, s32[256]{0:T(256)S(1)}, u32[]{:S(2)}, u32[]{:S(2)}) collective-permute-start(s32[256]{0:T(256)} %bitcast.92), channel_id=1, source_target_pairs={{0,3},{1,0},{2,1},{3,2},{4,7},{5,4},{6,5},{7,6},{8,11},{9,8},{10,9... | collective-permute-start | bytes 3080 | tf_op jit(solution)/shard_map/ppermute | solution.py:825
  50.3 11.5 %collective-permute-start.1 = (s32[256]{0:T(256)}, s32[256]{0:T(256)S(1)}, u32[]{:S(2)}, u32[]{:S(2)}) collective-permute-start(s32[256]{0:T(256)} %bitcast.93), channel_id=1, source_target_pairs={{0,2},{1,3},{2,0},{3,1},{4,6},{5,7},{6,4},{7,5},{8,10},{9,11},{10,... | collective-permute-start | bytes 3080 | tf_op jit(solution)/shard_map/ppermute | solution.py:825
  53.2 8.6 %collective-permute-start.2 = (s32[256]{0:T(256)}, s32[256]{0:T(256)S(1)}, u32[]{:S(2)}, u32[]{:S(2)}) collective-permute-start(s32[256]{0:T(256)} %bitcast.94), channel_id=1, source_target_pairs={{0,1},{1,2},{2,3},{3,0},{4,5},{5,6},{6,7},{7,4},{8,9},{9,10},{10,1... | collective-permute-start | bytes 3080 | tf_op jit(solution)/shard_map/ppermute | solution.py:825
  61.6 0.9 copy-start.28
  61.6 142.1 %reduce-scatter.3.cloned.1.call-start = ((), (), s32[]{:S(2)}) async-start(), calls=%async_computation.3 | async-start | bytes 2621440 | tf_op jit(solution)/shard_map/reduce_scatter | solution.py:899
  61.9 0.6 copy-start.19
  89.9 16.2 %copy-start = (s32[1040,128]{1,0:T(8,128)S(1)}, s32[1040,128]{1,0:T(8,128)}, u32[]{:S(2)}) copy-start(s32[1040,128]{1,0:T(8,128)} %broadcast_in_dim.34.window_ref) | copy-start | bytes 1597444
  89.9 16.2 %copy-start.9 = (bf16[1024,512]{1,0:T(8,128)(2,1)S(1)}, bf16[1024,512]{1,0:T(8,128)(2,1)}, u32[]{:S(2)}) copy-start(bf16[1024,512]{1,0:T(8,128)(2,1)} %get-tuple-element.64.scaled_ref) | copy-start | bytes 3145732
  89.9 115.9 %reduce-scatter.5.cloned.1.call-start = ((), (), s32[]{:S(2)}) async-start(), calls=%async_computation.5 | async-start | bytes 2621440 | tf_op jit(solution)/shard_map/reduce_scatter | solution.py:910
  111.0 5.6 %collective-permute-start.11 = (f32[2,1024]{1,0:T(2,128)S(1)}, f32[2,1024]{1,0:T(2,128)S(1)}, u32[]{:S(2)}, u32[]{:S(2)}) collective-permute-start(f32[2,1024]{1,0:T(2,128)S(1)} %pad_maximum_fusion.5), channel_id=1, source_target_pairs={{0,1},{1,2},{2,3},{3,0},{4,5},{5,6},{6,7},{7,4},{8,9},{9,10},{10,1... | collective-permute-start | bytes 24584 | tf_op jit(solution)/shard_map/ppermute | solution.py:825
  111.1 5.6 %collective-permute-start.10 = (f32[2,1024]{1,0:T(2,128)S(1)}, f32[2,1024]{1,0:T(2,128)S(1)}, u32[]{:S(2)}, u32[]{:S(2)}) collective-permute-start(f32[2,1024]{1,0:T(2,128)S(1)} %pad_maximum_fusion.5), channel_id=1, source_target_pairs={{0,2},{1,3},{2,0},{3,1},{4,6},{5,7},{6,4},{7,5},{8,10},{9,11},{10,... | collective-permute-start | bytes 24584 | tf_op jit(solution)/shard_map/ppermute | solution.py:825
  112.8 5.7 %collective-permute-start.9 = (f32[2,1024]{1,0:T(2,128)S(1)}, f32[2,1024]{1,0:T(2,128)S(1)}, u32[]{:S(2)}, u32[]{:S(2)}) collective-permute-start(f32[2,1024]{1,0:T(2,128)S(1)} %pad_maximum_fusion.5), channel_id=1, source_target_pairs={{0,3},{1,0},{2,1},{3,2},{4,7},{5,4},{6,5},{7,6},{8,11},{9,8},{10,9... | collective-permute-start | bytes 24584 | tf_op jit(solution)/shard_map/ppermute | solution.py:825
  142.7 15.8 %copy-start.13 = (f32[32,128]{1,0:T(8,128)}, f32[32,128]{1,0:T(8,128)S(1)}, u32[]{:S(2)}) copy-start(f32[32,128]{1,0:T(8,128)S(1)} %reshape.130) | copy-start | bytes 49156
  142.8 1.2 copy-start.8
  152.3 2.4 %copy-start.10 = (bf16[1024,1024]{1,0:T(8,128)(2,1)S(1)}, bf16[1024,1024]{1,0:T(8,128)(2,1)}, u32[]{:S(2)}) copy-start(bf16[1024,1024]{1,0:T(8,128)(2,1)} %get-tuple-element.99) | copy-start | bytes 6291460
  154.8 2.9 %collective-permute-start.12 = (bf16[528,896]{1,0:T(8,128)(2,1)}, bf16[528,896]{1,0:T(8,128)(2,1)}, u32[]{:S(2)}, u32[]{:S(2)}) collective-permute-start(bf16[528,896]{1,0:T(8,128)(2,1)} %pad_maximum_fusion), channel_id=1, source_target_pairs={{0,4},{4,0},{8,12},{12,8},{16,20},{20,16},{24,28},{28,24},{1,5},{5... | collective-permute-start | bytes 2838536 | tf_op jit(solution)/shard_map/ppermute | solution.py:807
  155.8 6.1 %collective-permute-start.18 = (bf16[2,2,128,1024]{3,2,1,0:T(8,128)(2,1)}, bf16[2,2,128,1024]{3,2,1,0:T(8,128)(2,1)}, u32[]{:S(2)}, u32[]{:S(2)}) collective-permute-start(bf16[2,2,128,1024]{3,2,1,0:T(8,128)(2,1)} %dynamic-slice_bitcast_fusion), channel_id=1, source_target_pairs={{0,4},{4,0},{8,12},{12,8},{16,20},{20,16},{24,28},{28,24},{1,5},{5... | collective-permute-start | bytes 3145736 | tf_op jit(solution)/shard_map/ppermute | solution.py:814
  156.3 3.5 %copy-start.12 = (bf16[1024,896]{1,0:T(8,128)(2,1)S(1)}, bf16[1024,896]{1,0:T(8,128)(2,1)}, u32[]{:S(2)}) copy-start(bf16[1024,896]{1,0:T(8,128)(2,1)} %get-tuple-element.97) | copy-start | bytes 5505028
  158.4 1.4 copy-start.15
  159.8 1.9 copy-start.20
  159.8 2.1 copy-start.11
  160.2 13.2 %collective-permute-start.13 = (bf16[272,896]{1,0:T(8,128)(2,1)S(1)}, bf16[272,896]{1,0:T(8,128)(2,1)S(1)}, u32[]{:S(2)}, u32[]{:S(2)}) collective-permute-start(bf16[272,896]{1,0:T(8,128)(2,1)S(1)} %pad_maximum_fusion.1), channel_id=1, source_target_pairs={{0,8},{4,12},{8,0},{12,4},{16,24},{20,28},{24,16},{28,20},{1,9},{5... | collective-permute-start | bytes 1462280 | tf_op jit(solution)/shard_map/ppermute | solution.py:807
  163.7 16.9 %collective-permute-start.19 = (bf16[2,128,1024]{2,1,0:T(8,128)(2,1)S(1)}, bf16[2,128,1024]{2,1,0:T(8,128)(2,1)S(1)}, u32[]{:S(2)}, u32[]{:S(2)}) collective-permute-start(bf16[2,128,1024]{2,1,0:T(8,128)(2,1)S(1)} %dynamic-slice_bitcast_fusion.1), channel_id=1, source_target_pairs={{0,16},{4,20},{8,24},{12,28},{16,0},{20,4},{24,8},{28,12},{1,17},{... | collective-permute-start | bytes 1572872 | tf_op jit(solution)/shard_map/ppermute | solution.py:814
  178.2 0.7 copy-start.18
  179.0 7.8 %copy-start.14 = (f32[32,128]{1,0:T(8,128)S(1)}, f32[32,128]{1,0:T(8,128)}, u32[]{:S(2)}) copy-start(f32[32,128]{1,0:T(8,128)} %copy-done.13) | copy-start | bytes 49156
  179.0 7.8 %copy-start.16 = (bf16[112,128]{1,0:T(8,128)(2,1)S(1)}, bf16[112,128]{1,0:T(8,128)(2,1)}, u32[]{:S(2)}) copy-start(bf16[112,128]{1,0:T(8,128)(2,1)} %copy-done.15) | copy-start | bytes 86020
  179.0 7.8 %copy-start.17 = (bf16[112,128]{1,0:T(8,128)(2,1)S(1)}, bf16[112,128]{1,0:T(8,128)(2,1)}, u32[]{:S(2)}) copy-start(bf16[112,128]{1,0:T(8,128)(2,1)} %slice.126) | copy-start | bytes 86020
  179.0 7.6 %collective-permute-start.14 = (bf16[144,896]{1,0:T(8,128)(2,1)S(1)}, bf16[144,896]{1,0:T(8,128)(2,1)S(1)}, u32[]{:S(2)}, u32[]{:S(2)}) collective-permute-start(bf16[144,896]{1,0:T(8,128)(2,1)S(1)} %pad_maximum_fusion.2), channel_id=1, source_target_pairs={{0,16},{4,20},{8,24},{12,28},{16,0},{20,4},{24,8},{28,12},{1,17},{... | collective-permute-start | bytes 774152 | tf_op jit(solution)/shard_map/ppermute | solution.py:807
  180.8 22.0 %collective-permute-start.20 = (bf16[128,1024]{1,0:T(8,128)(2,1)S(1)}, bf16[128,1024]{1,0:T(8,128)(2,1)S(1)}, u32[]{:S(2)}, u32[]{:S(2)}) collective-permute-start(bf16[128,1024]{1,0:T(8,128)(2,1)S(1)} %dynamic-slice_bitcast_fusion.2), channel_id=1, source_target_pairs={{0,8},{4,12},{8,0},{12,4},{16,24},{20,28},{24,16},{28,20},{1,9},{5... | collective-permute-start | bytes 786440 | tf_op jit(solution)/shard_map/ppermute | solution.py:814
  186.8 16.9 %copy-start.2 = (bf16[1,256,1024]{2,1,0:T(8,128)(2,1)S(1)}, bf16[1,256,1024]{2,1,0:T(8,128)(2,1)}, u32[]{:S(2)}) copy-start(bf16[1,256,1024]{2,1,0:T(8,128)(2,1)} %param.17) | copy-start | bytes 1572868
  186.9 8.7 %collective-permute-start.17 = (bf16[280,128]{1,0:T(8,128)(2,1)S(1)}, bf16[280,128]{1,0:T(8,128)(2,1)S(1)}, u32[]{:S(2)}, u32[]{:S(2)}) collective-permute-start(bf16[280,128]{1,0:T(8,128)(2,1)S(1)} %fusion.5), channel_id=1, source_target_pairs={{0,1},{1,2},{2,3},{3,0},{4,5},{5,6},{6,7},{7,4},{8,9},{9,10},{10,1... | collective-permute-start | bytes 215048 | tf_op jit(solution)/shard_map/ppermute | solution.py:825
  187.8 12.5 %collective-permute-start.16 = (bf16[280,128]{1,0:T(8,128)(2,1)S(1)}, bf16[280,128]{1,0:T(8,128)(2,1)S(1)}, u32[]{:S(2)}, u32[]{:S(2)}) collective-permute-start(bf16[280,128]{1,0:T(8,128)(2,1)S(1)} %fusion.5), channel_id=1, source_target_pairs={{0,2},{1,3},{2,0},{3,1},{4,6},{5,7},{6,4},{7,5},{8,10},{9,11},{10,... | collective-permute-start | bytes 215048 | tf_op jit(solution)/shard_map/ppermute | solution.py:825
  189.7 10.6 %collective-permute-start.15 = (bf16[280,128]{1,0:T(8,128)(2,1)S(1)}, bf16[280,128]{1,0:T(8,128)(2,1)S(1)}, u32[]{:S(2)}, u32[]{:S(2)}) collective-permute-start(bf16[280,128]{1,0:T(8,128)(2,1)S(1)} %fusion.5), channel_id=1, source_target_pairs={{0,3},{1,0},{2,1},{3,2},{4,7},{5,4},{6,5},{7,6},{8,11},{9,8},{10,9... | collective-permute-start | bytes 215048 | tf_op jit(solution)/shard_map/ppermute | solution.py:825
  200.3 5.4 %copy-start.1 = (bf16[1,256,1024]{2,1,0:T(8,128)(2,1)S(1)}, bf16[1,256,1024]{2,1,0:T(8,128)(2,1)}, u32[]{:S(2)}) copy-start(bf16[1,256,1024]{2,1,0:T(8,128)(2,1)} %param.19) | copy-start | bytes 1572868
  205.8 1.0 copy-start.3
Sparse Core Ops, SparseCore 0:
  12.7 38.3 all-gather.2
  61.7 44.2 all-gather.4
  108.4 42.6 reduce-scatter.2
  156.5 48.2 reduce-scatter.4

commit v12 on v11

--- a/solution.py
+++ b/solution.py
@@ -889,7 +889,7 @@
         heads, size, place, near_hidden, weights
     )
     cot_full = lax.all_gather(
-        after(cotangent[0], near_hidden[0], near_hidden[-1]), "tensor", axis=0, tiled=True
+        after(cotangent[0], near_hidden[1], near_hidden[-2]), "tensor", axis=0, tiled=True
     )
     scaled, out_part, square, *saved = run_forward(
         heads, size, window, seg_row, weights, kernel_x, kernel_bc, head, channel, z_proj, x_proj,

time: 218 us -> 207 us (0.950); the launches traced: 215 us -> 206 us
  waiting for transfers between devices: 70.9 us -> 64.4 us
  local copies, waits for them, and re-layouts: 24.6 us -> 22.2 us
    all_gather x1, waiting for transfers between devices: 16.1 us -> 7.24 us  [shards(): lax.all_gather(after(cotangent[0], near_hidden[1], near_hidden[-2]), 'ten...]
    reduce_scatter x1, waiting for transfers between devices: 0.01 us -> 3.44 us  [shards(): lax.psum_scatter(in_part, 'tensor', scatter_dimension=0, tiled=True)]
    unnamed x66 -> x52, local copies, waits for them, and re-layouts: 7.57 us -> 8.12 us
  transfers between devices with their start and end apart: 25 -> 25, of which waited for: 12 -> 16; matrix products, arithmetic and copies ran while one was open for 12% -> 11% of each run, Pallas kernels for 30% -> 31%
where the time goes in v12:
time: 207 us; the launch traced here: 206 us
  Pallas kernels  65.9 us (32%)
  waiting for transfers between devices  64.4 us (31%)
  starting transfers between devices  30.8 us (15%)
  local copies, waits for them, and re-layouts  22.2 us (11%)
  between operations  14.4 us (7%)
  other arithmetic  8.46 us (4%)
    pallas_call x1, Pallas kernels, run_backward(): pl.pallas_call(functools.partial(backward_kernel, heads, size, full_inner...  24.1 us
    ppermute x3, waiting for transfers between devices, line_step(): lax.ppermute(left, axis, [(i, i - 1) for i in range(1, n - step + 1)])  20.3 us
    pallas_call x1, Pallas kernels, run_forward(): pl.pallas_call(functools.partial(forward_kernel, heads, size), grid=(bloc...  18 us
    ppermute x9, starting transfers between devices, around(): lax.ppermute(values, axis, [(i, (i - k) % n) for i in range(n)])  13.9 us
    ppermute x3, waiting for transfers between devices, cube_scatter(): lax.ppermute(jnp.concatenate([send.reshape(rows, columns), rider]), axis,...  13.7 us
    ppermute x3, waiting for transfers between devices, line_step(): lax.ppermute(right, axis, [(i, i + 1) for i in range(step - 1, n - 1)])  10.2 us
    ppermute x9, waiting for transfers between devices, around(): lax.ppermute(values, axis, [(i, (i - k) % n) for i in range(n)])  9.16 us
    pallas_call x1, Pallas kernels, run_project(): pl.pallas_call(functools.partial(project_kernel, heads, size, len(near)),...  8.37 us
  transfers between devices with their start and end apart: 25, of which 16 were waited for; matrix products, arithmetic and copies ran while one was open for 11% of the time, Pallas kernels for 31%

profile of v12, /device:TPU:0, one launch (start us, length us, event | category | flops | bytes accessed | tf_op | source)
XLA Modules:
  0.0 206.2 jit_solution(3817302276162638905)
XLA Ops:
  7.3 0.7 pad_maximum_fusion.6
  8.2 0.9 copy-done.4
  9.0 0.9 copy-done.5
  10.0 0.9 copy-done.6
  10.9 0.8 copy-done.7
  11.7 0.8 pack.1
  12.6 5.0 %collective-permute-start.3 = (bf16[256,1024]{1,0:T(8,128)(2,1)}, bf16[256,1024]{1,0:T(8,128)(2,1)S(1)}, u32[]{:S(2)}, u32[]{:S(2)}) collective-permute-start(bf16[256,1024]{1,0:T(8,128)(2,1)} %bitcast.74), channel_id=1, source_target_pairs={{0,1},{1,2},{2,3},{4,5},{5,6},{6,7},{8,9},{9,10},{10,11},{12,13},{... | collective-permute-start | bytes 1572872 | tf_op jit(solution)/shard_map/ppermute | solution.py:758
  17.6 1.3 collective-permute-start.6
  18.9 10.2 %collective-permute-done.3.refs_2_ = bf16[256,1024]{1,0:T(8,128)(2,1)S(1)} collective-permute-done((bf16[256,1024]{1,0:T(8,128)(2,1)}, bf16[256,1024]{1,0:T(8,128)(2,1)S(1)}, u32[]{:S(2)}, u32[]{:S(2)}) %collective-permute-start.3) | collective-permute-done | bytes 524320 | tf_op jit(solution)/shard_map/ppermute | solution.py:758
  29.1 0.7 collective-permute-start.4
  29.8 3.4 %collective-permute-done.6.refs_4_ = bf16[256,1024]{1,0:T(8,128)(2,1)S(1)} collective-permute-done((bf16[256,1024]{1,0:T(8,128)(2,1)}, bf16[256,1024]{1,0:T(8,128)(2,1)S(1)}, u32[]{:S(2)}, u32[]{:S(2)}) %collective-permute-start.6) | collective-permute-done | bytes 524320 | tf_op jit(solution)/shard_map/ppermute | solution.py:759
  33.1 1.3 collective-permute-start.7
  34.4 1.1 collective-permute-start
  35.5 3.1 %collective-permute-start.1 = (s32[256]{0:T(256)}, s32[256]{0:T(256)S(1)}, u32[]{:S(2)}, u32[]{:S(2)}) collective-permute-start(s32[256]{0:T(256)} %bitcast.93), channel_id=1, source_target_pairs={{0,2},{1,3},{2,0},{3,1},{4,6},{5,7},{6,4},{7,5},{8,10},{9,11},{10,... | collective-permute-start | bytes 3080 | tf_op jit(solution)/shard_map/ppermute | solution.py:825
  38.6 1.9 collective-permute-start.2
  40.4 0.7 broadcast_in_dim.39
  41.2 0.7 pad_maximum_fusion.7.channel_ref
  41.9 0.7 pad_maximum_fusion.4.kernel_bc_ref
  42.6 5.1 %collective-permute-done.7.refs_5_ = bf16[256,1024]{1,0:T(8,128)(2,1)S(1)} collective-permute-done((bf16[256,1024]{1,0:T(8,128)(2,1)S(1)}, bf16[256,1024]{1,0:T(8,128)(2,1)S(1)}, u32[]{:S(2)}, u32[]{:S(2)}) %collective-permute-start.7) | collective-permute-done | bytes 524320 | tf_op jit(solution)/shard_map/ppermute | solution.py:759
  48.0 1.0 collective-permute-done.1
  49.0 0.7 collective-permute-start.5
  49.7 1.3 collective-permute-start.8
  51.2 11.8 %collective-permute-done.8.refs_6_ = bf16[256,1024]{1,0:T(8,128)(2,1)S(1)} collective-permute-done((bf16[256,1024]{1,0:T(8,128)(2,1)S(1)}, bf16[256,1024]{1,0:T(8,128)(2,1)S(1)}, u32[]{:S(2)}, u32[]{:S(2)}) %collective-permute-start.8) | collective-permute-done | bytes 524320 | tf_op jit(solution)/shard_map/ppermute | solution.py:759
  63.0 0.8 copy-done.21
  63.8 8.4 %project.1 = (bf16[1024,1024]{1,0:T(8,128)(2,1)}, bf16[1024,1024]{1,0:T(8,128)(2,1)}, f32[1024,512]{1,0:T(8,128)}, f32[1024,512]{1,0:T(8,128)}, f32[1024,384]{1,0:T(8,128)}, /*index=5*/f32[8,1024]{1,0:T(8,128)S(1)}) custom-call(s32[1]{0:T(128)} %bitcast.8.place_ref, bf16[256,1024]{1,0:T(8,128)(2,1)S(1)} %collective-permute-done.5.refs_0_, ...), custom_call_target="tpu_custom_call" | custom-call | flops 8000000000 | bytes 1048576 | tf_op jit(solution)/shard_map/project/pallas_call | solution.py:520
  72.2 1.0 broadcast_in_dim.34.window_ref
  73.2 18.0 %forward.1 = (bf16[1024,512]{1,0:T(8,128)(2,1)}, bf16[1024,1024]{1,0:T(8,128)(2,1)}, f32[8,1024]{1,0:T(8,128)S(1)}, f32[4,128,512]{2,1,0:T(8,128)}, f32[4,8,512]...) custom-call(s32[1040,128]{1,0:T(8,128)} %broadcast_in_dim.34.window_, ...), custom_call_target="tpu_custom_call" | custom-call | flops 14000000000 | bytes 1048576 | tf_op jit(solution)/shard_map/forward/pallas_call | solution.py:581
  91.3 7.2 %all-gather.5.cloned.1.call-done.cot_ref = bf16[1024,1024]{1,0:T(8,128)(2,1)} async-done(((bf16[256,1024]{1,0:T(8,128)(2,1)}), bf16[1024,1024]{1,0:T(8,128)(2,1)}) %all-gather.5.cloned.1.call-update) | async-done | bytes 2097168 | tf_op jit(solution)/shard_map/all_gather | solution.py:891
  98.6 5.0 %out_gradient.1 = (f32[1024,512]{1,0:T(8,128)}, f32[8,1024]{1,0:T(8,128)S(1)}) custom-call(bf16[1024,1024]{1,0:T(8,128)(2,1)} %all-gather.5.cloned.1.call-done.cot_ref, bf16[1024,1920]{1,0:T(8,128)(2,1)} %all-gather.3.cloned.1.call-done.refs_7_.weights_ref, bf16[1024,512]{1,0:T(8,128)(2,1)S(1)} %copy-done.9, s32[1040,128]{1,0:T(8,128)S(1)} %copy-done), custom_call_target="tpu_custom_call" | custom-call | flops 5000000000 | bytes 1048576 | tf_op jit(solution)/shard_map/out_gradient/pallas_call | solution.py:620
  103.7 1.7 collective-permute-start.10
  105.4 2.3 %collective-permute-start.9 = (f32[2,1024]{1,0:T(2,128)S(1)}, f32[2,1024]{1,0:T(2,128)S(1)}, u32[]{:S(2)}, u32[]{:S(2)}) collective-permute-start(f32[2,1024]{1,0:T(2,128)S(1)} %pad_maximum_fusion.5), channel_id=1, source_target_pairs={{0,3},{1,0},{2,1},{3,2},{4,7},{5,4},{6,5},{7,6},{8,11},{9,8},{10,9... | collective-permute-start | bytes 24584 | tf_op jit(solution)/shard_map/ppermute | solution.py:825
  107.6 1.6 collective-permute-done.11
  109.2 1.8 collective-permute-done.9
  111.1 24.1 %backward.1 = (bf16[1024,1408]{1,0:T(8,128)(2,1)}, bf16[1024,1024]{1,0:T(8,128)(2,1)}, bf16[1024,512]{1,0:T(8,128)(2,1)}, f32[8,512]{1,0:T(8,128)S(1)}, f32[8,25...) custom-call(f32[8,1024]{1,0:T(8,128)S(1)} %pad.29.stat_ref, ...), custom_call_target="tpu_custom_call" | custom-call | flops 2000000000 | bytes 1048576 | tf_op jit(solution)/shard_map/backward/pallas_call | solution.py:689
  135.4 1.2 copy-done.8
  136.6 8.3 %weight_gradients.1 = (bf16[1024,896]{1,0:T(8,128)(2,1)}, bf16[1024,1024]{1,0:T(8,128)(2,1)}) custom-call(bf16[1024,1024]{1,0:T(8,128)(2,1)} %all-gather.5.cloned.1.call-done.cot_ref, bf16[1024,512]{1,0:T(8,128)(2,1)S(1)} %copy-done.8, bf16[1024,1024]{1,0:T(8,128)(2,1)} %get-tuple-element.95.tokens_ref, bf16[1024,1408]{1,0:T(8,128)(2,1)} %get-tuple-element.96.grads_ref), custom_call_target="tpu_custom_call" | custom-call | flops 7000000000 | bytes 1048576 | tf_op jit(solution)/shard_map/weight_gradients/pallas_call | solution.py:654
  144.9 1.4 constant_dynamic-slice_fusion.1
  146.3 1.0 pad_maximum_fusion
  147.3 1.1 dynamic-slice_bitcast_fusion
  149.0 1.2 collective-permute-done.12
  150.2 0.8 slice.152
  151.1 1.3 slice.154
  152.7 1.5 collective-permute-start.13
  154.4 1.7 fusion
  156.1 1.6 collective-permute-start.19
  157.7 8.2 %collective-permute-done.13 = bf16[272,896]{1,0:T(8,128)(2,1)S(1)} collective-permute-done((bf16[272,896]{1,0:T(8,128)(2,1)S(1)}, bf16[272,896]{1,0:T(8,128)(2,1)S(1)}, u32[]{:S(2)}, u32[]{:S(2)}) %collective-permute-start.13) | collective-permute-done | bytes 487456 | tf_op jit(solution)/shard_map/ppermute | solution.py:807
  165.9 0.8 copy-done.13
  166.9 1.1 slice.157
  168.1 1.5 collective-permute-start.14
  170.2 1.3 collective-permute-start.20
  171.5 4.3 %collective-permute-done.14 = bf16[144,896]{1,0:T(8,128)(2,1)S(1)} collective-permute-done((bf16[144,896]{1,0:T(8,128)(2,1)S(1)}, bf16[144,896]{1,0:T(8,128)(2,1)S(1)}, u32[]{:S(2)}, u32[]{:S(2)}) %collective-permute-start.14) | collective-permute-done | bytes 258080 | tf_op jit(solution)/shard_map/ppermute | solution.py:807
  176.0 0.8 collective-permute-start.17
  176.8 1.9 collective-permute-start.16
  178.7 1.1 collective-permute-start.15
  181.0 0.7 slice.176
  181.7 0.7 copy.46
  183.7 1.0 collective-permute-done.17
  184.7 3.5 %collective-permute-done.16 = bf16[280,128]{1,0:T(8,128)(2,1)S(1)} collective-permute-done((bf16[280,128]{1,0:T(8,128)(2,1)S(1)}, bf16[280,128]{1,0:T(8,128)(2,1)S(1)}, u32[]{:S(2)}, u32[]{:S(2)}) %collective-permute-start.16) | collective-permute-done | bytes 71712 | tf_op jit(solution)/shard_map/ppermute | solution.py:825
  188.5 0.7 reshape.143
  191.0 0.8 fusion.10
  191.8 2.1 fusion.4
  193.9 3.4 %reduce-scatter.5.cloned.1.call-done.sum_ref = bf16[256,1024]{1,0:T(8,128)(2,1)} async-done(((bf16[1024,1024]{1,0:T(8,128)(2,1)}), bf16[256,1024]{1,0:T(8,128)(2,1)}) %reduce-scatter.5.cloned.1.call-update) | async-done | bytes 524304 | tf_op jit(solution)/shard_map/reduce_scatter | solution.py:910
  197.3 1.0 copy-done.3
  198.4 1.3 finish.1
  (129 shorter events, 7.6 us)
Async XLA Ops:
  7.2 40.7 %copy-start.15 = (s32[1,256]{1,0:T(1,128)S(1)}, s32[1,256]{1,0:T(1,128)}, u32[]{:S(2)}) copy-start(s32[1,256]{1,0:T(1,128)} %param.18) | copy-start | bytes 3076
  7.2 40.7 %copy-start.16 = (f32[512]{0:T(512)S(1)}, f32[512]{0:T(512)}, u32[]{:S(2)}) copy-start(f32[512]{0:T(512)} %param.26) | copy-start | bytes 6148
  7.2 40.7 %copy-start.14 = (f32[4,512]{1,0:T(4,128)S(1)}, f32[4,512]{1,0:T(4,128)}, u32[]{:S(2)}) copy-start(f32[4,512]{1,0:T(4,128)} %param.25) | copy-start | bytes 24580
  7.2 40.7 %copy-start.17 = (f32[8]{0:T(128)S(1)}, f32[8]{0:T(128)}, u32[]{:S(2)}) copy-start(f32[8]{0:T(128)} %param.30) | copy-start | bytes 100
  7.2 40.7 %copy-start.18 = (f32[8]{0:T(128)S(1)}, f32[8]{0:T(128)}, u32[]{:S(2)}) copy-start(f32[8]{0:T(128)} %param.29) | copy-start | bytes 100
  7.2 55.8 %all-gather.3.cloned.1.call-start = ((), (), s32[]{:S(2)}) async-start(), calls=%async_computation.2 | async-start | bytes 4423680 | tf_op jit(solution)/shard_map/all_gather | solution.py:872
  8.1 0.9 copy-start.4
  9.0 0.9 copy-start.5
  10.0 0.9 copy-start.6
  10.9 0.8 copy-start.7
  12.6 86.0 %all-gather.5.cloned.1.call-start = ((), (), s32[]{:S(2)}) async-start(), calls=%async_computation.4 | async-start | bytes 2621440 | tf_op jit(solution)/shard_map/all_gather | solution.py:891
  12.6 16.4 %collective-permute-start.3 = (bf16[256,1024]{1,0:T(8,128)(2,1)}, bf16[256,1024]{1,0:T(8,128)(2,1)S(1)}, u32[]{:S(2)}, u32[]{:S(2)}) collective-permute-start(bf16[256,1024]{1,0:T(8,128)(2,1)} %bitcast.74), channel_id=1, source_target_pairs={{0,1},{1,2},{2,3},{4,5},{5,6},{6,7},{8,9},{9,10},{10,11},{12,13},{... | collective-permute-start | bytes 1572872 | tf_op jit(solution)/shard_map/ppermute | solution.py:758
  17.6 15.5 %collective-permute-start.6 = (bf16[256,1024]{1,0:T(8,128)(2,1)}, bf16[256,1024]{1,0:T(8,128)(2,1)S(1)}, u32[]{:S(2)}, u32[]{:S(2)}) collective-permute-start(bf16[256,1024]{1,0:T(8,128)(2,1)} %bitcast.75), channel_id=1, source_target_pairs={{1,0},{2,1},{3,2},{5,4},{6,5},{7,6},{9,8},{10,9},{11,10},{13,12},{... | collective-permute-start | bytes 1572872 | tf_op jit(solution)/shard_map/ppermute | solution.py:759
  29.1 13.6 %collective-permute-start.4 = (bf16[256,1024]{1,0:T(8,128)(2,1)S(1)}, bf16[256,1024]{1,0:T(8,128)(2,1)S(1)}, u32[]{:S(2)}, u32[]{:S(2)}) collective-permute-start(bf16[256,1024]{1,0:T(8,128)(2,1)S(1)} %collective-permute-done.3.refs_2_), channel_id=1, source_target_pairs={{1,2},{2,3},{5,6},{6,7},{9,10},{10,11},{13,14},{14,15},{17,18},{18... | collective-permute-start | bytes 1572872 | tf_op jit(solution)/shard_map/ppermute | solution.py:758
  33.1 29.9 %copy-start.19 = (bf16[256,1024]{1,0:T(8,128)(2,1)}, bf16[256,1024]{1,0:T(8,128)(2,1)S(1)}, u32[]{:S(2)}) copy-start(bf16[256,1024]{1,0:T(8,128)(2,1)S(1)} %collective-permute-done.6.refs_4_) | copy-start | bytes 1572868
  33.1 14.7 %collective-permute-start.7 = (bf16[256,1024]{1,0:T(8,128)(2,1)S(1)}, bf16[256,1024]{1,0:T(8,128)(2,1)S(1)}, u32[]{:S(2)}, u32[]{:S(2)}) collective-permute-start(bf16[256,1024]{1,0:T(8,128)(2,1)S(1)} %collective-permute-done.6.refs_4_), channel_id=1, source_target_pairs={{1,0},{2,1},{5,4},{6,5},{9,8},{10,9},{13,12},{14,13},{17,16},{18,1... | collective-permute-start | bytes 1572872 | tf_op jit(solution)/shard_map/ppermute | solution.py:759
  34.4 13.5 %collective-permute-start = (s32[256]{0:T(256)}, s32[256]{0:T(256)S(1)}, u32[]{:S(2)}, u32[]{:S(2)}) collective-permute-start(s32[256]{0:T(256)} %bitcast.92), channel_id=1, source_target_pairs={{0,3},{1,0},{2,1},{3,2},{4,7},{5,4},{6,5},{7,6},{8,11},{9,8},{10,9... | collective-permute-start | bytes 3080 | tf_op jit(solution)/shard_map/ppermute | solution.py:825
  35.5 13.5 %collective-permute-start.1 = (s32[256]{0:T(256)}, s32[256]{0:T(256)S(1)}, u32[]{:S(2)}, u32[]{:S(2)}) collective-permute-start(s32[256]{0:T(256)} %bitcast.93), channel_id=1, source_target_pairs={{0,2},{1,3},{2,0},{3,1},{4,6},{5,7},{6,4},{7,5},{8,10},{9,11},{10,... | collective-permute-start | bytes 3080 | tf_op jit(solution)/shard_map/ppermute | solution.py:825
  38.6 12.4 %collective-permute-start.2 = (s32[256]{0:T(256)}, s32[256]{0:T(256)S(1)}, u32[]{:S(2)}, u32[]{:S(2)}) collective-permute-start(s32[256]{0:T(256)} %bitcast.94), channel_id=1, source_target_pairs={{0,1},{1,2},{2,3},{3,0},{4,5},{5,6},{6,7},{7,4},{8,9},{9,10},{10,1... | collective-permute-start | bytes 3080 | tf_op jit(solution)/shard_map/ppermute | solution.py:825
  47.8 15.3 %copy-start.20 = (bf16[256,1024]{1,0:T(8,128)(2,1)}, bf16[256,1024]{1,0:T(8,128)(2,1)S(1)}, u32[]{:S(2)}) copy-start(bf16[256,1024]{1,0:T(8,128)(2,1)S(1)} %collective-permute-done.7.refs_5_) | copy-start | bytes 1572868
  47.8 144.0 %reduce-scatter.3.cloned.1.call-start = ((), (), s32[]{:S(2)}) async-start(), calls=%async_computation.3 | async-start | bytes 2621440 | tf_op jit(solution)/shard_map/reduce_scatter | solution.py:899
  49.0 2.2 %collective-permute-start.5 = (bf16[256,1024]{1,0:T(8,128)(2,1)S(1)}, bf16[256,1024]{1,0:T(8,128)(2,1)S(1)}, u32[]{:S(2)}, u32[]{:S(2)}) collective-permute-start(bf16[256,1024]{1,0:T(8,128)(2,1)S(1)} %collective-permute-done.4.refs_1_), channel_id=1, source_target_pairs={{2,3},{6,7},{10,11},{14,15},{18,19},{22,23},{26,27},{30,31}} | collective-permute-start | bytes 1572872 | tf_op jit(solution)/shard_map/ppermute | solution.py:758
  49.7 13.4 %collective-permute-start.8 = (bf16[256,1024]{1,0:T(8,128)(2,1)S(1)}, bf16[256,1024]{1,0:T(8,128)(2,1)S(1)}, u32[]{:S(2)}, u32[]{:S(2)}) collective-permute-start(bf16[256,1024]{1,0:T(8,128)(2,1)S(1)} %collective-permute-done.7.refs_5_), channel_id=1, source_target_pairs={{1,0},{5,4},{9,8},{13,12},{17,16},{21,20},{25,24},{29,28}} | collective-permute-start | bytes 1572872 | tf_op jit(solution)/shard_map/ppermute | solution.py:759
  63.0 0.8 copy-start.21
  91.2 7.3 %copy-start = (s32[1040,128]{1,0:T(8,128)S(1)}, s32[1040,128]{1,0:T(8,128)}, u32[]{:S(2)}) copy-start(s32[1040,128]{1,0:T(8,128)} %broadcast_in_dim.34.window_ref) | copy-start | bytes 1597444
  91.3 7.3 %copy-start.9 = (bf16[1024,512]{1,0:T(8,128)(2,1)S(1)}, bf16[1024,512]{1,0:T(8,128)(2,1)}, u32[]{:S(2)}) copy-start(bf16[1024,512]{1,0:T(8,128)(2,1)} %get-tuple-element.64.scaled_ref) | copy-start | bytes 3145732
  91.3 106.0 %reduce-scatter.5.cloned.1.call-start = ((), (), s32[]{:S(2)}) async-start(), calls=%async_computation.5 | async-start | bytes 2621440 | tf_op jit(solution)/shard_map/reduce_scatter | solution.py:910
  103.6 5.6 %collective-permute-start.11 = (f32[2,1024]{1,0:T(2,128)S(1)}, f32[2,1024]{1,0:T(2,128)S(1)}, u32[]{:S(2)}, u32[]{:S(2)}) collective-permute-start(f32[2,1024]{1,0:T(2,128)S(1)} %pad_maximum_fusion.5), channel_id=1, source_target_pairs={{0,1},{1,2},{2,3},{3,0},{4,5},{5,6},{6,7},{7,4},{8,9},{9,10},{10,1... | collective-permute-start | bytes 24584 | tf_op jit(solution)/shard_map/ppermute | solution.py:825
  103.7 5.6 %collective-permute-start.10 = (f32[2,1024]{1,0:T(2,128)S(1)}, f32[2,1024]{1,0:T(2,128)S(1)}, u32[]{:S(2)}, u32[]{:S(2)}) collective-permute-start(f32[2,1024]{1,0:T(2,128)S(1)} %pad_maximum_fusion.5), channel_id=1, source_target_pairs={{0,2},{1,3},{2,0},{3,1},{4,6},{5,7},{6,4},{7,5},{8,10},{9,11},{10,... | collective-permute-start | bytes 24584 | tf_op jit(solution)/shard_map/ppermute | solution.py:825
  105.4 5.7 %collective-permute-start.9 = (f32[2,1024]{1,0:T(2,128)S(1)}, f32[2,1024]{1,0:T(2,128)S(1)}, u32[]{:S(2)}, u32[]{:S(2)}) collective-permute-start(f32[2,1024]{1,0:T(2,128)S(1)} %pad_maximum_fusion.5), channel_id=1, source_target_pairs={{0,3},{1,0},{2,1},{3,2},{4,7},{5,4},{6,5},{7,6},{8,11},{9,8},{10,9... | collective-permute-start | bytes 24584 | tf_op jit(solution)/shard_map/ppermute | solution.py:825
  135.4 1.2 copy-start.8
  144.9 2.4 %copy-start.10 = (bf16[1024,1024]{1,0:T(8,128)(2,1)S(1)}, bf16[1024,1024]{1,0:T(8,128)(2,1)}, u32[]{:S(2)}) copy-start(bf16[1024,1024]{1,0:T(8,128)(2,1)} %get-tuple-element.99) | copy-start | bytes 6291460
  147.3 2.9 %collective-permute-start.12 = (bf16[528,896]{1,0:T(8,128)(2,1)}, bf16[528,896]{1,0:T(8,128)(2,1)}, u32[]{:S(2)}, u32[]{:S(2)}) collective-permute-start(bf16[528,896]{1,0:T(8,128)(2,1)} %pad_maximum_fusion), channel_id=1, source_target_pairs={{0,4},{4,0},{8,12},{12,8},{16,20},{20,16},{24,28},{28,24},{1,5},{5... | collective-permute-start | bytes 2838536 | tf_op jit(solution)/shard_map/ppermute | solution.py:807
  148.4 6.0 %collective-permute-start.18 = (bf16[2,2,128,1024]{3,2,1,0:T(8,128)(2,1)}, bf16[2,2,128,1024]{3,2,1,0:T(8,128)(2,1)}, u32[]{:S(2)}, u32[]{:S(2)}) collective-permute-start(bf16[2,2,128,1024]{3,2,1,0:T(8,128)(2,1)} %dynamic-slice_bitcast_fusion), channel_id=1, source_target_pairs={{0,4},{4,0},{8,12},{12,8},{16,20},{20,16},{24,28},{28,24},{1,5},{5... | collective-permute-start | bytes 3145736 | tf_op jit(solution)/shard_map/ppermute | solution.py:814
  148.9 3.4 %copy-start.12 = (bf16[1024,896]{1,0:T(8,128)(2,1)S(1)}, bf16[1024,896]{1,0:T(8,128)(2,1)}, u32[]{:S(2)}) copy-start(bf16[1024,896]{1,0:T(8,128)(2,1)} %get-tuple-element.97) | copy-start | bytes 5505028
  152.3 2.1 copy-start.11
  152.7 13.2 %collective-permute-start.13 = (bf16[272,896]{1,0:T(8,128)(2,1)S(1)}, bf16[272,896]{1,0:T(8,128)(2,1)S(1)}, u32[]{:S(2)}, u32[]{:S(2)}) collective-permute-start(bf16[272,896]{1,0:T(8,128)(2,1)S(1)} %pad_maximum_fusion.1), channel_id=1, source_target_pairs={{0,8},{4,12},{8,0},{12,4},{16,24},{20,28},{24,16},{28,20},{1,9},{5... | collective-permute-start | bytes 1462280 | tf_op jit(solution)/shard_map/ppermute | solution.py:807
  156.1 13.8 %collective-permute-start.19 = (bf16[2,128,1024]{2,1,0:T(8,128)(2,1)S(1)}, bf16[2,128,1024]{2,1,0:T(8,128)(2,1)S(1)}, u32[]{:S(2)}, u32[]{:S(2)}) collective-permute-start(bf16[2,128,1024]{2,1,0:T(8,128)(2,1)S(1)} %dynamic-slice_bitcast_fusion.1), channel_id=1, source_target_pairs={{0,16},{4,20},{8,24},{12,28},{16,0},{20,4},{24,8},{28,12},{1,17},{... | collective-permute-start | bytes 1572872 | tf_op jit(solution)/shard_map/ppermute | solution.py:814
  165.9 0.8 copy-start.13
  168.1 7.6 %collective-permute-start.14 = (bf16[144,896]{1,0:T(8,128)(2,1)S(1)}, bf16[144,896]{1,0:T(8,128)(2,1)S(1)}, u32[]{:S(2)}, u32[]{:S(2)}) collective-permute-start(bf16[144,896]{1,0:T(8,128)(2,1)S(1)} %pad_maximum_fusion.2), channel_id=1, source_target_pairs={{0,16},{4,20},{8,24},{12,28},{16,0},{20,4},{24,8},{28,12},{1,17},{... | collective-permute-start | bytes 774152 | tf_op jit(solution)/shard_map/ppermute | solution.py:807
  170.2 20.7 %collective-permute-start.20 = (bf16[128,1024]{1,0:T(8,128)(2,1)S(1)}, bf16[128,1024]{1,0:T(8,128)(2,1)S(1)}, u32[]{:S(2)}, u32[]{:S(2)}) collective-permute-start(bf16[128,1024]{1,0:T(8,128)(2,1)S(1)} %dynamic-slice_bitcast_fusion.2), channel_id=1, source_target_pairs={{0,8},{4,12},{8,0},{12,4},{16,24},{20,28},{24,16},{28,20},{1,9},{5... | collective-permute-start | bytes 786440 | tf_op jit(solution)/shard_map/ppermute | solution.py:814
  175.9 15.9 %copy-start.2 = (bf16[1,256,1024]{2,1,0:T(8,128)(2,1)S(1)}, bf16[1,256,1024]{2,1,0:T(8,128)(2,1)}, u32[]{:S(2)}) copy-start(bf16[1,256,1024]{2,1,0:T(8,128)(2,1)} %param.17) | copy-start | bytes 1572868
  176.0 8.7 %collective-permute-start.17 = (bf16[280,128]{1,0:T(8,128)(2,1)S(1)}, bf16[280,128]{1,0:T(8,128)(2,1)S(1)}, u32[]{:S(2)}, u32[]{:S(2)}) collective-permute-start(bf16[280,128]{1,0:T(8,128)(2,1)S(1)} %fusion.5), channel_id=1, source_target_pairs={{0,1},{1,2},{2,3},{3,0},{4,5},{5,6},{6,7},{7,4},{8,9},{9,10},{10,1... | collective-permute-start | bytes 215048 | tf_op jit(solution)/shard_map/ppermute | solution.py:825
  176.8 11.4 %collective-permute-start.16 = (bf16[280,128]{1,0:T(8,128)(2,1)S(1)}, bf16[280,128]{1,0:T(8,128)(2,1)S(1)}, u32[]{:S(2)}, u32[]{:S(2)}) collective-permute-start(bf16[280,128]{1,0:T(8,128)(2,1)S(1)} %fusion.5), channel_id=1, source_target_pairs={{0,2},{1,3},{2,0},{3,1},{4,6},{5,7},{6,4},{7,5},{8,10},{9,11},{10,... | collective-permute-start | bytes 215048 | tf_op jit(solution)/shard_map/ppermute | solution.py:825
  178.7 9.7 %collective-permute-start.15 = (bf16[280,128]{1,0:T(8,128)(2,1)S(1)}, bf16[280,128]{1,0:T(8,128)(2,1)S(1)}, u32[]{:S(2)}, u32[]{:S(2)}) collective-permute-start(bf16[280,128]{1,0:T(8,128)(2,1)S(1)} %fusion.5), channel_id=1, source_target_pairs={{0,3},{1,0},{2,1},{3,2},{4,7},{5,4},{6,5},{7,6},{8,11},{9,8},{10,9... | collective-permute-start | bytes 215048 | tf_op jit(solution)/shard_map/ppermute | solution.py:825
  188.4 8.9 %copy-start.1 = (bf16[1,256,1024]{2,1,0:T(8,128)(2,1)S(1)}, bf16[1,256,1024]{2,1,0:T(8,128)(2,1)}, u32[]{:S(2)}) copy-start(bf16[1,256,1024]{2,1,0:T(8,128)(2,1)} %param.19) | copy-start | bytes 1572868
  197.3 1.0 copy-start.3
Sparse Core Ops, SparseCore 0:
  12.7 38.3 all-gather.2
  52.6 45.9 all-gather.4
  100.9 42.6 reduce-scatter.2
  149.1 48.2 reduce-scatter.4
